TPU v7x, 128 devices: a whole 4x4x4 slice. The times are simulated.
128 devices in a mesh: gx: 32 (over y, x, core), gy: 4 (over z).
Axes of the slice: x: 4, y: 4, z: 4, core: 2. Of those that a mesh axis runs over, the one named last changes fastest.
Arguments:
- flux_x: float32 [5, 512, 128, 128], P(None, 'gx', 'gy'), may hold values from -6 to 6
- flux_y: float32 [5, 512, 128, 128], P(None, 'gx', 'gy'), may hold values from -6 to 6
- state: float32 [5, 512, 128, 128], P(None, 'gx', 'gy'), may hold values from -10 to 10
- metric_x: float32 [512, 128], P('gx', 'gy'), may hold values from 0.5 to 2
- metric_y: float32 [512, 128], P('gx', 'gy'), may hold values from 0.5 to 2
- filter_gap: float32 [512], P('gx'), may hold values from 7.8125e-05 to 0.0003125
Outputs:
- section_state: float32 [5, 512, 128, 128], P(None, 'gx', 'gy')
All inputs are finite; a program needn't handle non-finite values.
Results may differ from a plain program's by a relative error of at most 0.0003.
Values sent between devices are 32-bit elements; how exact they have to be, the bound alone decides.
No kernel may reach another device: no remote copies, remote signals or barrier semaphores. Data moves between devices by JAX's collectives and lax.ppermute only.
A program may use at most 64 MiB of HBM per device.

v0:
```python
import jax
import jax.numpy as jnp
from jax import lax
from jax.sharding import PartitionSpec as P

STEP_SIZE = 0.5
DERIV_ALPHA = 1.0 / 3.0
PRECISE = lax.Precision.HIGHEST
STENCIL_WEIGHTS = (4.0 / 5.0, -1.0 / 5.0, 4.0 / 105.0, -1.0 / 280.0)


def carried_in(part, axis, combine, identity, reverse):
    count = lax.axis_size(axis)
    place = lax.axis_index(axis)
    ahead = count - 1 - place if reverse else place
    gathered = jax.tree.map(lambda a: lax.all_gather(a, axis), part)
    state = jax.tree.map(lambda a, e: jnp.zeros_like(a) + jnp.asarray(e, a.dtype), part, identity)

    def one(step, state):
        source = count - 1 - step if reverse else step
        return combine(
            state, jax.tree.map(lambda a: lax.dynamic_index_in_dim(a, source, 0, False), gathered)
        )

    return lax.fori_loop(0, ahead, one, state)


def with_halo(x, sides, width, wrap):
    for axis, dim in sides:
        count, length = (lax.axis_size(axis), x.shape[dim])
        up = [(i, (i + 1) % count) for i in range(count if wrap else count - 1)]
        down = [(j, i) for i, j in up]
        last = lax.slice_in_dim(x, length - width, length, axis=dim)
        first = lax.slice_in_dim(x, 0, width, axis=dim)
        before = lax.ppermute(last, axis, up)
        after = lax.ppermute(first, axis, down)
        x = jnp.concatenate([before, x, after], axis=dim)
    return x


def invert_block(couple):
    extent = couple.shape[0]
    row_ids = lax.broadcasted_iota(jnp.int32, (extent, extent), 0)
    col_ids = lax.broadcasted_iota(jnp.int32, (extent, extent), 1)
    matrix = jnp.where(row_ids == col_ids, 1.0, 0.0) + jnp.where(
        jnp.abs(row_ids - col_ids) == 1, couple[:, None], 0.0
    )
    augmented = jnp.concatenate([matrix, jnp.eye(extent, dtype=jnp.float32)], axis=1)
    for column in range(extent):
        pivot_row = augmented[column] / augmented[column, column]
        augmented = augmented - augmented[:, column : column + 1] * pivot_row[None, :]
        augmented = augmented.at[column].set(pivot_row)
    return augmented[:, extent:]


def join_pieces(earlier, later):
    head_a, tail_a, hleft_a, hright_a, tleft_a, tright_a = earlier
    head_b, tail_b, hleft_b, hright_b, tleft_b, tright_b = later
    divisor = 1.0 - tright_a * hleft_b
    tail_mid = (tail_a + tright_a * head_b) / divisor
    head_mid = (head_b + hleft_b * tail_a) / divisor
    return (
        head_a + hright_a * head_mid,
        tail_b + tleft_b * tail_mid,
        hleft_a + hright_a * hleft_b * tleft_a / divisor,
        hright_a * hright_b / divisor,
        tleft_b * tleft_a / divisor,
        tright_b + tleft_b * tright_a * hright_b / divisor,
    )


def swapped_join(earlier, later):
    return join_pieces(later, earlier)


def outer_values(head_vals, tail_vals, head_left, head_right, tail_left, tail_right):
    zeros_val = jnp.zeros_like(head_vals)
    zeros_coef = jnp.zeros_like(head_left)
    ones_coef = jnp.ones_like(head_left)
    identity = (zeros_val, zeros_val, zeros_coef, ones_coef, ones_coef, zeros_coef)
    before = carried_in(
        (head_vals, tail_vals, head_left, head_right, tail_left, tail_right),
        "gx",
        join_pieces,
        identity,
        False,
    )
    from_above = carried_in(
        (head_vals, tail_vals, head_left, head_right, tail_left, tail_right),
        "gx",
        swapped_join,
        identity,
        True,
    )
    return (before[1], before[5], from_above[0], from_above[2])


def per_device(flux_x, flux_y, state, metric_x, metric_y, filter_gap):
    extent = flux_x.shape[1]
    stacked = jnp.stack([flux_x, state])
    padded = with_halo(stacked, (("gx", 2),), 3, False)

    def offset(source, shift_by):
        return lax.slice_in_dim(source, 3 + shift_by, 3 + shift_by + extent, axis=1)

    flux_pad = padded[0]
    state_pad = padded[1]
    rhs_deriv = 7.0 / 9.0 * (offset(flux_pad, 1) - offset(flux_pad, -1)) + 1.0 / 36.0 * (
        offset(flux_pad, 2) - offset(flux_pad, -2)
    )
    filter_alpha = 0.5 - filter_gap
    weight = filter_alpha[None, :, None, None]
    rhs_filter = (11.0 / 16.0 + 5.0 * weight / 8.0) * state
    rhs_filter = rhs_filter + (15.0 / 32.0 + 17.0 * weight / 16.0) / 2.0 * (
        offset(state_pad, 1) + offset(state_pad, -1)
    )
    rhs_filter = rhs_filter + (-3.0 / 16.0 + 3.0 * weight / 8.0) / 2.0 * (
        offset(state_pad, 2) + offset(state_pad, -2)
    )
    rhs_filter = rhs_filter + (1.0 / 32.0 - weight / 16.0) / 2.0 * (
        offset(state_pad, 3) + offset(state_pad, -3)
    )
    couples = jnp.stack([jnp.full((extent,), DERIV_ALPHA, jnp.float32), filter_alpha])
    inverses = jnp.stack([invert_block(couples[0]), invert_block(couples[1])])
    solved = jnp.einsum(
        "sij,svjyz->sviyz", inverses, jnp.stack([rhs_deriv, rhs_filter]), precision=PRECISE
    )
    head_vals = solved[:, :, 0]
    tail_vals = solved[:, :, -1]
    coef_shape = (2, 1, 1, 1)
    head_left = jnp.reshape(-couples[:, 0] * inverses[:, 0, 0], coef_shape)
    head_right = jnp.reshape(-couples[:, -1] * inverses[:, 0, -1], coef_shape)
    tail_left = jnp.reshape(-couples[:, 0] * inverses[:, -1, 0], coef_shape)
    tail_right = jnp.reshape(-couples[:, -1] * inverses[:, -1, -1], coef_shape)
    below_val, below_coef, above_val, above_coef = outer_values(
        head_vals, tail_vals, head_left, head_right, tail_left, tail_right
    )
    own_head = head_vals + head_left * below_val + head_right * above_val
    own_tail = tail_vals + tail_left * below_val + tail_right * above_val
    keep_head = 1.0 - head_left * below_coef
    keep_tail = 1.0 - tail_right * above_coef
    cross_head = head_right * above_coef
    cross_tail = tail_left * below_coef
    determinant = keep_head * keep_tail - cross_head * cross_tail
    head_true = (own_head * keep_tail + cross_head * own_tail) / determinant
    tail_true = (keep_head * own_tail + cross_tail * own_head) / determinant
    left_value = below_val + below_coef * head_true
    right_value = above_val + above_coef * tail_true
    left_column = -couples[:, 0:1] * inverses[:, :, 0]
    right_column = -couples[:, -1:] * inverses[:, :, -1]
    result = (
        solved
        + left_column[:, None, :, None, None] * left_value[:, :, None]
        + right_column[:, None, :, None, None] * right_value[:, :, None]
    )
    y_padded = with_halo(flux_y, (("gy", 2),), 4, True)
    cells_y = flux_y.shape[2]
    deriv_y = jnp.zeros_like(flux_y)
    for distance, factor in enumerate(STENCIL_WEIGHTS, start=1):
        upper_part = lax.slice_in_dim(y_padded, 4 + distance, 4 + distance + cells_y, axis=2)
        lower_part = lax.slice_in_dim(y_padded, 4 - distance, 4 - distance + cells_y, axis=2)
        deriv_y = deriv_y + factor * (upper_part - lower_part)
    return result[1] - STEP_SIZE * (
        metric_x[None, :, :, None] * result[0] + metric_y[None, :, :, None] * deriv_y
    )


def solution(mesh):
    return jax.shard_map(
        per_device,
        mesh=mesh,
        in_specs=(
            P(None, "gx", "gy", None),
            P(None, "gx", "gy", None),
            P(None, "gx", "gy", None),
            P("gx", "gy"),
            P("gx", "gy"),
            P("gx"),
        ),
        out_specs=P(None, "gx", "gy", None),
        check_vma=False,
    )
```

profile of v0, /device:TPU:1, one launch (start us, length us, event | category | flops | bytes accessed | tf_op | source)
XLA Modules:
  0.0 251.2 jit_solution(7199387543539128958)
XLA Ops:
  6.5 3.3 %copy_bitcast_fusion = (f32[1,5,16,32,128]{4,2,3,1,0:T(8,128)S(1)}, f32[1,5,16,32,128]{4,2,3,1,0:T(8,128)S(1)}) fusion(f32[5,16,32,128]{3,2,1,0:T(8,128)} %param.74, f32[5,16,32,128]{3,2,1,0:T(8,128)} %param.76), kind=kLoop, calls=%fused_computation.83 | loop fusion | bytes 5242880 | tf_op jit(solution)/shard_map/stack | solution.py:100
  10.3 4.5 %collective-permute-start = (f32[2,5,3,32,128]{4,3,2,1,0:T(8,128)S(1)}, f32[2,5,3,32,128]{4,3,2,1,0:T(8,128)}, u32[]{:S(2)}, u32[]{:S(2)}) collective-permute-start(f32[2,5,3,32,128]{4,3,2,1,0:T(8,128)S(1)} %copy.31), channel_id=1, source_target_pairs={{0,4},{4,8},{8,12},{12,16},{16,20},{20,24},{24,28},{28,32},{32,36}... | collective-permute-start | bytes 1474568 | tf_op jit(solution)/shard_map/ppermute | solution.py:35
  15.6 1.9 collective-permute-start.1
  19.0 1.3 fusion.89
  90.0 1.4 copy.33
  91.3 1.4 copy.34
  94.9 1.3 fusion.49
  96.2 2.4 fusion.32
  98.6 1.5 copy-done
  102.0 1.1 fusion.98
  103.1 1.7 collective-permute-start.3
  104.8 2.2 collective-permute-start.2
  107.6 24.0 %all_gather.28 = f32[32,2,1,1,1]{1,4,3,2,0:T(1,128)S(1)} all-gather(f32[1,2,1,1,1]{1,4,3,2,0:T(1,128)S(1)} %get-tuple-element.791), channel_id=1, replica_groups=mesh['gx'=32,'gy'=4] {'gx'}, dimensions={0}, use_global_device_ids=true | all-gather | bytes 264 | tf_op jit(solution)/shard_map/all_gather | solution.py:16
  131.6 20.0 %all_gather.29 = f32[32,2,1,1,1]{1,4,3,2,0:T(1,128)S(1)} all-gather(f32[1,2,1,1,1]{1,4,3,2,0:T(1,128)S(1)} %get-tuple-element.792), channel_id=1, replica_groups=mesh['gx'=32,'gy'=4] {'gx'}, dimensions={0}, use_global_device_ids=true | all-gather | bytes 264 | tf_op jit(solution)/shard_map/all_gather | solution.py:16
  151.6 20.3 %all_gather.25 = f32[32,2,1,1,1]{1,4,3,2,0:T(1,128)S(1)} all-gather(f32[1,2,1,1,1]{1,4,3,2,0:T(1,128)S(1)} %get-tuple-element.789), channel_id=1, replica_groups=mesh['gx'=32,'gy'=4] {'gx'}, dimensions={0}, use_global_device_ids=true | all-gather | bytes 264 | tf_op jit(solution)/shard_map/all_gather | solution.py:16
  171.9 20.0 %all_gather.27 = f32[32,2,1,1,1]{1,4,3,2,0:T(1,128)S(1)} all-gather(f32[1,2,1,1,1]{1,4,3,2,0:T(1,128)S(1)} %get-tuple-element.790), channel_id=1, replica_groups=mesh['gx'=32,'gy'=4] {'gx'}, dimensions={0}, use_global_device_ids=true | all-gather | bytes 264 | tf_op jit(solution)/shard_map/all_gather | solution.py:16
  193.2 2.2 constant_dynamic-update-slice_fusion.1
  195.5 4.9 %all-gather.7.cloned.1.call-done = f32[64,5,1,32,128]{4,3,2,1,0:T(8,128)} async-done(((f32[2,5,1,32,128]{4,3,2,1,0:T(8,128)}), f32[64,5,1,32,128]{4,3,2,1,0:T(8,128)}) %all-gather.7.cloned.1.call-update) | async-done | bytes 5242896 | tf_op jit(solution)/shard_map/all_gather | solution.py:16
  200.5 35.7 %while.71 = (s32[]{:T(128)}, f32[2,5,32,128]{3,2,1,0:T(8,128)S(1)}, f32[2,1,1,1]{0,3,2,1:T(1,128)S(1)}, s32[]{:T(128)}, f32[32,2,5,32,128]{4,3,2,1,0:T(8,128)}, ...) while((s32[]{:T(128)}, f32[2,5,32,128]{3,2,1,0:T(8,128)S(1)}, ...), condition=%wide.region_3.4_spmd, body=%wide.region_2.3_spmd.sunk | while | flops 204818 | bytes 655663 | solution.py:25
  236.3 1.2 while.70
  238.2 1.1 multiply_add_fusion.2
  239.3 2.3 multiply_add_fusion
  241.6 1.2 fusion.40
  242.9 1.5 copy.45
  (370 shorter events, 113.8 us)
Async XLA Ops:
  6.5 189.0 %all-gather.5.cloned.1.call-start = ((), (), s32[]{:S(2)}) async-start(), calls=%async_computation | async-start | bytes 5406720 | tf_op jit(solution)/shard_map/all_gather | solution.py:16
  10.2 7.4 %copy-start.9 = (f32[16]{0:T(128)S(1)}, f32[16]{0:T(128)}, u32[]{:S(2)}) copy-start(f32[16]{0:T(128)} %param.79) | copy-start | bytes 196
  10.3 79.7 %collective-permute-start = (f32[2,5,3,32,128]{4,3,2,1,0:T(8,128)S(1)}, f32[2,5,3,32,128]{4,3,2,1,0:T(8,128)}, u32[]{:S(2)}, u32[]{:S(2)}) collective-permute-start(f32[2,5,3,32,128]{4,3,2,1,0:T(8,128)S(1)} %copy.31), channel_id=1, source_target_pairs={{0,4},{4,8},{8,12},{12,16},{16,20},{20,24},{24,28},{28,32},{32,36}... | collective-permute-start | bytes 1474568 | tf_op jit(solution)/shard_map/ppermute | solution.py:35
  15.6 75.7 %collective-permute-start.1 = (f32[2,5,3,32,128]{4,3,2,1,0:T(8,128)}, f32[2,5,3,32,128]{4,3,2,1,0:T(8,128)}, u32[]{:S(2)}, u32[]{:S(2)}) collective-permute-start(f32[2,5,3,32,128]{4,3,2,1,0:T(8,128)} %copy.32), channel_id=1, source_target_pairs={{4,0},{8,4},{12,8},{16,12},{20,16},{24,20},{28,24},{32,28},{36,32}... | collective-permute-start | bytes 1474568 | tf_op jit(solution)/shard_map/ppermute | solution.py:36
  93.6 1.3 copy-start.1
  98.6 1.5 copy-start
  100.1 6.9 %copy-start.3 = (f32[16,32]{1,0:T(8,128)S(1)}, f32[16,32]{1,0:T(8,128)}, u32[]{:S(2)}) copy-start(f32[16,32]{1,0:T(8,128)} %param.77) | copy-start | bytes 6148
  100.1 7.0 %copy-start.4 = (f32[16,32]{1,0:T(8,128)S(1)}, f32[16,32]{1,0:T(8,128)}, u32[]{:S(2)}) copy-start(f32[16,32]{1,0:T(8,128)} %param.78) | copy-start | bytes 6148
  101.2 99.3 %all-gather.7.cloned.1.call-start = ((), (), s32[]{:S(2)}) async-start(), calls=%async_computation.1 | async-start | bytes 5406720 | tf_op jit(solution)/shard_map/all_gather | solution.py:16
  103.1 90.1 %collective-permute-start.3 = (f32[5,16,4,128]{3,1,2,0:T(8,128)S(1)}, f32[5,16,4,128]{3,1,2,0:T(8,128)S(1)}, u32[]{:S(2)}, u32[]{:S(2)}) collective-permute-start(f32[5,16,4,128]{3,1,2,0:T(8,128)S(1)} %copy.53), channel_id=1, source_target_pairs={{0,1},{1,2},{2,3},{3,0},{4,5},{5,6},{6,7},{7,4},{8,9},{9,10},{10,1... | collective-permute-start | bytes 491528 | tf_op jit(solution)/shard_map/ppermute | solution.py:35
  104.8 90.6 %collective-permute-start.2 = (f32[5,16,4,128]{3,1,2,0:T(8,128)S(1)}, f32[5,16,4,128]{3,1,2,0:T(8,128)S(1)}, u32[]{:S(2)}, u32[]{:S(2)}) collective-permute-start(f32[5,16,4,128]{3,1,2,0:T(8,128)S(1)} %copy.54), channel_id=1, source_target_pairs={{1,0},{2,1},{3,2},{0,3},{5,4},{6,5},{7,6},{4,7},{9,8},{10,9},{11,1... | collective-permute-start | bytes 491528 | tf_op jit(solution)/shard_map/ppermute | solution.py:36
  107.6 87.9 %copy-start.5 = (f32[2]{0:T(128)}, f32[2]{0:T(128)S(1)}, u32[]{:S(2)}) copy-start(f32[2]{0:T(128)S(1)} %get-tuple-element.714) | copy-start | bytes 28
  107.6 87.9 %copy-start.6 = (f32[2]{0:T(128)}, f32[2]{0:T(128)S(1)}, u32[]{:S(2)}) copy-start(f32[2]{0:T(128)S(1)} %get-tuple-element.715) | copy-start | bytes 28
  107.6 87.9 %copy-start.7 = (f32[2]{0:T(128)}, f32[2]{0:T(128)S(1)}, u32[]{:S(2)}) copy-start(f32[2]{0:T(128)S(1)} %get-tuple-element.716) | copy-start | bytes 28
  107.6 87.9 %copy-start.8 = (f32[2]{0:T(128)}, f32[2]{0:T(128)S(1)}, u32[]{:S(2)}) copy-start(f32[2]{0:T(128)S(1)} %get-tuple-element.717) | copy-start | bytes 28
  236.3 1.9 copy-start.2
Sparse Core Ops, SparseCore 0:
  101.3 50.1 all-gather.4
  153.8 46.6 all-gather.6
where the time goes:
time: 253 us; the launch traced here: 251 us
  other arithmetic  89.2 us (35%)
  blocking collectives  84.2 us (33%)
  local copies, waits for them, and re-layouts  43.5 us (17%)
  between operations  14.3 us (6%)
  starting transfers between devices  10.4 us (4%)
  waiting for transfers between devices  5.69 us (2%)
    all_gather x4, blocking collectives, carried_in(): gathered = jax.tree.map(lambda a: lax.all_gather(a, axis), part)  84.2 us
    add x30, other arithmetic, join_pieces(): head_a + hright_a * head_mid  33.4 us
    div x31, other arithmetic, invert_block(): pivot_row = augmented[column] / augmented[column, column]  21.6 us
    slice x32, local copies, waits for them, and re-layouts, invert_block(): pivot_row = augmented[column] / augmented[column, column]  20.6 us
    mul x30, other arithmetic, invert_block(): augmented = augmented - augmented[:, column:column + 1] * pivot_row[None, :]  20.3 us
    ppermute x2, starting transfers between devices, with_halo(): before = lax.ppermute(last, axis, up)  6.22 us
    slice x32, local copies, waits for them, and re-layouts, invert_block(): augmented = augmented - augmented[:, column:column + 1] * pivot_row[None, :]  5.65 us
  transfers between devices with their start and end apart: 6, of which 1 were waited for; matrix products, arithmetic and copies ran while one was open for 32% of the time, Pallas kernels for 0%

commit v1 on v0

v1 whole, which is shorter than its diff:
```python
import jax
import jax.numpy as jnp
import numpy as np
from jax import lax
from jax.experimental import pallas as pl
from jax.experimental.pallas import tpu as pltpu
from jax.sharding import PartitionSpec as P

NV, NI, NJ, NK = 5, 16, 32, 128
PIECES = 32
ROWS = 24
SUB = 8
F32 = jnp.float32
Y_WEIGHTS = (4.0 / 5.0, -1.0 / 5.0, 4.0 / 105.0, -1.0 / 280.0)
D6 = (1.0, -6.0, 15.0, -20.0, 15.0, -6.0, 1.0)

C_C, C_MG, C_LEFT, C_RIGHT, C_ENDS, C_HALO, C_COUNT = 0, 16, 32, 48, 64, 68, 80


def constant_system():
    a = 1.0 / 3.0
    t = np.eye(NI) + a * (np.eye(NI, k=1) + np.eye(NI, k=-1))
    inv = np.linalg.inv(t)
    m, c = [], []
    prev = 0.0
    for _ in range(NI):
        m.append(1.0 / (1.0 - a * prev))
        prev = a * m[-1]
        c.append(prev)
    left, right = -a * inv[:, 0], -a * inv[:, -1]
    hl, hr, tl, tr = left[0], right[0], left[-1], right[-1]
    e = [tr]
    for _ in range(PIECES - 1):
        e.append(tr + tl * hr * e[-1] / (1.0 - hl * e[-1]))
    return dict(m=m, c=c, inv=inv, left=left, right=right, hl=hl, hr=hr, tl=tl, tr=tr, e=e)


CS = constant_system()
RHO = 25.0 / 36.0


def flux_weight(row, j):
    w = CS["inv"][row]
    lo = w[j - 1] if 0 <= j - 1 < NI else 0.0
    hi = w[j + 1] if 0 <= j + 1 < NI else 0.0
    return float(RHO * (lo - hi))


def splat(x):
    return jnp.full((SUB, NK), x, F32)


def parity(name):
    return lax.rem(lax.axis_index(name), 2)


def pack_x_body(s_lo, s_hi, f_lo, f_hi, one, two):
    core = parity("gx")

    def put(right, left):
        right[:, 0:3] = s_hi[:, 1:4]
        right[:, 3:4] = f_hi[...]
        left[:, 0:3] = s_lo[:, 0:3]
        left[:, 3:4] = f_lo[...]

    @pl.when(core == 0)
    def _():
        put(one, two)

    @pl.when(core == 1)
    def _():
        put(two, one)


def pack_x(state, flux_x):
    out = jax.ShapeDtypeStruct((NV, 4, NJ, NK), F32)
    return pl.pallas_call(
        pack_x_body,
        grid=(1,),
        out_shape=(out, out),
        in_specs=[
            pl.BlockSpec((NV, 4, NJ, NK), lambda g: (0, 0, 0, 0)),
            pl.BlockSpec((NV, 4, NJ, NK), lambda g: (0, 3, 0, 0)),
            pl.BlockSpec((NV, 1, NJ, NK), lambda g: (0, 0, 0, 0)),
            pl.BlockSpec((NV, 1, NJ, NK), lambda g: (0, NI - 1, 0, 0)),
        ],
        out_specs=[pl.BlockSpec((NV, 4, NJ, NK), lambda g: (0, 0, 0, 0))] * 2,
        compiler_params=pltpu.CompilerParams(vmem_limit_bytes=8 << 20),
        cost_estimate=pl.CostEstimate(flops=0, bytes_accessed=1 << 20, transcendentals=0),
        name="pack_x",
    )(state, state, flux_x, flux_x)


def pack_y_body(lo, hi, one, two):
    odd = parity("gy")

    def put(top, bottom):
        for v in range(NV):
            for i in range(NI):
                rows = pl.ds(4 * (i % 2), 4)
                top[v, i // 2, rows, :] = hi[v, i, 4:8, :]
                bottom[v, i // 2, rows, :] = lo[v, i, 0:4, :]

    @pl.when(odd == 0)
    def _():
        put(one, two)

    @pl.when(odd == 1)
    def _():
        put(two, one)


def pack_y(flux_y):
    out = jax.ShapeDtypeStruct((NV, NI // 2, SUB, NK), F32)
    return pl.pallas_call(
        pack_y_body,
        grid=(1,),
        out_shape=(out, out),
        in_specs=[
            pl.BlockSpec((NV, NI, SUB, NK), lambda g: (0, 0, 0, 0)),
            pl.BlockSpec((NV, NI, SUB, NK), lambda g: (0, 0, NJ // SUB - 1, 0)),
        ],
        out_specs=[pl.BlockSpec((NV, NI // 2, SUB, NK), lambda g: (0, 0, 0, 0))] * 2,
        compiler_params=pltpu.CompilerParams(vmem_limit_bytes=8 << 20),
        cost_estimate=pl.CostEstimate(flops=0, bytes_accessed=1 << 20, transcendentals=0),
        name="pack_y",
    )(flux_y, flux_y)


def own_body(gap, s, f, coef, part):
    core = parity("gx")
    piece = lax.axis_index("gx")
    alpha = [0.5 - splat(gap[i]) for i in range(NI)]
    g32 = [(0.5 - a) * (1.0 / 32.0) for a in alpha]
    m, c = [None] * NI, [None] * NI
    n, b = [None] * NI, [None] * NI
    for k in range(NI):
        m[k] = 1.0 / (1.0 - alpha[k] * c[k - 1]) if k else jnp.ones((SUB, NK), F32)
        c[k] = alpha[k] * m[k]
        r = NI - 1 - k
        n[r] = 1.0 / (1.0 - alpha[r] * b[r + 1]) if k else jnp.ones((SUB, NK), F32)
        b[r] = alpha[r] * n[r]
    left, right = [None] * NI, [None] * NI
    wh, wt = [None] * NI, [None] * NI
    left[0], right[NI - 1] = -b[0], -c[NI - 1]
    qh, qt = None, None
    for k in range(NI):
        r = NI - 1 - k
        if k:
            left[k] = -b[k] * left[k - 1]
            right[r] = -c[r] * right[r + 1]
            qh = -b[k - 1] if qh is None else -b[k - 1] * qh
            qt = -c[r + 1] if qt is None else -c[r + 1] * qt
            wh[k] = qh * n[k]
            wt[r] = qt * m[r]
        else:
            wh[0], wt[NI - 1] = n[0], m[NI - 1]
    for k in range(NI):
        coef[C_C + k] = c[k]
        coef[C_MG + k] = m[k] * g32[k]
        coef[C_LEFT + k] = left[k]
        coef[C_RIGHT + k] = right[k]
    coef[C_ENDS + 0] = -alpha[0] * wh[0]
    coef[C_ENDS + 1] = -alpha[NI - 1] * wh[NI - 1]
    coef[C_ENDS + 2] = -alpha[0] * wt[0]
    coef[C_ENDS + 3] = -alpha[NI - 1] * wt[NI - 1]
    vh = [wh[k] * g32[k] for k in range(NI)]
    vt = [wt[k] * g32[k] for k in range(NI)]

    def spread(v, j):
        terms = [D6[q + 3] * v[j - q] for q in range(-3, 4) if 0 <= j - q < NI]
        total = terms[0]
        for t in terms[1:]:
            total = total + t
        return total

    for q in range(3):
        for e, v in enumerate((vh, vt)):
            low, high = spread(v, q - 3), spread(v, NI + q)
            coef[C_HALO + 3 * e + q] = jnp.where(core == 0, high, low)
            coef[C_HALO + 6 + 3 * e + q] = jnp.where(core == 0, low, high)
    sh = [spread(vh, j) for j in range(NI)]
    st = [spread(vt, j) for j in range(NI)]
    first = jnp.where(piece == 0, 1.0 / 36.0, 0.0).astype(F32)
    last = jnp.where(piece == PIECES - 1, -1.0 / 36.0, 0.0).astype(F32)
    inv = CS["inv"]
    fh = [flux_weight(0, j) for j in range(NI)]
    ft = [flux_weight(NI - 1, j) for j in range(NI)]
    fh[0] = fh[0] + float(inv[0, 0]) * first
    ft[0] = ft[0] + float(inv[NI - 1, 0]) * first
    fh[NI - 1] = fh[NI - 1] + float(inv[0, NI - 1]) * last
    ft[NI - 1] = ft[NI - 1] + float(inv[NI - 1, NI - 1]) * last

    for i in range(NI):
        coef[C_COUNT + i] = sh[i]
        coef[C_COUNT + NI + i] = st[i]

    @pl.loop(0, NV)
    def _(v):
        for q in range(NJ // SUB):
            rows = pl.ds(SUB * q, SUB)
            sums = [None] * 4
            for i in range(NI):
                a, z = s[v, i, rows, :], f[v, i, rows, :]
                terms = (
                    coef[C_COUNT + i] * a,
                    coef[C_COUNT + NI + i] * a,
                    fh[i] * z,
                    ft[i] * z,
                )
                sums = [t if o is None else o + t for o, t in zip(sums, terms)]
            for e in range(4):
                part[e, v, rows, :] = sums[e]


def own_share(gap, state, flux_x):
    return pl.pallas_call(
        own_body,
        out_shape=(
            jax.ShapeDtypeStruct((C_COUNT + 2 * NI, SUB, NK), F32),
            jax.ShapeDtypeStruct((4, NV, NJ, NK), F32),
        ),
        in_specs=[
            pl.BlockSpec(memory_space=pltpu.SMEM),
            pl.BlockSpec(memory_space=pltpu.VMEM),
            pl.BlockSpec(memory_space=pltpu.VMEM),
        ],
        out_specs=(pl.BlockSpec(memory_space=pltpu.VMEM),) * 2,
        compiler_params=pltpu.CompilerParams(vmem_limit_bytes=12 << 20),
        cost_estimate=pl.CostEstimate(flops=1 << 24, bytes_accessed=4 << 20, transcendentals=0),
        name="own_share",
    )(gap, state, flux_x)


def ends_body(coef, part, one, two, out):
    core = parity("gx")
    is0 = core == 0
    fw = []
    for row in (0, NI - 1):
        low, high = flux_weight(row, -1), flux_weight(row, NI)
        fw.append((jnp.where(is0, high, low).astype(F32), jnp.where(is0, low, high).astype(F32)))

    for v in range(NV):
        for q in range(NJ // SUB):
            rows = pl.ds(SUB * q, SUB)
            a = [one[v, k, rows, :] for k in range(4)]
            b = [two[v, k, rows, :] for k in range(4)]
            for e in range(2):
                total = part[e, v, rows, :]
                for k in range(3):
                    total = total + coef[C_HALO + 3 * e + k] * a[k]
                    total = total + coef[C_HALO + 6 + 3 * e + k] * b[k]
                out[pl.ds(ROWS * SUB * q + NV * e + v, SUB, stride=ROWS), :] = total
                total = part[2 + e, v, rows, :] + fw[e][0] * a[3] + fw[e][1] * b[3]
                out[pl.ds(ROWS * SUB * q + NV * (2 + e) + v, SUB, stride=ROWS), :] = total
    for k in range(4):
        for q in range(NJ // SUB):
            out[pl.ds(ROWS * SUB * q + 4 * NV + k, SUB, stride=ROWS), :] = coef[C_ENDS + k]


def end_values(coef, part, one, two):
    return pl.pallas_call(
        ends_body,
        out_shape=jax.ShapeDtypeStruct((PIECES * ROWS, NK), F32),
        in_specs=[pl.BlockSpec(memory_space=pltpu.VMEM)] * 4,
        out_specs=pl.BlockSpec(memory_space=pltpu.VMEM),
        compiler_params=pltpu.CompilerParams(vmem_limit_bytes=12 << 20),
        cost_estimate=pl.CostEstimate(flops=1 << 20, bytes_accessed=1 << 20, transcendentals=0),
        name="end_values",
    )(coef, part, one, two)


def join_body(x, out):
    def row(p, k):
        return jnp.broadcast_to(x[pl.ds(ROWS * p + 4 * NV + k, 1), :], (NV, NK))

    def value(p, k):
        return x[pl.ds(ROWS * p + NV * k, NV), :]

    scale = 8.0
    num, den = [None] * PIECES, [None] * PIECES
    hl, hr, tl, tr = ([row(p, k) for p in range(PIECES)] for k in range(4))
    num[0], den[0] = tr[0], jnp.ones((NV, NK), F32)
    for p in range(1, PIECES):
        cross = tl[p] * hr[p] - tr[p] * hl[p]
        num[p] = (scale * tr[p]) * den[p - 1] + (scale * cross) * num[p - 1]
        den[p] = scale * den[p - 1] - (scale * hl[p]) * num[p - 1]
    inv = [None] + [1.0 / den[p] for p in range(1, PIECES)]
    e = [num[0]] + [num[p] * inv[p] for p in range(1, PIECES)]
    keep = [None] + [(scale * den[p - 1]) * inv[p] for p in range(1, PIECES)]

    fwd_f, fwd_d = [value(0, 1)], [value(0, 3)]
    chl, chr_, ctl, ce = CS["hl"], CS["hr"], CS["tl"], CS["e"]
    for p in range(1, PIECES):
        a = tl[p] * keep[p]
        fwd_f.append((value(p, 1) + (a * e[p - 1]) * value(p, 0)) + a * fwd_f[-1])
        k = ctl / (1.0 - chl * ce[p - 1])
        fwd_d.append((value(p, 3) + float(k * ce[p - 1]) * value(p, 2)) + float(k) * fwd_d[-1])

    zero = jnp.zeros((NV, NK), F32)
    right_f, right_d = zero, zero
    for p in range(PIECES - 1, -1, -1):
        if p:
            h = keep[p]
            head_f = (value(p, 0) + hl[p] * fwd_f[p - 1]) * h + (hr[p] * h) * right_f
            left_f = fwd_f[p - 1] + e[p - 1] * head_f
            k = 1.0 / (1.0 - chl * ce[p - 1])
            head_d = (float(k) * value(p, 2) + float(k * chl) * fwd_d[p - 1]) + float(k * chr_) * right_d
            left_d = fwd_d[p - 1] + float(ce[p - 1]) * head_d
        else:
            head_f = head_d = left_f = left_d = zero
        for k, val in enumerate((left_f, right_f, left_d, right_d)):
            out[pl.ds(ROWS * p + NV * k, NV), :] = val
        right_f, right_d = head_f, head_d


def join(x):
    return pl.pallas_call(
        join_body,
        out_shape=jax.ShapeDtypeStruct((PIECES * ROWS, NK), F32),
        in_specs=[pl.BlockSpec(memory_space=pltpu.VMEM)],
        out_specs=pl.BlockSpec(memory_space=pltpu.VMEM),
        compiler_params=pltpu.CompilerParams(vmem_limit_bytes=12 << 20),
        cost_estimate=pl.CostEstimate(flops=1 << 20, bytes_accessed=1 << 20, transcendentals=0),
        name="join",
    )(x)


def block_body(coef, s, f, fy, one, two, yone, ytwo, mx, my, base, mxb, pad):
    piece = lax.axis_index("gx")
    is0 = parity("gx") == 0
    even = parity("gy") == 0
    first = jnp.where(piece == 0, 1.0 / 36.0, 0.0).astype(F32)
    last = jnp.where(piece == PIECES - 1, -1.0 / 36.0, 0.0).astype(F32)
    mxt = jnp.transpose(mx[...] * -0.5)
    myt = jnp.transpose(my[...] * -0.5)
    for i in range(NI):
        mxb[i] = jnp.broadcast_to(mxt[:, i : i + 1], (NJ, NK))
        pad[NI + i, 0:NJ, :] = jnp.broadcast_to(myt[:, i : i + 1], (NJ, NK))

    @pl.loop(0, NV)
    def _(v):
        for i in range(NI):
            for q in range(NJ // SUB):
                pad[i, pl.ds(SUB + SUB * q, SUB), :] = fy[v, i, pl.ds(SUB * q, SUB), :]
            part = pl.ds(4 * (i % 2), 4)
            a, b = yone[v, i // 2, part, :], ytwo[v, i // 2, part, :]
            pad[i, SUB - 4 : SUB, :] = jnp.where(even, b, a)
            pad[i, SUB + NJ : SUB + NJ + 4, :] = jnp.where(even, a, b)

        for q in range(NJ // SUB):
            rows = pl.ds(SUB * q, SUB)
            a = [one[v, k, rows, :] for k in range(4)]
            b = [two[v, k, rows, :] for k in range(4)]
            low = [jnp.where(is0, b[k], a[k]) for k in range(4)]
            high = [jnp.where(is0, a[k], b[k]) for k in range(4)]
            st = low[:3] + [s[v, i, rows, :] for i in range(NI)] + high[:3]
            fl = [low[3]] + [f[v, i, rows, :] for i in range(NI)] + [high[3]]
            ye, yd, us = [], [], []
            for i in range(NI):
                d6 = (
                    (st[i] + st[i + 6])
                    - 6.0 * (st[i + 1] + st[i + 5])
                    + 15.0 * (st[i + 2] + st[i + 4])
                    - 20.0 * st[i + 3]
                )
                y = coef[C_MG + i] * d6
                ye.append(y - coef[C_C + i] * ye[-1] if i else y)
                u = fl[i + 2] - fl[i]
                us.append(u)
                r = float(RHO * CS["m"][i]) * u
                if i == 0:
                    r = r + (first * float(CS["m"][i])) * fl[1]
                if i == NI - 1:
                    r = r + (last * float(CS["m"][i])) * fl[NI]
                yd.append(r - float(CS["c"][i]) * yd[-1] if i else r)
            xe = xd = None
            for i in range(NI - 1, -1, -1):
                xe = ye[i] if xe is None else ye[i] - coef[C_C + i] * xe
                xd = yd[i] if xd is None else yd[i] - float(CS["c"][i]) * xd
                at = SUB + SUB * q
                dy = None
                for k, w in enumerate(Y_WEIGHTS, start=1):
                    t = w * (pad[i, pl.ds(at + k, SUB), :] - pad[i, pl.ds(at - k, SUB), :])
                    dy = t if dy is None else dy + t
                d = us[i] * (1.0 / 12.0) + xd
                base[v, i, rows, :] = (st[i + 3] + xe) + (mxb[i, rows, :] * d + pad[NI + i, rows, :] * dy)


def block(coef, state, flux_x, flux_y, one, two, yone, ytwo, mx, my):
    return pl.pallas_call(
        block_body,
        out_shape=(
            jax.ShapeDtypeStruct((NV, NI, NJ, NK), F32),
            jax.ShapeDtypeStruct((NI, NJ, NK), F32),
        ),
        in_specs=[pl.BlockSpec(memory_space=pltpu.VMEM)] * 10,
        out_specs=(pl.BlockSpec(memory_space=pltpu.VMEM),) * 2,
        scratch_shapes=[pltpu.VMEM((2 * NI, SUB + NJ + SUB, NK), F32)],
        compiler_params=pltpu.CompilerParams(vmem_limit_bytes=16 << 20),
        cost_estimate=pl.CostEstimate(flops=1 << 25, bytes_accessed=8 << 20, transcendentals=0),
        name="block",
    )(coef, state, flux_x, flux_y, one, two, yone, ytwo, mx, my)


def finish_body(coef, base, mxb, z, out):
    @pl.loop(0, NV)
    def _(v):
        for q in range(NJ // SUB):
            rows = pl.ds(SUB * q, SUB)
            lf, rf, ld, rd = (
                z[pl.ds(ROWS * SUB * q + NV * k + v, SUB, stride=ROWS), :] for k in range(4)
            )
            for i in range(NI):
                d = float(CS["left"][i]) * ld + float(CS["right"][i]) * rd
                e = coef[C_LEFT + i] * lf + coef[C_RIGHT + i] * rf
                out[v, i, rows, :] = (base[v, i, rows, :] + e) + mxb[i, rows, :] * d


def finish(coef, base, mxb, z):
    return pl.pallas_call(
        finish_body,
        out_shape=jax.ShapeDtypeStruct((NV, NI, NJ, NK), F32),
        in_specs=[pl.BlockSpec(memory_space=pltpu.VMEM)] * 4,
        out_specs=pl.BlockSpec(memory_space=pltpu.VMEM),
        compiler_params=pltpu.CompilerParams(vmem_limit_bytes=12 << 20),
        cost_estimate=pl.CostEstimate(flops=1 << 22, bytes_accessed=3 << 20, transcendentals=0),
        name="finish",
    )(coef, base, mxb, z)


def exchange(x):
    y = lax.all_to_all(x.reshape(PIECES, ROWS, NK), "gx", 0, 0, tiled=True)
    return y.reshape(PIECES * ROWS, NK)


def per_device(flux_x, flux_y, state, metric_x, metric_y, filter_gap):
    count_y = lax.axis_size("gy")
    pair_in = [(i, i ^ 1) for i in range(PIECES)]
    pair_out = [(i, i + 1 if i % 2 else i - 1) for i in range(1, PIECES - 1)]
    y_in = [(i, i ^ 1) for i in range(count_y)]
    y_out = [(i, (i + 1 if i % 2 else i - 1) % count_y) for i in range(count_y)]

    send_one, send_two = pack_x(state, flux_x)
    one = lax.ppermute(send_one, "gx", pair_in)
    two = lax.ppermute(send_two, "gx", pair_out)
    ysend_one, ysend_two = pack_y(flux_y)
    yone = lax.ppermute(ysend_one, "gy", y_in)
    ytwo = lax.ppermute(ysend_two, "gy", y_out)
    coef, part = own_share(filter_gap, state, flux_x)
    ends = exchange(end_values(coef, part, one, two))
    base, mxb = block(coef, state, flux_x, flux_y, one, two, yone, ytwo, metric_x, metric_y)
    outside = exchange(join(ends))
    return finish(coef, base, mxb, outside)


def solution(mesh):
    return jax.shard_map(
        per_device,
        mesh=mesh,
        in_specs=(
            P(None, "gx", "gy", None),
            P(None, "gx", "gy", None),
            P(None, "gx", "gy", None),
            P("gx", "gy"),
            P("gx", "gy"),
            P("gx"),
        ),
        out_specs=P(None, "gx", "gy", None),
        check_vma=False,
    )
```

time: 253 us -> 55.1 us (0.22)
  other arithmetic: 89.2 us -> 0 us
  blocking collectives: 84.2 us -> 19.1 us
  local copies, waits for them, and re-layouts: 43.5 us -> 9.34 us
  between operations: 14.3 us -> 0.16 us
  Pallas kernels: 0 us -> 5.28 us
    all_gather x4 -> x0, blocking collectives: 84.2 us -> none  [carried_in(): gathered = jax.tree.map(lambda a: lax.all_gather(a, axis), part)]
    add x66 -> x0, other arithmetic: 38.5 us -> none  [the longest x30 33.4 us: join_pieces(): head_a + hright_a * head_mid]
    slice x68 -> x0, local copies, waits for them, and re-layouts: 29.3 us -> none  [the longest x32 20.6 us: invert_block(): pivot_row = augmented[column] / augmented[column, column]]
    mul x35 -> x0, other arithmetic: 22.3 us -> none  [the longest x30 20.3 us: invert_block(): augmented = augmented - augmented[:, column:column + 1] * pivot_row[None, :]]
    div x31 -> x0, other arithmetic: 21.6 us -> none  [invert_block(): pivot_row = augmented[column] / augmented[column, column]]
    all_to_all x0 -> x1, blocking collectives: none -> 19.1 us  [exchange(): y = lax.all_to_all(x.reshape(PIECES, ROWS, NK), 'gx', 0, 0, tiled=True)]
    ppermute x4, waiting for transfers between devices: 0.01 us -> 8.02 us  [the longest x1 3.94 us: per_device(): two = lax.ppermute(send_two, 'gx', pair_out)]
    pallas_call x0 -> x7, Pallas kernels: none -> 5.28 us  [the longest x1 2.12 us: block(): pl.pallas_call(block_body, out_shape=(jax.ShapeDtypeStruct((NV, NI, NJ, N...]
  transfers between devices with their start and end apart: 6 -> 5, of which waited for: 1 -> 3; matrix products, arithmetic and copies ran while one was open for 32% -> 0% of each run, Pallas kernels for 0% -> 6%
where the time goes in v1:
time: 55.1 us; the launch traced here: 54.5 us
  blocking collectives  19.1 us (35%)
  starting transfers between devices  12.6 us (23%)
  local copies, waits for them, and re-layouts  9.34 us (17%)
  waiting for transfers between devices  8.03 us (15%)
  Pallas kernels  5.28 us (10%)
    all_to_all x1, blocking collectives, exchange(): y = lax.all_to_all(x.reshape(PIECES, ROWS, NK), 'gx', 0, 0, tiled=True)  19.1 us
    unnamed x36, local copies, waits for them, and re-layouts  9.34 us
    ppermute x1, waiting for transfers between devices, per_device(): two = lax.ppermute(send_two, 'gx', pair_out)  3.94 us
    all_to_all x1, starting transfers between devices, exchange(): y = lax.all_to_all(x.reshape(PIECES, ROWS, NK), 'gx', 0, 0, tiled=True)  3.9 us
    ppermute x1, starting transfers between devices, per_device(): two = lax.ppermute(send_two, 'gx', pair_out)  3.23 us
    ppermute x1, starting transfers between devices, per_device(): ytwo = lax.ppermute(ysend_two, 'gy', y_out)  2.24 us
    ppermute x1, waiting for transfers between devices, per_device(): ytwo = lax.ppermute(ysend_two, 'gy', y_out)  2.14 us
    pallas_call x1, Pallas kernels, block(): pl.pallas_call(block_body, out_shape=(jax.ShapeDtypeStruct((NV, NI, NJ, N...  2.12 us
  transfers between devices with their start and end apart: 5, of which 3 were waited for; matrix products, arithmetic and copies ran while one was open for 0% of the time, Pallas kernels for 6%

profile of v1, /device:TPU:1, one launch (start us, length us, event | category | flops | bytes accessed | tf_op | source)
XLA Modules:
  0.0 54.5 jit_solution(3547318305567918418)
XLA Ops:
  0.0 1.3 %copy-done = f32[5,16,32,128]{3,2,1,0:T(8,128)S(1)} copy-done((f32[5,16,32,128]{3,2,1,0:T(8,128)S(1)}, f32[5,16,32,128]{3,2,1,0:T(8,128)}, u32[]{:S(2)}) %copy-start) | copy-done | bytes 1310744
  1.3 1.3 %copy-done.2 = f32[5,16,32,128]{3,2,1,0:T(8,128)S(1)} copy-done((f32[5,16,32,128]{3,2,1,0:T(8,128)S(1)}, f32[5,16,32,128]{3,2,1,0:T(8,128)}, u32[]{:S(2)}) %copy-start.2) | copy-done | bytes 1310744
  2.7 1.5 %collective-permute-start = (f32[5,4,32,128]{3,2,1,0:T(8,128)S(1)}, f32[5,4,32,128]{3,2,1,0:T(8,128)S(1)}, u32[]{:S(2)}, u32[]{:S(2)}) collective-permute-start(f32[5,4,32,128]{3,2,1,0:T(8,128)S(1)} %get-tuple-element.14), channel_id=1, source_target_pairs={{0,4},{4,0},{8,12},{12,8},{16,20},{20,16},{24,28},{28,24},{32,36},... | collective-permute-start | bytes 983048 | tf_op jit(solution)/shard_map/ppermute | solution.py:445
  4.2 3.2 %collective-permute-start.1 = (f32[5,4,32,128]{3,2,1,0:T(8,128)S(1)}, f32[5,4,32,128]{3,2,1,0:T(8,128)S(1)}, u32[]{:S(2)}, u32[]{:S(2)}) collective-permute-start(f32[5,4,32,128]{3,2,1,0:T(8,128)S(1)} %get-tuple-element.15), channel_id=1, source_target_pairs={{4,8},{8,4},{12,16},{16,12},{20,24},{24,20},{28,32},{32,28},{36,40... | collective-permute-start | bytes 983048 | tf_op jit(solution)/shard_map/ppermute | solution.py:446
  7.5 1.1 %own_share.1 = (f32[112,8,128]{2,1,0:T(8,128)S(1)}, f32[4,5,32,128]{3,2,1,0:T(8,128)S(1)}) custom-call(f32[16]{0:T(128)S(1)} %copy-done.17, f32[5,16,32,128]{3,2,1,0:T(8,128)S(1)} %copy-done.1, f32[5,16,32,128]{3,2,1,0:T(8,128)S(1)} %copy-done.3), custom_call_target="tpu_custom_call" | custom-call | flops 16777216 | bytes 4194304 | tf_op jit(solution)/shard_map/own_share/pallas_call | solution.py:217
  8.7 3.9 %collective-permute-done.1.two = f32[5,4,32,128]{3,2,1,0:T(8,128)S(1)} collective-permute-done((f32[5,4,32,128]{3,2,1,0:T(8,128)S(1)}, f32[5,4,32,128]{3,2,1,0:T(8,128)S(1)}, u32[]{:S(2)}, u32[]{:S(2)}) %collective-permute-start.1) | collective-permute-done | bytes 327712 | tf_op jit(solution)/shard_map/ppermute | solution.py:446
  12.6 0.1 end_values.1
  12.7 0.6 %copy-done.11 = f32[5,4,32,128]{3,2,1,0:T(8,128)} copy-done((f32[5,4,32,128]{3,2,1,0:T(8,128)}, f32[5,4,32,128]{3,2,1,0:T(8,128)S(1)}, u32[]{:S(2)}) %copy-start.11) | copy-done | bytes 327704
  13.3 19.1 %all_to_all.10 = f32[32,24,128]{2,1,0:T(8,128)S(1)} all-to-all(f32[32,24,128]{2,1,0:T(8,128)S(1)} %bitcast.6), channel_id=1, replica_groups=mesh['gx'=32,'gy'=4] {'gx'}, dimensions={0} | all-to-all | bytes 786432 | tf_op jit(solution)/shard_map/all_to_all | solution.py:433
  32.4 0.2 join.1
  32.7 0.7 %copy-done.6 = f32[768,128]{1,0:T(8,128)} copy-done((f32[768,128]{1,0:T(8,128)}, f32[768,128]{1,0:T(8,128)S(1)}, u32[]{:S(2)}) %copy-start.6) | copy-done | bytes 393240
  33.4 3.9 %all-to-all-start.1 = ((f32[32,24,128]{2,1,0:T(8,128)}), f32[32,24,128]{2,1,0:T(8,128)S(1)}, u32[]{:S(2)}, u32[]{:S(2)}) async-start(f32[32,24,128]{2,1,0:T(8,128)} %bitcast.5), calls=%async_computation.1 | async-start | bytes 786432 | tf_op jit(solution)/shard_map/all_to_all | solution.py:433
  37.3 1.3 %copy-done.4 = f32[5,16,32,128]{3,2,1,0:T(8,128)S(1)} copy-done((f32[5,16,32,128]{3,2,1,0:T(8,128)S(1)}, f32[5,16,32,128]{3,2,1,0:T(8,128)}, u32[]{:S(2)}) %copy-start.4) | copy-done | bytes 1310744
  38.6 0.1 pack_y.1
  38.8 1.7 %collective-permute-start.2 = (f32[5,8,8,128]{3,2,1,0:T(8,128)S(1)}, f32[5,8,8,128]{3,2,1,0:T(8,128)S(1)}, u32[]{:S(2)}, u32[]{:S(2)}) collective-permute-start(f32[5,8,8,128]{3,2,1,0:T(8,128)S(1)} %get-tuple-element.16), channel_id=1, source_target_pairs={{0,1},{1,0},{2,3},{3,2},{4,5},{5,4},{6,7},{7,6},{8,9},{9,8},{10,11... | collective-permute-start | bytes 491528 | tf_op jit(solution)/shard_map/ppermute | solution.py:448
  40.5 2.2 %collective-permute-start.3 = (f32[5,8,8,128]{3,2,1,0:T(8,128)S(1)}, f32[5,8,8,128]{3,2,1,0:T(8,128)S(1)}, u32[]{:S(2)}, u32[]{:S(2)}) collective-permute-start(f32[5,8,8,128]{3,2,1,0:T(8,128)S(1)} %get-tuple-element.17), channel_id=1, source_target_pairs={{0,3},{1,2},{2,1},{3,0},{4,7},{5,6},{6,5},{7,4},{8,11},{9,10},{10,... | collective-permute-start | bytes 491528 | tf_op jit(solution)/shard_map/ppermute | solution.py:449
  42.7 1.9 %collective-permute-done.2.yone = f32[5,8,8,128]{3,2,1,0:T(8,128)S(1)} collective-permute-done((f32[5,8,8,128]{3,2,1,0:T(8,128)S(1)}, f32[5,8,8,128]{3,2,1,0:T(8,128)S(1)}, u32[]{:S(2)}, u32[]{:S(2)}) %collective-permute-start.2) | collective-permute-done | bytes 163872 | tf_op jit(solution)/shard_map/ppermute | solution.py:448
  44.7 2.1 %collective-permute-done.3.ytwo = f32[5,8,8,128]{3,2,1,0:T(8,128)S(1)} collective-permute-done((f32[5,8,8,128]{3,2,1,0:T(8,128)S(1)}, f32[5,8,8,128]{3,2,1,0:T(8,128)S(1)}, u32[]{:S(2)}, u32[]{:S(2)}) %collective-permute-start.3) | collective-permute-done | bytes 163872 | tf_op jit(solution)/shard_map/ppermute | solution.py:449
  46.8 2.1 %block.1 = (f32[5,16,32,128]{3,2,1,0:T(8,128)S(1)}, f32[16,32,128]{2,1,0:T(8,128)S(1)}) custom-call(f32[112,8,128]{2,1,0:T(8,128)S(1)} %get-tuple-element.13.coef, f32[5,16,32,128]{3,2,1,0:T(8,128)S(1)} %copy-done.1, f32[5,16,32,128]{3,2,1,0:T(8,128)S(1)} %copy-done.3, f32[5,16,32,128]{3,2,1,0:T(8,128)S(1)} %copy-done.5, f32[5,4,32,128]{3,2,1,0:T(8,128)S(1)} %copy-done.10, ...), custom_call_target="tpu_custom_call" | custom-call | flops 33554432 | bytes 8388608 | tf_op jit(solution)/shard_map/block/pallas_call | solution.py:391
  49.0 1.0 %copy-done.7 = f32[5,16,32,128]{3,2,1,0:T(8,128)} copy-done((f32[5,16,32,128]{3,2,1,0:T(8,128)}, f32[5,16,32,128]{3,2,1,0:T(8,128)S(1)}, u32[]{:S(2)}) %copy-start.7) | copy-done | bytes 1310744
  50.0 0.7 %copy-done.13 = f32[16,32,128]{2,1,0:T(8,128)} copy-done((f32[16,32,128]{2,1,0:T(8,128)}, f32[16,32,128]{2,1,0:T(8,128)S(1)}, u32[]{:S(2)}) %copy-start.13) | copy-done | bytes 262168
  50.7 1.3 %copy-done.8 = f32[5,16,32,128]{3,2,1,0:T(8,128)S(1)} copy-done((f32[5,16,32,128]{3,2,1,0:T(8,128)S(1)}, f32[5,16,32,128]{3,2,1,0:T(8,128)}, u32[]{:S(2)}) %copy-start.8) | copy-done | bytes 1310744
  52.0 0.9 %copy-done.14 = f32[16,32,128]{2,1,0:T(8,128)S(1)} copy-done((f32[16,32,128]{2,1,0:T(8,128)S(1)}, f32[16,32,128]{2,1,0:T(8,128)}, u32[]{:S(2)}) %copy-start.14) | copy-done | bytes 262168
  53.0 1.5 %finish.1 = f32[5,16,32,128]{3,2,1,0:T(8,128)} custom-call(f32[112,8,128]{2,1,0:T(8,128)S(1)} %get-tuple-element.13.coef, f32[5,16,32,128]{3,2,1,0:T(8,128)S(1)} %copy-done.8, f32[16,32,128]{2,1,0:T(8,128)S(1)} %copy-done.14, f32[768,128]{1,0:T(8,128)S(1)} %bitcast.4), custom_call_target="tpu_custom_call" | custom-call | flops 4194304 | bytes 3145728 | tf_op jit(solution)/shard_map/finish/pallas_call | solution.py:421
  (30 shorter events, 0.1 us)
Async XLA Ops:
  0.0 1.3 %copy-start = (f32[5,16,32,128]{3,2,1,0:T(8,128)S(1)}, f32[5,16,32,128]{3,2,1,0:T(8,128)}, u32[]{:S(2)}) copy-start(f32[5,16,32,128]{3,2,1,0:T(8,128)} %s.3) | copy-start | bytes 3932164
  1.3 1.3 %copy-start.2 = (f32[5,16,32,128]{3,2,1,0:T(8,128)S(1)}, f32[5,16,32,128]{3,2,1,0:T(8,128)}, u32[]{:S(2)}) copy-start(f32[5,16,32,128]{3,2,1,0:T(8,128)} %f.3) | copy-start | bytes 3932164
  2.6 4.8 %copy-start.1 = (f32[5,16,32,128]{3,2,1,0:T(8,128)S(1)}, f32[5,16,32,128]{3,2,1,0:T(8,128)}, u32[]{:S(2)}) copy-start(f32[5,16,32,128]{3,2,1,0:T(8,128)} %s.3) | copy-start | bytes 3932164
  2.6 4.9 %copy-start.3 = (f32[5,16,32,128]{3,2,1,0:T(8,128)S(1)}, f32[5,16,32,128]{3,2,1,0:T(8,128)}, u32[]{:S(2)}) copy-start(f32[5,16,32,128]{3,2,1,0:T(8,128)} %f.3) | copy-start | bytes 3932164
  2.6 4.9 %copy-start.17 = (f32[16]{0:T(128)S(1)}, f32[16]{0:T(128)}, u32[]{:S(2)}) copy-start(f32[16]{0:T(128)} %gap.1) | copy-start | bytes 196
  2.7 5.9 %collective-permute-start = (f32[5,4,32,128]{3,2,1,0:T(8,128)S(1)}, f32[5,4,32,128]{3,2,1,0:T(8,128)S(1)}, u32[]{:S(2)}, u32[]{:S(2)}) collective-permute-start(f32[5,4,32,128]{3,2,1,0:T(8,128)S(1)} %get-tuple-element.14), channel_id=1, source_target_pairs={{0,4},{4,0},{8,12},{12,8},{16,20},{20,16},{24,28},{28,24},{32,36},... | collective-permute-start | bytes 983048 | tf_op jit(solution)/shard_map/ppermute | solution.py:445
  4.2 8.4 %collective-permute-start.1 = (f32[5,4,32,128]{3,2,1,0:T(8,128)S(1)}, f32[5,4,32,128]{3,2,1,0:T(8,128)S(1)}, u32[]{:S(2)}, u32[]{:S(2)}) collective-permute-start(f32[5,4,32,128]{3,2,1,0:T(8,128)S(1)} %get-tuple-element.15), channel_id=1, source_target_pairs={{4,8},{8,4},{12,16},{16,12},{20,24},{24,20},{28,32},{32,28},{36,40... | collective-permute-start | bytes 983048 | tf_op jit(solution)/shard_map/ppermute | solution.py:446
  8.7 23.8 %copy-start.9 = (f32[5,4,32,128]{3,2,1,0:T(8,128)}, f32[5,4,32,128]{3,2,1,0:T(8,128)S(1)}, u32[]{:S(2)}) copy-start(f32[5,4,32,128]{3,2,1,0:T(8,128)S(1)} %collective-permute-done.one) | copy-start | bytes 983044
  12.6 0.7 %copy-start.11 = (f32[5,4,32,128]{3,2,1,0:T(8,128)}, f32[5,4,32,128]{3,2,1,0:T(8,128)S(1)}, u32[]{:S(2)}) copy-start(f32[5,4,32,128]{3,2,1,0:T(8,128)S(1)} %collective-permute-done.1.two) | copy-start | bytes 983044
  32.6 0.7 %copy-start.6 = (f32[768,128]{1,0:T(8,128)}, f32[768,128]{1,0:T(8,128)S(1)}, u32[]{:S(2)}) copy-start(f32[768,128]{1,0:T(8,128)S(1)} %join.1) | copy-start | bytes 1179652
  33.4 17.3 %all-to-all-start.1 = ((f32[32,24,128]{2,1,0:T(8,128)}), f32[32,24,128]{2,1,0:T(8,128)S(1)}, u32[]{:S(2)}, u32[]{:S(2)}) async-start(f32[32,24,128]{2,1,0:T(8,128)} %bitcast.5), calls=%async_computation.1 | async-start | bytes 786432 | tf_op jit(solution)/shard_map/all_to_all | solution.py:433
  37.3 1.3 %copy-start.4 = (f32[5,16,32,128]{3,2,1,0:T(8,128)S(1)}, f32[5,16,32,128]{3,2,1,0:T(8,128)}, u32[]{:S(2)}) copy-start(f32[5,16,32,128]{3,2,1,0:T(8,128)} %fy.1) | copy-start | bytes 3932164
  38.6 8.2 %copy-start.5 = (f32[5,16,32,128]{3,2,1,0:T(8,128)S(1)}, f32[5,16,32,128]{3,2,1,0:T(8,128)}, u32[]{:S(2)}) copy-start(f32[5,16,32,128]{3,2,1,0:T(8,128)} %fy.1) | copy-start | bytes 3932164
  38.6 8.2 %copy-start.10 = (f32[5,4,32,128]{3,2,1,0:T(8,128)S(1)}, f32[5,4,32,128]{3,2,1,0:T(8,128)}, u32[]{:S(2)}) copy-start(f32[5,4,32,128]{3,2,1,0:T(8,128)} %copy-done.9) | copy-start | bytes 983044
  38.6 8.2 %copy-start.12 = (f32[5,4,32,128]{3,2,1,0:T(8,128)S(1)}, f32[5,4,32,128]{3,2,1,0:T(8,128)}, u32[]{:S(2)}) copy-start(f32[5,4,32,128]{3,2,1,0:T(8,128)} %copy-done.11) | copy-start | bytes 983044
  38.6 8.2 %copy-start.15 = (f32[16,32]{1,0:T(8,128)S(1)}, f32[16,32]{1,0:T(8,128)}, u32[]{:S(2)}) copy-start(f32[16,32]{1,0:T(8,128)} %mx.1) | copy-start | bytes 6148
  38.6 8.2 %copy-start.16 = (f32[16,32]{1,0:T(8,128)S(1)}, f32[16,32]{1,0:T(8,128)}, u32[]{:S(2)}) copy-start(f32[16,32]{1,0:T(8,128)} %my.1) | copy-start | bytes 6148
  38.8 5.9 %collective-permute-start.2 = (f32[5,8,8,128]{3,2,1,0:T(8,128)S(1)}, f32[5,8,8,128]{3,2,1,0:T(8,128)S(1)}, u32[]{:S(2)}, u32[]{:S(2)}) collective-permute-start(f32[5,8,8,128]{3,2,1,0:T(8,128)S(1)} %get-tuple-element.16), channel_id=1, source_target_pairs={{0,1},{1,0},{2,3},{3,2},{4,5},{5,4},{6,7},{7,6},{8,9},{9,8},{10,11... | collective-permute-start | bytes 491528 | tf_op jit(solution)/shard_map/ppermute | solution.py:448
  40.5 6.3 %collective-permute-start.3 = (f32[5,8,8,128]{3,2,1,0:T(8,128)S(1)}, f32[5,8,8,128]{3,2,1,0:T(8,128)S(1)}, u32[]{:S(2)}, u32[]{:S(2)}) collective-permute-start(f32[5,8,8,128]{3,2,1,0:T(8,128)S(1)} %get-tuple-element.17), channel_id=1, source_target_pairs={{0,3},{1,2},{2,1},{3,0},{4,7},{5,6},{6,5},{7,4},{8,11},{9,10},{10,... | collective-permute-start | bytes 491528 | tf_op jit(solution)/shard_map/ppermute | solution.py:449
  49.0 1.1 %copy-start.7 = (f32[5,16,32,128]{3,2,1,0:T(8,128)}, f32[5,16,32,128]{3,2,1,0:T(8,128)S(1)}, u32[]{:S(2)}) copy-start(f32[5,16,32,128]{3,2,1,0:T(8,128)S(1)} %get-tuple-element.18.base) | copy-start | bytes 3932164
  50.0 0.7 %copy-start.13 = (f32[16,32,128]{2,1,0:T(8,128)}, f32[16,32,128]{2,1,0:T(8,128)S(1)}, u32[]{:S(2)}) copy-start(f32[16,32,128]{2,1,0:T(8,128)S(1)} %get-tuple-element.19.mxb) | copy-start | bytes 786436
  50.7 1.3 %copy-start.8 = (f32[5,16,32,128]{3,2,1,0:T(8,128)S(1)}, f32[5,16,32,128]{3,2,1,0:T(8,128)}, u32[]{:S(2)}) copy-start(f32[5,16,32,128]{3,2,1,0:T(8,128)} %copy-done.7) | copy-start | bytes 3932164
  52.0 0.9 %copy-start.14 = (f32[16,32,128]{2,1,0:T(8,128)S(1)}, f32[16,32,128]{2,1,0:T(8,128)}, u32[]{:S(2)}) copy-start(f32[16,32,128]{2,1,0:T(8,128)} %copy-done.13) | copy-start | bytes 786436

commit v2 on v1

--- a/solution.py
+++ b/solution.py
@@ -14,7 +14,9 @@
 Y_WEIGHTS = (4.0 / 5.0, -1.0 / 5.0, 4.0 / 105.0, -1.0 / 280.0)
 D6 = (1.0, -6.0, 15.0, -20.0, 15.0, -6.0, 1.0)
 
-C_C, C_MG, C_LEFT, C_RIGHT, C_ENDS, C_HALO, C_COUNT = 0, 16, 32, 48, 64, 68, 80
+C_C, C_MG = 0, NI
+C_LEFT, C_RIGHT = 0, NI
+C_ENDS, C_HALO = 0, 4
 
 
 def constant_system():
@@ -50,84 +52,89 @@
     return jnp.full((SUB, NK), x, F32)
 
 
+def in_hbm(*arrays):
+    return tuple(pltpu.with_memory_space_constraint(a, pltpu.HBM) for a in arrays)
+
+
 def parity(name):
     return lax.rem(lax.axis_index(name), 2)
 
 
-def pack_x_body(s_lo, s_hi, f_lo, f_hi, one, two):
-    core = parity("gx")
-
-    def put(right, left):
-        right[:, 0:3] = s_hi[:, 1:4]
-        right[:, 3:4] = f_hi[...]
-        left[:, 0:3] = s_lo[:, 0:3]
-        left[:, 3:4] = f_lo[...]
+def pack_body(s, f, fy, one, two, yone, ytwo, lo, hi, sem):
+    core, odd = parity("gx"), parity("gy")
+    copies = [
+        pltpu.make_async_copy(fy.at[:, :, 0:SUB, :], lo, sem.at[0]),
+        pltpu.make_async_copy(fy.at[:, :, NJ - SUB : NJ, :], hi, sem.at[1]),
+    ]
+    for c in copies:
+        c.start()
+
+    def faces(right, left):
+        moves = [
+            pltpu.make_async_copy(s.at[:, NI - 3 : NI], right.at[:, 0:3], sem.at[2]),
+            pltpu.make_async_copy(f.at[:, NI - 1 : NI], right.at[:, 3:4], sem.at[3]),
+            pltpu.make_async_copy(s.at[:, 0:3], left.at[:, 0:3], sem.at[4]),
+            pltpu.make_async_copy(f.at[:, 0:1], left.at[:, 3:4], sem.at[5]),
+        ]
+        for c in moves:
+            c.start()
+        for c in moves:
+            c.wait()
+
+    def rows(top, bottom):
+        for v in range(NV):
+            for i in range(NI):
+                part = pl.ds(4 * (i % 2), 4)
+                top[v, i // 2, part, :] = hi[v, i, 4:8, :]
+                bottom[v, i // 2, part, :] = lo[v, i, 0:4, :]
 
     @pl.when(core == 0)
     def _():
-        put(one, two)
+        faces(one, two)
 
     @pl.when(core == 1)
     def _():
-        put(two, one)
-
-
-def pack_x(state, flux_x):
-    out = jax.ShapeDtypeStruct((NV, 4, NJ, NK), F32)
-    return pl.pallas_call(
-        pack_x_body,
-        grid=(1,),
-        out_shape=(out, out),
-        in_specs=[
-            pl.BlockSpec((NV, 4, NJ, NK), lambda g: (0, 0, 0, 0)),
-            pl.BlockSpec((NV, 4, NJ, NK), lambda g: (0, 3, 0, 0)),
-            pl.BlockSpec((NV, 1, NJ, NK), lambda g: (0, 0, 0, 0)),
-            pl.BlockSpec((NV, 1, NJ, NK), lambda g: (0, NI - 1, 0, 0)),
-        ],
-        out_specs=[pl.BlockSpec((NV, 4, NJ, NK), lambda g: (0, 0, 0, 0))] * 2,
-        compiler_params=pltpu.CompilerParams(vmem_limit_bytes=8 << 20),
-        cost_estimate=pl.CostEstimate(flops=0, bytes_accessed=1 << 20, transcendentals=0),
-        name="pack_x",
-    )(state, state, flux_x, flux_x)
-
-
-def pack_y_body(lo, hi, one, two):
-    odd = parity("gy")
-
-    def put(top, bottom):
-        for v in range(NV):
-            for i in range(NI):
-                rows = pl.ds(4 * (i % 2), 4)
-                top[v, i // 2, rows, :] = hi[v, i, 4:8, :]
-                bottom[v, i // 2, rows, :] = lo[v, i, 0:4, :]
+        faces(two, one)
+
+    for c in copies:
+        c.wait()
 
     @pl.when(odd == 0)
     def _():
-        put(one, two)
+        rows(yone, ytwo)
 
     @pl.when(odd == 1)
     def _():
-        put(two, one)
-
-
-def pack_y(flux_y):
-    out = jax.ShapeDtypeStruct((NV, NI // 2, SUB, NK), F32)
+        rows(ytwo, yone)
+
+
+def pack(state, flux_x, flux_y):
+    x_out = jax.ShapeDtypeStruct((NV, 4, NJ, NK), F32)
+    y_out = jax.ShapeDtypeStruct((NV, NI // 2, SUB, NK), F32)
     return pl.pallas_call(
-        pack_y_body,
-        grid=(1,),
-        out_shape=(out, out),
-        in_specs=[
-            pl.BlockSpec((NV, NI, SUB, NK), lambda g: (0, 0, 0, 0)),
-            pl.BlockSpec((NV, NI, SUB, NK), lambda g: (0, 0, NJ // SUB - 1, 0)),
+        pack_body,
+        out_shape=(x_out, x_out, y_out, y_out),
+        in_specs=[pl.BlockSpec(memory_space=pltpu.HBM)] * 3,
+        out_specs=(pl.BlockSpec(memory_space=pltpu.VMEM),) * 4,
+        scratch_shapes=[
+            pltpu.VMEM((NV, NI, SUB, NK), F32),
+            pltpu.VMEM((NV, NI, SUB, NK), F32),
+            pltpu.SemaphoreType.DMA((6,)),
         ],
-        out_specs=[pl.BlockSpec((NV, NI // 2, SUB, NK), lambda g: (0, 0, 0, 0))] * 2,
         compiler_params=pltpu.CompilerParams(vmem_limit_bytes=8 << 20),
-        cost_estimate=pl.CostEstimate(flops=0, bytes_accessed=1 << 20, transcendentals=0),
-        name="pack_y",
-    )(flux_y, flux_y)
-
-
-def own_body(gap, s, f, coef, part):
+        cost_estimate=pl.CostEstimate(flops=0, bytes_accessed=2 << 20, transcendentals=0),
+        name="pack",
+    )(*in_hbm(state, flux_x, flux_y))
+
+
+def own_body(gap, s_hbm, f_hbm, inner, outer, edge, part, s, f, own, sem):
+    loads = [
+        (pltpu.make_async_copy(s_hbm.at[v], s.at[v], sem.at[0, v]), pltpu.make_async_copy(f_hbm.at[v], f.at[v], sem.at[1, v]))
+        for v in range(NV)
+    ]
+    for pair in loads:
+        for c in pair:
+            c.start()
     core = parity("gx")
     piece = lax.axis_index("gx")
     alpha = [0.5 - splat(gap[i]) for i in range(NI)]
@@ -156,14 +163,14 @@
         else:
             wh[0], wt[NI - 1] = n[0], m[NI - 1]
     for k in range(NI):
-        coef[C_C + k] = c[k]
-        coef[C_MG + k] = m[k] * g32[k]
-        coef[C_LEFT + k] = left[k]
-        coef[C_RIGHT + k] = right[k]
-    coef[C_ENDS + 0] = -alpha[0] * wh[0]
-    coef[C_ENDS + 1] = -alpha[NI - 1] * wh[NI - 1]
-    coef[C_ENDS + 2] = -alpha[0] * wt[0]
-    coef[C_ENDS + 3] = -alpha[NI - 1] * wt[NI - 1]
+        inner[C_C + k] = c[k]
+        inner[C_MG + k] = m[k] * g32[k]
+        outer[C_LEFT + k] = left[k]
+        outer[C_RIGHT + k] = right[k]
+    edge[C_ENDS + 0] = -alpha[0] * wh[0]
+    edge[C_ENDS + 1] = -alpha[NI - 1] * wh[NI - 1]
+    edge[C_ENDS + 2] = -alpha[0] * wt[0]
+    edge[C_ENDS + 3] = -alpha[NI - 1] * wt[NI - 1]
     vh = [wh[k] * g32[k] for k in range(NI)]
     vt = [wt[k] * g32[k] for k in range(NI)]
 
@@ -177,8 +184,8 @@
     for q in range(3):
         for e, v in enumerate((vh, vt)):
             low, high = spread(v, q - 3), spread(v, NI + q)
-            coef[C_HALO + 3 * e + q] = jnp.where(core == 0, high, low)
-            coef[C_HALO + 6 + 3 * e + q] = jnp.where(core == 0, low, high)
+            edge[C_HALO + 3 * e + q] = jnp.where(core == 0, high, low)
+            edge[C_HALO + 6 + 3 * e + q] = jnp.where(core == 0, low, high)
     sh = [spread(vh, j) for j in range(NI)]
     st = [spread(vt, j) for j in range(NI)]
     first = jnp.where(piece == 0, 1.0 / 36.0, 0.0).astype(F32)
@@ -192,19 +199,20 @@
     ft[NI - 1] = ft[NI - 1] + float(inv[NI - 1, NI - 1]) * last
 
     for i in range(NI):
-        coef[C_COUNT + i] = sh[i]
-        coef[C_COUNT + NI + i] = st[i]
-
-    @pl.loop(0, NV)
-    def _(v):
+        own[i] = sh[i]
+        own[NI + i] = st[i]
+
+    for v in range(NV):
+        for c in loads[v]:
+            c.wait()
         for q in range(NJ // SUB):
             rows = pl.ds(SUB * q, SUB)
             sums = [None] * 4
             for i in range(NI):
                 a, z = s[v, i, rows, :], f[v, i, rows, :]
                 terms = (
-                    coef[C_COUNT + i] * a,
-                    coef[C_COUNT + NI + i] * a,
+                    own[i] * a,
+                    own[NI + i] * a,
                     fh[i] * z,
                     ft[i] * z,
                 )
@@ -217,22 +225,30 @@
     return pl.pallas_call(
         own_body,
         out_shape=(
-            jax.ShapeDtypeStruct((C_COUNT + 2 * NI, SUB, NK), F32),
+            jax.ShapeDtypeStruct((2 * NI, SUB, NK), F32),
+            jax.ShapeDtypeStruct((2 * NI, SUB, NK), F32),
+            jax.ShapeDtypeStruct((16, SUB, NK), F32),
             jax.ShapeDtypeStruct((4, NV, NJ, NK), F32),
         ),
         in_specs=[
             pl.BlockSpec(memory_space=pltpu.SMEM),
-            pl.BlockSpec(memory_space=pltpu.VMEM),
-            pl.BlockSpec(memory_space=pltpu.VMEM),
+            pl.BlockSpec(memory_space=pltpu.HBM),
+            pl.BlockSpec(memory_space=pltpu.HBM),
         ],
-        out_specs=(pl.BlockSpec(memory_space=pltpu.VMEM),) * 2,
+        out_specs=(pl.BlockSpec(memory_space=pltpu.VMEM),) * 4,
+        scratch_shapes=[
+            pltpu.VMEM((NV, NI, NJ, NK), F32),
+            pltpu.VMEM((NV, NI, NJ, NK), F32),
+            pltpu.VMEM((2 * NI, SUB, NK), F32),
+            pltpu.SemaphoreType.DMA((2, NV)),
+        ],
         compiler_params=pltpu.CompilerParams(vmem_limit_bytes=12 << 20),
         cost_estimate=pl.CostEstimate(flops=1 << 24, bytes_accessed=4 << 20, transcendentals=0),
         name="own_share",
-    )(gap, state, flux_x)
-
-
-def ends_body(coef, part, one, two, out):
+    )(gap, *in_hbm(state, flux_x))
+
+
+def ends_body(edge, part, one, two, out):
     core = parity("gx")
     is0 = core == 0
     fw = []
@@ -248,17 +264,17 @@
             for e in range(2):
                 total = part[e, v, rows, :]
                 for k in range(3):
-                    total = total + coef[C_HALO + 3 * e + k] * a[k]
-                    total = total + coef[C_HALO + 6 + 3 * e + k] * b[k]
+                    total = total + edge[C_HALO + 3 * e + k] * a[k]
+                    total = total + edge[C_HALO + 6 + 3 * e + k] * b[k]
                 out[pl.ds(ROWS * SUB * q + NV * e + v, SUB, stride=ROWS), :] = total
                 total = part[2 + e, v, rows, :] + fw[e][0] * a[3] + fw[e][1] * b[3]
                 out[pl.ds(ROWS * SUB * q + NV * (2 + e) + v, SUB, stride=ROWS), :] = total
     for k in range(4):
         for q in range(NJ // SUB):
-            out[pl.ds(ROWS * SUB * q + 4 * NV + k, SUB, stride=ROWS), :] = coef[C_ENDS + k]
-
-
-def end_values(coef, part, one, two):
+            out[pl.ds(ROWS * SUB * q + 4 * NV + k, SUB, stride=ROWS), :] = edge[C_ENDS + k]
+
+
+def end_values(edge, part, one, two):
     return pl.pallas_call(
         ends_body,
         out_shape=jax.ShapeDtypeStruct((PIECES * ROWS, NK), F32),
@@ -267,7 +283,7 @@
         compiler_params=pltpu.CompilerParams(vmem_limit_bytes=12 << 20),
         cost_estimate=pl.CostEstimate(flops=1 << 20, bytes_accessed=1 << 20, transcendentals=0),
         name="end_values",
-    )(coef, part, one, two)
+    )(edge, part, one, two)
 
 
 def join_body(x, out):
@@ -326,7 +342,14 @@
     )(x)
 
 
-def block_body(coef, s, f, fy, one, two, yone, ytwo, mx, my, base, mxb, pad):
+def block_body(inner, s_hbm, f_hbm, fy_hbm, one, two, yone, ytwo, mx, my, base, mxb, s, f, fy, pad, sem):
+    loads = [
+        [pltpu.make_async_copy(h.at[v], t.at[v], sem.at[k, v]) for k, (h, t) in enumerate(((fy_hbm, fy), (s_hbm, s), (f_hbm, f)))]
+        for v in range(NV)
+    ]
+    for group in loads:
+        for c in group:
+            c.start()
     piece = lax.axis_index("gx")
     is0 = parity("gx") == 0
     even = parity("gy") == 0
@@ -337,6 +360,10 @@
     for i in range(NI):
         mxb[i] = jnp.broadcast_to(mxt[:, i : i + 1], (NJ, NK))
         pad[NI + i, 0:NJ, :] = jnp.broadcast_to(myt[:, i : i + 1], (NJ, NK))
+
+    for v in range(NV):
+        for c in loads[v]:
+            c.wait()
 
     @pl.loop(0, NV)
     def _(v):
@@ -364,8 +391,8 @@
                     + 15.0 * (st[i + 2] + st[i + 4])
                     - 20.0 * st[i + 3]
                 )
-                y = coef[C_MG + i] * d6
-                ye.append(y - coef[C_C + i] * ye[-1] if i else y)
+                y = inner[C_MG + i] * d6
+                ye.append(y - inner[C_C + i] * ye[-1] if i else y)
                 u = fl[i + 2] - fl[i]
                 us.append(u)
                 r = float(RHO * CS["m"][i]) * u
@@ -376,7 +403,7 @@
                 yd.append(r - float(CS["c"][i]) * yd[-1] if i else r)
             xe = xd = None
             for i in range(NI - 1, -1, -1):
-                xe = ye[i] if xe is None else ye[i] - coef[C_C + i] * xe
+                xe = ye[i] if xe is None else ye[i] - inner[C_C + i] * xe
                 xd = yd[i] if xd is None else yd[i] - float(CS["c"][i]) * xd
                 at = SUB + SUB * q
                 dy = None
@@ -387,25 +414,27 @@
                 base[v, i, rows, :] = (st[i + 3] + xe) + (mxb[i, rows, :] * d + pad[NI + i, rows, :] * dy)
 
 
-def block(coef, state, flux_x, flux_y, one, two, yone, ytwo, mx, my):
+def block(inner, state, flux_x, flux_y, one, two, yone, ytwo, mx, my):
+    vmem, hbm = pl.BlockSpec(memory_space=pltpu.VMEM), pl.BlockSpec(memory_space=pltpu.HBM)
     return pl.pallas_call(
         block_body,
         out_shape=(
             jax.ShapeDtypeStruct((NV, NI, NJ, NK), F32),
             jax.ShapeDtypeStruct((NI, NJ, NK), F32),
         ),
-        in_specs=[pl.BlockSpec(memory_space=pltpu.VMEM)] * 10,
-        out_specs=(pl.BlockSpec(memory_space=pltpu.VMEM),) * 2,
-        scratch_shapes=[pltpu.VMEM((2 * NI, SUB + NJ + SUB, NK), F32)],
+        in_specs=[vmem] + [hbm] * 3 + [vmem] * 6,
+        out_specs=(vmem, vmem),
+        scratch_shapes=[pltpu.VMEM((NV, NI, NJ, NK), F32)] * 3
+        + [pltpu.VMEM((2 * NI, SUB + NJ + SUB, NK), F32), pltpu.SemaphoreType.DMA((3, NV))],
         compiler_params=pltpu.CompilerParams(vmem_limit_bytes=16 << 20),
         cost_estimate=pl.CostEstimate(flops=1 << 25, bytes_accessed=8 << 20, transcendentals=0),
         name="block",
-    )(coef, state, flux_x, flux_y, one, two, yone, ytwo, mx, my)
-
-
-def finish_body(coef, base, mxb, z, out):
-    @pl.loop(0, NV)
-    def _(v):
+    )(inner, *in_hbm(state, flux_x, flux_y), one, two, yone, ytwo, mx, my)
+
+
+def finish_body(outer, base, mxb, z, out_hbm, out, sem):
+    stores = [pltpu.make_async_copy(out.at[v], out_hbm.at[v], sem.at[v]) for v in range(NV)]
+    for v in range(NV):
         for q in range(NJ // SUB):
             rows = pl.ds(SUB * q, SUB)
             lf, rf, ld, rd = (
@@ -413,20 +442,24 @@
             )
             for i in range(NI):
                 d = float(CS["left"][i]) * ld + float(CS["right"][i]) * rd
-                e = coef[C_LEFT + i] * lf + coef[C_RIGHT + i] * rf
+                e = outer[C_LEFT + i] * lf + outer[C_RIGHT + i] * rf
                 out[v, i, rows, :] = (base[v, i, rows, :] + e) + mxb[i, rows, :] * d
-
-
-def finish(coef, base, mxb, z):
+        stores[v].start()
+    for c in stores:
+        c.wait()
+
+
+def finish(outer, base, mxb, z):
     return pl.pallas_call(
         finish_body,
         out_shape=jax.ShapeDtypeStruct((NV, NI, NJ, NK), F32),
         in_specs=[pl.BlockSpec(memory_space=pltpu.VMEM)] * 4,
-        out_specs=pl.BlockSpec(memory_space=pltpu.VMEM),
+        out_specs=pl.BlockSpec(memory_space=pltpu.HBM),
+        scratch_shapes=[pltpu.VMEM((NV, NI, NJ, NK), F32), pltpu.SemaphoreType.DMA((NV,))],
         compiler_params=pltpu.CompilerParams(vmem_limit_bytes=12 << 20),
         cost_estimate=pl.CostEstimate(flops=1 << 22, bytes_accessed=3 << 20, transcendentals=0),
         name="finish",
-    )(coef, base, mxb, z)
+    )(outer, base, mxb, z)
 
 
 def exchange(x):
@@ -441,17 +474,19 @@
     y_in = [(i, i ^ 1) for i in range(count_y)]
     y_out = [(i, (i + 1 if i % 2 else i - 1) % count_y) for i in range(count_y)]
 
-    send_one, send_two = pack_x(state, flux_x)
+    send_one, send_two, ysend_one, ysend_two = pack(state, flux_x, flux_y)
     one = lax.ppermute(send_one, "gx", pair_in)
     two = lax.ppermute(send_two, "gx", pair_out)
-    ysend_one, ysend_two = pack_y(flux_y)
     yone = lax.ppermute(ysend_one, "gy", y_in)
     ytwo = lax.ppermute(ysend_two, "gy", y_out)
-    coef, part = own_share(filter_gap, state, flux_x)
-    ends = exchange(end_values(coef, part, one, two))
-    base, mxb = block(coef, state, flux_x, flux_y, one, two, yone, ytwo, metric_x, metric_y)
+    inner, outer, edge, part = own_share(filter_gap, state, flux_x)
+    ends = end_values(edge, part, one, two)
+    ends, yone, ytwo = lax.optimization_barrier((ends, yone, ytwo))
+    ends = exchange(ends)
+    base, mxb = block(inner, state, flux_x, flux_y, one, two, yone, ytwo, metric_x, metric_y)
+    ends, base, mxb = lax.optimization_barrier((ends, base, mxb))
     outside = exchange(join(ends))
-    return finish(coef, base, mxb, outside)
+    return finish(outer, base, mxb, outside)
 
 
 def solution(mesh):

time: 55.1 us -> 48 us (0.87)
  local copies, waits for them, and re-layouts: 9.34 us -> 0.02 us
  blocking collectives: 19.1 us -> 13.8 us
  starting transfers between devices: 12.6 us -> 17.6 us
  Pallas kernels: 5.28 us -> 10.1 us
  waiting for transfers between devices: 8.03 us -> 6.15 us
    unnamed x36 -> x6, local copies, waits for them, and re-layouts: 9.34 us -> 0.02 us
    all_to_all x1, waiting for transfers between devices: 0.01 us -> 6.14 us  [exchange(): y = lax.all_to_all(x.reshape(PIECES, ROWS, NK), 'gx', 0, 0, tiled=True)]
    all_to_all x1, blocking collectives: 19.1 us -> 13.8 us  [exchange(): y = lax.all_to_all(x.reshape(PIECES, ROWS, NK), 'gx', 0, 0, tiled=True)]
    all_to_all x1, starting transfers between devices: 3.9 us -> 9.08 us  [exchange(): y = lax.all_to_all(x.reshape(PIECES, ROWS, NK), 'gx', 0, 0, tiled=True)]
    ppermute x1, waiting for transfers between devices: 3.94 us -> 0.01 us  [per_device(): two = lax.ppermute(send_two, 'gx', pair_out)]
    pallas_call x3 -> x2, Pallas kernels: 1.34 us -> 3.76 us  [the longest x1 2.37 us: own_share(): pl.pallas_call(own_body, out_shape=(jax.ShapeDtypeStruct((2 * NI, SUB, NK...]
    ppermute x1, waiting for transfers between devices: 2.14 us -> 0.01 us  [per_device(): ytwo = lax.ppermute(ysend_two, 'gy', y_out)]
    ppermute x1, waiting for transfers between devices: 1.94 us -> 0.01 us  [per_device(): yone = lax.ppermute(ysend_one, 'gy', y_in)]
  transfers between devices with their start and end apart: 5 -> 5, of which waited for: 3 -> 1; matrix products, arithmetic and copies ran while one was open for 0% -> 0% of each run, Pallas kernels for 6% -> 15%
where the time goes in v2:
time: 48 us; the launch traced here: 47.7 us
  starting transfers between devices  17.6 us (37%)
  blocking collectives  13.8 us (29%)
  Pallas kernels  10.1 us (21%)
  waiting for transfers between devices  6.15 us (13%)
    all_to_all x1, blocking collectives, exchange(): y = lax.all_to_all(x.reshape(PIECES, ROWS, NK), 'gx', 0, 0, tiled=True)  13.8 us
    all_to_all x1, starting transfers between devices, exchange(): y = lax.all_to_all(x.reshape(PIECES, ROWS, NK), 'gx', 0, 0, tiled=True)  9.08 us
    all_to_all x1, waiting for transfers between devices, exchange(): y = lax.all_to_all(x.reshape(PIECES, ROWS, NK), 'gx', 0, 0, tiled=True)  6.14 us
    pallas_call x1, Pallas kernels, block(): pl.pallas_call(block_body, out_shape=(jax.ShapeDtypeStruct((NV, NI, NJ, N...  4.01 us
    ppermute x1, starting transfers between devices, per_device(): two = lax.ppermute(send_two, 'gx', pair_out)  3.1 us
    pallas_call x1, Pallas kernels, own_share(): pl.pallas_call(own_body, out_shape=(jax.ShapeDtypeStruct((2 * NI, SUB, NK...  2.37 us
    ppermute x1, starting transfers between devices, per_device(): ytwo = lax.ppermute(ysend_two, 'gy', y_out)  2.24 us
    ppermute x1, starting transfers between devices, per_device(): yone = lax.ppermute(ysend_one, 'gy', y_in)  1.72 us
  transfers between devices with their start and end apart: 5, of which 1 were waited for; matrix products, arithmetic and copies ran while one was open for 0% of the time, Pallas kernels for 15%

profile of v2, /device:TPU:1, one launch (start us, length us, event | category | flops | bytes accessed | tf_op | source)
XLA Modules:
  0.0 47.7 jit_solution(1209107607773539034)
XLA Ops:
  0.0 0.0 copy-start.2
  0.0 1.4 %pack.1 = (f32[5,4,32,128]{3,2,1,0:T(8,128)S(1)}, f32[5,4,32,128]{3,2,1,0:T(8,128)S(1)}, f32[5,8,8,128]{3,2,1,0:T(8,128)S(1)}, f32[5,8,8,128]{3,2,1,0:T(8,128)S(1)}) custom-call(f32[5,16,32,128]{3,2,1,0:T(8,128)} %s_hbm.3, f32[5,16,32,128]{3,2,1,0:T(8,128)} %f_hbm.3, f32[5,16,32,128]{3,2,1,0:T(8,128)} %fy_hbm.1), custom_call_target="tpu_custom_call" | custom-call | bytes 2097152 | tf_op jit(solution)/shard_map/pack/pallas_call | solution.py:114
  1.4 1.5 %collective-permute-start = (f32[5,4,32,128]{3,2,1,0:T(8,128)S(1)}, f32[5,4,32,128]{3,2,1,0:T(8,128)S(1)}, u32[]{:S(2)}, u32[]{:S(2)}) collective-permute-start(f32[5,4,32,128]{3,2,1,0:T(8,128)S(1)} %get-tuple-element.24), channel_id=1, source_target_pairs={{0,4},{4,0},{8,12},{12,8},{16,20},{20,16},{24,28},{28,24},{32,36},... | collective-permute-start | bytes 983048 | tf_op jit(solution)/shard_map/ppermute | solution.py:478
  2.9 3.1 %collective-permute-start.1 = (f32[5,4,32,128]{3,2,1,0:T(8,128)S(1)}, f32[5,4,32,128]{3,2,1,0:T(8,128)S(1)}, u32[]{:S(2)}, u32[]{:S(2)}) collective-permute-start(f32[5,4,32,128]{3,2,1,0:T(8,128)S(1)} %get-tuple-element.25), channel_id=1, source_target_pairs={{4,8},{8,4},{12,16},{16,12},{20,24},{24,20},{28,32},{32,28},{36,40... | collective-permute-start | bytes 983048 | tf_op jit(solution)/shard_map/ppermute | solution.py:479
  6.0 1.7 %collective-permute-start.2 = (f32[5,8,8,128]{3,2,1,0:T(8,128)S(1)}, f32[5,8,8,128]{3,2,1,0:T(8,128)S(1)}, u32[]{:S(2)}, u32[]{:S(2)}) collective-permute-start(f32[5,8,8,128]{3,2,1,0:T(8,128)S(1)} %get-tuple-element.26), channel_id=1, source_target_pairs={{0,1},{1,0},{2,3},{3,2},{4,5},{5,4},{6,7},{7,6},{8,9},{9,8},{10,11... | collective-permute-start | bytes 491528 | tf_op jit(solution)/shard_map/ppermute | solution.py:480
  7.7 2.2 %collective-permute-start.3 = (f32[5,8,8,128]{3,2,1,0:T(8,128)S(1)}, f32[5,8,8,128]{3,2,1,0:T(8,128)S(1)}, u32[]{:S(2)}, u32[]{:S(2)}) collective-permute-start(f32[5,8,8,128]{3,2,1,0:T(8,128)S(1)} %get-tuple-element.27), channel_id=1, source_target_pairs={{0,3},{1,2},{2,1},{3,0},{4,7},{5,6},{6,5},{7,4},{8,11},{9,10},{10,... | collective-permute-start | bytes 491528 | tf_op jit(solution)/shard_map/ppermute | solution.py:481
  10.0 0.0 copy-done.2
  10.0 2.4 %own_share.1 = (f32[32,8,128]{2,1,0:T(8,128)S(1)}, f32[32,8,128]{2,1,0:T(8,128)S(1)}, f32[16,8,128]{2,1,0:T(8,128)S(1)}, f32[4,5,32,128]{3,2,1,0:T(8,128)S(1)}) custom-call(f32[16]{0:T(128)S(1)} %copy-done.2, f32[5,16,32,128]{3,2,1,0:T(8,128)} %s_hbm.3, f32[5,16,32,128]{3,2,1,0:T(8,128)} %f_hbm.3), custom_call_target="tpu_custom_call" | custom-call | flops 16777216 | bytes 4194304 | tf_op jit(solution)/shard_map/own_share/pallas_call | solution.py:225
  12.4 0.0 copy-start
  12.4 0.0 copy-start.1
  12.4 0.0 collective-permute-done.one
  12.4 0.0 collective-permute-done.1.two
  12.4 0.9 %end_values.1 = f32[768,128]{1,0:T(8,128)} custom-call(f32[16,8,128]{2,1,0:T(8,128)S(1)} %get-tuple-element.22.edge, f32[4,5,32,128]{3,2,1,0:T(8,128)S(1)} %get-tuple-element.23.part, f32[5,4,32,128]{3,2,1,0:T(8,128)S(1)} %collective-permute-done.one, f32[5,4,32,128]{3,2,1,0:T(8,128)S(1)} %collective-permute-done.1.two), custom_call_target="tpu_custom_call" | custom-call | flops 1048576 | bytes 1048576 | tf_op jit(solution)/shard_map/end_values/pallas_call | solution.py:278
  13.3 0.0 collective-permute-done.2.yone
  13.3 0.0 collective-permute-done.3.ytwo
  13.3 9.1 %all-to-all-start = ((f32[32,24,128]{2,1,0:T(8,128)}), f32[32,24,128]{2,1,0:T(8,128)S(1)}, u32[]{:S(2)}, u32[]{:S(2)}) async-start(f32[32,24,128]{2,1,0:T(8,128)} %bitcast), calls=%async_computation | async-start | bytes 786432 | tf_op jit(solution)/shard_map/all_to_all | solution.py:466
  22.4 0.0 copy-done
  22.4 0.0 copy-done.1
  22.4 4.0 %block.1 = (f32[5,16,32,128]{3,2,1,0:T(8,128)S(1)}, f32[16,32,128]{2,1,0:T(8,128)S(1)}) custom-call(f32[32,8,128]{2,1,0:T(8,128)S(1)} %get-tuple-element.29.inner, f32[5,16,32,128]{3,2,1,0:T(8,128)} %s_hbm.3, f32[5,16,32,128]{3,2,1,0:T(8,128)} %f_hbm.3, f32[5,16,32,128]{3,2,1,0:T(8,128)} %fy_hbm.1, f32[5,4,32,128]{3,2,1,0:T(8,128)S(1)} %collective-permute-done.one, ...), custom_call_target="tpu_custom_call" | custom-call | flops 33554432 | bytes 8388608 | tf_op jit(solution)/shard_map/block/pallas_call | solution.py:419
  26.4 6.1 %all-to-all-done = f32[32,24,128]{2,1,0:T(8,128)S(1)} async-done(((f32[32,24,128]{2,1,0:T(8,128)}), f32[32,24,128]{2,1,0:T(8,128)S(1)}, u32[]{:S(2)}, u32[]{:S(2)}) %all-to-all-start) | async-done | bytes 393248 | tf_op jit(solution)/shard_map/all_to_all | solution.py:466
  32.5 0.2 join.1
  32.8 13.8 %all_to_all.10 = f32[32,24,128]{2,1,0:T(8,128)S(1)} all-to-all(f32[32,24,128]{2,1,0:T(8,128)S(1)} %bitcast.5), channel_id=1, replica_groups=mesh['gx'=32,'gy'=4] {'gx'}, dimensions={0} | all-to-all | bytes 786432 | tf_op jit(solution)/shard_map/all_to_all | solution.py:466
  46.5 1.2 %finish.1 = f32[5,16,32,128]{3,2,1,0:T(8,128)} custom-call(f32[32,8,128]{2,1,0:T(8,128)S(1)} %get-tuple-element.21.outer, f32[5,16,32,128]{3,2,1,0:T(8,128)S(1)} %get-tuple-element.34.base, f32[16,32,128]{2,1,0:T(8,128)S(1)} %get-tuple-element.35.mxb, f32[768,128]{1,0:T(8,128)S(1)} %bitcast.6), custom_call_target="tpu_custom_call" | custom-call | flops 4194304 | bytes 3145728 | tf_op jit(solution)/shard_map/finish/pallas_call | solution.py:453
Async XLA Ops:
  0.0 10.0 %copy-start.2 = (f32[16]{0:T(128)S(1)}, f32[16]{0:T(128)}, u32[]{:S(2)}) copy-start(f32[16]{0:T(128)} %gap.1) | copy-start | bytes 196
  1.4 11.0 %collective-permute-start = (f32[5,4,32,128]{3,2,1,0:T(8,128)S(1)}, f32[5,4,32,128]{3,2,1,0:T(8,128)S(1)}, u32[]{:S(2)}, u32[]{:S(2)}) collective-permute-start(f32[5,4,32,128]{3,2,1,0:T(8,128)S(1)} %get-tuple-element.24), channel_id=1, source_target_pairs={{0,4},{4,0},{8,12},{12,8},{16,20},{20,16},{24,28},{28,24},{32,36},... | collective-permute-start | bytes 983048 | tf_op jit(solution)/shard_map/ppermute | solution.py:478
  2.9 9.5 %collective-permute-start.1 = (f32[5,4,32,128]{3,2,1,0:T(8,128)S(1)}, f32[5,4,32,128]{3,2,1,0:T(8,128)S(1)}, u32[]{:S(2)}, u32[]{:S(2)}) collective-permute-start(f32[5,4,32,128]{3,2,1,0:T(8,128)S(1)} %get-tuple-element.25), channel_id=1, source_target_pairs={{4,8},{8,4},{12,16},{16,12},{20,24},{24,20},{28,32},{32,28},{36,40... | collective-permute-start | bytes 983048 | tf_op jit(solution)/shard_map/ppermute | solution.py:479
  6.0 7.3 %collective-permute-start.2 = (f32[5,8,8,128]{3,2,1,0:T(8,128)S(1)}, f32[5,8,8,128]{3,2,1,0:T(8,128)S(1)}, u32[]{:S(2)}, u32[]{:S(2)}) collective-permute-start(f32[5,8,8,128]{3,2,1,0:T(8,128)S(1)} %get-tuple-element.26), channel_id=1, source_target_pairs={{0,1},{1,0},{2,3},{3,2},{4,5},{5,4},{6,7},{7,6},{8,9},{9,8},{10,11... | collective-permute-start | bytes 491528 | tf_op jit(solution)/shard_map/ppermute | solution.py:480
  7.7 5.6 %collective-permute-start.3 = (f32[5,8,8,128]{3,2,1,0:T(8,128)S(1)}, f32[5,8,8,128]{3,2,1,0:T(8,128)S(1)}, u32[]{:S(2)}, u32[]{:S(2)}) collective-permute-start(f32[5,8,8,128]{3,2,1,0:T(8,128)S(1)} %get-tuple-element.27), channel_id=1, source_target_pairs={{0,3},{1,2},{2,1},{3,0},{4,7},{5,6},{6,5},{7,4},{8,11},{9,10},{10,... | collective-permute-start | bytes 491528 | tf_op jit(solution)/shard_map/ppermute | solution.py:481
  12.4 10.0 %copy-start = (f32[16,32]{1,0:T(8,128)S(1)}, f32[16,32]{1,0:T(8,128)}, u32[]{:S(2)}) copy-start(f32[16,32]{1,0:T(8,128)} %mx.1) | copy-start | bytes 6148
  12.4 10.0 %copy-start.1 = (f32[16,32]{1,0:T(8,128)S(1)}, f32[16,32]{1,0:T(8,128)}, u32[]{:S(2)}) copy-start(f32[16,32]{1,0:T(8,128)} %my.1) | copy-start | bytes 6148
  13.3 19.3 %all-to-all-start = ((f32[32,24,128]{2,1,0:T(8,128)}), f32[32,24,128]{2,1,0:T(8,128)S(1)}, u32[]{:S(2)}, u32[]{:S(2)}) async-start(f32[32,24,128]{2,1,0:T(8,128)} %bitcast), calls=%async_computation | async-start | bytes 786432 | tf_op jit(solution)/shard_map/all_to_all | solution.py:466

commit v3 on v2

--- a/solution.py
+++ b/solution.py
@@ -7,16 +7,17 @@
 from jax.sharding import PartitionSpec as P
 
 NV, NI, NJ, NK = 5, 16, 32, 128
-PIECES = 32
-ROWS = 24
+PIECES, PAIRS, HALF = 32, 16, 16
+ROWS, WIDE = 24, 64
+EDGE = 12 * NV * HALF
 SUB = 8
 F32 = jnp.float32
 Y_WEIGHTS = (4.0 / 5.0, -1.0 / 5.0, 4.0 / 105.0, -1.0 / 280.0)
+RHO = 25.0 / 36.0
 D6 = (1.0, -6.0, 15.0, -20.0, 15.0, -6.0, 1.0)
 
 C_C, C_MG = 0, NI
 C_LEFT, C_RIGHT = 0, NI
-C_ENDS, C_HALO = 0, 4
 
 
 def constant_system():
@@ -31,14 +32,22 @@
         c.append(prev)
     left, right = -a * inv[:, 0], -a * inv[:, -1]
     hl, hr, tl, tr = left[0], right[0], left[-1], right[-1]
-    e = [tr]
-    for _ in range(PIECES - 1):
-        e.append(tr + tl * hr * e[-1] / (1.0 - hl * e[-1]))
-    return dict(m=m, c=c, inv=inv, left=left, right=right, hl=hl, hr=hr, tl=tl, tr=tr, e=e)
+    d = 1.0 / (1.0 - tr * hl)
+    w = RHO * np.array([-inv[0, 0], -inv[-1, 0], inv[0, -1], inv[-1, -1]])
+    pair = dict(inv=d, inv_hl=d * hl, inv_tr=d * tr, down=[hl * tl * d, hr * d, tl * d, tr * hr * d])
+    pair["low"] = [w[0] + hr * hl * d * w[1], tl * d * w[1]]
+    pair["high"] = [hr * d * w[2], w[3] + tl * tr * d * w[2]]
+    for k in pair:
+        pair[k] = [float(t) for t in pair[k]] if isinstance(pair[k], list) else float(pair[k])
+    p = dict(hl=hl + hr * hl * tl * d, hr=hr * hr * d, tl=tl * tl * d, tr=tr + tl * tr * hr * d)
+    e = [p["tr"]]
+    for _ in range(PAIRS - 1):
+        e.append(p["tr"] + p["tl"] * p["hr"] * e[-1] / (1.0 - p["hl"] * e[-1]))
+    pair.update(p, e=e)
+    return dict(m=m, c=c, inv=inv, left=left, right=right, hl=hl, hr=hr, tl=tl, tr=tr, pair=pair)
 
 
 CS = constant_system()
-RHO = 25.0 / 36.0
 
 
 def flux_weight(row, j):
@@ -127,13 +136,16 @@
     )(*in_hbm(state, flux_x, flux_y))
 
 
-def own_body(gap, s_hbm, f_hbm, inner, outer, edge, part, s, f, own, sem):
+def own_body(gap, s_hbm, f_hbm, inner, outer, mine, send, s, f, own, sem):
     loads = [
-        (pltpu.make_async_copy(s_hbm.at[v], s.at[v], sem.at[0, v]), pltpu.make_async_copy(f_hbm.at[v], f.at[v], sem.at[1, v]))
+        (
+            pltpu.make_async_copy(s_hbm.at[v], s.at[v], sem.at[0, v]),
+            pltpu.make_async_copy(f_hbm.at[v], f.at[v], sem.at[1, v]),
+        )
         for v in range(NV)
     ]
-    for pair in loads:
-        for c in pair:
+    for both in loads:
+        for c in both:
             c.start()
     core = parity("gx")
     piece = lax.axis_index("gx")
@@ -167,10 +179,6 @@
         inner[C_MG + k] = m[k] * g32[k]
         outer[C_LEFT + k] = left[k]
         outer[C_RIGHT + k] = right[k]
-    edge[C_ENDS + 0] = -alpha[0] * wh[0]
-    edge[C_ENDS + 1] = -alpha[NI - 1] * wh[NI - 1]
-    edge[C_ENDS + 2] = -alpha[0] * wt[0]
-    edge[C_ENDS + 3] = -alpha[NI - 1] * wt[NI - 1]
     vh = [wh[k] * g32[k] for k in range(NI)]
     vt = [wt[k] * g32[k] for k in range(NI)]
 
@@ -181,13 +189,15 @@
             total = total + t
         return total
 
-    for q in range(3):
-        for e, v in enumerate((vh, vt)):
-            low, high = spread(v, q - 3), spread(v, NI + q)
-            edge[C_HALO + 3 * e + q] = jnp.where(core == 0, high, low)
-            edge[C_HALO + 6 + 3 * e + q] = jnp.where(core == 0, low, high)
-    sh = [spread(vh, j) for j in range(NI)]
-    st = [spread(vt, j) for j in range(NI)]
+    edge = [-alpha[0] * wh[0], -alpha[NI - 1] * wh[NI - 1], -alpha[0] * wt[0], -alpha[NI - 1] * wt[NI - 1]]
+    low = [spread(v, q - 3) for v in (vh, vt) for q in range(3)]
+    high = [spread(v, NI + q) for v in (vh, vt) for q in range(3)]
+    edge += [jnp.where(core == 0, h, l) for h, l in zip(high, low)]
+    edge += [jnp.where(core == 0, l, h) for h, l in zip(high, low)]
+    for k, t in enumerate(edge):
+        mine[pl.ds(EDGE + k, 1), :] = t[0:1]
+        send[pl.ds(EDGE + k, 1), :] = t[0:1]
+
     first = jnp.where(piece == 0, 1.0 / 36.0, 0.0).astype(F32)
     last = jnp.where(piece == PIECES - 1, -1.0 / 36.0, 0.0).astype(F32)
     inv = CS["inv"]
@@ -199,43 +209,37 @@
     ft[NI - 1] = ft[NI - 1] + float(inv[NI - 1, NI - 1]) * last
 
     for i in range(NI):
-        own[i] = sh[i]
-        own[NI + i] = st[i]
-
+        own[i] = spread(vh, i)
+        own[NI + i] = spread(vt, i)
+
+    s_in, f_in = (NI - 3) * (1 - core), (NI - 1) * (1 - core)
+    s_out, f_out = (NI - 3) * core, (NI - 1) * core
     for v in range(NV):
         for c in loads[v]:
             c.wait()
-        for q in range(NJ // SUB):
-            rows = pl.ds(SUB * q, SUB)
-            sums = [None] * 4
-            for i in range(NI):
-                a, z = s[v, i, rows, :], f[v, i, rows, :]
-                terms = (
-                    own[i] * a,
-                    own[NI + i] * a,
-                    fh[i] * z,
-                    ft[i] * z,
-                )
-                sums = [t if o is None else o + t for o, t in zip(sums, terms)]
-            for e in range(4):
-                part[e, v, rows, :] = sums[e]
+        for out, half in ((mine, core), (send, 1 - core)):
+            for r in range(HALF // SUB):
+                rows = pl.ds(pl.multiple_of(HALF * half + SUB * r, SUB), SUB)
+                sums = [None] * 4
+                for i in range(NI):
+                    a, z = s[v, i, rows, :], f[v, i, rows, :]
+                    terms = (own[i] * a, own[NI + i] * a, fh[i] * z, ft[i] * z)
+                    sums = [t if o is None else o + t for o, t in zip(sums, terms)]
+                faces = [s[v, s_in + k, rows, :] for k in range(3)] + [f[v, f_in, rows, :]]
+                faces += [s[v, s_out + k, rows, :] for k in range(3)] + [f[v, f_out, rows, :]]
+                for k, t in enumerate(sums + faces):
+                    out[pl.ds((NV * k + v) * HALF + SUB * r, SUB), :] = t
 
 
 def own_share(gap, state, flux_x):
+    vmem, hbm = pl.BlockSpec(memory_space=pltpu.VMEM), pl.BlockSpec(memory_space=pltpu.HBM)
+    coef = jax.ShapeDtypeStruct((2 * NI, SUB, NK), F32)
+    values = jax.ShapeDtypeStruct((EDGE + 16, NK), F32)
     return pl.pallas_call(
         own_body,
-        out_shape=(
-            jax.ShapeDtypeStruct((2 * NI, SUB, NK), F32),
-            jax.ShapeDtypeStruct((2 * NI, SUB, NK), F32),
-            jax.ShapeDtypeStruct((16, SUB, NK), F32),
-            jax.ShapeDtypeStruct((4, NV, NJ, NK), F32),
-        ),
-        in_specs=[
-            pl.BlockSpec(memory_space=pltpu.SMEM),
-            pl.BlockSpec(memory_space=pltpu.HBM),
-            pl.BlockSpec(memory_space=pltpu.HBM),
-        ],
-        out_specs=(pl.BlockSpec(memory_space=pltpu.VMEM),) * 4,
+        out_shape=(coef, coef, values, values),
+        in_specs=[pl.BlockSpec(memory_space=pltpu.SMEM), hbm, hbm],
+        out_specs=(vmem,) * 4,
         scratch_shapes=[
             pltpu.VMEM((NV, NI, NJ, NK), F32),
             pltpu.VMEM((NV, NI, NJ, NK), F32),
@@ -248,108 +252,194 @@
     )(gap, *in_hbm(state, flux_x))
 
 
-def ends_body(edge, part, one, two, out):
-    core = parity("gx")
-    is0 = core == 0
-    fw = []
-    for row in (0, NI - 1):
-        low, high = flux_weight(row, -1), flux_weight(row, NI)
-        fw.append((jnp.where(is0, high, low).astype(F32), jnp.where(is0, low, high).astype(F32)))
-
-    for v in range(NV):
-        for q in range(NJ // SUB):
-            rows = pl.ds(SUB * q, SUB)
-            a = [one[v, k, rows, :] for k in range(4)]
-            b = [two[v, k, rows, :] for k in range(4)]
-            for e in range(2):
-                total = part[e, v, rows, :]
-                for k in range(3):
-                    total = total + edge[C_HALO + 3 * e + k] * a[k]
-                    total = total + edge[C_HALO + 6 + 3 * e + k] * b[k]
-                out[pl.ds(ROWS * SUB * q + NV * e + v, SUB, stride=ROWS), :] = total
-                total = part[2 + e, v, rows, :] + fw[e][0] * a[3] + fw[e][1] * b[3]
-                out[pl.ds(ROWS * SUB * q + NV * (2 + e) + v, SUB, stride=ROWS), :] = total
-    for k in range(4):
-        for q in range(NJ // SUB):
-            out[pl.ds(ROWS * SUB * q + 4 * NV + k, SUB, stride=ROWS), :] = edge[C_ENDS + k]
-
-
-def end_values(edge, part, one, two):
-    return pl.pallas_call(
-        ends_body,
-        out_shape=jax.ShapeDtypeStruct((PIECES * ROWS, NK), F32),
-        in_specs=[pl.BlockSpec(memory_space=pltpu.VMEM)] * 4,
-        out_specs=pl.BlockSpec(memory_space=pltpu.VMEM),
-        compiler_params=pltpu.CompilerParams(vmem_limit_bytes=12 << 20),
+def pair_body(mine, got, out, mids):
+    is0 = parity("gx") == 0
+
+    def both(rows):
+        x, y = mine[rows, :], got[rows, :]
+        return jnp.where(is0, x, y), jnp.where(is0, y, x)
+
+    ca, cb = zip(*(both(pl.ds(EDGE + k, 1)) for k in range(16)))
+    ca, cb = ([jnp.broadcast_to(t, (SUB, NK)) for t in c] for c in (ca, cb))
+    hla, hra, tla, tra = ca[:4]
+    hlb, hrb, tlb, trb = cb[:4]
+    inv = 1.0 / (1.0 - tra * hlb)
+    down = [hlb * tla * inv, hrb * inv, tla * inv, tra * hrb * inv]
+    for k, t in enumerate(down):
+        mids[pl.ds(4 * NV * HALF + k, 1), :] = t[0:1]
+    cross_h, cross_t = hra * inv, tlb * inv
+    edge = [hla + hra * down[0], hra * down[1], tlb * down[2], trb + tlb * down[3]]
+    edge += [ca[10 + q] + (cross_h * hlb) * ca[13 + q] for q in range(3)]
+    edge += [cross_t * ca[13 + q] for q in range(3)]
+    edge += [cross_h * cb[10 + q] for q in range(3)]
+    edge += [cb[13 + q] + (cross_t * tra) * cb[10 + q] for q in range(3)]
+    lane = lax.broadcasted_iota(jnp.int32, (SUB, NK), 1)
+    packed = jnp.zeros((SUB, NK), F32)
+    for k, t in enumerate(edge):
+        packed = jnp.where(lane == k, t, packed)
+
+    k = CS["pair"]
+    for r in range(HALF // SUB):
+        at = WIDE * SUB * r
+        out[pl.ds(at + 12 * NV, SUB, stride=WIDE), :] = packed
+        for v in range(NV):
+            a, b = zip(*(both(pl.ds((NV * e + v) * HALF + SUB * r, SUB)) for e in range(12)))
+            ha, ta, hb, tb = a[0], a[1], b[0], b[1]
+            for q in range(3):
+                ha, ta = ha + ca[4 + q] * b[4 + q], ta + ca[7 + q] * b[4 + q]
+                hb, tb = hb + cb[4 + q] * a[4 + q], tb + cb[7 + q] * a[4 + q]
+            head = (hb + hlb * ta) * inv
+            tail = (ta + tra * hb) * inv
+            da, ea = a[2] + flux_weight(0, NI) * b[7], a[3] + flux_weight(NI - 1, NI) * b[7]
+            db, eb = b[2] + flux_weight(0, -1) * a[7], b[3] + flux_weight(NI - 1, -1) * a[7]
+            dhead = k["inv"] * db + k["inv_hl"] * ea
+            dtail = k["inv"] * ea + k["inv_tr"] * db
+            values = [ha + hra * head, tb + tlb * tail, da + float(CS["hr"]) * dhead, eb + float(CS["tl"]) * dtail]
+            values += list(a[8:12]) + list(b[8:12])
+            for e, t in enumerate(values):
+                out[pl.ds(at + NV * e + v, SUB, stride=WIDE), :] = t
+            for e, t in enumerate((head, tail, dhead, dtail)):
+                mids[pl.ds((NV * e + v) * HALF + SUB * r, SUB), :] = t
+
+
+def pair(mine, got):
+    vmem = pl.BlockSpec(memory_space=pltpu.VMEM)
+    return pl.pallas_call(
+        pair_body,
+        out_shape=(
+            jax.ShapeDtypeStruct((PAIRS * WIDE, NK), F32),
+            jax.ShapeDtypeStruct((4 * NV * HALF + SUB, NK), F32),
+        ),
+        in_specs=[vmem] * 2,
+        out_specs=(vmem,) * 2,
+        compiler_params=pltpu.CompilerParams(vmem_limit_bytes=8 << 20),
         cost_estimate=pl.CostEstimate(flops=1 << 20, bytes_accessed=1 << 20, transcendentals=0),
-        name="end_values",
-    )(edge, part, one, two)
-
-
-def join_body(x, out):
+        name="pair",
+    )(mine, got)
+
+
+def join_body(x, out, coef):
+    for r in range(PAIRS // SUB):
+        packed = x[pl.ds(WIDE * SUB * r + 12 * NV, SUB, stride=WIDE), :]
+        for k in range(16):
+            coef[pl.ds(PAIRS * k + SUB * r, SUB), :] = jnp.broadcast_to(packed[:, k : k + 1], (SUB, NK))
+
     def row(p, k):
-        return jnp.broadcast_to(x[pl.ds(ROWS * p + 4 * NV + k, 1), :], (NV, NK))
+        return jnp.broadcast_to(coef[pl.ds(PAIRS * k + p, 1), :], (NV, NK))
 
     def value(p, k):
-        return x[pl.ds(ROWS * p + NV * k, NV), :]
+        return x[pl.ds(WIDE * p + NV * k, NV), :]
+
+    c = CS["pair"]
+    head_f, tail_f, head_d, tail_d = [], [], [], []
+    for p in range(PAIRS):
+        h, t, dh, dt = (value(p, k) for k in range(4))
+        if p:
+            for q in range(3):
+                z = value(p - 1, 8 + q)
+                h, t = h + row(p, 4 + q) * z, t + row(p, 7 + q) * z
+            z = value(p - 1, 11)
+            dh, dt = dh + c["low"][0] * z, dt + c["low"][1] * z
+        if p < PAIRS - 1:
+            for q in range(3):
+                z = value(p + 1, 4 + q)
+                h, t = h + row(p, 10 + q) * z, t + row(p, 13 + q) * z
+            z = value(p + 1, 7)
+            dh, dt = dh + c["high"][0] * z, dt + c["high"][1] * z
+        head_f.append(h)
+        tail_f.append(t)
+        head_d.append(dh)
+        tail_d.append(dt)
 
     scale = 8.0
-    num, den = [None] * PIECES, [None] * PIECES
-    hl, hr, tl, tr = ([row(p, k) for p in range(PIECES)] for k in range(4))
+    num, den = [None] * PAIRS, [None] * PAIRS
+    hl, hr, tl, tr = ([row(p, k) for p in range(PAIRS)] for k in range(4))
     num[0], den[0] = tr[0], jnp.ones((NV, NK), F32)
-    for p in range(1, PIECES):
+    for p in range(1, PAIRS):
         cross = tl[p] * hr[p] - tr[p] * hl[p]
         num[p] = (scale * tr[p]) * den[p - 1] + (scale * cross) * num[p - 1]
         den[p] = scale * den[p - 1] - (scale * hl[p]) * num[p - 1]
-    inv = [None] + [1.0 / den[p] for p in range(1, PIECES)]
-    e = [num[0]] + [num[p] * inv[p] for p in range(1, PIECES)]
-    keep = [None] + [(scale * den[p - 1]) * inv[p] for p in range(1, PIECES)]
-
-    fwd_f, fwd_d = [value(0, 1)], [value(0, 3)]
-    chl, chr_, ctl, ce = CS["hl"], CS["hr"], CS["tl"], CS["e"]
-    for p in range(1, PIECES):
+    inv = [None] + [1.0 / den[p] for p in range(1, PAIRS)]
+    e = [num[0]] + [num[p] * inv[p] for p in range(1, PAIRS)]
+    keep = [None] + [(scale * den[p - 1]) * inv[p] for p in range(1, PAIRS)]
+
+    fwd_f, fwd_d = [tail_f[0]], [tail_d[0]]
+    chl, chr_, ctl, ce = c["hl"], c["hr"], c["tl"], c["e"]
+    for p in range(1, PAIRS):
         a = tl[p] * keep[p]
-        fwd_f.append((value(p, 1) + (a * e[p - 1]) * value(p, 0)) + a * fwd_f[-1])
+        fwd_f.append((tail_f[p] + (a * e[p - 1]) * head_f[p]) + a * fwd_f[-1])
         k = ctl / (1.0 - chl * ce[p - 1])
-        fwd_d.append((value(p, 3) + float(k * ce[p - 1]) * value(p, 2)) + float(k) * fwd_d[-1])
+        fwd_d.append((tail_d[p] + float(k * ce[p - 1]) * head_d[p]) + float(k) * fwd_d[-1])
 
     zero = jnp.zeros((NV, NK), F32)
     right_f, right_d = zero, zero
-    for p in range(PIECES - 1, -1, -1):
+    for p in range(PAIRS - 1, -1, -1):
         if p:
             h = keep[p]
-            head_f = (value(p, 0) + hl[p] * fwd_f[p - 1]) * h + (hr[p] * h) * right_f
-            left_f = fwd_f[p - 1] + e[p - 1] * head_f
+            at_f = (head_f[p] + hl[p] * fwd_f[p - 1]) * h + (hr[p] * h) * right_f
+            left_f = fwd_f[p - 1] + e[p - 1] * at_f
             k = 1.0 / (1.0 - chl * ce[p - 1])
-            head_d = (float(k) * value(p, 2) + float(k * chl) * fwd_d[p - 1]) + float(k * chr_) * right_d
-            left_d = fwd_d[p - 1] + float(ce[p - 1]) * head_d
+            at_d = (float(k) * head_d[p] + float(k * chl) * fwd_d[p - 1]) + float(k * chr_) * right_d
+            left_d = fwd_d[p - 1] + float(ce[p - 1]) * at_d
         else:
-            head_f = head_d = left_f = left_d = zero
+            at_f = at_d = left_f = left_d = zero
         for k, val in enumerate((left_f, right_f, left_d, right_d)):
             out[pl.ds(ROWS * p + NV * k, NV), :] = val
-        right_f, right_d = head_f, head_d
+        right_f, right_d = at_f, at_d
 
 
 def join(x):
+    vmem = pl.BlockSpec(memory_space=pltpu.VMEM)
     return pl.pallas_call(
         join_body,
-        out_shape=jax.ShapeDtypeStruct((PIECES * ROWS, NK), F32),
-        in_specs=[pl.BlockSpec(memory_space=pltpu.VMEM)],
-        out_specs=pl.BlockSpec(memory_space=pltpu.VMEM),
-        compiler_params=pltpu.CompilerParams(vmem_limit_bytes=12 << 20),
+        out_shape=jax.ShapeDtypeStruct((PAIRS * ROWS, NK), F32),
+        in_specs=[vmem],
+        out_specs=vmem,
+        scratch_shapes=[pltpu.VMEM((16 * PAIRS, NK), F32)],
+        compiler_params=pltpu.CompilerParams(vmem_limit_bytes=8 << 20),
         cost_estimate=pl.CostEstimate(flops=1 << 20, bytes_accessed=1 << 20, transcendentals=0),
         name="join",
     )(x)
 
 
+def split_body(z, mids, own, send):
+    is0 = parity("gx") == 0
+    c = CS["pair"]
+    down = [jnp.broadcast_to(mids[pl.ds(4 * NV * HALF + k, 1), :], (SUB, NK)) for k in range(4)]
+    for r in range(HALF // SUB):
+        for v in range(NV):
+            lf, rf, ld, rd = (z[pl.ds(ROWS * SUB * r + NV * k + v, SUB, stride=ROWS), :] for k in range(4))
+            head, tail, dhead, dtail = (mids[pl.ds((NV * k + v) * HALF + SUB * r, SUB), :] for k in range(4))
+            head = head + down[0] * lf + down[1] * rf
+            tail = tail + down[2] * lf + down[3] * rf
+            dhead = dhead + c["down"][0] * ld + c["down"][1] * rd
+            dtail = dtail + c["down"][2] * ld + c["down"][3] * rd
+            a, b = (lf, head, ld, dhead), (tail, rf, dtail, rd)
+            for k in range(4):
+                rows = pl.ds((NV * k + v) * HALF + SUB * r, SUB)
+                own[rows, :] = jnp.where(is0, a[k], b[k])
+                send[rows, :] = jnp.where(is0, b[k], a[k])
+
+
+def split(z, mids):
+    vmem = pl.BlockSpec(memory_space=pltpu.VMEM)
+    out = jax.ShapeDtypeStruct((4 * NV * HALF, NK), F32)
+    return pl.pallas_call(
+        split_body,
+        out_shape=(out, out),
+        in_specs=[vmem] * 2,
+        out_specs=(vmem,) * 2,
+        compiler_params=pltpu.CompilerParams(vmem_limit_bytes=8 << 20),
+        cost_estimate=pl.CostEstimate(flops=1 << 20, bytes_accessed=1 << 20, transcendentals=0),
+        name="split",
+    )(z, mids)
+
+
 def block_body(inner, s_hbm, f_hbm, fy_hbm, one, two, yone, ytwo, mx, my, base, mxb, s, f, fy, pad, sem):
-    loads = [
-        [pltpu.make_async_copy(h.at[v], t.at[v], sem.at[k, v]) for k, (h, t) in enumerate(((fy_hbm, fy), (s_hbm, s), (f_hbm, f)))]
-        for v in range(NV)
-    ]
-    for group in loads:
-        for c in group:
-            c.start()
+    moves = ((fy_hbm, fy), (s_hbm, s), (f_hbm, f))
+    for v in range(NV):
+        for k, (h, t) in enumerate(moves):
+            pltpu.make_async_copy(h.at[v], t.at[v], sem.at[k, v]).start()
     piece = lax.axis_index("gx")
     is0 = parity("gx") == 0
     even = parity("gy") == 0
@@ -361,12 +451,10 @@
         mxb[i] = jnp.broadcast_to(mxt[:, i : i + 1], (NJ, NK))
         pad[NI + i, 0:NJ, :] = jnp.broadcast_to(myt[:, i : i + 1], (NJ, NK))
 
-    for v in range(NV):
-        for c in loads[v]:
-            c.wait()
-
     @pl.loop(0, NV)
     def _(v):
+        for k, (h, t) in enumerate(moves):
+            pltpu.make_async_copy(h.at[v], t.at[v], sem.at[k, v]).wait()
         for i in range(NI):
             for q in range(NJ // SUB):
                 pad[i, pl.ds(SUB + SUB * q, SUB), :] = fy[v, i, pl.ds(SUB * q, SUB), :]
@@ -432,39 +520,40 @@
     )(inner, *in_hbm(state, flux_x, flux_y), one, two, yone, ytwo, mx, my)
 
 
-def finish_body(outer, base, mxb, z, out_hbm, out, sem):
+def finish_body(outer, base, mxb, own, got, out_hbm, out, sem):
+    core = parity("gx")
     stores = [pltpu.make_async_copy(out.at[v], out_hbm.at[v], sem.at[v]) for v in range(NV)]
     for v in range(NV):
-        for q in range(NJ // SUB):
-            rows = pl.ds(SUB * q, SUB)
-            lf, rf, ld, rd = (
-                z[pl.ds(ROWS * SUB * q + NV * k + v, SUB, stride=ROWS), :] for k in range(4)
-            )
-            for i in range(NI):
-                d = float(CS["left"][i]) * ld + float(CS["right"][i]) * rd
-                e = outer[C_LEFT + i] * lf + outer[C_RIGHT + i] * rf
-                out[v, i, rows, :] = (base[v, i, rows, :] + e) + mxb[i, rows, :] * d
+        for z, half in ((own, core), (got, 1 - core)):
+            for r in range(HALF // SUB):
+                rows = pl.ds(pl.multiple_of(HALF * half + SUB * r, SUB), SUB)
+                lf, rf, ld, rd = (z[pl.ds((NV * k + v) * HALF + SUB * r, SUB), :] for k in range(4))
+                for i in range(NI):
+                    d = float(CS["left"][i]) * ld + float(CS["right"][i]) * rd
+                    e = outer[C_LEFT + i] * lf + outer[C_RIGHT + i] * rf
+                    out[v, i, rows, :] = (base[v, i, rows, :] + e) + mxb[i, rows, :] * d
         stores[v].start()
     for c in stores:
         c.wait()
 
 
-def finish(outer, base, mxb, z):
+def finish(outer, base, mxb, own, got):
     return pl.pallas_call(
         finish_body,
         out_shape=jax.ShapeDtypeStruct((NV, NI, NJ, NK), F32),
-        in_specs=[pl.BlockSpec(memory_space=pltpu.VMEM)] * 4,
+        in_specs=[pl.BlockSpec(memory_space=pltpu.VMEM)] * 5,
         out_specs=pl.BlockSpec(memory_space=pltpu.HBM),
         scratch_shapes=[pltpu.VMEM((NV, NI, NJ, NK), F32), pltpu.SemaphoreType.DMA((NV,))],
         compiler_params=pltpu.CompilerParams(vmem_limit_bytes=12 << 20),
         cost_estimate=pl.CostEstimate(flops=1 << 22, bytes_accessed=3 << 20, transcendentals=0),
         name="finish",
-    )(outer, base, mxb, z)
-
-
-def exchange(x):
-    y = lax.all_to_all(x.reshape(PIECES, ROWS, NK), "gx", 0, 0, tiled=True)
-    return y.reshape(PIECES * ROWS, NK)
+    )(outer, base, mxb, own, got)
+
+
+def exchange(x, rows):
+    groups = [[2 * p + c for p in range(PAIRS)] for c in range(2)]
+    y = lax.all_to_all(x.reshape(PAIRS, rows, NK), "gx", 0, 0, tiled=True, axis_index_groups=groups)
+    return y.reshape(PAIRS * rows, NK)
 
 
 def per_device(flux_x, flux_y, state, metric_x, metric_y, filter_gap):
@@ -474,19 +563,21 @@
     y_in = [(i, i ^ 1) for i in range(count_y)]
     y_out = [(i, (i + 1 if i % 2 else i - 1) % count_y) for i in range(count_y)]
 
+    inner, outer, mine, send = own_share(filter_gap, state, flux_x)
+    ends, mids = pair(mine, lax.ppermute(send, "gx", pair_in))
+    ends, state, flux_x, flux_y = lax.optimization_barrier((ends, state, flux_x, flux_y))
+    ends = exchange(ends, WIDE)
     send_one, send_two, ysend_one, ysend_two = pack(state, flux_x, flux_y)
     one = lax.ppermute(send_one, "gx", pair_in)
     two = lax.ppermute(send_two, "gx", pair_out)
     yone = lax.ppermute(ysend_one, "gy", y_in)
     ytwo = lax.ppermute(ysend_two, "gy", y_out)
-    inner, outer, edge, part = own_share(filter_gap, state, flux_x)
-    ends = end_values(edge, part, one, two)
-    ends, yone, ytwo = lax.optimization_barrier((ends, yone, ytwo))
-    ends = exchange(ends)
+    outside = join(ends)
+    outside, one, two, yone, ytwo = lax.optimization_barrier((outside, one, two, yone, ytwo))
     base, mxb = block(inner, state, flux_x, flux_y, one, two, yone, ytwo, metric_x, metric_y)
-    ends, base, mxb = lax.optimization_barrier((ends, base, mxb))
-    outside = exchange(join(ends))
-    return finish(outer, base, mxb, outside)
+    outside, base, mxb = lax.optimization_barrier((exchange(outside, ROWS), base, mxb))
+    own, send = split(outside, mids)
+    return finish(outer, base, mxb, own, lax.ppermute(send, "gx", pair_in))
 
 
 def solution(mesh):

time: 48 us -> 46.7 us (0.973)
  blocking collectives: 13.8 us -> 0 us
  starting transfers between devices: 17.6 us -> 26.5 us
  waiting for transfers between devices: 6.15 us -> 8.79 us
  local copies, waits for them, and re-layouts: 0.02 us -> 0.67 us
    all_to_all x1 -> x0, blocking collectives: 13.8 us -> none  [exchange(): y = lax.all_to_all(x.reshape(PIECES, ROWS, NK), 'gx', 0, 0, tiled=True)]
    all_to_all x1 -> x2, starting transfers between devices: 9.08 us -> 14.4 us  [exchange(): lax.all_to_all(x.reshape(PAIRS, rows, NK), 'gx', 0, 0, tiled=True, axis_i...]
    ppermute x0 -> x2, starting transfers between devices: none -> 3.93 us  [the longest x1 2.43 us: per_device(): return finish(outer, base, mxb, own, lax.ppermute(send, 'gx', pair_in))]
    ppermute x0 -> x2, waiting for transfers between devices: none -> 2.53 us  [the longest x1 1.5 us: per_device(): ends, mids = pair(mine, lax.ppermute(send, 'gx', pair_in))]
    ppermute x1, waiting for transfers between devices: 0.01 us -> 1.12 us  [per_device(): ytwo = lax.ppermute(ysend_two, 'gy', y_out)]
    pallas_call x3 -> x4, Pallas kernels: 3.47 us -> 4.54 us  [the longest x1 2.37 us: own_share(): pl.pallas_call(own_body, out_shape=(coef, coef, values, values), in_specs...]
    all_to_all x1 -> x2, waiting for transfers between devices: 6.14 us -> 5.13 us  [exchange(): lax.all_to_all(x.reshape(PAIRS, rows, NK), 'gx', 0, 0, tiled=True, axis_i...]
    pallas_call x1, Pallas kernels: 4.01 us -> 3.21 us  [block(): pl.pallas_call(block_body, out_shape=(jax.ShapeDtypeStruct((NV, NI, NJ, N...]
  transfers between devices with their start and end apart: 5 -> 8, of which waited for: 1 -> 5; matrix products, arithmetic and copies ran while one was open for 0% -> 0% of each run, Pallas kernels for 15% -> 12%
where the time goes in v3:
time: 46.7 us; the launch traced here: 46.4 us
  starting transfers between devices  26.5 us (57%)
  Pallas kernels  10.3 us (22%)
  waiting for transfers between devices  8.79 us (19%)
  local copies, waits for them, and re-layouts  0.67 us (1%)
    all_to_all x2, starting transfers between devices, exchange(): lax.all_to_all(x.reshape(PAIRS, rows, NK), 'gx', 0, 0, tiled=True, axis_i...  14.4 us
    all_to_all x2, waiting for transfers between devices, exchange(): lax.all_to_all(x.reshape(PAIRS, rows, NK), 'gx', 0, 0, tiled=True, axis_i...  5.13 us
    ppermute x1, starting transfers between devices, per_device(): two = lax.ppermute(send_two, 'gx', pair_out)  3.45 us
    pallas_call x1, Pallas kernels, block(): pl.pallas_call(block_body, out_shape=(jax.ShapeDtypeStruct((NV, NI, NJ, N...  3.21 us
    ppermute x1, starting transfers between devices, per_device(): return finish(outer, base, mxb, own, lax.ppermute(send, 'gx', pair_in))  2.43 us
    pallas_call x1, Pallas kernels, own_share(): pl.pallas_call(own_body, out_shape=(coef, coef, values, values), in_specs...  2.37 us
    ppermute x1, starting transfers between devices, per_device(): ytwo = lax.ppermute(ysend_two, 'gy', y_out)  2.24 us
    ppermute x1, starting transfers between devices, per_device(): yone = lax.ppermute(ysend_one, 'gy', y_in)  1.72 us
  transfers between devices with their start and end apart: 8, of which 5 were waited for; matrix products, arithmetic and copies ran while one was open for 0% of the time, Pallas kernels for 12%

profile of v3, /device:TPU:1, one launch (start us, length us, event | category | flops | bytes accessed | tf_op | source)
XLA Modules:
  0.0 46.4 jit_solution(8194928883135127947)
XLA Ops:
  0.0 0.7 %copy-done.2 = f32[16]{0:T(128)S(1)} copy-done((f32[16]{0:T(128)S(1)}, f32[16]{0:T(128)}, u32[]{:S(2)}) %copy-start.2) | copy-done | bytes 88
  0.7 2.4 %own_share.1 = (f32[32,8,128]{2,1,0:T(8,128)S(1)}, f32[32,8,128]{2,1,0:T(8,128)S(1)}, f32[976,128]{1,0:T(8,128)S(1)}, f32[976,128]{1,0:T(8,128)S(1)}) custom-call(f32[16]{0:T(128)S(1)} %copy-done.2, f32[5,16,32,128]{3,2,1,0:T(8,128)} %s_hbm.2, f32[5,16,32,128]{3,2,1,0:T(8,128)} %f_hbm.2), custom_call_target="tpu_custom_call" | custom-call | flops 16777216 | bytes 4194304 | tf_op jit(solution)/shard_map/own_share/pallas_call | solution.py:238
  3.0 1.5 %collective-permute-start = (f32[976,128]{1,0:T(8,128)S(1)}, f32[976,128]{1,0:T(8,128)S(1)}, u32[]{:S(2)}, u32[]{:S(2)}) collective-permute-start(f32[976,128]{1,0:T(8,128)S(1)} %get-tuple-element.33), channel_id=1, source_target_pairs={{0,4},{4,0},{8,12},{12,8},{16,20},{20,16},{24,28},{28,24},{32,36},... | collective-permute-start | bytes 1499144 | tf_op jit(solution)/shard_map/ppermute | solution.py:567
  4.5 1.5 %collective-permute-done.got = f32[976,128]{1,0:T(8,128)S(1)} collective-permute-done((f32[976,128]{1,0:T(8,128)S(1)}, f32[976,128]{1,0:T(8,128)S(1)}, u32[]{:S(2)}, u32[]{:S(2)}) %collective-permute-start) | collective-permute-done | bytes 499744 | tf_op jit(solution)/shard_map/ppermute | solution.py:567
  6.0 1.2 %pair.1 = (f32[1024,128]{1,0:T(8,128)}, f32[328,128]{1,0:T(8,128)S(1)}) custom-call(f32[976,128]{1,0:T(8,128)S(1)} %get-tuple-element.32.mine, f32[976,128]{1,0:T(8,128)S(1)} %collective-permute-done.got), custom_call_target="tpu_custom_call" | custom-call | flops 1048576 | bytes 1048576 | tf_op jit(solution)/shard_map/pair/pallas_call | solution.py:307
  7.2 6.8 %all-to-all-start = ((f32[16,64,128]{2,1,0:T(8,128)}), f32[16,64,128]{2,1,0:T(8,128)S(1)}, u32[]{:S(2)}, u32[]{:S(2)}) async-start(f32[16,64,128]{2,1,0:T(8,128)} %bitcast), calls=%async_computation | async-start | bytes 1048576 | tf_op jit(solution)/shard_map/all_to_all | solution.py:555
  14.1 0.0 copy-start
  14.1 0.0 copy-start.1
  14.1 1.4 %pack.1 = (f32[5,4,32,128]{3,2,1,0:T(8,128)S(1)}, f32[5,4,32,128]{3,2,1,0:T(8,128)S(1)}, f32[5,8,8,128]{3,2,1,0:T(8,128)S(1)}, f32[5,8,8,128]{3,2,1,0:T(8,128)S(1)}) custom-call(f32[5,16,32,128]{3,2,1,0:T(8,128)} %s_hbm.2, f32[5,16,32,128]{3,2,1,0:T(8,128)} %f_hbm.2, f32[5,16,32,128]{3,2,1,0:T(8,128)} %fy_hbm), custom_call_target="tpu_custom_call" | custom-call | bytes 2097152 | tf_op jit(solution)/shard_map/pack/pallas_call | solution.py:123
  15.5 0.7 %collective-permute-start.1 = (f32[5,4,32,128]{3,2,1,0:T(8,128)S(1)}, f32[5,4,32,128]{3,2,1,0:T(8,128)S(1)}, u32[]{:S(2)}, u32[]{:S(2)}) collective-permute-start(f32[5,4,32,128]{3,2,1,0:T(8,128)S(1)} %get-tuple-element.39), channel_id=1, source_target_pairs={{0,4},{4,0},{8,12},{12,8},{16,20},{20,16},{24,28},{28,24},{32,36},... | collective-permute-start | bytes 983048 | tf_op jit(solution)/shard_map/ppermute | solution.py:571
  16.2 3.4 %collective-permute-start.2 = (f32[5,4,32,128]{3,2,1,0:T(8,128)S(1)}, f32[5,4,32,128]{3,2,1,0:T(8,128)S(1)}, u32[]{:S(2)}, u32[]{:S(2)}) collective-permute-start(f32[5,4,32,128]{3,2,1,0:T(8,128)S(1)} %get-tuple-element.40), channel_id=1, source_target_pairs={{4,8},{8,4},{12,16},{16,12},{20,24},{24,20},{28,32},{32,28},{36,40... | collective-permute-start | bytes 983048 | tf_op jit(solution)/shard_map/ppermute | solution.py:572
  19.7 1.7 %collective-permute-start.3 = (f32[5,8,8,128]{3,2,1,0:T(8,128)S(1)}, f32[5,8,8,128]{3,2,1,0:T(8,128)S(1)}, u32[]{:S(2)}, u32[]{:S(2)}) collective-permute-start(f32[5,8,8,128]{3,2,1,0:T(8,128)S(1)} %get-tuple-element.41), channel_id=1, source_target_pairs={{0,1},{1,0},{2,3},{3,2},{4,5},{5,4},{6,7},{7,6},{8,9},{9,8},{10,11... | collective-permute-start | bytes 491528 | tf_op jit(solution)/shard_map/ppermute | solution.py:573
  21.4 2.2 %collective-permute-start.4 = (f32[5,8,8,128]{3,2,1,0:T(8,128)S(1)}, f32[5,8,8,128]{3,2,1,0:T(8,128)S(1)}, u32[]{:S(2)}, u32[]{:S(2)}) collective-permute-start(f32[5,8,8,128]{3,2,1,0:T(8,128)S(1)} %get-tuple-element.42), channel_id=1, source_target_pairs={{0,3},{1,2},{2,1},{3,0},{4,7},{5,6},{6,5},{7,4},{8,11},{9,10},{10,... | collective-permute-start | bytes 491528 | tf_op jit(solution)/shard_map/ppermute | solution.py:574
  23.6 1.1 %all-to-all-done = f32[16,64,128]{2,1,0:T(8,128)S(1)} async-done(((f32[16,64,128]{2,1,0:T(8,128)}), f32[16,64,128]{2,1,0:T(8,128)S(1)}, u32[]{:S(2)}, u32[]{:S(2)}) %all-to-all-start) | async-done | bytes 524320 | tf_op jit(solution)/shard_map/all_to_all | solution.py:555
  24.8 0.9 %join.1 = f32[384,128]{1,0:T(8,128)} custom-call(f32[1024,128]{1,0:T(8,128)S(1)} %bitcast.4), custom_call_target="tpu_custom_call" | custom-call | flops 1048576 | bytes 1048576 | tf_op jit(solution)/shard_map/join/pallas_call | solution.py:393
  25.7 0.0 collective-permute-done.3.yone
  25.7 1.1 %collective-permute-done.4.ytwo = f32[5,8,8,128]{3,2,1,0:T(8,128)S(1)} collective-permute-done((f32[5,8,8,128]{3,2,1,0:T(8,128)S(1)}, f32[5,8,8,128]{3,2,1,0:T(8,128)S(1)}, u32[]{:S(2)}, u32[]{:S(2)}) %collective-permute-start.4) | collective-permute-done | bytes 163872 | tf_op jit(solution)/shard_map/ppermute | solution.py:574
  26.8 7.6 %all-to-all-start.1 = ((f32[16,24,128]{2,1,0:T(8,128)}), f32[16,24,128]{2,1,0:T(8,128)S(1)}, u32[]{:S(2)}, u32[]{:S(2)}) async-start(f32[16,24,128]{2,1,0:T(8,128)} %bitcast.2), calls=%async_computation.1 | async-start | bytes 393216 | tf_op jit(solution)/shard_map/all_to_all | solution.py:555
  34.5 3.2 %block.1 = (f32[5,16,32,128]{3,2,1,0:T(8,128)S(1)}, f32[16,32,128]{2,1,0:T(8,128)S(1)}) custom-call(f32[32,8,128]{2,1,0:T(8,128)S(1)} %get-tuple-element.44.inner, f32[5,16,32,128]{3,2,1,0:T(8,128)} %s_hbm.2, f32[5,16,32,128]{3,2,1,0:T(8,128)} %f_hbm.2, f32[5,16,32,128]{3,2,1,0:T(8,128)} %fy_hbm, f32[5,4,32,128]{3,2,1,0:T(8,128)S(1)} %collective-permute-done.1.one, ...), custom_call_target="tpu_custom_call" | custom-call | flops 33554432 | bytes 8388608 | tf_op jit(solution)/shard_map/block/pallas_call | solution.py:507
  37.7 4.0 %all-to-all-done.1 = f32[16,24,128]{2,1,0:T(8,128)S(1)} async-done(((f32[16,24,128]{2,1,0:T(8,128)}), f32[16,24,128]{2,1,0:T(8,128)S(1)}, u32[]{:S(2)}, u32[]{:S(2)}) %all-to-all-start.1) | async-done | bytes 196640 | tf_op jit(solution)/shard_map/all_to_all | solution.py:555
  41.7 0.1 split.1
  41.7 2.4 %collective-permute-start.5 = (f32[320,128]{1,0:T(8,128)S(1)}, f32[320,128]{1,0:T(8,128)S(1)}, u32[]{:S(2)}, u32[]{:S(2)}) collective-permute-start(f32[320,128]{1,0:T(8,128)S(1)} %get-tuple-element.56), channel_id=1, source_target_pairs={{0,4},{4,0},{8,12},{12,8},{16,20},{20,16},{24,28},{28,24},{32,36},... | collective-permute-start | bytes 491528 | tf_op jit(solution)/shard_map/ppermute | solution.py:580
  44.2 1.0 %collective-permute-done.5.got = f32[320,128]{1,0:T(8,128)S(1)} collective-permute-done((f32[320,128]{1,0:T(8,128)S(1)}, f32[320,128]{1,0:T(8,128)S(1)}, u32[]{:S(2)}, u32[]{:S(2)}) %collective-permute-start.5) | collective-permute-done | bytes 163872 | tf_op jit(solution)/shard_map/ppermute | solution.py:580
  45.2 1.2 %finish.1 = f32[5,16,32,128]{3,2,1,0:T(8,128)} custom-call(f32[32,8,128]{2,1,0:T(8,128)S(1)} %get-tuple-element.31.outer, f32[5,16,32,128]{3,2,1,0:T(8,128)S(1)} %get-tuple-element.51.base, f32[16,32,128]{2,1,0:T(8,128)S(1)} %get-tuple-element.52.mxb, f32[320,128]{1,0:T(8,128)S(1)} %get-tuple-element.55.own, f32[320,128]{1,0:T(8,128)S(1)} %collective-permute-done.5.got), custom_call_target="tpu_custom_call" | custom-call | flops 4194304 | bytes 3145728 | tf_op jit(solution)/shard_map/finish/pallas_call | solution.py:541
  (5 shorter events, 0.0 us)
Async XLA Ops:
  0.0 0.7 %copy-start.2 = (f32[16]{0:T(128)S(1)}, f32[16]{0:T(128)}, u32[]{:S(2)}) copy-start(f32[16]{0:T(128)} %gap.1) | copy-start | bytes 196
  3.0 3.0 %collective-permute-start = (f32[976,128]{1,0:T(8,128)S(1)}, f32[976,128]{1,0:T(8,128)S(1)}, u32[]{:S(2)}, u32[]{:S(2)}) collective-permute-start(f32[976,128]{1,0:T(8,128)S(1)} %get-tuple-element.33), channel_id=1, source_target_pairs={{0,4},{4,0},{8,12},{12,8},{16,20},{20,16},{24,28},{28,24},{32,36},... | collective-permute-start | bytes 1499144 | tf_op jit(solution)/shard_map/ppermute | solution.py:567
  7.2 17.6 %all-to-all-start = ((f32[16,64,128]{2,1,0:T(8,128)}), f32[16,64,128]{2,1,0:T(8,128)S(1)}, u32[]{:S(2)}, u32[]{:S(2)}) async-start(f32[16,64,128]{2,1,0:T(8,128)} %bitcast), calls=%async_computation | async-start | bytes 1048576 | tf_op jit(solution)/shard_map/all_to_all | solution.py:555
  14.1 20.4 %copy-start = (f32[16,32]{1,0:T(8,128)S(1)}, f32[16,32]{1,0:T(8,128)}, u32[]{:S(2)}) copy-start(f32[16,32]{1,0:T(8,128)} %mx.1) | copy-start | bytes 6148
  14.1 20.4 %copy-start.1 = (f32[16,32]{1,0:T(8,128)S(1)}, f32[16,32]{1,0:T(8,128)}, u32[]{:S(2)}) copy-start(f32[16,32]{1,0:T(8,128)} %my.1) | copy-start | bytes 6148
  15.5 11.4 %collective-permute-start.1 = (f32[5,4,32,128]{3,2,1,0:T(8,128)S(1)}, f32[5,4,32,128]{3,2,1,0:T(8,128)S(1)}, u32[]{:S(2)}, u32[]{:S(2)}) collective-permute-start(f32[5,4,32,128]{3,2,1,0:T(8,128)S(1)} %get-tuple-element.39), channel_id=1, source_target_pairs={{0,4},{4,0},{8,12},{12,8},{16,20},{20,16},{24,28},{28,24},{32,36},... | collective-permute-start | bytes 983048 | tf_op jit(solution)/shard_map/ppermute | solution.py:571
  16.2 10.6 %collective-permute-start.2 = (f32[5,4,32,128]{3,2,1,0:T(8,128)S(1)}, f32[5,4,32,128]{3,2,1,0:T(8,128)S(1)}, u32[]{:S(2)}, u32[]{:S(2)}) collective-permute-start(f32[5,4,32,128]{3,2,1,0:T(8,128)S(1)} %get-tuple-element.40), channel_id=1, source_target_pairs={{4,8},{8,4},{12,16},{16,12},{20,24},{24,20},{28,32},{32,28},{36,40... | collective-permute-start | bytes 983048 | tf_op jit(solution)/shard_map/ppermute | solution.py:572
  19.7 6.0 %collective-permute-start.3 = (f32[5,8,8,128]{3,2,1,0:T(8,128)S(1)}, f32[5,8,8,128]{3,2,1,0:T(8,128)S(1)}, u32[]{:S(2)}, u32[]{:S(2)}) collective-permute-start(f32[5,8,8,128]{3,2,1,0:T(8,128)S(1)} %get-tuple-element.41), channel_id=1, source_target_pairs={{0,1},{1,0},{2,3},{3,2},{4,5},{5,4},{6,7},{7,6},{8,9},{9,8},{10,11... | collective-permute-start | bytes 491528 | tf_op jit(solution)/shard_map/ppermute | solution.py:573
  21.4 5.4 %collective-permute-start.4 = (f32[5,8,8,128]{3,2,1,0:T(8,128)S(1)}, f32[5,8,8,128]{3,2,1,0:T(8,128)S(1)}, u32[]{:S(2)}, u32[]{:S(2)}) collective-permute-start(f32[5,8,8,128]{3,2,1,0:T(8,128)S(1)} %get-tuple-element.42), channel_id=1, source_target_pairs={{0,3},{1,2},{2,1},{3,0},{4,7},{5,6},{6,5},{7,4},{8,11},{9,10},{10,... | collective-permute-start | bytes 491528 | tf_op jit(solution)/shard_map/ppermute | solution.py:574
  26.8 14.8 %all-to-all-start.1 = ((f32[16,24,128]{2,1,0:T(8,128)}), f32[16,24,128]{2,1,0:T(8,128)S(1)}, u32[]{:S(2)}, u32[]{:S(2)}) async-start(f32[16,24,128]{2,1,0:T(8,128)} %bitcast.2), calls=%async_computation.1 | async-start | bytes 393216 | tf_op jit(solution)/shard_map/all_to_all | solution.py:555
  41.7 3.5 %collective-permute-start.5 = (f32[320,128]{1,0:T(8,128)S(1)}, f32[320,128]{1,0:T(8,128)S(1)}, u32[]{:S(2)}, u32[]{:S(2)}) collective-permute-start(f32[320,128]{1,0:T(8,128)S(1)} %get-tuple-element.56), channel_id=1, source_target_pairs={{0,4},{4,0},{8,12},{12,8},{16,20},{20,16},{24,28},{28,24},{32,36},... | collective-permute-start | bytes 491528 | tf_op jit(solution)/shard_map/ppermute | solution.py:580

commit v4 on v3

--- a/solution.py
+++ b/solution.py
@@ -17,7 +17,7 @@
 D6 = (1.0, -6.0, 15.0, -20.0, 15.0, -6.0, 1.0)
 
 C_C, C_MG = 0, NI
-C_LEFT, C_RIGHT = 0, NI
+C_LEFT, C_RIGHT, C_FAR = 0, NI, 2 * NI
 
 
 def constant_system():
@@ -136,7 +136,9 @@
     )(*in_hbm(state, flux_x, flux_y))
 
 
-def own_body(gap, s_hbm, f_hbm, inner, outer, mine, send, s, f, own, sem):
+def own_body(gap_hbm, s_hbm, f_hbm, inner, outer, mine, send, gap, s, f, own, gap_sem, sem):
+    gap_load = pltpu.make_async_copy(gap_hbm, gap, gap_sem)
+    gap_load.start()
     loads = [
         (
             pltpu.make_async_copy(s_hbm.at[v], s.at[v], sem.at[0, v]),
@@ -149,6 +151,7 @@
             c.start()
     core = parity("gx")
     piece = lax.axis_index("gx")
+    gap_load.wait()
     alpha = [0.5 - splat(gap[i]) for i in range(NI)]
     g32 = [(0.5 - a) * (1.0 / 32.0) for a in alpha]
     m, c = [None] * NI, [None] * NI
@@ -194,6 +197,8 @@
     high = [spread(v, NI + q) for v in (vh, vt) for q in range(3)]
     edge += [jnp.where(core == 0, h, l) for h, l in zip(high, low)]
     edge += [jnp.where(core == 0, l, h) for h, l in zip(high, low)]
+    for q in range(3):
+        outer[C_FAR + q] = jnp.where(core == 0, edge[13 + q], edge[10 + q])
     for k, t in enumerate(edge):
         mine[pl.ds(EDGE + k, 1), :] = t[0:1]
         send[pl.ds(EDGE + k, 1), :] = t[0:1]
@@ -234,25 +239,28 @@
 def own_share(gap, state, flux_x):
     vmem, hbm = pl.BlockSpec(memory_space=pltpu.VMEM), pl.BlockSpec(memory_space=pltpu.HBM)
     coef = jax.ShapeDtypeStruct((2 * NI, SUB, NK), F32)
+    coef_far = jax.ShapeDtypeStruct((2 * NI + 3, SUB, NK), F32)
     values = jax.ShapeDtypeStruct((EDGE + 16, NK), F32)
     return pl.pallas_call(
         own_body,
-        out_shape=(coef, coef, values, values),
-        in_specs=[pl.BlockSpec(memory_space=pltpu.SMEM), hbm, hbm],
+        out_shape=(coef, coef_far, values, values),
+        in_specs=[hbm, hbm, hbm],
         out_specs=(vmem,) * 4,
         scratch_shapes=[
+            pltpu.SMEM((NI,), F32),
             pltpu.VMEM((NV, NI, NJ, NK), F32),
             pltpu.VMEM((NV, NI, NJ, NK), F32),
             pltpu.VMEM((2 * NI, SUB, NK), F32),
+            pltpu.SemaphoreType.DMA,
             pltpu.SemaphoreType.DMA((2, NV)),
         ],
         compiler_params=pltpu.CompilerParams(vmem_limit_bytes=12 << 20),
         cost_estimate=pl.CostEstimate(flops=1 << 24, bytes_accessed=4 << 20, transcendentals=0),
         name="own_share",
-    )(gap, *in_hbm(state, flux_x))
-
-
-def pair_body(mine, got, out, mids):
+    )(*in_hbm(gap, state, flux_x))
+
+
+def pair_body(mine, got, out_hbm, mids, out, sem):
     is0 = parity("gx") == 0
 
     def both(rows):
@@ -264,7 +272,7 @@
     hla, hra, tla, tra = ca[:4]
     hlb, hrb, tlb, trb = cb[:4]
     inv = 1.0 / (1.0 - tra * hlb)
-    down = [hlb * tla * inv, hrb * inv, tla * inv, tra * hrb * inv]
+    down = [hlb * tla * inv, hrb * inv, tla * inv, tra * hrb * inv, hlb * inv, inv, tra * inv]
     for k, t in enumerate(down):
         mids[pl.ds(4 * NV * HALF + k, 1), :] = t[0:1]
     cross_h, cross_t = hra * inv, tlb * inv
@@ -279,6 +287,8 @@
         packed = jnp.where(lane == k, t, packed)
 
     k = CS["pair"]
+    blocks = [pl.ds(WIDE * SUB * r, WIDE * SUB) for r in range(HALF // SUB)]
+    stores = [pltpu.make_async_copy(out.at[b], out_hbm.at[b], sem.at[r]) for r, b in enumerate(blocks)]
     for r in range(HALF // SUB):
         at = WIDE * SUB * r
         out[pl.ds(at + 12 * NV, SUB, stride=WIDE), :] = packed
@@ -300,6 +310,9 @@
                 out[pl.ds(at + NV * e + v, SUB, stride=WIDE), :] = t
             for e, t in enumerate((head, tail, dhead, dtail)):
                 mids[pl.ds((NV * e + v) * HALF + SUB * r, SUB), :] = t
+        stores[r].start()
+    for c in stores:
+        c.wait()
 
 
 def pair(mine, got):
@@ -311,14 +324,15 @@
             jax.ShapeDtypeStruct((4 * NV * HALF + SUB, NK), F32),
         ),
         in_specs=[vmem] * 2,
-        out_specs=(vmem,) * 2,
+        out_specs=(pl.BlockSpec(memory_space=pltpu.HBM), vmem),
+        scratch_shapes=[pltpu.VMEM((PAIRS * WIDE, NK), F32), pltpu.SemaphoreType.DMA((HALF // SUB,))],
         compiler_params=pltpu.CompilerParams(vmem_limit_bytes=8 << 20),
         cost_estimate=pl.CostEstimate(flops=1 << 20, bytes_accessed=1 << 20, transcendentals=0),
         name="pair",
     )(mine, got)
 
 
-def join_body(x, out, coef):
+def join_body(x, out_hbm, out, coef, sem):
     for r in range(PAIRS // SUB):
         packed = x[pl.ds(WIDE * SUB * r + 12 * NV, SUB, stride=WIDE), :]
         for k in range(16):
@@ -371,6 +385,8 @@
         k = ctl / (1.0 - chl * ce[p - 1])
         fwd_d.append((tail_d[p] + float(k * ce[p - 1]) * head_d[p]) + float(k) * fwd_d[-1])
 
+    blocks = [pl.ds(ROWS * SUB * r, ROWS * SUB) for r in range(PAIRS // SUB)]
+    stores = [pltpu.make_async_copy(out.at[b], out_hbm.at[b], sem.at[r]) for r, b in enumerate(blocks)]
     zero = jnp.zeros((NV, NK), F32)
     right_f, right_d = zero, zero
     for p in range(PAIRS - 1, -1, -1):
@@ -386,6 +402,10 @@
         for k, val in enumerate((left_f, right_f, left_d, right_d)):
             out[pl.ds(ROWS * p + NV * k, NV), :] = val
         right_f, right_d = at_f, at_d
+        if p % SUB == 0:
+            stores[p // SUB].start()
+    for t in stores:
+        t.wait()
 
 
 def join(x):
@@ -394,26 +414,61 @@
         join_body,
         out_shape=jax.ShapeDtypeStruct((PAIRS * ROWS, NK), F32),
         in_specs=[vmem],
-        out_specs=vmem,
-        scratch_shapes=[pltpu.VMEM((16 * PAIRS, NK), F32)],
+        out_specs=pl.BlockSpec(memory_space=pltpu.HBM),
+        scratch_shapes=[
+            pltpu.VMEM((PAIRS * ROWS, NK), F32),
+            pltpu.VMEM((16 * PAIRS, NK), F32),
+            pltpu.SemaphoreType.DMA((PAIRS // SUB,)),
+        ],
         compiler_params=pltpu.CompilerParams(vmem_limit_bytes=8 << 20),
         cost_estimate=pl.CostEstimate(flops=1 << 20, bytes_accessed=1 << 20, transcendentals=0),
         name="join",
     )(x)
 
 
-def split_body(z, mids, own, send):
+def far_body(outer, two, own, send):
+    core = parity("gx")
+    wd = jnp.where(core == 0, flux_weight(NI - 1, -1), flux_weight(0, NI)).astype(F32)
+    for out, half in ((own, core), (send, 1 - core)):
+        for v in range(NV):
+            for r in range(HALF // SUB):
+                rows = pl.ds(pl.multiple_of(HALF * half + SUB * r, SUB), SUB)
+                a = [two[v, k, rows, :] for k in range(4)]
+                f = outer[C_FAR] * a[0] + outer[C_FAR + 1] * a[1] + outer[C_FAR + 2] * a[2]
+                for k, t in enumerate((f, wd * a[3])):
+                    out[pl.ds((NV * k + v) * HALF + SUB * r, SUB), :] = t
+
+
+def far(outer, two):
+    vmem = pl.BlockSpec(memory_space=pltpu.VMEM)
+    out = jax.ShapeDtypeStruct((2 * NV * HALF, NK), F32)
+    return pl.pallas_call(
+        far_body,
+        out_shape=(out, out),
+        in_specs=[vmem] * 2,
+        out_specs=(vmem,) * 2,
+        compiler_params=pltpu.CompilerParams(vmem_limit_bytes=8 << 20),
+        cost_estimate=pl.CostEstimate(flops=1 << 18, bytes_accessed=1 << 19, transcendentals=0),
+        name="far",
+    )(outer, two)
+
+
+def split_body(z, mids, far_own, far_got, own, send):
     is0 = parity("gx") == 0
     c = CS["pair"]
-    down = [jnp.broadcast_to(mids[pl.ds(4 * NV * HALF + k, 1), :], (SUB, NK)) for k in range(4)]
+    down = [jnp.broadcast_to(mids[pl.ds(4 * NV * HALF + k, 1), :], (SUB, NK)) for k in range(7)]
     for r in range(HALF // SUB):
         for v in range(NV):
             lf, rf, ld, rd = (z[pl.ds(ROWS * SUB * r + NV * k + v, SUB, stride=ROWS), :] for k in range(4))
             head, tail, dhead, dtail = (mids[pl.ds((NV * k + v) * HALF + SUB * r, SUB), :] for k in range(4))
-            head = head + down[0] * lf + down[1] * rf
-            tail = tail + down[2] * lf + down[3] * rf
-            dhead = dhead + c["down"][0] * ld + c["down"][1] * rd
-            dtail = dtail + c["down"][2] * ld + c["down"][3] * rd
+            fo, do = (far_own[pl.ds((NV * k + v) * HALF + SUB * r, SUB), :] for k in range(2))
+            fg, dg = (far_got[pl.ds((NV * k + v) * HALF + SUB * r, SUB), :] for k in range(2))
+            fa, da = jnp.where(is0, fo, fg), jnp.where(is0, do, dg)
+            fb, db = jnp.where(is0, fg, fo), jnp.where(is0, dg, do)
+            head = (head + down[4] * fa + down[5] * fb) + down[0] * lf + down[1] * rf
+            tail = (tail + down[5] * fa + down[6] * fb) + down[2] * lf + down[3] * rf
+            dhead = (dhead + c["inv_hl"] * da + c["inv"] * db) + c["down"][0] * ld + c["down"][1] * rd
+            dtail = (dtail + c["inv"] * da + c["inv_tr"] * db) + c["down"][2] * ld + c["down"][3] * rd
             a, b = (lf, head, ld, dhead), (tail, rf, dtail, rd)
             for k in range(4):
                 rows = pl.ds((NV * k + v) * HALF + SUB * r, SUB)
@@ -421,18 +476,18 @@
                 send[rows, :] = jnp.where(is0, b[k], a[k])
 
 
-def split(z, mids):
+def split(z, mids, far_own, far_got):
     vmem = pl.BlockSpec(memory_space=pltpu.VMEM)
     out = jax.ShapeDtypeStruct((4 * NV * HALF, NK), F32)
     return pl.pallas_call(
         split_body,
         out_shape=(out, out),
-        in_specs=[vmem] * 2,
+        in_specs=[vmem] * 4,
         out_specs=(vmem,) * 2,
         compiler_params=pltpu.CompilerParams(vmem_limit_bytes=8 << 20),
         cost_estimate=pl.CostEstimate(flops=1 << 20, bytes_accessed=1 << 20, transcendentals=0),
         name="split",
-    )(z, mids)
+    )(z, mids, far_own, far_got)
 
 
 def block_body(inner, s_hbm, f_hbm, fy_hbm, one, two, yone, ytwo, mx, my, base, mxb, s, f, fy, pad, sem):
@@ -564,19 +619,23 @@
     y_out = [(i, (i + 1 if i % 2 else i - 1) % count_y) for i in range(count_y)]
 
     inner, outer, mine, send = own_share(filter_gap, state, flux_x)
-    ends, mids = pair(mine, lax.ppermute(send, "gx", pair_in))
-    ends, state, flux_x, flux_y = lax.optimization_barrier((ends, state, flux_x, flux_y))
+    send, state, flux_x, flux_y = lax.optimization_barrier((send, state, flux_x, flux_y))
+    got = lax.ppermute(send, "gx", pair_in)
+    got, *faces = lax.optimization_barrier((got, *pack(state, flux_x, flux_y)))
+    ends, mids = pair(mine, got)
+    ends, send_one, send_two, ysend_one, ysend_two = lax.optimization_barrier((ends, *faces))
     ends = exchange(ends, WIDE)
-    send_one, send_two, ysend_one, ysend_two = pack(state, flux_x, flux_y)
     one = lax.ppermute(send_one, "gx", pair_in)
     two = lax.ppermute(send_two, "gx", pair_out)
     yone = lax.ppermute(ysend_one, "gy", y_in)
     ytwo = lax.ppermute(ysend_two, "gy", y_out)
     outside = join(ends)
     outside, one, two, yone, ytwo = lax.optimization_barrier((outside, one, two, yone, ytwo))
+    far_own, far_send = far(outer, two)
+    far_got = lax.ppermute(far_send, "gx", pair_in)
     base, mxb = block(inner, state, flux_x, flux_y, one, two, yone, ytwo, metric_x, metric_y)
-    outside, base, mxb = lax.optimization_barrier((exchange(outside, ROWS), base, mxb))
-    own, send = split(outside, mids)
+    outside, base, mxb, far_got = lax.optimization_barrier((exchange(outside, ROWS), base, mxb, far_got))
+    own, send = split(outside, mids, far_own, far_got)
     return finish(outer, base, mxb, own, lax.ppermute(send, "gx", pair_in))
 
 

time: 46.7 us -> 44.1 us (0.944)
  waiting for transfers between devices: 8.79 us -> 6.79 us
  local copies, waits for them, and re-layouts: 0.67 us -> 0.01 us
  Pallas kernels: 10.3 us -> 9.67 us
  starting transfers between devices: 26.5 us -> 27.1 us
    ppermute x1 -> x2, waiting for transfers between devices: 1.5 us -> 0.12 us  [the longest x1 0.12 us: per_device(): got = lax.ppermute(send, 'gx', pair_in)]
    ppermute x1 -> x2, starting transfers between devices: 1.5 us -> 2.83 us  [the longest x1 1.5 us: per_device(): got = lax.ppermute(send, 'gx', pair_in)]
    ppermute x1, waiting for transfers between devices: 1.12 us -> 0.01 us  [per_device(): ytwo = lax.ppermute(ysend_two, 'gy', y_out)]
    all_to_all x2, starting transfers between devices: 14.4 us -> 13.7 us  [exchange(): lax.all_to_all(x.reshape(PAIRS, rows, NK), 'gx', 0, 0, tiled=True, axis_i...]
    unnamed x6 -> x4, local copies, waits for them, and re-layouts: 0.67 us -> 0.01 us
    pallas_call x2 -> x3, Pallas kernels: 2.42 us -> 1.96 us  [the longest x1 1.84 us: own_share(): pl.pallas_call(own_body, out_shape=(coef, coef_far, values, values), in_s...]
  transfers between devices with their start and end apart: 8 -> 9, of which waited for: 5 -> 5; matrix products, arithmetic and copies ran while one was open for 0% -> 0% of each run, Pallas kernels for 12% -> 13%
where the time goes in v4:
time: 44.1 us; the launch traced here: 43.7 us
  starting transfers between devices  27.1 us (61%)
  Pallas kernels  9.67 us (22%)
  waiting for transfers between devices  6.79 us (15%)
    all_to_all x2, starting transfers between devices, exchange(): lax.all_to_all(x.reshape(PAIRS, rows, NK), 'gx', 0, 0, tiled=True, axis_i...  13.7 us
    all_to_all x2, waiting for transfers between devices, exchange(): lax.all_to_all(x.reshape(PAIRS, rows, NK), 'gx', 0, 0, tiled=True, axis_i...  5.34 us
    ppermute x1, starting transfers between devices, per_device(): two = lax.ppermute(send_two, 'gx', pair_out)  3.37 us
    pallas_call x1, Pallas kernels, block(): pl.pallas_call(block_body, out_shape=(jax.ShapeDtypeStruct((NV, NI, NJ, N...  3.12 us
    ppermute x1, starting transfers between devices, per_device(): return finish(outer, base, mxb, own, lax.ppermute(send, 'gx', pair_in))  2.44 us
    ppermute x1, starting transfers between devices, per_device(): ytwo = lax.ppermute(ysend_two, 'gy', y_out)  2.24 us
    pallas_call x1, Pallas kernels, own_share(): pl.pallas_call(own_body, out_shape=(coef, coef_far, values, values), in_s...  1.84 us
    ppermute x1, starting transfers between devices, per_device(): yone = lax.ppermute(ysend_one, 'gy', y_in)  1.72 us
  transfers between devices with their start and end apart: 9, of which 5 were waited for; matrix products, arithmetic and copies ran while one was open for 0% of the time, Pallas kernels for 13%

profile of v4, /device:TPU:1, one launch (start us, length us, event | category | flops | bytes accessed | tf_op | source)
XLA Modules:
  0.0 43.7 jit_solution(16920631481266004675)
XLA Ops:
  0.0 1.8 %own_share.1 = (f32[32,8,128]{2,1,0:T(8,128)S(1)}, f32[35,8,128]{2,1,0:T(8,128)S(1)}, f32[976,128]{1,0:T(8,128)S(1)}, f32[976,128]{1,0:T(8,128)S(1)}) custom-call(f32[16]{0:T(128)} %gap_hbm.1, f32[5,16,32,128]{3,2,1,0:T(8,128)} %s_hbm.2, f32[5,16,32,128]{3,2,1,0:T(8,128)} %f_hbm.2), custom_call_target="tpu_custom_call" | custom-call | flops 16777216 | bytes 4194304 | tf_op jit(solution)/shard_map/own_share/pallas_call | solution.py:244
  1.8 1.5 %collective-permute-start = (f32[976,128]{1,0:T(8,128)S(1)}, f32[976,128]{1,0:T(8,128)S(1)}, u32[]{:S(2)}, u32[]{:S(2)}) collective-permute-start(f32[976,128]{1,0:T(8,128)S(1)} %get-tuple-element.47), channel_id=1, source_target_pairs={{0,4},{4,0},{8,12},{12,8},{16,20},{20,16},{24,28},{28,24},{32,36},... | collective-permute-start | bytes 1499144 | tf_op jit(solution)/shard_map/ppermute | solution.py:623
  3.4 1.4 %pack.1 = (f32[5,4,32,128]{3,2,1,0:T(8,128)S(1)}, f32[5,4,32,128]{3,2,1,0:T(8,128)S(1)}, f32[5,8,8,128]{3,2,1,0:T(8,128)S(1)}, f32[5,8,8,128]{3,2,1,0:T(8,128)S(1)}) custom-call(f32[5,16,32,128]{3,2,1,0:T(8,128)} %s_hbm.2, f32[5,16,32,128]{3,2,1,0:T(8,128)} %f_hbm.2, f32[5,16,32,128]{3,2,1,0:T(8,128)} %fy_hbm), custom_call_target="tpu_custom_call" | custom-call | bytes 2097152 | tf_op jit(solution)/shard_map/pack/pallas_call | solution.py:123
  4.7 0.1 collective-permute-done.got
  4.9 1.1 %pair.1 = (f32[1024,128]{1,0:T(8,128)}, f32[328,128]{1,0:T(8,128)S(1)}) custom-call(f32[976,128]{1,0:T(8,128)S(1)} %get-tuple-element.45.mine, f32[976,128]{1,0:T(8,128)S(1)} %collective-permute-done.got), custom_call_target="tpu_custom_call" | custom-call | flops 1048576 | bytes 1048576 | tf_op jit(solution)/shard_map/pair/pallas_call | solution.py:320
  6.0 0.0 copy-start
  6.0 0.0 copy-start.1
  6.0 6.8 %all-to-all-start = ((f32[16,64,128]{2,1,0:T(8,128)}), f32[16,64,128]{2,1,0:T(8,128)S(1)}, u32[]{:S(2)}, u32[]{:S(2)}) async-start(f32[16,64,128]{2,1,0:T(8,128)} %bitcast), calls=%async_computation | async-start | bytes 1048576 | tf_op jit(solution)/shard_map/all_to_all | solution.py:610
  12.8 0.7 %collective-permute-start.1 = (f32[5,4,32,128]{3,2,1,0:T(8,128)S(1)}, f32[5,4,32,128]{3,2,1,0:T(8,128)S(1)}, u32[]{:S(2)}, u32[]{:S(2)}) collective-permute-start(f32[5,4,32,128]{3,2,1,0:T(8,128)S(1)} %get-tuple-element.62), channel_id=1, source_target_pairs={{0,4},{4,0},{8,12},{12,8},{16,20},{20,16},{24,28},{28,24},{32,36},... | collective-permute-start | bytes 983048 | tf_op jit(solution)/shard_map/ppermute | solution.py:628
  13.6 3.4 %collective-permute-start.2 = (f32[5,4,32,128]{3,2,1,0:T(8,128)S(1)}, f32[5,4,32,128]{3,2,1,0:T(8,128)S(1)}, u32[]{:S(2)}, u32[]{:S(2)}) collective-permute-start(f32[5,4,32,128]{3,2,1,0:T(8,128)S(1)} %get-tuple-element.63), channel_id=1, source_target_pairs={{4,8},{8,4},{12,16},{16,12},{20,24},{24,20},{28,32},{32,28},{36,40... | collective-permute-start | bytes 983048 | tf_op jit(solution)/shard_map/ppermute | solution.py:629
  17.0 1.7 %collective-permute-start.3 = (f32[5,8,8,128]{3,2,1,0:T(8,128)S(1)}, f32[5,8,8,128]{3,2,1,0:T(8,128)S(1)}, u32[]{:S(2)}, u32[]{:S(2)}) collective-permute-start(f32[5,8,8,128]{3,2,1,0:T(8,128)S(1)} %get-tuple-element.64), channel_id=1, source_target_pairs={{0,1},{1,0},{2,3},{3,2},{4,5},{5,4},{6,7},{7,6},{8,9},{9,8},{10,11... | collective-permute-start | bytes 491528 | tf_op jit(solution)/shard_map/ppermute | solution.py:630
  18.7 2.2 %collective-permute-start.4 = (f32[5,8,8,128]{3,2,1,0:T(8,128)S(1)}, f32[5,8,8,128]{3,2,1,0:T(8,128)S(1)}, u32[]{:S(2)}, u32[]{:S(2)}) collective-permute-start(f32[5,8,8,128]{3,2,1,0:T(8,128)S(1)} %get-tuple-element.65), channel_id=1, source_target_pairs={{0,3},{1,2},{2,1},{3,0},{4,7},{5,6},{6,5},{7,4},{8,11},{9,10},{10,... | collective-permute-start | bytes 491528 | tf_op jit(solution)/shard_map/ppermute | solution.py:631
  20.9 2.6 %all-to-all-done = f32[16,64,128]{2,1,0:T(8,128)S(1)} async-done(((f32[16,64,128]{2,1,0:T(8,128)}), f32[16,64,128]{2,1,0:T(8,128)S(1)}, u32[]{:S(2)}, u32[]{:S(2)}) %all-to-all-start) | async-done | bytes 524320 | tf_op jit(solution)/shard_map/all_to_all | solution.py:610
  23.6 0.9 %join.1 = f32[384,128]{1,0:T(8,128)} custom-call(f32[1024,128]{1,0:T(8,128)S(1)} %bitcast.4), custom_call_target="tpu_custom_call" | custom-call | flops 1048576 | bytes 1048576 | tf_op jit(solution)/shard_map/join/pallas_call | solution.py:413
  24.5 0.0 collective-permute-done.3.yone
  24.5 0.3 collective-permute-done.2.two
  24.8 6.9 %all-to-all-start.1 = ((f32[16,24,128]{2,1,0:T(8,128)}), f32[16,24,128]{2,1,0:T(8,128)S(1)}, u32[]{:S(2)}, u32[]{:S(2)}) async-start(f32[16,24,128]{2,1,0:T(8,128)} %bitcast.2), calls=%async_computation.1 | async-start | bytes 393216 | tf_op jit(solution)/shard_map/all_to_all | solution.py:610
  31.8 1.3 %collective-permute-start.5 = (f32[160,128]{1,0:T(8,128)S(1)}, f32[160,128]{1,0:T(8,128)S(1)}, u32[]{:S(2)}, u32[]{:S(2)}) collective-permute-start(f32[160,128]{1,0:T(8,128)S(1)} %get-tuple-element.74), channel_id=1, source_target_pairs={{0,4},{4,0},{8,12},{12,8},{16,20},{20,16},{24,28},{28,24},{32,36},... | collective-permute-start | bytes 245768 | tf_op jit(solution)/shard_map/ppermute | solution.py:635
  33.1 3.1 %block.1 = (f32[5,16,32,128]{3,2,1,0:T(8,128)S(1)}, f32[16,32,128]{2,1,0:T(8,128)S(1)}) custom-call(f32[32,8,128]{2,1,0:T(8,128)S(1)} %get-tuple-element.67.inner, f32[5,16,32,128]{3,2,1,0:T(8,128)} %s_hbm.2, f32[5,16,32,128]{3,2,1,0:T(8,128)} %f_hbm.2, f32[5,16,32,128]{3,2,1,0:T(8,128)} %fy_hbm, f32[5,4,32,128]{3,2,1,0:T(8,128)S(1)} %collective-permute-done.1.one, ...), custom_call_target="tpu_custom_call" | custom-call | flops 33554432 | bytes 8388608 | tf_op jit(solution)/shard_map/block/pallas_call | solution.py:562
  36.3 2.7 %all-to-all-done.1 = f32[16,24,128]{2,1,0:T(8,128)S(1)} async-done(((f32[16,24,128]{2,1,0:T(8,128)}), f32[16,24,128]{2,1,0:T(8,128)S(1)}, u32[]{:S(2)}, u32[]{:S(2)}) %all-to-all-start.1) | async-done | bytes 196640 | tf_op jit(solution)/shard_map/all_to_all | solution.py:610
  39.0 0.1 split.1
  39.0 2.4 %collective-permute-start.6 = (f32[320,128]{1,0:T(8,128)S(1)}, f32[320,128]{1,0:T(8,128)S(1)}, u32[]{:S(2)}, u32[]{:S(2)}) collective-permute-start(f32[320,128]{1,0:T(8,128)S(1)} %get-tuple-element.82), channel_id=1, source_target_pairs={{0,4},{4,0},{8,12},{12,8},{16,20},{20,16},{24,28},{28,24},{32,36},... | collective-permute-start | bytes 491528 | tf_op jit(solution)/shard_map/ppermute | solution.py:639
  41.5 1.0 %collective-permute-done.6.got = f32[320,128]{1,0:T(8,128)S(1)} collective-permute-done((f32[320,128]{1,0:T(8,128)S(1)}, f32[320,128]{1,0:T(8,128)S(1)}, u32[]{:S(2)}, u32[]{:S(2)}) %collective-permute-start.6) | collective-permute-done | bytes 163872 | tf_op jit(solution)/shard_map/ppermute | solution.py:639
  42.5 1.2 %finish.1 = f32[5,16,32,128]{3,2,1,0:T(8,128)} custom-call(f32[35,8,128]{2,1,0:T(8,128)S(1)} %get-tuple-element.44.outer, f32[5,16,32,128]{3,2,1,0:T(8,128)S(1)} %get-tuple-element.75.base, f32[16,32,128]{2,1,0:T(8,128)S(1)} %get-tuple-element.76.mxb, f32[320,128]{1,0:T(8,128)S(1)} %get-tuple-element.81.own, f32[320,128]{1,0:T(8,128)S(1)} %collective-permute-done.6.got), custom_call_target="tpu_custom_call" | custom-call | flops 4194304 | bytes 3145728 | tf_op jit(solution)/shard_map/finish/pallas_call | solution.py:596
  (6 shorter events, 0.1 us)
Async XLA Ops:
  1.8 3.0 %collective-permute-start = (f32[976,128]{1,0:T(8,128)S(1)}, f32[976,128]{1,0:T(8,128)S(1)}, u32[]{:S(2)}, u32[]{:S(2)}) collective-permute-start(f32[976,128]{1,0:T(8,128)S(1)} %get-tuple-element.47), channel_id=1, source_target_pairs={{0,4},{4,0},{8,12},{12,8},{16,20},{20,16},{24,28},{28,24},{32,36},... | collective-permute-start | bytes 1499144 | tf_op jit(solution)/shard_map/ppermute | solution.py:623
  6.0 27.1 %copy-start = (f32[16,32]{1,0:T(8,128)S(1)}, f32[16,32]{1,0:T(8,128)}, u32[]{:S(2)}) copy-start(f32[16,32]{1,0:T(8,128)} %mx.1) | copy-start | bytes 6148
  6.0 27.1 %copy-start.1 = (f32[16,32]{1,0:T(8,128)S(1)}, f32[16,32]{1,0:T(8,128)}, u32[]{:S(2)}) copy-start(f32[16,32]{1,0:T(8,128)} %my.1) | copy-start | bytes 6148
  6.0 17.6 %all-to-all-start = ((f32[16,64,128]{2,1,0:T(8,128)}), f32[16,64,128]{2,1,0:T(8,128)S(1)}, u32[]{:S(2)}, u32[]{:S(2)}) async-start(f32[16,64,128]{2,1,0:T(8,128)} %bitcast), calls=%async_computation | async-start | bytes 1048576 | tf_op jit(solution)/shard_map/all_to_all | solution.py:610
  12.8 11.7 %collective-permute-start.1 = (f32[5,4,32,128]{3,2,1,0:T(8,128)S(1)}, f32[5,4,32,128]{3,2,1,0:T(8,128)S(1)}, u32[]{:S(2)}, u32[]{:S(2)}) collective-permute-start(f32[5,4,32,128]{3,2,1,0:T(8,128)S(1)} %get-tuple-element.62), channel_id=1, source_target_pairs={{0,4},{4,0},{8,12},{12,8},{16,20},{20,16},{24,28},{28,24},{32,36},... | collective-permute-start | bytes 983048 | tf_op jit(solution)/shard_map/ppermute | solution.py:628
  13.6 11.3 %collective-permute-start.2 = (f32[5,4,32,128]{3,2,1,0:T(8,128)S(1)}, f32[5,4,32,128]{3,2,1,0:T(8,128)S(1)}, u32[]{:S(2)}, u32[]{:S(2)}) collective-permute-start(f32[5,4,32,128]{3,2,1,0:T(8,128)S(1)} %get-tuple-element.63), channel_id=1, source_target_pairs={{4,8},{8,4},{12,16},{16,12},{20,24},{24,20},{28,32},{32,28},{36,40... | collective-permute-start | bytes 983048 | tf_op jit(solution)/shard_map/ppermute | solution.py:629
  17.0 7.5 %collective-permute-start.3 = (f32[5,8,8,128]{3,2,1,0:T(8,128)S(1)}, f32[5,8,8,128]{3,2,1,0:T(8,128)S(1)}, u32[]{:S(2)}, u32[]{:S(2)}) collective-permute-start(f32[5,8,8,128]{3,2,1,0:T(8,128)S(1)} %get-tuple-element.64), channel_id=1, source_target_pairs={{0,1},{1,0},{2,3},{3,2},{4,5},{5,4},{6,7},{7,6},{8,9},{9,8},{10,11... | collective-permute-start | bytes 491528 | tf_op jit(solution)/shard_map/ppermute | solution.py:630
  18.7 5.8 %collective-permute-start.4 = (f32[5,8,8,128]{3,2,1,0:T(8,128)S(1)}, f32[5,8,8,128]{3,2,1,0:T(8,128)S(1)}, u32[]{:S(2)}, u32[]{:S(2)}) collective-permute-start(f32[5,8,8,128]{3,2,1,0:T(8,128)S(1)} %get-tuple-element.65), channel_id=1, source_target_pairs={{0,3},{1,2},{2,1},{3,0},{4,7},{5,6},{6,5},{7,4},{8,11},{9,10},{10,... | collective-permute-start | bytes 491528 | tf_op jit(solution)/shard_map/ppermute | solution.py:631
  24.8 14.1 %all-to-all-start.1 = ((f32[16,24,128]{2,1,0:T(8,128)}), f32[16,24,128]{2,1,0:T(8,128)S(1)}, u32[]{:S(2)}, u32[]{:S(2)}) async-start(f32[16,24,128]{2,1,0:T(8,128)} %bitcast.2), calls=%async_computation.1 | async-start | bytes 393216 | tf_op jit(solution)/shard_map/all_to_all | solution.py:610
  31.8 4.5 %collective-permute-start.5 = (f32[160,128]{1,0:T(8,128)S(1)}, f32[160,128]{1,0:T(8,128)S(1)}, u32[]{:S(2)}, u32[]{:S(2)}) collective-permute-start(f32[160,128]{1,0:T(8,128)S(1)} %get-tuple-element.74), channel_id=1, source_target_pairs={{0,4},{4,0},{8,12},{12,8},{16,20},{20,16},{24,28},{28,24},{32,36},... | collective-permute-start | bytes 245768 | tf_op jit(solution)/shard_map/ppermute | solution.py:635
  39.0 3.5 %collective-permute-start.6 = (f32[320,128]{1,0:T(8,128)S(1)}, f32[320,128]{1,0:T(8,128)S(1)}, u32[]{:S(2)}, u32[]{:S(2)}) collective-permute-start(f32[320,128]{1,0:T(8,128)S(1)} %get-tuple-element.82), channel_id=1, source_target_pairs={{0,4},{4,0},{8,12},{12,8},{16,20},{20,16},{24,28},{28,24},{32,36},... | collective-permute-start | bytes 491528 | tf_op jit(solution)/shard_map/ppermute | solution.py:639

commit v5 on v4

--- a/solution.py
+++ b/solution.py
@@ -570,7 +570,7 @@
         scratch_shapes=[pltpu.VMEM((NV, NI, NJ, NK), F32)] * 3
         + [pltpu.VMEM((2 * NI, SUB + NJ + SUB, NK), F32), pltpu.SemaphoreType.DMA((3, NV))],
         compiler_params=pltpu.CompilerParams(vmem_limit_bytes=16 << 20),
-        cost_estimate=pl.CostEstimate(flops=1 << 25, bytes_accessed=8 << 20, transcendentals=0),
+        cost_estimate=pl.CostEstimate(flops=1 << 25, bytes_accessed=64 << 20, transcendentals=0),
         name="block",
     )(inner, *in_hbm(state, flux_x, flux_y), one, two, yone, ytwo, mx, my)
 
@@ -630,7 +630,8 @@
     yone = lax.ppermute(ysend_one, "gy", y_in)
     ytwo = lax.ppermute(ysend_two, "gy", y_out)
     outside = join(ends)
-    outside, one, two, yone, ytwo = lax.optimization_barrier((outside, one, two, yone, ytwo))
+    outside, one = lax.optimization_barrier((outside, one))
+    two, yone, ytwo = lax.optimization_barrier((two, yone, ytwo))
     far_own, far_send = far(outer, two)
     far_got = lax.ppermute(far_send, "gx", pair_in)
     base, mxb = block(inner, state, flux_x, flux_y, one, two, yone, ytwo, metric_x, metric_y)

time: 44.1 us -> 42 us (0.952)
  waiting for transfers between devices: 6.79 us -> 4.89 us
    all_to_all x2, starting transfers between devices: 13.7 us -> 10.4 us  [exchange(): lax.all_to_all(x.reshape(PAIRS, rows, NK), 'gx', 0, 0, tiled=True, axis_i...]
    all_to_all x2, waiting for transfers between devices: 5.34 us -> 3.74 us  [exchange(): lax.all_to_all(x.reshape(PAIRS, rows, NK), 'gx', 0, 0, tiled=True, axis_i...]
    ppermute x1, starting transfers between devices: 1.33 us -> 2.92 us  [per_device(): far_got = lax.ppermute(far_send, 'gx', pair_in)]
    ppermute x1, starting transfers between devices: 2.44 us -> 3.98 us  [per_device(): return finish(outer, base, mxb, own, lax.ppermute(send, 'gx', pair_in))]
  transfers between devices with their start and end apart: 9 -> 9, of which waited for: 5 -> 4; matrix products, arithmetic and copies ran while one was open for 0% -> 0% of each run, Pallas kernels for 13% -> 13%
where the time goes in v5:
time: 42 us; the launch traced here: 41.6 us
  starting transfers between devices  26.9 us (64%)
  Pallas kernels  9.67 us (23%)
  waiting for transfers between devices  4.89 us (12%)
    all_to_all x2, starting transfers between devices, exchange(): lax.all_to_all(x.reshape(PAIRS, rows, NK), 'gx', 0, 0, tiled=True, axis_i...  10.4 us
    ppermute x1, starting transfers between devices, per_device(): return finish(outer, base, mxb, own, lax.ppermute(send, 'gx', pair_in))  3.98 us
    all_to_all x2, waiting for transfers between devices, exchange(): lax.all_to_all(x.reshape(PAIRS, rows, NK), 'gx', 0, 0, tiled=True, axis_i...  3.74 us
    ppermute x1, starting transfers between devices, per_device(): two = lax.ppermute(send_two, 'gx', pair_out)  3.37 us
    pallas_call x1, Pallas kernels, block(): pl.pallas_call(block_body, out_shape=(jax.ShapeDtypeStruct((NV, NI, NJ, N...  3.12 us
    ppermute x1, starting transfers between devices, per_device(): far_got = lax.ppermute(far_send, 'gx', pair_in)  2.92 us
    ppermute x1, starting transfers between devices, per_device(): ytwo = lax.ppermute(ysend_two, 'gy', y_out)  2.24 us
    pallas_call x1, Pallas kernels, own_share(): pl.pallas_call(own_body, out_shape=(coef, coef_far, values, values), in_s...  1.84 us
  transfers between devices with their start and end apart: 9, of which 4 were waited for; matrix products, arithmetic and copies ran while one was open for 0% of the time, Pallas kernels for 13%

profile of v5, /device:TPU:1, one launch (start us, length us, event | category | flops | bytes accessed | tf_op | source)
XLA Modules:
  0.0 41.6 jit_solution(15537242866202005023)
XLA Ops:
  0.0 1.8 %own_share.1 = (f32[32,8,128]{2,1,0:T(8,128)S(1)}, f32[35,8,128]{2,1,0:T(8,128)S(1)}, f32[976,128]{1,0:T(8,128)S(1)}, f32[976,128]{1,0:T(8,128)S(1)}) custom-call(f32[16]{0:T(128)} %gap_hbm.1, f32[5,16,32,128]{3,2,1,0:T(8,128)} %s_hbm.2, f32[5,16,32,128]{3,2,1,0:T(8,128)} %f_hbm.2), custom_call_target="tpu_custom_call" | custom-call | flops 16777216 | bytes 4194304 | tf_op jit(solution)/shard_map/own_share/pallas_call | solution.py:244
  1.8 1.5 %collective-permute-start = (f32[976,128]{1,0:T(8,128)S(1)}, f32[976,128]{1,0:T(8,128)S(1)}, u32[]{:S(2)}, u32[]{:S(2)}) collective-permute-start(f32[976,128]{1,0:T(8,128)S(1)} %get-tuple-element.47), channel_id=1, source_target_pairs={{0,4},{4,0},{8,12},{12,8},{16,20},{20,16},{24,28},{28,24},{32,36},... | collective-permute-start | bytes 1499144 | tf_op jit(solution)/shard_map/ppermute | solution.py:623
  3.4 1.4 %pack.1 = (f32[5,4,32,128]{3,2,1,0:T(8,128)S(1)}, f32[5,4,32,128]{3,2,1,0:T(8,128)S(1)}, f32[5,8,8,128]{3,2,1,0:T(8,128)S(1)}, f32[5,8,8,128]{3,2,1,0:T(8,128)S(1)}) custom-call(f32[5,16,32,128]{3,2,1,0:T(8,128)} %s_hbm.2, f32[5,16,32,128]{3,2,1,0:T(8,128)} %f_hbm.2, f32[5,16,32,128]{3,2,1,0:T(8,128)} %fy_hbm), custom_call_target="tpu_custom_call" | custom-call | bytes 2097152 | tf_op jit(solution)/shard_map/pack/pallas_call | solution.py:123
  4.7 0.1 collective-permute-done.got
  4.9 1.1 %pair.1 = (f32[1024,128]{1,0:T(8,128)}, f32[328,128]{1,0:T(8,128)S(1)}) custom-call(f32[976,128]{1,0:T(8,128)S(1)} %get-tuple-element.45.mine, f32[976,128]{1,0:T(8,128)S(1)} %collective-permute-done.got), custom_call_target="tpu_custom_call" | custom-call | flops 1048576 | bytes 1048576 | tf_op jit(solution)/shard_map/pair/pallas_call | solution.py:320
  6.0 0.0 copy-start
  6.0 0.0 copy-start.1
  6.0 6.8 %all-to-all-start = ((f32[16,64,128]{2,1,0:T(8,128)}), f32[16,64,128]{2,1,0:T(8,128)S(1)}, u32[]{:S(2)}, u32[]{:S(2)}) async-start(f32[16,64,128]{2,1,0:T(8,128)} %bitcast), calls=%async_computation | async-start | bytes 1048576 | tf_op jit(solution)/shard_map/all_to_all | solution.py:610
  12.8 0.7 %collective-permute-start.1 = (f32[5,4,32,128]{3,2,1,0:T(8,128)S(1)}, f32[5,4,32,128]{3,2,1,0:T(8,128)S(1)}, u32[]{:S(2)}, u32[]{:S(2)}) collective-permute-start(f32[5,4,32,128]{3,2,1,0:T(8,128)S(1)} %get-tuple-element.62), channel_id=1, source_target_pairs={{0,4},{4,0},{8,12},{12,8},{16,20},{20,16},{24,28},{28,24},{32,36},... | collective-permute-start | bytes 983048 | tf_op jit(solution)/shard_map/ppermute | solution.py:628
  13.6 3.4 %collective-permute-start.2 = (f32[5,4,32,128]{3,2,1,0:T(8,128)S(1)}, f32[5,4,32,128]{3,2,1,0:T(8,128)S(1)}, u32[]{:S(2)}, u32[]{:S(2)}) collective-permute-start(f32[5,4,32,128]{3,2,1,0:T(8,128)S(1)} %get-tuple-element.66), channel_id=1, source_target_pairs={{4,8},{8,4},{12,16},{16,12},{20,24},{24,20},{28,32},{32,28},{36,40... | collective-permute-start | bytes 983048 | tf_op jit(solution)/shard_map/ppermute | solution.py:629
  17.0 1.7 %collective-permute-start.3 = (f32[5,8,8,128]{3,2,1,0:T(8,128)S(1)}, f32[5,8,8,128]{3,2,1,0:T(8,128)S(1)}, u32[]{:S(2)}, u32[]{:S(2)}) collective-permute-start(f32[5,8,8,128]{3,2,1,0:T(8,128)S(1)} %get-tuple-element.67), channel_id=1, source_target_pairs={{0,1},{1,0},{2,3},{3,2},{4,5},{5,4},{6,7},{7,6},{8,9},{9,8},{10,11... | collective-permute-start | bytes 491528 | tf_op jit(solution)/shard_map/ppermute | solution.py:630
  18.7 2.2 %collective-permute-start.4 = (f32[5,8,8,128]{3,2,1,0:T(8,128)S(1)}, f32[5,8,8,128]{3,2,1,0:T(8,128)S(1)}, u32[]{:S(2)}, u32[]{:S(2)}) collective-permute-start(f32[5,8,8,128]{3,2,1,0:T(8,128)S(1)} %get-tuple-element.68), channel_id=1, source_target_pairs={{0,3},{1,2},{2,1},{3,0},{4,7},{5,6},{6,5},{7,4},{8,11},{9,10},{10,... | collective-permute-start | bytes 491528 | tf_op jit(solution)/shard_map/ppermute | solution.py:631
  20.9 2.6 %all-to-all-done = f32[16,64,128]{2,1,0:T(8,128)S(1)} async-done(((f32[16,64,128]{2,1,0:T(8,128)}), f32[16,64,128]{2,1,0:T(8,128)S(1)}, u32[]{:S(2)}, u32[]{:S(2)}) %all-to-all-start) | async-done | bytes 524320 | tf_op jit(solution)/shard_map/all_to_all | solution.py:610
  23.6 0.9 %join.1 = f32[384,128]{1,0:T(8,128)} custom-call(f32[1024,128]{1,0:T(8,128)S(1)} %bitcast.4), custom_call_target="tpu_custom_call" | custom-call | flops 1048576 | bytes 1048576 | tf_op jit(solution)/shard_map/join/pallas_call | solution.py:413
  24.5 0.0 collective-permute-done.1.one
  24.5 3.6 %all-to-all-start.1 = ((f32[16,24,128]{2,1,0:T(8,128)}), f32[16,24,128]{2,1,0:T(8,128)S(1)}, u32[]{:S(2)}, u32[]{:S(2)}) async-start(f32[16,24,128]{2,1,0:T(8,128)} %bitcast.2), calls=%async_computation.1 | async-start | bytes 393216 | tf_op jit(solution)/shard_map/all_to_all | solution.py:610
  28.1 0.0 collective-permute-done.4.ytwo
  28.2 2.9 %collective-permute-start.5 = (f32[160,128]{1,0:T(8,128)S(1)}, f32[160,128]{1,0:T(8,128)S(1)}, u32[]{:S(2)}, u32[]{:S(2)}) collective-permute-start(f32[160,128]{1,0:T(8,128)S(1)} %get-tuple-element.74), channel_id=1, source_target_pairs={{0,4},{4,0},{8,12},{12,8},{16,20},{20,16},{24,28},{28,24},{32,36},... | collective-permute-start | bytes 245768 | tf_op jit(solution)/shard_map/ppermute | solution.py:636
  31.1 3.1 %block.1 = (f32[5,16,32,128]{3,2,1,0:T(8,128)S(1)}, f32[16,32,128]{2,1,0:T(8,128)S(1)}) custom-call(f32[32,8,128]{2,1,0:T(8,128)S(1)} %get-tuple-element.64.inner, f32[5,16,32,128]{3,2,1,0:T(8,128)} %s_hbm.2, f32[5,16,32,128]{3,2,1,0:T(8,128)} %f_hbm.2, f32[5,16,32,128]{3,2,1,0:T(8,128)} %fy_hbm, f32[5,4,32,128]{3,2,1,0:T(8,128)S(1)} %collective-permute-done.1.one, ...), custom_call_target="tpu_custom_call" | custom-call | flops 33554432 | bytes 67108864 | tf_op jit(solution)/shard_map/block/pallas_call | solution.py:562
  34.2 1.1 %all-to-all-done.1 = f32[16,24,128]{2,1,0:T(8,128)S(1)} async-done(((f32[16,24,128]{2,1,0:T(8,128)}), f32[16,24,128]{2,1,0:T(8,128)S(1)}, u32[]{:S(2)}, u32[]{:S(2)}) %all-to-all-start.1) | async-done | bytes 196640 | tf_op jit(solution)/shard_map/all_to_all | solution.py:610
  35.3 0.1 split.1
  35.4 4.0 %collective-permute-start.6 = (f32[320,128]{1,0:T(8,128)S(1)}, f32[320,128]{1,0:T(8,128)S(1)}, u32[]{:S(2)}, u32[]{:S(2)}) collective-permute-start(f32[320,128]{1,0:T(8,128)S(1)} %get-tuple-element.82), channel_id=1, source_target_pairs={{0,4},{4,0},{8,12},{12,8},{16,20},{20,16},{24,28},{28,24},{32,36},... | collective-permute-start | bytes 491528 | tf_op jit(solution)/shard_map/ppermute | solution.py:640
  39.4 1.0 %collective-permute-done.6.got = f32[320,128]{1,0:T(8,128)S(1)} collective-permute-done((f32[320,128]{1,0:T(8,128)S(1)}, f32[320,128]{1,0:T(8,128)S(1)}, u32[]{:S(2)}, u32[]{:S(2)}) %collective-permute-start.6) | collective-permute-done | bytes 163872 | tf_op jit(solution)/shard_map/ppermute | solution.py:640
  40.4 1.2 %finish.1 = f32[5,16,32,128]{3,2,1,0:T(8,128)} custom-call(f32[35,8,128]{2,1,0:T(8,128)S(1)} %get-tuple-element.44.outer, f32[5,16,32,128]{3,2,1,0:T(8,128)S(1)} %get-tuple-element.75.base, f32[16,32,128]{2,1,0:T(8,128)S(1)} %get-tuple-element.76.mxb, f32[320,128]{1,0:T(8,128)S(1)} %get-tuple-element.81.own, f32[320,128]{1,0:T(8,128)S(1)} %collective-permute-done.6.got), custom_call_target="tpu_custom_call" | custom-call | flops 4194304 | bytes 3145728 | tf_op jit(solution)/shard_map/finish/pallas_call | solution.py:596
  (6 shorter events, 0.1 us)
Async XLA Ops:
  1.8 3.0 %collective-permute-start = (f32[976,128]{1,0:T(8,128)S(1)}, f32[976,128]{1,0:T(8,128)S(1)}, u32[]{:S(2)}, u32[]{:S(2)}) collective-permute-start(f32[976,128]{1,0:T(8,128)S(1)} %get-tuple-element.47), channel_id=1, source_target_pairs={{0,4},{4,0},{8,12},{12,8},{16,20},{20,16},{24,28},{28,24},{32,36},... | collective-permute-start | bytes 1499144 | tf_op jit(solution)/shard_map/ppermute | solution.py:623
  6.0 25.1 %copy-start = (f32[16,32]{1,0:T(8,128)S(1)}, f32[16,32]{1,0:T(8,128)}, u32[]{:S(2)}) copy-start(f32[16,32]{1,0:T(8,128)} %mx.1) | copy-start | bytes 6148
  6.0 25.1 %copy-start.1 = (f32[16,32]{1,0:T(8,128)S(1)}, f32[16,32]{1,0:T(8,128)}, u32[]{:S(2)}) copy-start(f32[16,32]{1,0:T(8,128)} %my.1) | copy-start | bytes 6148
  6.0 17.6 %all-to-all-start = ((f32[16,64,128]{2,1,0:T(8,128)}), f32[16,64,128]{2,1,0:T(8,128)S(1)}, u32[]{:S(2)}, u32[]{:S(2)}) async-start(f32[16,64,128]{2,1,0:T(8,128)} %bitcast), calls=%async_computation | async-start | bytes 1048576 | tf_op jit(solution)/shard_map/all_to_all | solution.py:610
  12.8 11.7 %collective-permute-start.1 = (f32[5,4,32,128]{3,2,1,0:T(8,128)S(1)}, f32[5,4,32,128]{3,2,1,0:T(8,128)S(1)}, u32[]{:S(2)}, u32[]{:S(2)}) collective-permute-start(f32[5,4,32,128]{3,2,1,0:T(8,128)S(1)} %get-tuple-element.62), channel_id=1, source_target_pairs={{0,4},{4,0},{8,12},{12,8},{16,20},{20,16},{24,28},{28,24},{32,36},... | collective-permute-start | bytes 983048 | tf_op jit(solution)/shard_map/ppermute | solution.py:628
  13.6 14.5 %collective-permute-start.2 = (f32[5,4,32,128]{3,2,1,0:T(8,128)S(1)}, f32[5,4,32,128]{3,2,1,0:T(8,128)S(1)}, u32[]{:S(2)}, u32[]{:S(2)}) collective-permute-start(f32[5,4,32,128]{3,2,1,0:T(8,128)S(1)} %get-tuple-element.66), channel_id=1, source_target_pairs={{4,8},{8,4},{12,16},{16,12},{20,24},{24,20},{28,32},{32,28},{36,40... | collective-permute-start | bytes 983048 | tf_op jit(solution)/shard_map/ppermute | solution.py:629
  17.0 11.1 %collective-permute-start.3 = (f32[5,8,8,128]{3,2,1,0:T(8,128)S(1)}, f32[5,8,8,128]{3,2,1,0:T(8,128)S(1)}, u32[]{:S(2)}, u32[]{:S(2)}) collective-permute-start(f32[5,8,8,128]{3,2,1,0:T(8,128)S(1)} %get-tuple-element.67), channel_id=1, source_target_pairs={{0,1},{1,0},{2,3},{3,2},{4,5},{5,4},{6,7},{7,6},{8,9},{9,8},{10,11... | collective-permute-start | bytes 491528 | tf_op jit(solution)/shard_map/ppermute | solution.py:630
  18.7 9.4 %collective-permute-start.4 = (f32[5,8,8,128]{3,2,1,0:T(8,128)S(1)}, f32[5,8,8,128]{3,2,1,0:T(8,128)S(1)}, u32[]{:S(2)}, u32[]{:S(2)}) collective-permute-start(f32[5,8,8,128]{3,2,1,0:T(8,128)S(1)} %get-tuple-element.68), channel_id=1, source_target_pairs={{0,3},{1,2},{2,1},{3,0},{4,7},{5,6},{6,5},{7,4},{8,11},{9,10},{10,... | collective-permute-start | bytes 491528 | tf_op jit(solution)/shard_map/ppermute | solution.py:631
  24.5 10.8 %all-to-all-start.1 = ((f32[16,24,128]{2,1,0:T(8,128)}), f32[16,24,128]{2,1,0:T(8,128)S(1)}, u32[]{:S(2)}, u32[]{:S(2)}) async-start(f32[16,24,128]{2,1,0:T(8,128)} %bitcast.2), calls=%async_computation.1 | async-start | bytes 393216 | tf_op jit(solution)/shard_map/all_to_all | solution.py:610
  28.2 6.1 %collective-permute-start.5 = (f32[160,128]{1,0:T(8,128)S(1)}, f32[160,128]{1,0:T(8,128)S(1)}, u32[]{:S(2)}, u32[]{:S(2)}) collective-permute-start(f32[160,128]{1,0:T(8,128)S(1)} %get-tuple-element.74), channel_id=1, source_target_pairs={{0,4},{4,0},{8,12},{12,8},{16,20},{20,16},{24,28},{28,24},{32,36},... | collective-permute-start | bytes 245768 | tf_op jit(solution)/shard_map/ppermute | solution.py:636
  35.4 5.0 %collective-permute-start.6 = (f32[320,128]{1,0:T(8,128)S(1)}, f32[320,128]{1,0:T(8,128)S(1)}, u32[]{:S(2)}, u32[]{:S(2)}) collective-permute-start(f32[320,128]{1,0:T(8,128)S(1)} %get-tuple-element.82), channel_id=1, source_target_pairs={{0,4},{4,0},{8,12},{12,8},{16,20},{20,16},{24,28},{28,24},{32,36},... | collective-permute-start | bytes 491528 | tf_op jit(solution)/shard_map/ppermute | solution.py:640

commit v6 on v5

--- a/solution.py
+++ b/solution.py
@@ -8,12 +8,14 @@
 
 NV, NI, NJ, NK = 5, 16, 32, 128
 PIECES, PAIRS, HALF = 32, 16, 16
-ROWS, WIDE = 24, 64
-EDGE = 12 * NV * HALF
+VALUES = 10
+ROWS, WIDE = 24, 56
+EDGE = VALUES * NV * HALF
 SUB = 8
 F32 = jnp.float32
 Y_WEIGHTS = (4.0 / 5.0, -1.0 / 5.0, 4.0 / 105.0, -1.0 / 280.0)
 RHO = 25.0 / 36.0
+BETA = 3.0 * RHO
 D6 = (1.0, -6.0, 15.0, -20.0, 15.0, -6.0, 1.0)
 
 C_C, C_MG = 0, NI
@@ -33,10 +35,7 @@
     left, right = -a * inv[:, 0], -a * inv[:, -1]
     hl, hr, tl, tr = left[0], right[0], left[-1], right[-1]
     d = 1.0 / (1.0 - tr * hl)
-    w = RHO * np.array([-inv[0, 0], -inv[-1, 0], inv[0, -1], inv[-1, -1]])
     pair = dict(inv=d, inv_hl=d * hl, inv_tr=d * tr, down=[hl * tl * d, hr * d, tl * d, tr * hr * d])
-    pair["low"] = [w[0] + hr * hl * d * w[1], tl * d * w[1]]
-    pair["high"] = [hr * d * w[2], w[3] + tl * tr * d * w[2]]
     for k in pair:
         pair[k] = [float(t) for t in pair[k]] if isinstance(pair[k], list) else float(pair[k])
     p = dict(hl=hl + hr * hl * tl * d, hr=hr * hr * d, tl=tl * tl * d, tr=tr + tl * tr * hr * d)
@@ -69,74 +68,48 @@
     return lax.rem(lax.axis_index(name), 2)
 
 
-def pack_body(s, f, fy, one, two, yone, ytwo, lo, hi, sem):
+def pack_body(s, f, fy, one, two, yone, ytwo, sem):
     core, odd = parity("gx"), parity("gy")
-    copies = [
-        pltpu.make_async_copy(fy.at[:, :, 0:SUB, :], lo, sem.at[0]),
-        pltpu.make_async_copy(fy.at[:, :, NJ - SUB : NJ, :], hi, sem.at[1]),
-    ]
-    for c in copies:
-        c.start()
-
-    def faces(right, left):
-        moves = [
-            pltpu.make_async_copy(s.at[:, NI - 3 : NI], right.at[:, 0:3], sem.at[2]),
-            pltpu.make_async_copy(f.at[:, NI - 1 : NI], right.at[:, 3:4], sem.at[3]),
-            pltpu.make_async_copy(s.at[:, 0:3], left.at[:, 0:3], sem.at[4]),
-            pltpu.make_async_copy(f.at[:, 0:1], left.at[:, 3:4], sem.at[5]),
-        ]
-        for c in moves:
+
+    def move(right, left, top, bottom):
+        pairs = (
+            (s.at[:, NI - 3 : NI], right.at[:, 0:3]),
+            (f.at[:, NI - 1 : NI], right.at[:, 3:4]),
+            (s.at[:, 0:3], left.at[:, 0:3]),
+            (f.at[:, 0:1], left.at[:, 3:4]),
+            (fy.at[:, :, NJ - SUB : NJ, :], top),
+            (fy.at[:, :, 0:SUB, :], bottom),
+        )
+        copies = [pltpu.make_async_copy(x, y, sem.at[k]) for k, (x, y) in enumerate(pairs)]
+        for c in copies:
             c.start()
-        for c in moves:
+        for c in copies:
             c.wait()
 
-    def rows(top, bottom):
-        for v in range(NV):
-            for i in range(NI):
-                part = pl.ds(4 * (i % 2), 4)
-                top[v, i // 2, part, :] = hi[v, i, 4:8, :]
-                bottom[v, i // 2, part, :] = lo[v, i, 0:4, :]
-
-    @pl.when(core == 0)
-    def _():
-        faces(one, two)
-
-    @pl.when(core == 1)
-    def _():
-        faces(two, one)
-
-    for c in copies:
-        c.wait()
-
-    @pl.when(odd == 0)
-    def _():
-        rows(yone, ytwo)
-
-    @pl.when(odd == 1)
-    def _():
-        rows(ytwo, yone)
+    for c, x in enumerate(((one, two), (two, one))):
+        for o, y in enumerate(((yone, ytwo), (ytwo, yone))):
+
+            @pl.when((core == c) & (odd == o))
+            def _(x=x, y=y):
+                move(*x, *y)
 
 
 def pack(state, flux_x, flux_y):
     x_out = jax.ShapeDtypeStruct((NV, 4, NJ, NK), F32)
-    y_out = jax.ShapeDtypeStruct((NV, NI // 2, SUB, NK), F32)
+    y_out = jax.ShapeDtypeStruct((NV, NI, SUB, NK), F32)
     return pl.pallas_call(
         pack_body,
         out_shape=(x_out, x_out, y_out, y_out),
         in_specs=[pl.BlockSpec(memory_space=pltpu.HBM)] * 3,
         out_specs=(pl.BlockSpec(memory_space=pltpu.VMEM),) * 4,
-        scratch_shapes=[
-            pltpu.VMEM((NV, NI, SUB, NK), F32),
-            pltpu.VMEM((NV, NI, SUB, NK), F32),
-            pltpu.SemaphoreType.DMA((6,)),
-        ],
+        scratch_shapes=[pltpu.SemaphoreType.DMA((6,))],
         compiler_params=pltpu.CompilerParams(vmem_limit_bytes=8 << 20),
         cost_estimate=pl.CostEstimate(flops=0, bytes_accessed=2 << 20, transcendentals=0),
         name="pack",
     )(*in_hbm(state, flux_x, flux_y))
 
 
-def own_body(gap_hbm, s_hbm, f_hbm, inner, outer, mine, send, gap, s, f, own, gap_sem, sem):
+def own_body(gap_hbm, s_hbm, f_hbm, inner_hbm, outer, mine, send, inner, gap, s, f, own, gap_sem, inner_sem, sem):
     gap_load = pltpu.make_async_copy(gap_hbm, gap, gap_sem)
     gap_load.start()
     loads = [
@@ -182,6 +155,8 @@
         inner[C_MG + k] = m[k] * g32[k]
         outer[C_LEFT + k] = left[k]
         outer[C_RIGHT + k] = right[k]
+    inner_store = pltpu.make_async_copy(inner, inner_hbm, inner_sem)
+    inner_store.start()
     vh = [wh[k] * g32[k] for k in range(NI)]
     vt = [wt[k] * g32[k] for k in range(NI)]
 
@@ -208,17 +183,16 @@
     inv = CS["inv"]
     fh = [flux_weight(0, j) for j in range(NI)]
     ft = [flux_weight(NI - 1, j) for j in range(NI)]
-    fh[0] = fh[0] + float(inv[0, 0]) * first
+    fh[0] = (fh[0] - BETA) + float(inv[0, 0]) * first
     ft[0] = ft[0] + float(inv[NI - 1, 0]) * first
     fh[NI - 1] = fh[NI - 1] + float(inv[0, NI - 1]) * last
-    ft[NI - 1] = ft[NI - 1] + float(inv[NI - 1, NI - 1]) * last
+    ft[NI - 1] = (ft[NI - 1] + BETA) + float(inv[NI - 1, NI - 1]) * last
 
     for i in range(NI):
         own[i] = spread(vh, i)
         own[NI + i] = spread(vt, i)
 
-    s_in, f_in = (NI - 3) * (1 - core), (NI - 1) * (1 - core)
-    s_out, f_out = (NI - 3) * core, (NI - 1) * core
+    s_in, s_out = (NI - 3) * (1 - core), (NI - 3) * core
     for v in range(NV):
         for c in loads[v]:
             c.wait()
@@ -230,10 +204,10 @@
                     a, z = s[v, i, rows, :], f[v, i, rows, :]
                     terms = (own[i] * a, own[NI + i] * a, fh[i] * z, ft[i] * z)
                     sums = [t if o is None else o + t for o, t in zip(sums, terms)]
-                faces = [s[v, s_in + k, rows, :] for k in range(3)] + [f[v, f_in, rows, :]]
-                faces += [s[v, s_out + k, rows, :] for k in range(3)] + [f[v, f_out, rows, :]]
+                faces = [s[v, s_in + k, rows, :] for k in range(3)] + [s[v, s_out + k, rows, :] for k in range(3)]
                 for k, t in enumerate(sums + faces):
                     out[pl.ds((NV * k + v) * HALF + SUB * r, SUB), :] = t
+    inner_store.wait()
 
 
 def own_share(gap, state, flux_x):
@@ -245,12 +219,14 @@
         own_body,
         out_shape=(coef, coef_far, values, values),
         in_specs=[hbm, hbm, hbm],
-        out_specs=(vmem,) * 4,
+        out_specs=(hbm, vmem, vmem, vmem),
         scratch_shapes=[
+            pltpu.VMEM((2 * NI, SUB, NK), F32),
             pltpu.SMEM((NI,), F32),
             pltpu.VMEM((NV, NI, NJ, NK), F32),
             pltpu.VMEM((NV, NI, NJ, NK), F32),
             pltpu.VMEM((2 * NI, SUB, NK), F32),
+            pltpu.SemaphoreType.DMA,
             pltpu.SemaphoreType.DMA,
             pltpu.SemaphoreType.DMA((2, NV)),
         ],
@@ -291,21 +267,20 @@
     stores = [pltpu.make_async_copy(out.at[b], out_hbm.at[b], sem.at[r]) for r, b in enumerate(blocks)]
     for r in range(HALF // SUB):
         at = WIDE * SUB * r
-        out[pl.ds(at + 12 * NV, SUB, stride=WIDE), :] = packed
+        out[pl.ds(at + VALUES * NV, SUB, stride=WIDE), :] = packed
         for v in range(NV):
-            a, b = zip(*(both(pl.ds((NV * e + v) * HALF + SUB * r, SUB)) for e in range(12)))
+            a, b = zip(*(both(pl.ds((NV * e + v) * HALF + SUB * r, SUB)) for e in range(VALUES)))
             ha, ta, hb, tb = a[0], a[1], b[0], b[1]
             for q in range(3):
                 ha, ta = ha + ca[4 + q] * b[4 + q], ta + ca[7 + q] * b[4 + q]
                 hb, tb = hb + cb[4 + q] * a[4 + q], tb + cb[7 + q] * a[4 + q]
             head = (hb + hlb * ta) * inv
             tail = (ta + tra * hb) * inv
-            da, ea = a[2] + flux_weight(0, NI) * b[7], a[3] + flux_weight(NI - 1, NI) * b[7]
-            db, eb = b[2] + flux_weight(0, -1) * a[7], b[3] + flux_weight(NI - 1, -1) * a[7]
+            da, ea, db, eb = a[2], a[3], b[2], b[3]
             dhead = k["inv"] * db + k["inv_hl"] * ea
             dtail = k["inv"] * ea + k["inv_tr"] * db
             values = [ha + hra * head, tb + tlb * tail, da + float(CS["hr"]) * dhead, eb + float(CS["tl"]) * dtail]
-            values += list(a[8:12]) + list(b[8:12])
+            values += list(a[7:10]) + list(b[7:10])
             for e, t in enumerate(values):
                 out[pl.ds(at + NV * e + v, SUB, stride=WIDE), :] = t
             for e, t in enumerate((head, tail, dhead, dtail)):
@@ -334,7 +309,7 @@
 
 def join_body(x, out_hbm, out, coef, sem):
     for r in range(PAIRS // SUB):
-        packed = x[pl.ds(WIDE * SUB * r + 12 * NV, SUB, stride=WIDE), :]
+        packed = x[pl.ds(WIDE * SUB * r + VALUES * NV, SUB, stride=WIDE), :]
         for k in range(16):
             coef[pl.ds(PAIRS * k + SUB * r, SUB), :] = jnp.broadcast_to(packed[:, k : k + 1], (SUB, NK))
 
@@ -350,16 +325,12 @@
         h, t, dh, dt = (value(p, k) for k in range(4))
         if p:
             for q in range(3):
-                z = value(p - 1, 8 + q)
+                z = value(p - 1, 7 + q)
                 h, t = h + row(p, 4 + q) * z, t + row(p, 7 + q) * z
-            z = value(p - 1, 11)
-            dh, dt = dh + c["low"][0] * z, dt + c["low"][1] * z
         if p < PAIRS - 1:
             for q in range(3):
                 z = value(p + 1, 4 + q)
                 h, t = h + row(p, 10 + q) * z, t + row(p, 13 + q) * z
-            z = value(p + 1, 7)
-            dh, dt = dh + c["high"][0] * z, dt + c["high"][1] * z
         head_f.append(h)
         tail_f.append(t)
         head_d.append(dh)
@@ -426,22 +397,21 @@
     )(x)
 
 
-def far_body(outer, two, own, send):
+def far_body(outer, two, own, other):
     core = parity("gx")
-    wd = jnp.where(core == 0, flux_weight(NI - 1, -1), flux_weight(0, NI)).astype(F32)
-    for out, half in ((own, core), (send, 1 - core)):
+    for out, half in ((own, core), (other, 1 - core)):
         for v in range(NV):
             for r in range(HALF // SUB):
                 rows = pl.ds(pl.multiple_of(HALF * half + SUB * r, SUB), SUB)
-                a = [two[v, k, rows, :] for k in range(4)]
-                f = outer[C_FAR] * a[0] + outer[C_FAR + 1] * a[1] + outer[C_FAR + 2] * a[2]
-                for k, t in enumerate((f, wd * a[3])):
-                    out[pl.ds((NV * k + v) * HALF + SUB * r, SUB), :] = t
+                a = [two[v, k, rows, :] for k in range(3)]
+                out[pl.ds(v * HALF + SUB * r, SUB), :] = (
+                    outer[C_FAR] * a[0] + outer[C_FAR + 1] * a[1] + outer[C_FAR + 2] * a[2]
+                )
 
 
 def far(outer, two):
     vmem = pl.BlockSpec(memory_space=pltpu.VMEM)
-    out = jax.ShapeDtypeStruct((2 * NV * HALF, NK), F32)
+    out = jax.ShapeDtypeStruct((NV * HALF, NK), F32)
     return pl.pallas_call(
         far_body,
         out_shape=(out, out),
@@ -453,44 +423,47 @@
     )(outer, two)
 
 
-def split_body(z, mids, far_own, far_got, own, send):
+def split_body(z, mids, far_own, far_other, own, send):
     is0 = parity("gx") == 0
     c = CS["pair"]
     down = [jnp.broadcast_to(mids[pl.ds(4 * NV * HALF + k, 1), :], (SUB, NK)) for k in range(7)]
+    head_far, tail_far = jnp.where(is0, down[4], down[5]), jnp.where(is0, down[5], down[6])
     for r in range(HALF // SUB):
         for v in range(NV):
             lf, rf, ld, rd = (z[pl.ds(ROWS * SUB * r + NV * k + v, SUB, stride=ROWS), :] for k in range(4))
             head, tail, dhead, dtail = (mids[pl.ds((NV * k + v) * HALF + SUB * r, SUB), :] for k in range(4))
-            fo, do = (far_own[pl.ds((NV * k + v) * HALF + SUB * r, SUB), :] for k in range(2))
-            fg, dg = (far_got[pl.ds((NV * k + v) * HALF + SUB * r, SUB), :] for k in range(2))
-            fa, da = jnp.where(is0, fo, fg), jnp.where(is0, do, dg)
-            fb, db = jnp.where(is0, fg, fo), jnp.where(is0, dg, do)
-            head = (head + down[4] * fa + down[5] * fb) + down[0] * lf + down[1] * rf
-            tail = (tail + down[5] * fa + down[6] * fb) + down[2] * lf + down[3] * rf
-            dhead = (dhead + c["inv_hl"] * da + c["inv"] * db) + c["down"][0] * ld + c["down"][1] * rd
-            dtail = (dtail + c["inv"] * da + c["inv_tr"] * db) + c["down"][2] * ld + c["down"][3] * rd
+            part = pl.ds(v * HALF + SUB * r, SUB)
+            w = far_own[part, :]
+            head = (head + head_far * w) + down[0] * lf + down[1] * rf
+            tail = (tail + tail_far * w) + down[2] * lf + down[3] * rf
+            dhead = dhead + c["down"][0] * ld + c["down"][1] * rd
+            dtail = dtail + c["down"][2] * ld + c["down"][3] * rd
             a, b = (lf, head, ld, dhead), (tail, rf, dtail, rd)
             for k in range(4):
                 rows = pl.ds((NV * k + v) * HALF + SUB * r, SUB)
                 own[rows, :] = jnp.where(is0, a[k], b[k])
                 send[rows, :] = jnp.where(is0, b[k], a[k])
-
-
-def split(z, mids, far_own, far_got):
+            send[pl.ds((4 * NV + v) * HALF + SUB * r, SUB), :] = far_other[part, :]
+
+
+def split(z, mids, far_own, far_other):
     vmem = pl.BlockSpec(memory_space=pltpu.VMEM)
-    out = jax.ShapeDtypeStruct((4 * NV * HALF, NK), F32)
+    own = jax.ShapeDtypeStruct((4 * NV * HALF, NK), F32)
+    send = jax.ShapeDtypeStruct((5 * NV * HALF, NK), F32)
     return pl.pallas_call(
         split_body,
-        out_shape=(out, out),
+        out_shape=(own, send),
         in_specs=[vmem] * 4,
         out_specs=(vmem,) * 2,
         compiler_params=pltpu.CompilerParams(vmem_limit_bytes=8 << 20),
         cost_estimate=pl.CostEstimate(flops=1 << 20, bytes_accessed=1 << 20, transcendentals=0),
         name="split",
-    )(z, mids, far_own, far_got)
-
-
-def block_body(inner, s_hbm, f_hbm, fy_hbm, one, two, yone, ytwo, mx, my, base, mxb, s, f, fy, pad, sem):
+    )(z, mids, far_own, far_other)
+
+
+def block_body(inner_hbm, s_hbm, f_hbm, fy_hbm, one, two, yone, ytwo, mx, my, base, mxb, inner, s, f, fy, pad, inner_sem, sem):
+    inner_load = pltpu.make_async_copy(inner_hbm, inner, inner_sem)
+    inner_load.start()
     moves = ((fy_hbm, fy), (s_hbm, s), (f_hbm, f))
     for v in range(NV):
         for k, (h, t) in enumerate(moves):
@@ -506,6 +479,8 @@
         mxb[i] = jnp.broadcast_to(mxt[:, i : i + 1], (NJ, NK))
         pad[NI + i, 0:NJ, :] = jnp.broadcast_to(myt[:, i : i + 1], (NJ, NK))
 
+    inner_load.wait()
+
     @pl.loop(0, NV)
     def _(v):
         for k, (h, t) in enumerate(moves):
@@ -513,10 +488,9 @@
         for i in range(NI):
             for q in range(NJ // SUB):
                 pad[i, pl.ds(SUB + SUB * q, SUB), :] = fy[v, i, pl.ds(SUB * q, SUB), :]
-            part = pl.ds(4 * (i % 2), 4)
-            a, b = yone[v, i // 2, part, :], ytwo[v, i // 2, part, :]
-            pad[i, SUB - 4 : SUB, :] = jnp.where(even, b, a)
-            pad[i, SUB + NJ : SUB + NJ + 4, :] = jnp.where(even, a, b)
+            a, b = yone[v, i], ytwo[v, i]
+            pad[i, 0:SUB, :] = jnp.where(even, b, a)
+            pad[i, SUB + NJ : SUB + NJ + SUB, :] = jnp.where(even, a, b)
 
         for q in range(NJ // SUB):
             rows = pl.ds(SUB * q, SUB)
@@ -538,7 +512,8 @@
                 ye.append(y - inner[C_C + i] * ye[-1] if i else y)
                 u = fl[i + 2] - fl[i]
                 us.append(u)
-                r = float(RHO * CS["m"][i]) * u
+                r = fl[2] if i == 0 else -fl[NI - 1] if i == NI - 1 else u
+                r = float(RHO * CS["m"][i]) * r
                 if i == 0:
                     r = r + (first * float(CS["m"][i])) * fl[1]
                 if i == NI - 1:
@@ -565,24 +540,35 @@
             jax.ShapeDtypeStruct((NV, NI, NJ, NK), F32),
             jax.ShapeDtypeStruct((NI, NJ, NK), F32),
         ),
-        in_specs=[vmem] + [hbm] * 3 + [vmem] * 6,
+        in_specs=[hbm] * 4 + [vmem] * 6,
         out_specs=(vmem, vmem),
-        scratch_shapes=[pltpu.VMEM((NV, NI, NJ, NK), F32)] * 3
-        + [pltpu.VMEM((2 * NI, SUB + NJ + SUB, NK), F32), pltpu.SemaphoreType.DMA((3, NV))],
+        scratch_shapes=[pltpu.VMEM((2 * NI, SUB, NK), F32)]
+        + [pltpu.VMEM((NV, NI, NJ, NK), F32)] * 3
+        + [pltpu.VMEM((2 * NI, SUB + NJ + SUB, NK), F32), pltpu.SemaphoreType.DMA, pltpu.SemaphoreType.DMA((3, NV))],
         compiler_params=pltpu.CompilerParams(vmem_limit_bytes=16 << 20),
         cost_estimate=pl.CostEstimate(flops=1 << 25, bytes_accessed=64 << 20, transcendentals=0),
         name="block",
-    )(inner, *in_hbm(state, flux_x, flux_y), one, two, yone, ytwo, mx, my)
-
-
-def finish_body(outer, base, mxb, own, got, out_hbm, out, sem):
+    )(*in_hbm(inner, state, flux_x, flux_y), one, two, yone, ytwo, mx, my)
+
+
+def finish_body(outer, base, mxb, own, got, mids, far_other, out_hbm, out, sem):
     core = parity("gx")
+    is0 = core == 0
+    hl_inv, inv, tr_inv = (jnp.broadcast_to(mids[pl.ds(4 * NV * HALF + k, 1), :], (SUB, NK)) for k in (4, 5, 6))
+    zero = jnp.zeros((SUB, NK), F32)
+    own_far = (jnp.where(is0, zero, inv), jnp.where(is0, inv, zero))
+    got_far = (jnp.where(is0, zero, tr_inv), jnp.where(is0, hl_inv, zero))
     stores = [pltpu.make_async_copy(out.at[v], out_hbm.at[v], sem.at[v]) for v in range(NV)]
     for v in range(NV):
-        for z, half in ((own, core), (got, 1 - core)):
+        for z, half, far_w, far_z, far_at in (
+            (own, core, own_far, got, 4 * NV),
+            (got, 1 - core, got_far, far_other, 0),
+        ):
             for r in range(HALF // SUB):
                 rows = pl.ds(pl.multiple_of(HALF * half + SUB * r, SUB), SUB)
                 lf, rf, ld, rd = (z[pl.ds((NV * k + v) * HALF + SUB * r, SUB), :] for k in range(4))
+                w = far_z[pl.ds((far_at + v) * HALF + SUB * r, SUB), :]
+                lf, rf = lf + far_w[0] * w, rf + far_w[1] * w
                 for i in range(NI):
                     d = float(CS["left"][i]) * ld + float(CS["right"][i]) * rd
                     e = outer[C_LEFT + i] * lf + outer[C_RIGHT + i] * rf
@@ -592,17 +578,17 @@
         c.wait()
 
 
-def finish(outer, base, mxb, own, got):
+def finish(outer, base, mxb, own, got, mids, far_other):
     return pl.pallas_call(
         finish_body,
         out_shape=jax.ShapeDtypeStruct((NV, NI, NJ, NK), F32),
-        in_specs=[pl.BlockSpec(memory_space=pltpu.VMEM)] * 5,
+        in_specs=[pl.BlockSpec(memory_space=pltpu.VMEM)] * 7,
         out_specs=pl.BlockSpec(memory_space=pltpu.HBM),
         scratch_shapes=[pltpu.VMEM((NV, NI, NJ, NK), F32), pltpu.SemaphoreType.DMA((NV,))],
         compiler_params=pltpu.CompilerParams(vmem_limit_bytes=12 << 20),
         cost_estimate=pl.CostEstimate(flops=1 << 22, bytes_accessed=3 << 20, transcendentals=0),
         name="finish",
-    )(outer, base, mxb, own, got)
+    )(outer, base, mxb, own, got, mids, far_other)
 
 
 def exchange(x, rows):
@@ -632,12 +618,12 @@
     outside = join(ends)
     outside, one = lax.optimization_barrier((outside, one))
     two, yone, ytwo = lax.optimization_barrier((two, yone, ytwo))
-    far_own, far_send = far(outer, two)
-    far_got = lax.ppermute(far_send, "gx", pair_in)
+    far_own, far_other = far(outer, two)
     base, mxb = block(inner, state, flux_x, flux_y, one, two, yone, ytwo, metric_x, metric_y)
-    outside, base, mxb, far_got = lax.optimization_barrier((exchange(outside, ROWS), base, mxb, far_got))
-    own, send = split(outside, mids, far_own, far_got)
-    return finish(outer, base, mxb, own, lax.ppermute(send, "gx", pair_in))
+    outside, base, mxb, far_own = lax.optimization_barrier((exchange(outside, ROWS), base, mxb, far_own))
+    own, send = split(outside, mids, far_own, far_other)
+    got = lax.ppermute(send, "gx", pair_in)
+    return finish(outer, base, mxb, own, got, mids, far_other)
 
 
 def solution(mesh):

time: 42 us -> 41.4 us (0.986)
  starting transfers between devices: 26.9 us -> 23 us
  waiting for transfers between devices: 4.89 us -> 6.83 us
  Pallas kernels: 9.67 us -> 11 us
    ppermute x2 -> x0, starting transfers between devices: 6.89 us -> none  [the longest x1 3.98 us: per_device(): return finish(outer, base, mxb, own, lax.ppermute(send, 'gx', pair_in))]
    ppermute x1 -> x2, starting transfers between devices: 1.5 us -> 4.82 us  [per_device(): got = lax.ppermute(send, 'gx', pair_in)]
    all_to_all x2, waiting for transfers between devices: 3.74 us -> 5.74 us  [exchange(): lax.all_to_all(x.reshape(PAIRS, rows, NK), 'gx', 0, 0, tiled=True, axis_i...]
    ppermute x2 -> x0, waiting for transfers between devices: 1.03 us -> none  [the longest x1 1.03 us: per_device(): return finish(outer, base, mxb, own, lax.ppermute(send, 'gx', pair_in))]
    ppermute x1 -> x2, waiting for transfers between devices: 0.12 us -> 1.08 us  [per_device(): got = lax.ppermute(send, 'gx', pair_in)]
    pallas_call x1, Pallas kernels: 3.12 us -> 3.98 us  [block(): pl.pallas_call(block_body, out_shape=(jax.ShapeDtypeStruct((NV, NI, NJ, N...]
    pallas_call x1, Pallas kernels: 1.38 us -> 2.16 us  [pack(): pl.pallas_call(pack_body, out_shape=(x_out, x_out, y_out, y_out), in_spec...]
  transfers between devices with their start and end apart: 9 -> 8, of which waited for: 4 -> 3; matrix products, arithmetic and copies ran while one was open for 0% -> 0% of each run, Pallas kernels for 13% -> 17%
where the time goes in v6:
time: 41.4 us; the launch traced here: 41 us
  starting transfers between devices  23 us (56%)
  Pallas kernels  11 us (27%)
  waiting for transfers between devices  6.83 us (16%)
    all_to_all x2, starting transfers between devices, exchange(): lax.all_to_all(x.reshape(PAIRS, rows, NK), 'gx', 0, 0, tiled=True, axis_i...  10.4 us
    all_to_all x2, waiting for transfers between devices, exchange(): lax.all_to_all(x.reshape(PAIRS, rows, NK), 'gx', 0, 0, tiled=True, axis_i...  5.74 us
    ppermute x2, starting transfers between devices, per_device(): got = lax.ppermute(send, 'gx', pair_in)  4.82 us
    pallas_call x1, Pallas kernels, block(): pl.pallas_call(block_body, out_shape=(jax.ShapeDtypeStruct((NV, NI, NJ, N...  3.98 us
    ppermute x1, starting transfers between devices, per_device(): two = lax.ppermute(send_two, 'gx', pair_out)  3.37 us
    ppermute x1, starting transfers between devices, per_device(): ytwo = lax.ppermute(ysend_two, 'gy', y_out)  2.23 us
    pallas_call x1, Pallas kernels, pack(): pl.pallas_call(pack_body, out_shape=(x_out, x_out, y_out, y_out), in_spec...  2.16 us
    pallas_call x1, Pallas kernels, own_share(): pl.pallas_call(own_body, out_shape=(coef, coef_far, values, values), in_s...  1.85 us
  transfers between devices with their start and end apart: 8, of which 3 were waited for; matrix products, arithmetic and copies ran while one was open for 0% of the time, Pallas kernels for 17%

profile of v6, /device:TPU:1, one launch (start us, length us, event | category | flops | bytes accessed | tf_op | source)
XLA Modules:
  0.0 41.0 jit_solution(15591090147780689284)
XLA Ops:
  0.0 1.8 %own_share.1 = (f32[32,8,128]{2,1,0:T(8,128)S(1)}, f32[35,8,128]{2,1,0:T(8,128)S(1)}, f32[816,128]{1,0:T(8,128)S(1)}, f32[816,128]{1,0:T(8,128)S(1)}) custom-call(f32[16]{0:T(128)} %gap_hbm.1, f32[5,16,32,128]{3,2,1,0:T(8,128)} %s_hbm.2, f32[5,16,32,128]{3,2,1,0:T(8,128)} %f_hbm.2), custom_call_target="tpu_custom_call" | custom-call | flops 16777216 | bytes 4194304 | tf_op jit(solution)/shard_map/own_share/pallas_call | solution.py:218
  1.9 1.5 %collective-permute-start = (f32[816,128]{1,0:T(8,128)S(1)}, f32[816,128]{1,0:T(8,128)S(1)}, u32[]{:S(2)}, u32[]{:S(2)}) collective-permute-start(f32[816,128]{1,0:T(8,128)S(1)} %get-tuple-element.47), channel_id=1, source_target_pairs={{0,4},{4,0},{8,12},{12,8},{16,20},{20,16},{24,28},{28,24},{32,36},... | collective-permute-start | bytes 1253384 | tf_op jit(solution)/shard_map/ppermute | solution.py:609
  3.4 2.2 %pack.1 = (f32[5,4,32,128]{3,2,1,0:T(8,128)}, f32[5,4,32,128]{3,2,1,0:T(8,128)S(1)}, f32[5,16,8,128]{3,2,1,0:T(8,128)S(1)}, f32[5,16,8,128]{3,2,1,0:T(8,128)S(1)}) custom-call(f32[5,16,32,128]{3,2,1,0:T(8,128)} %s_hbm.2, f32[5,16,32,128]{3,2,1,0:T(8,128)} %f_hbm.2, f32[5,16,32,128]{3,2,1,0:T(8,128)} %fy_hbm), custom_call_target="tpu_custom_call" | custom-call | bytes 2097152 | tf_op jit(solution)/shard_map/pack/pallas_call | solution.py:100
  5.5 0.0 collective-permute-done.got
  5.6 0.9 %pair.1 = (f32[896,128]{1,0:T(8,128)}, f32[328,128]{1,0:T(8,128)S(1)}) custom-call(f32[816,128]{1,0:T(8,128)S(1)} %get-tuple-element.45.mine, f32[816,128]{1,0:T(8,128)S(1)} %collective-permute-done.got), custom_call_target="tpu_custom_call" | custom-call | flops 1048576 | bytes 1048576 | tf_op jit(solution)/shard_map/pair/pallas_call | solution.py:295
  6.4 0.0 copy-start.1
  6.4 0.0 copy-start.2
  6.5 6.8 %all-to-all-start = ((f32[16,56,128]{2,1,0:T(8,128)}), f32[16,56,128]{2,1,0:T(8,128)S(1)}, u32[]{:S(2)}, u32[]{:S(2)}) async-start(f32[16,56,128]{2,1,0:T(8,128)} %bitcast), calls=%async_computation | async-start | bytes 917504 | tf_op jit(solution)/shard_map/all_to_all | solution.py:596
  13.3 0.4 collective-permute-start.1
  13.7 3.4 %collective-permute-start.2 = (f32[5,4,32,128]{3,2,1,0:T(8,128)S(1)}, f32[5,4,32,128]{3,2,1,0:T(8,128)S(1)}, u32[]{:S(2)}, u32[]{:S(2)}) collective-permute-start(f32[5,4,32,128]{3,2,1,0:T(8,128)S(1)} %get-tuple-element.66), channel_id=1, source_target_pairs={{4,8},{8,4},{12,16},{16,12},{20,24},{24,20},{28,32},{32,28},{36,40... | collective-permute-start | bytes 983048 | tf_op jit(solution)/shard_map/ppermute | solution.py:615
  17.1 1.7 %collective-permute-start.3 = (f32[5,16,8,128]{3,2,1,0:T(8,128)S(1)}, f32[5,16,8,128]{3,2,1,0:T(8,128)S(1)}, u32[]{:S(2)}, u32[]{:S(2)}) collective-permute-start(f32[5,16,8,128]{3,2,1,0:T(8,128)S(1)} %get-tuple-element.67), channel_id=1, source_target_pairs={{0,1},{1,0},{2,3},{3,2},{4,5},{5,4},{6,7},{7,6},{8,9},{9,8},{10,11... | collective-permute-start | bytes 983048 | tf_op jit(solution)/shard_map/ppermute | solution.py:616
  18.8 2.2 %collective-permute-start.4 = (f32[5,16,8,128]{3,2,1,0:T(8,128)S(1)}, f32[5,16,8,128]{3,2,1,0:T(8,128)S(1)}, u32[]{:S(2)}, u32[]{:S(2)}) collective-permute-start(f32[5,16,8,128]{3,2,1,0:T(8,128)S(1)} %get-tuple-element.68), channel_id=1, source_target_pairs={{0,3},{1,2},{2,1},{3,0},{4,7},{5,6},{6,5},{7,4},{8,11},{9,10},{10,... | collective-permute-start | bytes 983048 | tf_op jit(solution)/shard_map/ppermute | solution.py:617
  21.0 2.6 %all-to-all-done = f32[16,56,128]{2,1,0:T(8,128)S(1)} async-done(((f32[16,56,128]{2,1,0:T(8,128)}), f32[16,56,128]{2,1,0:T(8,128)S(1)}, u32[]{:S(2)}, u32[]{:S(2)}) %all-to-all-start) | async-done | bytes 458784 | tf_op jit(solution)/shard_map/all_to_all | solution.py:596
  23.7 0.9 %join.1 = f32[384,128]{1,0:T(8,128)} custom-call(f32[896,128]{1,0:T(8,128)S(1)} %bitcast.4), custom_call_target="tpu_custom_call" | custom-call | flops 1048576 | bytes 1048576 | tf_op jit(solution)/shard_map/join/pallas_call | solution.py:384
  24.6 0.0 collective-permute-done.1.one
  24.6 3.6 %all-to-all-start.1 = ((f32[16,24,128]{2,1,0:T(8,128)}), f32[16,24,128]{2,1,0:T(8,128)S(1)}, u32[]{:S(2)}, u32[]{:S(2)}) async-start(f32[16,24,128]{2,1,0:T(8,128)} %bitcast.2), calls=%async_computation.1 | async-start | bytes 393216 | tf_op jit(solution)/shard_map/all_to_all | solution.py:596
  28.2 0.0 collective-permute-done.3.yone
  28.2 0.0 collective-permute-done.4.ytwo
  28.3 4.0 %block.1 = (f32[5,16,32,128]{3,2,1,0:T(8,128)S(1)}, f32[16,32,128]{2,1,0:T(8,128)S(1)}) custom-call(f32[32,8,128]{2,1,0:T(8,128)} %copy-done, f32[5,16,32,128]{3,2,1,0:T(8,128)} %s_hbm.2, f32[5,16,32,128]{3,2,1,0:T(8,128)} %f_hbm.2, f32[5,16,32,128]{3,2,1,0:T(8,128)} %fy_hbm, f32[5,4,32,128]{3,2,1,0:T(8,128)S(1)} %collective-permute-done.1.one, ...), custom_call_target="tpu_custom_call" | custom-call | flops 33554432 | bytes 67108864 | tf_op jit(solution)/shard_map/block/pallas_call | solution.py:537
  32.3 3.1 %all-to-all-done.1 = f32[16,24,128]{2,1,0:T(8,128)S(1)} async-done(((f32[16,24,128]{2,1,0:T(8,128)}), f32[16,24,128]{2,1,0:T(8,128)S(1)}, u32[]{:S(2)}, u32[]{:S(2)}) %all-to-all-start.1) | async-done | bytes 196640 | tf_op jit(solution)/shard_map/all_to_all | solution.py:596
  35.4 0.1 split.1
  35.4 3.3 %collective-permute-start.5 = (f32[400,128]{1,0:T(8,128)S(1)}, f32[400,128]{1,0:T(8,128)S(1)}, u32[]{:S(2)}, u32[]{:S(2)}) collective-permute-start(f32[400,128]{1,0:T(8,128)S(1)} %get-tuple-element.82), channel_id=1, source_target_pairs={{0,4},{4,0},{8,12},{12,8},{16,20},{20,16},{24,28},{28,24},{32,36},... | collective-permute-start | bytes 614408 | tf_op jit(solution)/shard_map/ppermute | solution.py:625
  38.8 1.1 %collective-permute-done.5.got = f32[400,128]{1,0:T(8,128)S(1)} collective-permute-done((f32[400,128]{1,0:T(8,128)S(1)}, f32[400,128]{1,0:T(8,128)S(1)}, u32[]{:S(2)}, u32[]{:S(2)}) %collective-permute-start.5) | collective-permute-done | bytes 204832 | tf_op jit(solution)/shard_map/ppermute | solution.py:625
  39.8 1.2 %finish.1 = f32[5,16,32,128]{3,2,1,0:T(8,128)} custom-call(f32[35,8,128]{2,1,0:T(8,128)S(1)} %get-tuple-element.44.outer, f32[5,16,32,128]{3,2,1,0:T(8,128)S(1)} %get-tuple-element.75.base, f32[16,32,128]{2,1,0:T(8,128)S(1)} %get-tuple-element.76.mxb, f32[320,128]{1,0:T(8,128)S(1)} %get-tuple-element.81.own, f32[400,128]{1,0:T(8,128)S(1)} %collective-permute-done.5.got, ...), custom_call_target="tpu_custom_call" | custom-call | flops 4194304 | bytes 3145728 | tf_op jit(solution)/shard_map/finish/pallas_call | solution.py:582
  (6 shorter events, 0.0 us)
Async XLA Ops:
  1.9 3.7 %copy-start = (f32[32,8,128]{2,1,0:T(8,128)}, f32[32,8,128]{2,1,0:T(8,128)S(1)}, u32[]{:S(2)}) copy-start(f32[32,8,128]{2,1,0:T(8,128)S(1)} %get-tuple-element.64.inner_hbm) | copy-start | bytes 393220
  1.9 3.7 %collective-permute-start = (f32[816,128]{1,0:T(8,128)S(1)}, f32[816,128]{1,0:T(8,128)S(1)}, u32[]{:S(2)}, u32[]{:S(2)}) collective-permute-start(f32[816,128]{1,0:T(8,128)S(1)} %get-tuple-element.47), channel_id=1, source_target_pairs={{0,4},{4,0},{8,12},{12,8},{16,20},{20,16},{24,28},{28,24},{32,36},... | collective-permute-start | bytes 1253384 | tf_op jit(solution)/shard_map/ppermute | solution.py:609
  6.4 21.8 %copy-start.1 = (f32[16,32]{1,0:T(8,128)S(1)}, f32[16,32]{1,0:T(8,128)}, u32[]{:S(2)}) copy-start(f32[16,32]{1,0:T(8,128)} %mx.1) | copy-start | bytes 6148
  6.4 21.8 %copy-start.2 = (f32[16,32]{1,0:T(8,128)S(1)}, f32[16,32]{1,0:T(8,128)}, u32[]{:S(2)}) copy-start(f32[16,32]{1,0:T(8,128)} %my.1) | copy-start | bytes 6148
  6.5 17.2 %all-to-all-start = ((f32[16,56,128]{2,1,0:T(8,128)}), f32[16,56,128]{2,1,0:T(8,128)S(1)}, u32[]{:S(2)}, u32[]{:S(2)}) async-start(f32[16,56,128]{2,1,0:T(8,128)} %bitcast), calls=%async_computation | async-start | bytes 917504 | tf_op jit(solution)/shard_map/all_to_all | solution.py:596
  13.3 11.3 %collective-permute-start.1 = (f32[5,4,32,128]{3,2,1,0:T(8,128)}, f32[5,4,32,128]{3,2,1,0:T(8,128)S(1)}, u32[]{:S(2)}, u32[]{:S(2)}) collective-permute-start(f32[5,4,32,128]{3,2,1,0:T(8,128)} %get-tuple-element.62), channel_id=1, source_target_pairs={{0,4},{4,0},{8,12},{12,8},{16,20},{20,16},{24,28},{28,24},{32,36},... | collective-permute-start | bytes 983048 | tf_op jit(solution)/shard_map/ppermute | solution.py:614
  13.7 14.5 %collective-permute-start.2 = (f32[5,4,32,128]{3,2,1,0:T(8,128)S(1)}, f32[5,4,32,128]{3,2,1,0:T(8,128)S(1)}, u32[]{:S(2)}, u32[]{:S(2)}) collective-permute-start(f32[5,4,32,128]{3,2,1,0:T(8,128)S(1)} %get-tuple-element.66), channel_id=1, source_target_pairs={{4,8},{8,4},{12,16},{16,12},{20,24},{24,20},{28,32},{32,28},{36,40... | collective-permute-start | bytes 983048 | tf_op jit(solution)/shard_map/ppermute | solution.py:615
  17.1 11.1 %collective-permute-start.3 = (f32[5,16,8,128]{3,2,1,0:T(8,128)S(1)}, f32[5,16,8,128]{3,2,1,0:T(8,128)S(1)}, u32[]{:S(2)}, u32[]{:S(2)}) collective-permute-start(f32[5,16,8,128]{3,2,1,0:T(8,128)S(1)} %get-tuple-element.67), channel_id=1, source_target_pairs={{0,1},{1,0},{2,3},{3,2},{4,5},{5,4},{6,7},{7,6},{8,9},{9,8},{10,11... | collective-permute-start | bytes 983048 | tf_op jit(solution)/shard_map/ppermute | solution.py:616
  18.8 9.4 %collective-permute-start.4 = (f32[5,16,8,128]{3,2,1,0:T(8,128)S(1)}, f32[5,16,8,128]{3,2,1,0:T(8,128)S(1)}, u32[]{:S(2)}, u32[]{:S(2)}) collective-permute-start(f32[5,16,8,128]{3,2,1,0:T(8,128)S(1)} %get-tuple-element.68), channel_id=1, source_target_pairs={{0,3},{1,2},{2,1},{3,0},{4,7},{5,6},{6,5},{7,4},{8,11},{9,10},{10,... | collective-permute-start | bytes 983048 | tf_op jit(solution)/shard_map/ppermute | solution.py:617
  24.6 10.8 %all-to-all-start.1 = ((f32[16,24,128]{2,1,0:T(8,128)}), f32[16,24,128]{2,1,0:T(8,128)S(1)}, u32[]{:S(2)}, u32[]{:S(2)}) async-start(f32[16,24,128]{2,1,0:T(8,128)} %bitcast.2), calls=%async_computation.1 | async-start | bytes 393216 | tf_op jit(solution)/shard_map/all_to_all | solution.py:596
  35.4 4.4 %collective-permute-start.5 = (f32[400,128]{1,0:T(8,128)S(1)}, f32[400,128]{1,0:T(8,128)S(1)}, u32[]{:S(2)}, u32[]{:S(2)}) collective-permute-start(f32[400,128]{1,0:T(8,128)S(1)} %get-tuple-element.82), channel_id=1, source_target_pairs={{0,4},{4,0},{8,12},{12,8},{16,20},{20,16},{24,28},{28,24},{32,36},... | collective-permute-start | bytes 614408 | tf_op jit(solution)/shard_map/ppermute | solution.py:625

commit v7 on v6

--- a/solution.py
+++ b/solution.py
@@ -68,41 +68,67 @@
     return lax.rem(lax.axis_index(name), 2)
 
 
-def pack_body(s, f, fy, one, two, yone, ytwo, sem):
+def pack_body(s, f, fy, one, two, yone, ytwo, lo, hi, sem):
     core, odd = parity("gx"), parity("gy")
-
-    def move(right, left, top, bottom):
-        pairs = (
-            (s.at[:, NI - 3 : NI], right.at[:, 0:3]),
-            (f.at[:, NI - 1 : NI], right.at[:, 3:4]),
-            (s.at[:, 0:3], left.at[:, 0:3]),
-            (f.at[:, 0:1], left.at[:, 3:4]),
-            (fy.at[:, :, NJ - SUB : NJ, :], top),
-            (fy.at[:, :, 0:SUB, :], bottom),
-        )
-        copies = [pltpu.make_async_copy(x, y, sem.at[k]) for k, (x, y) in enumerate(pairs)]
-        for c in copies:
+    copies = [
+        pltpu.make_async_copy(fy.at[:, :, 0:SUB, :], lo, sem.at[0]),
+        pltpu.make_async_copy(fy.at[:, :, NJ - SUB : NJ, :], hi, sem.at[1]),
+    ]
+    for c in copies:
+        c.start()
+
+    def faces(right, left):
+        moves = [
+            pltpu.make_async_copy(s.at[:, NI - 3 : NI], right.at[:, 0:3], sem.at[2]),
+            pltpu.make_async_copy(f.at[:, NI - 1 : NI], right.at[:, 3:4], sem.at[3]),
+            pltpu.make_async_copy(s.at[:, 0:3], left.at[:, 0:3], sem.at[4]),
+            pltpu.make_async_copy(f.at[:, 0:1], left.at[:, 3:4], sem.at[5]),
+        ]
+        for c in moves:
             c.start()
-        for c in copies:
+        for c in moves:
             c.wait()
 
-    for c, x in enumerate(((one, two), (two, one))):
-        for o, y in enumerate(((yone, ytwo), (ytwo, yone))):
-
-            @pl.when((core == c) & (odd == o))
-            def _(x=x, y=y):
-                move(*x, *y)
+    def rows(top, bottom):
+        for v in range(NV):
+            for i in range(NI):
+                part = pl.ds(4 * (i % 2), 4)
+                top[v, i // 2, part, :] = hi[v, i, 4:8, :]
+                bottom[v, i // 2, part, :] = lo[v, i, 0:4, :]
+
+    @pl.when(core == 0)
+    def _():
+        faces(one, two)
+
+    @pl.when(core == 1)
+    def _():
+        faces(two, one)
+
+    for c in copies:
+        c.wait()
+
+    @pl.when(odd == 0)
+    def _():
+        rows(yone, ytwo)
+
+    @pl.when(odd == 1)
+    def _():
+        rows(ytwo, yone)
 
 
 def pack(state, flux_x, flux_y):
     x_out = jax.ShapeDtypeStruct((NV, 4, NJ, NK), F32)
-    y_out = jax.ShapeDtypeStruct((NV, NI, SUB, NK), F32)
+    y_out = jax.ShapeDtypeStruct((NV, NI // 2, SUB, NK), F32)
     return pl.pallas_call(
         pack_body,
         out_shape=(x_out, x_out, y_out, y_out),
         in_specs=[pl.BlockSpec(memory_space=pltpu.HBM)] * 3,
         out_specs=(pl.BlockSpec(memory_space=pltpu.VMEM),) * 4,
-        scratch_shapes=[pltpu.SemaphoreType.DMA((6,))],
+        scratch_shapes=[
+            pltpu.VMEM((NV, NI, SUB, NK), F32),
+            pltpu.VMEM((NV, NI, SUB, NK), F32),
+            pltpu.SemaphoreType.DMA((6,)),
+        ],
         compiler_params=pltpu.CompilerParams(vmem_limit_bytes=8 << 20),
         cost_estimate=pl.CostEstimate(flops=0, bytes_accessed=2 << 20, transcendentals=0),
         name="pack",
@@ -488,9 +514,10 @@
         for i in range(NI):
             for q in range(NJ // SUB):
                 pad[i, pl.ds(SUB + SUB * q, SUB), :] = fy[v, i, pl.ds(SUB * q, SUB), :]
-            a, b = yone[v, i], ytwo[v, i]
-            pad[i, 0:SUB, :] = jnp.where(even, b, a)
-            pad[i, SUB + NJ : SUB + NJ + SUB, :] = jnp.where(even, a, b)
+            part = pl.ds(4 * (i % 2), 4)
+            a, b = yone[v, i // 2, part, :], ytwo[v, i // 2, part, :]
+            pad[i, SUB - 4 : SUB, :] = jnp.where(even, b, a)
+            pad[i, SUB + NJ : SUB + NJ + 4, :] = jnp.where(even, a, b)
 
         for q in range(NJ // SUB):
             rows = pl.ds(SUB * q, SUB)
@@ -546,7 +573,7 @@
         + [pltpu.VMEM((NV, NI, NJ, NK), F32)] * 3
         + [pltpu.VMEM((2 * NI, SUB + NJ + SUB, NK), F32), pltpu.SemaphoreType.DMA, pltpu.SemaphoreType.DMA((3, NV))],
         compiler_params=pltpu.CompilerParams(vmem_limit_bytes=16 << 20),
-        cost_estimate=pl.CostEstimate(flops=1 << 25, bytes_accessed=64 << 20, transcendentals=0),
+        cost_estimate=pl.CostEstimate(flops=1 << 30, bytes_accessed=64 << 20, transcendentals=0),
         name="block",
     )(*in_hbm(inner, state, flux_x, flux_y), one, two, yone, ytwo, mx, my)
 

time: 41.4 us -> 41 us (level)
  starting transfers between devices: 23 us -> 24 us
  waiting for transfers between devices: 6.83 us -> 6.08 us
  Pallas kernels: 11 us -> 10.3 us
    pallas_call x1, Pallas kernels: 2.16 us -> 1.38 us  [pack(): pl.pallas_call(pack_body, out_shape=(x_out, x_out, y_out, y_out), in_spec...]
    all_to_all x2, waiting for transfers between devices: 5.74 us -> 4.99 us  [exchange(): lax.all_to_all(x.reshape(PAIRS, rows, NK), 'gx', 0, 0, tiled=True, axis_i...]
    all_to_all x2, starting transfers between devices: 10.4 us -> 11.1 us  [exchange(): lax.all_to_all(x.reshape(PAIRS, rows, NK), 'gx', 0, 0, tiled=True, axis_i...]
  transfers between devices with their start and end apart: 8 -> 8, of which waited for: 3 -> 3; matrix products, arithmetic and copies ran while one was open for 0% -> 0% of each run, Pallas kernels for 17% -> 16%
where the time goes in v7:
time: 41 us; the launch traced here: 40.6 us
  starting transfers between devices  24 us (59%)
  Pallas kernels  10.3 us (25%)
  waiting for transfers between devices  6.08 us (15%)
    all_to_all x2, starting transfers between devices, exchange(): lax.all_to_all(x.reshape(PAIRS, rows, NK), 'gx', 0, 0, tiled=True, axis_i...  11.1 us
    all_to_all x2, waiting for transfers between devices, exchange(): lax.all_to_all(x.reshape(PAIRS, rows, NK), 'gx', 0, 0, tiled=True, axis_i...  4.99 us
    ppermute x2, starting transfers between devices, per_device(): got = lax.ppermute(send, 'gx', pair_in)  4.83 us
    pallas_call x1, Pallas kernels, block(): pl.pallas_call(block_body, out_shape=(jax.ShapeDtypeStruct((NV, NI, NJ, N...  4.01 us
    ppermute x1, starting transfers between devices, per_device(): two = lax.ppermute(send_two, 'gx', pair_out)  3.37 us
    ppermute x1, starting transfers between devices, per_device(): ytwo = lax.ppermute(ysend_two, 'gy', y_out)  2.24 us
    pallas_call x1, Pallas kernels, own_share(): pl.pallas_call(own_body, out_shape=(coef, coef_far, values, values), in_s...  1.85 us
    ppermute x1, starting transfers between devices, per_device(): yone = lax.ppermute(ysend_one, 'gy', y_in)  1.72 us
  transfers between devices with their start and end apart: 8, of which 3 were waited for; matrix products, arithmetic and copies ran while one was open for 0% of the time, Pallas kernels for 16%

profile of v7, /device:TPU:1, one launch (start us, length us, event | category | flops | bytes accessed | tf_op | source)
XLA Modules:
  0.0 40.6 jit_solution(12982913744821913734)
XLA Ops:
  0.0 1.8 %own_share.1 = (f32[32,8,128]{2,1,0:T(8,128)S(1)}, f32[35,8,128]{2,1,0:T(8,128)S(1)}, f32[816,128]{1,0:T(8,128)S(1)}, f32[816,128]{1,0:T(8,128)S(1)}) custom-call(f32[16]{0:T(128)} %gap_hbm.1, f32[5,16,32,128]{3,2,1,0:T(8,128)} %s_hbm.2, f32[5,16,32,128]{3,2,1,0:T(8,128)} %f_hbm.2), custom_call_target="tpu_custom_call" | custom-call | flops 16777216 | bytes 4194304 | tf_op jit(solution)/shard_map/own_share/pallas_call | solution.py:244
  1.9 1.5 %collective-permute-start = (f32[816,128]{1,0:T(8,128)S(1)}, f32[816,128]{1,0:T(8,128)S(1)}, u32[]{:S(2)}, u32[]{:S(2)}) collective-permute-start(f32[816,128]{1,0:T(8,128)S(1)} %get-tuple-element.47), channel_id=1, source_target_pairs={{0,4},{4,0},{8,12},{12,8},{16,20},{20,16},{24,28},{28,24},{32,36},... | collective-permute-start | bytes 1253384 | tf_op jit(solution)/shard_map/ppermute | solution.py:636
  3.4 1.4 %pack.1 = (f32[5,4,32,128]{3,2,1,0:T(8,128)S(1)}, f32[5,4,32,128]{3,2,1,0:T(8,128)S(1)}, f32[5,8,8,128]{3,2,1,0:T(8,128)S(1)}, f32[5,8,8,128]{3,2,1,0:T(8,128)S(1)}) custom-call(f32[5,16,32,128]{3,2,1,0:T(8,128)} %s_hbm.2, f32[5,16,32,128]{3,2,1,0:T(8,128)} %f_hbm.2, f32[5,16,32,128]{3,2,1,0:T(8,128)} %fy_hbm), custom_call_target="tpu_custom_call" | custom-call | bytes 2097152 | tf_op jit(solution)/shard_map/pack/pallas_call | solution.py:122
  4.8 0.0 collective-permute-done.got
  4.8 0.9 %pair.1 = (f32[896,128]{1,0:T(8,128)}, f32[328,128]{1,0:T(8,128)S(1)}) custom-call(f32[816,128]{1,0:T(8,128)S(1)} %get-tuple-element.45.mine, f32[816,128]{1,0:T(8,128)S(1)} %collective-permute-done.got), custom_call_target="tpu_custom_call" | custom-call | flops 1048576 | bytes 1048576 | tf_op jit(solution)/shard_map/pair/pallas_call | solution.py:321
  5.6 0.0 copy-start.1
  5.7 0.0 copy-start.2
  5.7 6.8 %all-to-all-start = ((f32[16,56,128]{2,1,0:T(8,128)}), f32[16,56,128]{2,1,0:T(8,128)S(1)}, u32[]{:S(2)}, u32[]{:S(2)}) async-start(f32[16,56,128]{2,1,0:T(8,128)} %bitcast), calls=%async_computation | async-start | bytes 917504 | tf_op jit(solution)/shard_map/all_to_all | solution.py:623
  12.5 0.7 %collective-permute-start.1 = (f32[5,4,32,128]{3,2,1,0:T(8,128)S(1)}, f32[5,4,32,128]{3,2,1,0:T(8,128)S(1)}, u32[]{:S(2)}, u32[]{:S(2)}) collective-permute-start(f32[5,4,32,128]{3,2,1,0:T(8,128)S(1)} %get-tuple-element.62), channel_id=1, source_target_pairs={{0,4},{4,0},{8,12},{12,8},{16,20},{20,16},{24,28},{28,24},{32,36},... | collective-permute-start | bytes 983048 | tf_op jit(solution)/shard_map/ppermute | solution.py:641
  13.2 3.4 %collective-permute-start.2 = (f32[5,4,32,128]{3,2,1,0:T(8,128)S(1)}, f32[5,4,32,128]{3,2,1,0:T(8,128)S(1)}, u32[]{:S(2)}, u32[]{:S(2)}) collective-permute-start(f32[5,4,32,128]{3,2,1,0:T(8,128)S(1)} %get-tuple-element.66), channel_id=1, source_target_pairs={{4,8},{8,4},{12,16},{16,12},{20,24},{24,20},{28,32},{32,28},{36,40... | collective-permute-start | bytes 983048 | tf_op jit(solution)/shard_map/ppermute | solution.py:642
  16.6 1.7 %collective-permute-start.3 = (f32[5,8,8,128]{3,2,1,0:T(8,128)S(1)}, f32[5,8,8,128]{3,2,1,0:T(8,128)S(1)}, u32[]{:S(2)}, u32[]{:S(2)}) collective-permute-start(f32[5,8,8,128]{3,2,1,0:T(8,128)S(1)} %get-tuple-element.67), channel_id=1, source_target_pairs={{0,1},{1,0},{2,3},{3,2},{4,5},{5,4},{6,7},{7,6},{8,9},{9,8},{10,11... | collective-permute-start | bytes 491528 | tf_op jit(solution)/shard_map/ppermute | solution.py:643
  18.3 2.2 %collective-permute-start.4 = (f32[5,8,8,128]{3,2,1,0:T(8,128)S(1)}, f32[5,8,8,128]{3,2,1,0:T(8,128)S(1)}, u32[]{:S(2)}, u32[]{:S(2)}) collective-permute-start(f32[5,8,8,128]{3,2,1,0:T(8,128)S(1)} %get-tuple-element.68), channel_id=1, source_target_pairs={{0,3},{1,2},{2,1},{3,0},{4,7},{5,6},{6,5},{7,4},{8,11},{9,10},{10,... | collective-permute-start | bytes 491528 | tf_op jit(solution)/shard_map/ppermute | solution.py:644
  20.6 1.9 %all-to-all-done = f32[16,56,128]{2,1,0:T(8,128)S(1)} async-done(((f32[16,56,128]{2,1,0:T(8,128)}), f32[16,56,128]{2,1,0:T(8,128)S(1)}, u32[]{:S(2)}, u32[]{:S(2)}) %all-to-all-start) | async-done | bytes 458784 | tf_op jit(solution)/shard_map/all_to_all | solution.py:623
  22.5 0.9 %join.1 = f32[384,128]{1,0:T(8,128)} custom-call(f32[896,128]{1,0:T(8,128)S(1)} %bitcast.4), custom_call_target="tpu_custom_call" | custom-call | flops 1048576 | bytes 1048576 | tf_op jit(solution)/shard_map/join/pallas_call | solution.py:410
  23.4 0.0 collective-permute-done.1.one
  23.4 4.3 %all-to-all-start.1 = ((f32[16,24,128]{2,1,0:T(8,128)}), f32[16,24,128]{2,1,0:T(8,128)S(1)}, u32[]{:S(2)}, u32[]{:S(2)}) async-start(f32[16,24,128]{2,1,0:T(8,128)} %bitcast.2), calls=%async_computation.1 | async-start | bytes 393216 | tf_op jit(solution)/shard_map/all_to_all | solution.py:623
  27.7 0.0 collective-permute-done.3.yone
  27.7 0.0 collective-permute-done.4.ytwo
  27.8 4.0 %block.1 = (f32[5,16,32,128]{3,2,1,0:T(8,128)S(1)}, f32[16,32,128]{2,1,0:T(8,128)S(1)}) custom-call(f32[32,8,128]{2,1,0:T(8,128)} %copy-done, f32[5,16,32,128]{3,2,1,0:T(8,128)} %s_hbm.2, f32[5,16,32,128]{3,2,1,0:T(8,128)} %f_hbm.2, f32[5,16,32,128]{3,2,1,0:T(8,128)} %fy_hbm, f32[5,4,32,128]{3,2,1,0:T(8,128)S(1)} %collective-permute-done.1.one, ...), custom_call_target="tpu_custom_call" | custom-call | flops 1073741824 | bytes 67108864 | tf_op jit(solution)/shard_map/block/pallas_call | solution.py:564
  31.8 3.1 %all-to-all-done.1 = f32[16,24,128]{2,1,0:T(8,128)S(1)} async-done(((f32[16,24,128]{2,1,0:T(8,128)}), f32[16,24,128]{2,1,0:T(8,128)S(1)}, u32[]{:S(2)}, u32[]{:S(2)}) %all-to-all-start.1) | async-done | bytes 196640 | tf_op jit(solution)/shard_map/all_to_all | solution.py:623
  34.9 0.1 split.1
  35.0 3.3 %collective-permute-start.5 = (f32[400,128]{1,0:T(8,128)S(1)}, f32[400,128]{1,0:T(8,128)S(1)}, u32[]{:S(2)}, u32[]{:S(2)}) collective-permute-start(f32[400,128]{1,0:T(8,128)S(1)} %get-tuple-element.82), channel_id=1, source_target_pairs={{0,4},{4,0},{8,12},{12,8},{16,20},{20,16},{24,28},{28,24},{32,36},... | collective-permute-start | bytes 614408 | tf_op jit(solution)/shard_map/ppermute | solution.py:652
  38.3 1.1 %collective-permute-done.5.got = f32[400,128]{1,0:T(8,128)S(1)} collective-permute-done((f32[400,128]{1,0:T(8,128)S(1)}, f32[400,128]{1,0:T(8,128)S(1)}, u32[]{:S(2)}, u32[]{:S(2)}) %collective-permute-start.5) | collective-permute-done | bytes 204832 | tf_op jit(solution)/shard_map/ppermute | solution.py:652
  39.4 1.2 %finish.1 = f32[5,16,32,128]{3,2,1,0:T(8,128)} custom-call(f32[35,8,128]{2,1,0:T(8,128)S(1)} %get-tuple-element.44.outer, f32[5,16,32,128]{3,2,1,0:T(8,128)S(1)} %get-tuple-element.75.base, f32[16,32,128]{2,1,0:T(8,128)S(1)} %get-tuple-element.76.mxb, f32[320,128]{1,0:T(8,128)S(1)} %get-tuple-element.81.own, f32[400,128]{1,0:T(8,128)S(1)} %collective-permute-done.5.got, ...), custom_call_target="tpu_custom_call" | custom-call | flops 4194304 | bytes 3145728 | tf_op jit(solution)/shard_map/finish/pallas_call | solution.py:609
  (6 shorter events, 0.0 us)
Async XLA Ops:
  1.9 2.9 %copy-start = (f32[32,8,128]{2,1,0:T(8,128)}, f32[32,8,128]{2,1,0:T(8,128)S(1)}, u32[]{:S(2)}) copy-start(f32[32,8,128]{2,1,0:T(8,128)S(1)} %get-tuple-element.64.inner_hbm) | copy-start | bytes 393220
  1.9 2.9 %collective-permute-start = (f32[816,128]{1,0:T(8,128)S(1)}, f32[816,128]{1,0:T(8,128)S(1)}, u32[]{:S(2)}, u32[]{:S(2)}) collective-permute-start(f32[816,128]{1,0:T(8,128)S(1)} %get-tuple-element.47), channel_id=1, source_target_pairs={{0,4},{4,0},{8,12},{12,8},{16,20},{20,16},{24,28},{28,24},{32,36},... | collective-permute-start | bytes 1253384 | tf_op jit(solution)/shard_map/ppermute | solution.py:636
  5.6 22.1 %copy-start.1 = (f32[16,32]{1,0:T(8,128)S(1)}, f32[16,32]{1,0:T(8,128)}, u32[]{:S(2)}) copy-start(f32[16,32]{1,0:T(8,128)} %mx.1) | copy-start | bytes 6148
  5.7 22.1 %copy-start.2 = (f32[16,32]{1,0:T(8,128)S(1)}, f32[16,32]{1,0:T(8,128)}, u32[]{:S(2)}) copy-start(f32[16,32]{1,0:T(8,128)} %my.1) | copy-start | bytes 6148
  5.7 16.8 %all-to-all-start = ((f32[16,56,128]{2,1,0:T(8,128)}), f32[16,56,128]{2,1,0:T(8,128)S(1)}, u32[]{:S(2)}, u32[]{:S(2)}) async-start(f32[16,56,128]{2,1,0:T(8,128)} %bitcast), calls=%async_computation | async-start | bytes 917504 | tf_op jit(solution)/shard_map/all_to_all | solution.py:623
  12.5 10.9 %collective-permute-start.1 = (f32[5,4,32,128]{3,2,1,0:T(8,128)S(1)}, f32[5,4,32,128]{3,2,1,0:T(8,128)S(1)}, u32[]{:S(2)}, u32[]{:S(2)}) collective-permute-start(f32[5,4,32,128]{3,2,1,0:T(8,128)S(1)} %get-tuple-element.62), channel_id=1, source_target_pairs={{0,4},{4,0},{8,12},{12,8},{16,20},{20,16},{24,28},{28,24},{32,36},... | collective-permute-start | bytes 983048 | tf_op jit(solution)/shard_map/ppermute | solution.py:641
  13.2 14.5 %collective-permute-start.2 = (f32[5,4,32,128]{3,2,1,0:T(8,128)S(1)}, f32[5,4,32,128]{3,2,1,0:T(8,128)S(1)}, u32[]{:S(2)}, u32[]{:S(2)}) collective-permute-start(f32[5,4,32,128]{3,2,1,0:T(8,128)S(1)} %get-tuple-element.66), channel_id=1, source_target_pairs={{4,8},{8,4},{12,16},{16,12},{20,24},{24,20},{28,32},{32,28},{36,40... | collective-permute-start | bytes 983048 | tf_op jit(solution)/shard_map/ppermute | solution.py:642
  16.6 11.1 %collective-permute-start.3 = (f32[5,8,8,128]{3,2,1,0:T(8,128)S(1)}, f32[5,8,8,128]{3,2,1,0:T(8,128)S(1)}, u32[]{:S(2)}, u32[]{:S(2)}) collective-permute-start(f32[5,8,8,128]{3,2,1,0:T(8,128)S(1)} %get-tuple-element.67), channel_id=1, source_target_pairs={{0,1},{1,0},{2,3},{3,2},{4,5},{5,4},{6,7},{7,6},{8,9},{9,8},{10,11... | collective-permute-start | bytes 491528 | tf_op jit(solution)/shard_map/ppermute | solution.py:643
  18.3 9.4 %collective-permute-start.4 = (f32[5,8,8,128]{3,2,1,0:T(8,128)S(1)}, f32[5,8,8,128]{3,2,1,0:T(8,128)S(1)}, u32[]{:S(2)}, u32[]{:S(2)}) collective-permute-start(f32[5,8,8,128]{3,2,1,0:T(8,128)S(1)} %get-tuple-element.68), channel_id=1, source_target_pairs={{0,3},{1,2},{2,1},{3,0},{4,7},{5,6},{6,5},{7,4},{8,11},{9,10},{10,... | collective-permute-start | bytes 491528 | tf_op jit(solution)/shard_map/ppermute | solution.py:644
  23.4 11.5 %all-to-all-start.1 = ((f32[16,24,128]{2,1,0:T(8,128)}), f32[16,24,128]{2,1,0:T(8,128)S(1)}, u32[]{:S(2)}, u32[]{:S(2)}) async-start(f32[16,24,128]{2,1,0:T(8,128)} %bitcast.2), calls=%async_computation.1 | async-start | bytes 393216 | tf_op jit(solution)/shard_map/all_to_all | solution.py:623
  35.0 4.4 %collective-permute-start.5 = (f32[400,128]{1,0:T(8,128)S(1)}, f32[400,128]{1,0:T(8,128)S(1)}, u32[]{:S(2)}, u32[]{:S(2)}) collective-permute-start(f32[400,128]{1,0:T(8,128)S(1)} %get-tuple-element.82), channel_id=1, source_target_pairs={{0,4},{4,0},{8,12},{12,8},{16,20},{20,16},{24,28},{28,24},{32,36},... | collective-permute-start | bytes 614408 | tf_op jit(solution)/shard_map/ppermute | solution.py:652

commit v8 on v7

--- a/solution.py
+++ b/solution.py
@@ -135,7 +135,7 @@
     )(*in_hbm(state, flux_x, flux_y))
 
 
-def own_body(gap_hbm, s_hbm, f_hbm, inner_hbm, outer, mine, send, inner, gap, s, f, own, gap_sem, inner_sem, sem):
+def own_body(gap_hbm, s_hbm, f_hbm, inner, outer, mine, send, gap, s, f, own, gap_sem, sem):
     gap_load = pltpu.make_async_copy(gap_hbm, gap, gap_sem)
     gap_load.start()
     loads = [
@@ -181,8 +181,6 @@
         inner[C_MG + k] = m[k] * g32[k]
         outer[C_LEFT + k] = left[k]
         outer[C_RIGHT + k] = right[k]
-    inner_store = pltpu.make_async_copy(inner, inner_hbm, inner_sem)
-    inner_store.start()
     vh = [wh[k] * g32[k] for k in range(NI)]
     vt = [wt[k] * g32[k] for k in range(NI)]
 
@@ -233,7 +231,6 @@
                 faces = [s[v, s_in + k, rows, :] for k in range(3)] + [s[v, s_out + k, rows, :] for k in range(3)]
                 for k, t in enumerate(sums + faces):
                     out[pl.ds((NV * k + v) * HALF + SUB * r, SUB), :] = t
-    inner_store.wait()
 
 
 def own_share(gap, state, flux_x):
@@ -245,14 +242,12 @@
         own_body,
         out_shape=(coef, coef_far, values, values),
         in_specs=[hbm, hbm, hbm],
-        out_specs=(hbm, vmem, vmem, vmem),
+        out_specs=(vmem,) * 4,
         scratch_shapes=[
-            pltpu.VMEM((2 * NI, SUB, NK), F32),
             pltpu.SMEM((NI,), F32),
             pltpu.VMEM((NV, NI, NJ, NK), F32),
             pltpu.VMEM((NV, NI, NJ, NK), F32),
             pltpu.VMEM((2 * NI, SUB, NK), F32),
-            pltpu.SemaphoreType.DMA,
             pltpu.SemaphoreType.DMA,
             pltpu.SemaphoreType.DMA((2, NV)),
         ],
@@ -487,9 +482,7 @@
     )(z, mids, far_own, far_other)
 
 
-def block_body(inner_hbm, s_hbm, f_hbm, fy_hbm, one, two, yone, ytwo, mx, my, base, mxb, inner, s, f, fy, pad, inner_sem, sem):
-    inner_load = pltpu.make_async_copy(inner_hbm, inner, inner_sem)
-    inner_load.start()
+def block_body(inner, s_hbm, f_hbm, fy_hbm, one, two, yone, ytwo, mx, my, base, mxb, s, f, fy, pad, sem):
     moves = ((fy_hbm, fy), (s_hbm, s), (f_hbm, f))
     for v in range(NV):
         for k, (h, t) in enumerate(moves):
@@ -504,8 +497,6 @@
     for i in range(NI):
         mxb[i] = jnp.broadcast_to(mxt[:, i : i + 1], (NJ, NK))
         pad[NI + i, 0:NJ, :] = jnp.broadcast_to(myt[:, i : i + 1], (NJ, NK))
-
-    inner_load.wait()
 
     @pl.loop(0, NV)
     def _(v):
@@ -567,15 +558,14 @@
             jax.ShapeDtypeStruct((NV, NI, NJ, NK), F32),
             jax.ShapeDtypeStruct((NI, NJ, NK), F32),
         ),
-        in_specs=[hbm] * 4 + [vmem] * 6,
+        in_specs=[vmem] + [hbm] * 3 + [vmem] * 6,
         out_specs=(vmem, vmem),
-        scratch_shapes=[pltpu.VMEM((2 * NI, SUB, NK), F32)]
-        + [pltpu.VMEM((NV, NI, NJ, NK), F32)] * 3
-        + [pltpu.VMEM((2 * NI, SUB + NJ + SUB, NK), F32), pltpu.SemaphoreType.DMA, pltpu.SemaphoreType.DMA((3, NV))],
+        scratch_shapes=[pltpu.VMEM((NV, NI, NJ, NK), F32)] * 3
+        + [pltpu.VMEM((2 * NI, SUB + NJ + SUB, NK), F32), pltpu.SemaphoreType.DMA((3, NV))],
         compiler_params=pltpu.CompilerParams(vmem_limit_bytes=16 << 20),
         cost_estimate=pl.CostEstimate(flops=1 << 30, bytes_accessed=64 << 20, transcendentals=0),
         name="block",
-    )(*in_hbm(inner, state, flux_x, flux_y), one, two, yone, ytwo, mx, my)
+    )(inner, *in_hbm(state, flux_x, flux_y), one, two, yone, ytwo, mx, my)
 
 
 def finish_body(outer, base, mxb, own, got, mids, far_other, out_hbm, out, sem):

time: 41 us -> 40.9 us (level)
  Pallas kernels: 10.3 us -> 9.52 us
  waiting for transfers between devices: 6.08 us -> 6.83 us
    pallas_call x1, Pallas kernels: 4.01 us -> 3.25 us  [block(): pl.pallas_call(block_body, out_shape=(jax.ShapeDtypeStruct((NV, NI, NJ, N...]
    all_to_all x2, waiting for transfers between devices: 4.99 us -> 5.73 us  [exchange(): lax.all_to_all(x.reshape(PAIRS, rows, NK), 'gx', 0, 0, tiled=True, axis_i...]
  transfers between devices with their start and end apart: 8 -> 8, of which waited for: 3 -> 3; matrix products, arithmetic and copies ran while one was open for 0% -> 0% of each run, Pallas kernels for 16% -> 14%
where the time goes in v8:
time: 40.9 us; the launch traced here: 40.5 us
  starting transfers between devices  24 us (59%)
  Pallas kernels  9.52 us (23%)
  waiting for transfers between devices  6.83 us (17%)
    all_to_all x2, starting transfers between devices, exchange(): lax.all_to_all(x.reshape(PAIRS, rows, NK), 'gx', 0, 0, tiled=True, axis_i...  11.2 us
    all_to_all x2, waiting for transfers between devices, exchange(): lax.all_to_all(x.reshape(PAIRS, rows, NK), 'gx', 0, 0, tiled=True, axis_i...  5.73 us
    ppermute x2, starting transfers between devices, per_device(): got = lax.ppermute(send, 'gx', pair_in)  4.82 us
    ppermute x1, starting transfers between devices, per_device(): two = lax.ppermute(send_two, 'gx', pair_out)  3.37 us
    pallas_call x1, Pallas kernels, block(): pl.pallas_call(block_body, out_shape=(jax.ShapeDtypeStruct((NV, NI, NJ, N...  3.25 us
    ppermute x1, starting transfers between devices, per_device(): ytwo = lax.ppermute(ysend_two, 'gy', y_out)  2.24 us
    pallas_call x1, Pallas kernels, own_share(): pl.pallas_call(own_body, out_shape=(coef, coef_far, values, values), in_s...  1.84 us
    ppermute x1, starting transfers between devices, per_device(): yone = lax.ppermute(ysend_one, 'gy', y_in)  1.72 us
  transfers between devices with their start and end apart: 8, of which 3 were waited for; matrix products, arithmetic and copies ran while one was open for 0% of the time, Pallas kernels for 14%

profile of v8, /device:TPU:1, one launch (start us, length us, event | category | flops | bytes accessed | tf_op | source)
XLA Modules:
  0.0 40.5 jit_solution(13498262616767799252)
XLA Ops:
  0.0 1.8 %own_share.1 = (f32[32,8,128]{2,1,0:T(8,128)S(1)}, f32[35,8,128]{2,1,0:T(8,128)S(1)}, f32[816,128]{1,0:T(8,128)S(1)}, f32[816,128]{1,0:T(8,128)S(1)}) custom-call(f32[16]{0:T(128)} %gap_hbm.1, f32[5,16,32,128]{3,2,1,0:T(8,128)} %s_hbm.2, f32[5,16,32,128]{3,2,1,0:T(8,128)} %f_hbm.2), custom_call_target="tpu_custom_call" | custom-call | flops 16777216 | bytes 4194304 | tf_op jit(solution)/shard_map/own_share/pallas_call | solution.py:241
  1.8 1.5 %collective-permute-start = (f32[816,128]{1,0:T(8,128)S(1)}, f32[816,128]{1,0:T(8,128)S(1)}, u32[]{:S(2)}, u32[]{:S(2)}) collective-permute-start(f32[816,128]{1,0:T(8,128)S(1)} %get-tuple-element.47), channel_id=1, source_target_pairs={{0,4},{4,0},{8,12},{12,8},{16,20},{20,16},{24,28},{28,24},{32,36},... | collective-permute-start | bytes 1253384 | tf_op jit(solution)/shard_map/ppermute | solution.py:626
  3.3 1.4 %pack.1 = (f32[5,4,32,128]{3,2,1,0:T(8,128)S(1)}, f32[5,4,32,128]{3,2,1,0:T(8,128)S(1)}, f32[5,8,8,128]{3,2,1,0:T(8,128)S(1)}, f32[5,8,8,128]{3,2,1,0:T(8,128)S(1)}) custom-call(f32[5,16,32,128]{3,2,1,0:T(8,128)} %s_hbm.2, f32[5,16,32,128]{3,2,1,0:T(8,128)} %f_hbm.2, f32[5,16,32,128]{3,2,1,0:T(8,128)} %fy_hbm), custom_call_target="tpu_custom_call" | custom-call | bytes 2097152 | tf_op jit(solution)/shard_map/pack/pallas_call | solution.py:122
  4.7 0.0 collective-permute-done.got
  4.7 0.9 %pair.1 = (f32[896,128]{1,0:T(8,128)}, f32[328,128]{1,0:T(8,128)S(1)}) custom-call(f32[816,128]{1,0:T(8,128)S(1)} %get-tuple-element.45.mine, f32[816,128]{1,0:T(8,128)S(1)} %collective-permute-done.got), custom_call_target="tpu_custom_call" | custom-call | flops 1048576 | bytes 1048576 | tf_op jit(solution)/shard_map/pair/pallas_call | solution.py:316
  5.6 0.0 copy-start
  5.6 0.0 copy-start.1
  5.6 6.8 %all-to-all-start = ((f32[16,56,128]{2,1,0:T(8,128)}), f32[16,56,128]{2,1,0:T(8,128)S(1)}, u32[]{:S(2)}, u32[]{:S(2)}) async-start(f32[16,56,128]{2,1,0:T(8,128)} %bitcast), calls=%async_computation | async-start | bytes 917504 | tf_op jit(solution)/shard_map/all_to_all | solution.py:613
  12.5 0.7 %collective-permute-start.1 = (f32[5,4,32,128]{3,2,1,0:T(8,128)S(1)}, f32[5,4,32,128]{3,2,1,0:T(8,128)S(1)}, u32[]{:S(2)}, u32[]{:S(2)}) collective-permute-start(f32[5,4,32,128]{3,2,1,0:T(8,128)S(1)} %get-tuple-element.62), channel_id=1, source_target_pairs={{0,4},{4,0},{8,12},{12,8},{16,20},{20,16},{24,28},{28,24},{32,36},... | collective-permute-start | bytes 983048 | tf_op jit(solution)/shard_map/ppermute | solution.py:631
  13.2 3.4 %collective-permute-start.2 = (f32[5,4,32,128]{3,2,1,0:T(8,128)S(1)}, f32[5,4,32,128]{3,2,1,0:T(8,128)S(1)}, u32[]{:S(2)}, u32[]{:S(2)}) collective-permute-start(f32[5,4,32,128]{3,2,1,0:T(8,128)S(1)} %get-tuple-element.66), channel_id=1, source_target_pairs={{4,8},{8,4},{12,16},{16,12},{20,24},{24,20},{28,32},{32,28},{36,40... | collective-permute-start | bytes 983048 | tf_op jit(solution)/shard_map/ppermute | solution.py:632
  16.6 1.7 %collective-permute-start.3 = (f32[5,8,8,128]{3,2,1,0:T(8,128)S(1)}, f32[5,8,8,128]{3,2,1,0:T(8,128)S(1)}, u32[]{:S(2)}, u32[]{:S(2)}) collective-permute-start(f32[5,8,8,128]{3,2,1,0:T(8,128)S(1)} %get-tuple-element.67), channel_id=1, source_target_pairs={{0,1},{1,0},{2,3},{3,2},{4,5},{5,4},{6,7},{7,6},{8,9},{9,8},{10,11... | collective-permute-start | bytes 491528 | tf_op jit(solution)/shard_map/ppermute | solution.py:633
  18.3 2.2 %collective-permute-start.4 = (f32[5,8,8,128]{3,2,1,0:T(8,128)S(1)}, f32[5,8,8,128]{3,2,1,0:T(8,128)S(1)}, u32[]{:S(2)}, u32[]{:S(2)}) collective-permute-start(f32[5,8,8,128]{3,2,1,0:T(8,128)S(1)} %get-tuple-element.68), channel_id=1, source_target_pairs={{0,3},{1,2},{2,1},{3,0},{4,7},{5,6},{6,5},{7,4},{8,11},{9,10},{10,... | collective-permute-start | bytes 491528 | tf_op jit(solution)/shard_map/ppermute | solution.py:634
  20.6 1.9 %all-to-all-done = f32[16,56,128]{2,1,0:T(8,128)S(1)} async-done(((f32[16,56,128]{2,1,0:T(8,128)}), f32[16,56,128]{2,1,0:T(8,128)S(1)}, u32[]{:S(2)}, u32[]{:S(2)}) %all-to-all-start) | async-done | bytes 458784 | tf_op jit(solution)/shard_map/all_to_all | solution.py:613
  22.4 0.9 %join.1 = f32[384,128]{1,0:T(8,128)} custom-call(f32[896,128]{1,0:T(8,128)S(1)} %bitcast.4), custom_call_target="tpu_custom_call" | custom-call | flops 1048576 | bytes 1048576 | tf_op jit(solution)/shard_map/join/pallas_call | solution.py:405
  23.4 0.0 collective-permute-done.1.one
  23.4 4.3 %all-to-all-start.1 = ((f32[16,24,128]{2,1,0:T(8,128)}), f32[16,24,128]{2,1,0:T(8,128)S(1)}, u32[]{:S(2)}, u32[]{:S(2)}) async-start(f32[16,24,128]{2,1,0:T(8,128)} %bitcast.2), calls=%async_computation.1 | async-start | bytes 393216 | tf_op jit(solution)/shard_map/all_to_all | solution.py:613
  27.7 0.0 collective-permute-done.3.yone
  27.7 0.0 collective-permute-done.4.ytwo
  27.8 3.2 %block.1 = (f32[5,16,32,128]{3,2,1,0:T(8,128)S(1)}, f32[16,32,128]{2,1,0:T(8,128)S(1)}) custom-call(f32[32,8,128]{2,1,0:T(8,128)S(1)} %get-tuple-element.64.inner, f32[5,16,32,128]{3,2,1,0:T(8,128)} %s_hbm.2, f32[5,16,32,128]{3,2,1,0:T(8,128)} %f_hbm.2, f32[5,16,32,128]{3,2,1,0:T(8,128)} %fy_hbm, f32[5,4,32,128]{3,2,1,0:T(8,128)S(1)} %collective-permute-done.1.one, ...), custom_call_target="tpu_custom_call" | custom-call | flops 1073741824 | bytes 67108864 | tf_op jit(solution)/shard_map/block/pallas_call | solution.py:555
  31.0 3.8 %all-to-all-done.1 = f32[16,24,128]{2,1,0:T(8,128)S(1)} async-done(((f32[16,24,128]{2,1,0:T(8,128)}), f32[16,24,128]{2,1,0:T(8,128)S(1)}, u32[]{:S(2)}, u32[]{:S(2)}) %all-to-all-start.1) | async-done | bytes 196640 | tf_op jit(solution)/shard_map/all_to_all | solution.py:613
  34.9 0.1 split.1
  34.9 3.3 %collective-permute-start.5 = (f32[400,128]{1,0:T(8,128)S(1)}, f32[400,128]{1,0:T(8,128)S(1)}, u32[]{:S(2)}, u32[]{:S(2)}) collective-permute-start(f32[400,128]{1,0:T(8,128)S(1)} %get-tuple-element.82), channel_id=1, source_target_pairs={{0,4},{4,0},{8,12},{12,8},{16,20},{20,16},{24,28},{28,24},{32,36},... | collective-permute-start | bytes 614408 | tf_op jit(solution)/shard_map/ppermute | solution.py:642
  38.3 1.1 %collective-permute-done.5.got = f32[400,128]{1,0:T(8,128)S(1)} collective-permute-done((f32[400,128]{1,0:T(8,128)S(1)}, f32[400,128]{1,0:T(8,128)S(1)}, u32[]{:S(2)}, u32[]{:S(2)}) %collective-permute-start.5) | collective-permute-done | bytes 204832 | tf_op jit(solution)/shard_map/ppermute | solution.py:642
  39.3 1.2 %finish.1 = f32[5,16,32,128]{3,2,1,0:T(8,128)} custom-call(f32[35,8,128]{2,1,0:T(8,128)S(1)} %get-tuple-element.44.outer, f32[5,16,32,128]{3,2,1,0:T(8,128)S(1)} %get-tuple-element.75.base, f32[16,32,128]{2,1,0:T(8,128)S(1)} %get-tuple-element.76.mxb, f32[320,128]{1,0:T(8,128)S(1)} %get-tuple-element.81.own, f32[400,128]{1,0:T(8,128)S(1)} %collective-permute-done.5.got, ...), custom_call_target="tpu_custom_call" | custom-call | flops 4194304 | bytes 3145728 | tf_op jit(solution)/shard_map/finish/pallas_call | solution.py:599
  (4 shorter events, 0.0 us)
Async XLA Ops:
  1.8 2.9 %collective-permute-start = (f32[816,128]{1,0:T(8,128)S(1)}, f32[816,128]{1,0:T(8,128)S(1)}, u32[]{:S(2)}, u32[]{:S(2)}) collective-permute-start(f32[816,128]{1,0:T(8,128)S(1)} %get-tuple-element.47), channel_id=1, source_target_pairs={{0,4},{4,0},{8,12},{12,8},{16,20},{20,16},{24,28},{28,24},{32,36},... | collective-permute-start | bytes 1253384 | tf_op jit(solution)/shard_map/ppermute | solution.py:626
  5.6 22.1 %copy-start = (f32[16,32]{1,0:T(8,128)S(1)}, f32[16,32]{1,0:T(8,128)}, u32[]{:S(2)}) copy-start(f32[16,32]{1,0:T(8,128)} %mx.1) | copy-start | bytes 6148
  5.6 22.1 %copy-start.1 = (f32[16,32]{1,0:T(8,128)S(1)}, f32[16,32]{1,0:T(8,128)}, u32[]{:S(2)}) copy-start(f32[16,32]{1,0:T(8,128)} %my.1) | copy-start | bytes 6148
  5.6 16.8 %all-to-all-start = ((f32[16,56,128]{2,1,0:T(8,128)}), f32[16,56,128]{2,1,0:T(8,128)S(1)}, u32[]{:S(2)}, u32[]{:S(2)}) async-start(f32[16,56,128]{2,1,0:T(8,128)} %bitcast), calls=%async_computation | async-start | bytes 917504 | tf_op jit(solution)/shard_map/all_to_all | solution.py:613
  12.5 10.9 %collective-permute-start.1 = (f32[5,4,32,128]{3,2,1,0:T(8,128)S(1)}, f32[5,4,32,128]{3,2,1,0:T(8,128)S(1)}, u32[]{:S(2)}, u32[]{:S(2)}) collective-permute-start(f32[5,4,32,128]{3,2,1,0:T(8,128)S(1)} %get-tuple-element.62), channel_id=1, source_target_pairs={{0,4},{4,0},{8,12},{12,8},{16,20},{20,16},{24,28},{28,24},{32,36},... | collective-permute-start | bytes 983048 | tf_op jit(solution)/shard_map/ppermute | solution.py:631
  13.2 14.5 %collective-permute-start.2 = (f32[5,4,32,128]{3,2,1,0:T(8,128)S(1)}, f32[5,4,32,128]{3,2,1,0:T(8,128)S(1)}, u32[]{:S(2)}, u32[]{:S(2)}) collective-permute-start(f32[5,4,32,128]{3,2,1,0:T(8,128)S(1)} %get-tuple-element.66), channel_id=1, source_target_pairs={{4,8},{8,4},{12,16},{16,12},{20,24},{24,20},{28,32},{32,28},{36,40... | collective-permute-start | bytes 983048 | tf_op jit(solution)/shard_map/ppermute | solution.py:632
  16.6 11.1 %collective-permute-start.3 = (f32[5,8,8,128]{3,2,1,0:T(8,128)S(1)}, f32[5,8,8,128]{3,2,1,0:T(8,128)S(1)}, u32[]{:S(2)}, u32[]{:S(2)}) collective-permute-start(f32[5,8,8,128]{3,2,1,0:T(8,128)S(1)} %get-tuple-element.67), channel_id=1, source_target_pairs={{0,1},{1,0},{2,3},{3,2},{4,5},{5,4},{6,7},{7,6},{8,9},{9,8},{10,11... | collective-permute-start | bytes 491528 | tf_op jit(solution)/shard_map/ppermute | solution.py:633
  18.3 9.4 %collective-permute-start.4 = (f32[5,8,8,128]{3,2,1,0:T(8,128)S(1)}, f32[5,8,8,128]{3,2,1,0:T(8,128)S(1)}, u32[]{:S(2)}, u32[]{:S(2)}) collective-permute-start(f32[5,8,8,128]{3,2,1,0:T(8,128)S(1)} %get-tuple-element.68), channel_id=1, source_target_pairs={{0,3},{1,2},{2,1},{3,0},{4,7},{5,6},{6,5},{7,4},{8,11},{9,10},{10,... | collective-permute-start | bytes 491528 | tf_op jit(solution)/shard_map/ppermute | solution.py:634
  23.4 11.5 %all-to-all-start.1 = ((f32[16,24,128]{2,1,0:T(8,128)}), f32[16,24,128]{2,1,0:T(8,128)S(1)}, u32[]{:S(2)}, u32[]{:S(2)}) async-start(f32[16,24,128]{2,1,0:T(8,128)} %bitcast.2), calls=%async_computation.1 | async-start | bytes 393216 | tf_op jit(solution)/shard_map/all_to_all | solution.py:613
  34.9 4.4 %collective-permute-start.5 = (f32[400,128]{1,0:T(8,128)S(1)}, f32[400,128]{1,0:T(8,128)S(1)}, u32[]{:S(2)}, u32[]{:S(2)}) collective-permute-start(f32[400,128]{1,0:T(8,128)S(1)} %get-tuple-element.82), channel_id=1, source_target_pairs={{0,4},{4,0},{8,12},{12,8},{16,20},{20,16},{24,28},{28,24},{32,36},... | collective-permute-start | bytes 614408 | tf_op jit(solution)/shard_map/ppermute | solution.py:642

commit v9 on v8

--- a/solution.py
+++ b/solution.py
@@ -482,34 +482,23 @@
     )(z, mids, far_own, far_other)
 
 
-def block_body(inner, s_hbm, f_hbm, fy_hbm, one, two, yone, ytwo, mx, my, base, mxb, s, f, fy, pad, sem):
-    moves = ((fy_hbm, fy), (s_hbm, s), (f_hbm, f))
+def block_body(inner, s_hbm, f_hbm, one, two, mx, base, mxb, s, f, sem):
+    moves = ((s_hbm, s), (f_hbm, f))
     for v in range(NV):
         for k, (h, t) in enumerate(moves):
             pltpu.make_async_copy(h.at[v], t.at[v], sem.at[k, v]).start()
     piece = lax.axis_index("gx")
     is0 = parity("gx") == 0
-    even = parity("gy") == 0
     first = jnp.where(piece == 0, 1.0 / 36.0, 0.0).astype(F32)
     last = jnp.where(piece == PIECES - 1, -1.0 / 36.0, 0.0).astype(F32)
     mxt = jnp.transpose(mx[...] * -0.5)
-    myt = jnp.transpose(my[...] * -0.5)
     for i in range(NI):
         mxb[i] = jnp.broadcast_to(mxt[:, i : i + 1], (NJ, NK))
-        pad[NI + i, 0:NJ, :] = jnp.broadcast_to(myt[:, i : i + 1], (NJ, NK))
 
     @pl.loop(0, NV)
     def _(v):
         for k, (h, t) in enumerate(moves):
             pltpu.make_async_copy(h.at[v], t.at[v], sem.at[k, v]).wait()
-        for i in range(NI):
-            for q in range(NJ // SUB):
-                pad[i, pl.ds(SUB + SUB * q, SUB), :] = fy[v, i, pl.ds(SUB * q, SUB), :]
-            part = pl.ds(4 * (i % 2), 4)
-            a, b = yone[v, i // 2, part, :], ytwo[v, i // 2, part, :]
-            pad[i, SUB - 4 : SUB, :] = jnp.where(even, b, a)
-            pad[i, SUB + NJ : SUB + NJ + 4, :] = jnp.where(even, a, b)
-
         for q in range(NJ // SUB):
             rows = pl.ds(SUB * q, SUB)
             a = [one[v, k, rows, :] for k in range(4)]
@@ -541,16 +530,11 @@
             for i in range(NI - 1, -1, -1):
                 xe = ye[i] if xe is None else ye[i] - inner[C_C + i] * xe
                 xd = yd[i] if xd is None else yd[i] - float(CS["c"][i]) * xd
-                at = SUB + SUB * q
-                dy = None
-                for k, w in enumerate(Y_WEIGHTS, start=1):
-                    t = w * (pad[i, pl.ds(at + k, SUB), :] - pad[i, pl.ds(at - k, SUB), :])
-                    dy = t if dy is None else dy + t
                 d = us[i] * (1.0 / 12.0) + xd
-                base[v, i, rows, :] = (st[i + 3] + xe) + (mxb[i, rows, :] * d + pad[NI + i, rows, :] * dy)
-
-
-def block(inner, state, flux_x, flux_y, one, two, yone, ytwo, mx, my):
+                base[v, i, rows, :] = (st[i + 3] + xe) + mxb[i, rows, :] * d
+
+
+def block(inner, state, flux_x, one, two, mx):
     vmem, hbm = pl.BlockSpec(memory_space=pltpu.VMEM), pl.BlockSpec(memory_space=pltpu.HBM)
     return pl.pallas_call(
         block_body,
@@ -558,14 +542,61 @@
             jax.ShapeDtypeStruct((NV, NI, NJ, NK), F32),
             jax.ShapeDtypeStruct((NI, NJ, NK), F32),
         ),
-        in_specs=[vmem] + [hbm] * 3 + [vmem] * 6,
+        in_specs=[vmem, hbm, hbm] + [vmem] * 3,
         out_specs=(vmem, vmem),
-        scratch_shapes=[pltpu.VMEM((NV, NI, NJ, NK), F32)] * 3
-        + [pltpu.VMEM((2 * NI, SUB + NJ + SUB, NK), F32), pltpu.SemaphoreType.DMA((3, NV))],
+        scratch_shapes=[pltpu.VMEM((NV, NI, NJ, NK), F32)] * 2 + [pltpu.SemaphoreType.DMA((2, NV))],
         compiler_params=pltpu.CompilerParams(vmem_limit_bytes=16 << 20),
-        cost_estimate=pl.CostEstimate(flops=1 << 30, bytes_accessed=64 << 20, transcendentals=0),
+        cost_estimate=pl.CostEstimate(flops=1 << 25, bytes_accessed=8 << 20, transcendentals=0),
         name="block",
-    )(inner, *in_hbm(state, flux_x, flux_y), one, two, yone, ytwo, mx, my)
+    )(inner, *in_hbm(state, flux_x), one, two, mx)
+
+
+def ydiff_body(base, fy_hbm, yone, ytwo, my, out, fy, myb, pad, sem):
+    for v in range(NV):
+        pltpu.make_async_copy(fy_hbm.at[v], fy.at[v], sem.at[v]).start()
+    even = parity("gy") == 0
+    myt = jnp.transpose(my[...] * -0.5)
+    for i in range(NI):
+        myb[i] = jnp.broadcast_to(myt[:, i : i + 1], (NJ, NK))
+
+    @pl.loop(0, NV)
+    def _(v):
+        pltpu.make_async_copy(fy_hbm.at[v], fy.at[v], sem.at[v]).wait()
+        for i in range(NI):
+            for q in range(NJ // SUB):
+                pad[i, pl.ds(SUB + SUB * q, SUB), :] = fy[v, i, pl.ds(SUB * q, SUB), :]
+            part = pl.ds(4 * (i % 2), 4)
+            a, b = yone[v, i // 2, part, :], ytwo[v, i // 2, part, :]
+            pad[i, SUB - 4 : SUB, :] = jnp.where(even, b, a)
+            pad[i, SUB + NJ : SUB + NJ + 4, :] = jnp.where(even, a, b)
+        for i in range(NI):
+            for q in range(NJ // SUB):
+                rows, at = pl.ds(SUB * q, SUB), SUB + SUB * q
+                dy = None
+                for k, w in enumerate(Y_WEIGHTS, start=1):
+                    t = w * (pad[i, pl.ds(at + k, SUB), :] - pad[i, pl.ds(at - k, SUB), :])
+                    dy = t if dy is None else dy + t
+                out[v, i, rows, :] = base[v, i, rows, :] + myb[i, rows, :] * dy
+
+
+def ydiff(base, flux_y, yone, ytwo, my):
+    vmem, hbm = pl.BlockSpec(memory_space=pltpu.VMEM), pl.BlockSpec(memory_space=pltpu.HBM)
+    return pl.pallas_call(
+        ydiff_body,
+        out_shape=jax.ShapeDtypeStruct((NV, NI, NJ, NK), F32),
+        in_specs=[vmem, hbm] + [vmem] * 3,
+        out_specs=vmem,
+        scratch_shapes=[
+            pltpu.VMEM((NV, NI, NJ, NK), F32),
+            pltpu.VMEM((NI, NJ, NK), F32),
+            pltpu.VMEM((NI, SUB + NJ + SUB, NK), F32),
+            pltpu.SemaphoreType.DMA((NV,)),
+        ],
+        input_output_aliases={0: 0},
+        compiler_params=pltpu.CompilerParams(vmem_limit_bytes=16 << 20),
+        cost_estimate=pl.CostEstimate(flops=1 << 25, bytes_accessed=4 << 20, transcendentals=0),
+        name="ydiff",
+    )(base, *in_hbm(flux_y), yone, ytwo, my)
 
 
 def finish_body(outer, base, mxb, own, got, mids, far_other, out_hbm, out, sem):
@@ -634,9 +665,9 @@
     ytwo = lax.ppermute(ysend_two, "gy", y_out)
     outside = join(ends)
     outside, one = lax.optimization_barrier((outside, one))
-    two, yone, ytwo = lax.optimization_barrier((two, yone, ytwo))
     far_own, far_other = far(outer, two)
-    base, mxb = block(inner, state, flux_x, flux_y, one, two, yone, ytwo, metric_x, metric_y)
+    base, mxb = block(inner, state, flux_x, one, two, metric_x)
+    base = ydiff(base, flux_y, yone, ytwo, metric_y)
     outside, base, mxb, far_own = lax.optimization_barrier((exchange(outside, ROWS), base, mxb, far_own))
     own, send = split(outside, mids, far_own, far_other)
     got = lax.ppermute(send, "gx", pair_in)

time: 40.9 us -> 43.8 us (1.071)
  Pallas kernels: 9.52 us -> 11.4 us
  waiting for transfers between devices: 6.83 us -> 7.56 us
    pallas_call x0 -> x1, Pallas kernels: none -> 2.65 us  [ydiff(): pl.pallas_call(ydiff_body, out_shape=jax.ShapeDtypeStruct((NV, NI, NJ, NK...]
    ppermute x2, starting transfers between devices: 4.82 us -> 5.91 us  [per_device(): got = lax.ppermute(send, 'gx', pair_in)]
    pallas_call x1, Pallas kernels: 3.25 us -> 2.45 us  [block(): pl.pallas_call(block_body, out_shape=(jax.ShapeDtypeStruct((NV, NI, NJ, N...]
    all_to_all x2, starting transfers between devices: 11.2 us -> 10.4 us  [exchange(): lax.all_to_all(x.reshape(PAIRS, rows, NK), 'gx', 0, 0, tiled=True, axis_i...]
    ppermute x1, waiting for transfers between devices: 0.01 us -> 0.62 us  [per_device(): ytwo = lax.ppermute(ysend_two, 'gy', y_out)]
  transfers between devices with their start and end apart: 8 -> 8, of which waited for: 3 -> 3; matrix products, arithmetic and copies ran while one was open for 0% -> 0% of each run, Pallas kernels for 14% -> 17%
where the time goes in v9:
time: 43.8 us; the launch traced here: 43.4 us
  starting transfers between devices  24.3 us (55%)
  Pallas kernels  11.4 us (26%)
  waiting for transfers between devices  7.56 us (17%)
    all_to_all x2, starting transfers between devices, exchange(): lax.all_to_all(x.reshape(PAIRS, rows, NK), 'gx', 0, 0, tiled=True, axis_i...  10.4 us
    ppermute x2, starting transfers between devices, per_device(): got = lax.ppermute(send, 'gx', pair_in)  5.91 us
    all_to_all x2, waiting for transfers between devices, exchange(): lax.all_to_all(x.reshape(PAIRS, rows, NK), 'gx', 0, 0, tiled=True, axis_i...  5.86 us
    ppermute x1, starting transfers between devices, per_device(): two = lax.ppermute(send_two, 'gx', pair_out)  3.37 us
    pallas_call x1, Pallas kernels, ydiff(): pl.pallas_call(ydiff_body, out_shape=jax.ShapeDtypeStruct((NV, NI, NJ, NK...  2.65 us
    pallas_call x1, Pallas kernels, block(): pl.pallas_call(block_body, out_shape=(jax.ShapeDtypeStruct((NV, NI, NJ, N...  2.45 us
    ppermute x1, starting transfers between devices, per_device(): ytwo = lax.ppermute(ysend_two, 'gy', y_out)  2.24 us
    pallas_call x1, Pallas kernels, own_share(): pl.pallas_call(own_body, out_shape=(coef, coef_far, values, values), in_s...  1.84 us
  transfers between devices with their start and end apart: 8, of which 3 were waited for; matrix products, arithmetic and copies ran while one was open for 0% of the time, Pallas kernels for 17%

profile of v9, /device:TPU:1, one launch (start us, length us, event | category | flops | bytes accessed | tf_op | source)
XLA Modules:
  0.0 43.4 jit_solution(1289095827132164988)
XLA Ops:
  0.0 1.8 %own_share.1 = (f32[32,8,128]{2,1,0:T(8,128)S(1)}, f32[35,8,128]{2,1,0:T(8,128)S(1)}, f32[816,128]{1,0:T(8,128)S(1)}, f32[816,128]{1,0:T(8,128)S(1)}) custom-call(f32[16]{0:T(128)} %gap_hbm.1, f32[5,16,32,128]{3,2,1,0:T(8,128)} %s_hbm.2, f32[5,16,32,128]{3,2,1,0:T(8,128)} %f_hbm.2), custom_call_target="tpu_custom_call" | custom-call | flops 16777216 | bytes 4194304 | tf_op jit(solution)/shard_map/own_share/pallas_call | solution.py:241
  1.8 1.5 %collective-permute-start = (f32[816,128]{1,0:T(8,128)S(1)}, f32[816,128]{1,0:T(8,128)S(1)}, u32[]{:S(2)}, u32[]{:S(2)}) collective-permute-start(f32[816,128]{1,0:T(8,128)S(1)} %get-tuple-element.44), channel_id=1, source_target_pairs={{0,4},{4,0},{8,12},{12,8},{16,20},{20,16},{24,28},{28,24},{32,36},... | collective-permute-start | bytes 1253384 | tf_op jit(solution)/shard_map/ppermute | solution.py:657
  3.3 1.4 %pack.1 = (f32[5,4,32,128]{3,2,1,0:T(8,128)S(1)}, f32[5,4,32,128]{3,2,1,0:T(8,128)S(1)}, f32[5,8,8,128]{3,2,1,0:T(8,128)S(1)}, f32[5,8,8,128]{3,2,1,0:T(8,128)S(1)}) custom-call(f32[5,16,32,128]{3,2,1,0:T(8,128)} %s_hbm.2, f32[5,16,32,128]{3,2,1,0:T(8,128)} %f_hbm.2, f32[5,16,32,128]{3,2,1,0:T(8,128)} %fy_hbm), custom_call_target="tpu_custom_call" | custom-call | bytes 2097152 | tf_op jit(solution)/shard_map/pack/pallas_call | solution.py:122
  4.7 0.9 %pair.1 = (f32[896,128]{1,0:T(8,128)}, f32[328,128]{1,0:T(8,128)S(1)}) custom-call(f32[816,128]{1,0:T(8,128)S(1)} %get-tuple-element.42.mine, f32[816,128]{1,0:T(8,128)S(1)} %collective-permute-done.got), custom_call_target="tpu_custom_call" | custom-call | flops 1048576 | bytes 1048576 | tf_op jit(solution)/shard_map/pair/pallas_call | solution.py:316
  5.6 0.0 copy-start
  5.6 6.8 %all-to-all-start = ((f32[16,56,128]{2,1,0:T(8,128)}), f32[16,56,128]{2,1,0:T(8,128)S(1)}, u32[]{:S(2)}, u32[]{:S(2)}) async-start(f32[16,56,128]{2,1,0:T(8,128)} %bitcast), calls=%async_computation | async-start | bytes 917504 | tf_op jit(solution)/shard_map/all_to_all | solution.py:644
  12.5 0.7 %collective-permute-start.1 = (f32[5,4,32,128]{3,2,1,0:T(8,128)S(1)}, f32[5,4,32,128]{3,2,1,0:T(8,128)S(1)}, u32[]{:S(2)}, u32[]{:S(2)}) collective-permute-start(f32[5,4,32,128]{3,2,1,0:T(8,128)S(1)} %get-tuple-element.59), channel_id=1, source_target_pairs={{0,4},{4,0},{8,12},{12,8},{16,20},{20,16},{24,28},{28,24},{32,36},... | collective-permute-start | bytes 983048 | tf_op jit(solution)/shard_map/ppermute | solution.py:662
  13.2 3.4 %collective-permute-start.2 = (f32[5,4,32,128]{3,2,1,0:T(8,128)S(1)}, f32[5,4,32,128]{3,2,1,0:T(8,128)S(1)}, u32[]{:S(2)}, u32[]{:S(2)}) collective-permute-start(f32[5,4,32,128]{3,2,1,0:T(8,128)S(1)} %get-tuple-element.63), channel_id=1, source_target_pairs={{4,8},{8,4},{12,16},{16,12},{20,24},{24,20},{28,32},{32,28},{36,40... | collective-permute-start | bytes 983048 | tf_op jit(solution)/shard_map/ppermute | solution.py:663
  16.6 5.9 %all-to-all-done = f32[16,56,128]{2,1,0:T(8,128)S(1)} async-done(((f32[16,56,128]{2,1,0:T(8,128)}), f32[16,56,128]{2,1,0:T(8,128)S(1)}, u32[]{:S(2)}, u32[]{:S(2)}) %all-to-all-start) | async-done | bytes 458784 | tf_op jit(solution)/shard_map/all_to_all | solution.py:644
  22.4 0.9 %join.1 = f32[384,128]{1,0:T(8,128)} custom-call(f32[896,128]{1,0:T(8,128)S(1)} %bitcast.4), custom_call_target="tpu_custom_call" | custom-call | flops 1048576 | bytes 1048576 | tf_op jit(solution)/shard_map/join/pallas_call | solution.py:405
  23.4 3.5 %all-to-all-start.1 = ((f32[16,24,128]{2,1,0:T(8,128)}), f32[16,24,128]{2,1,0:T(8,128)S(1)}, u32[]{:S(2)}, u32[]{:S(2)}) async-start(f32[16,24,128]{2,1,0:T(8,128)} %bitcast.2), calls=%async_computation.1 | async-start | bytes 393216 | tf_op jit(solution)/shard_map/all_to_all | solution.py:644
  26.9 1.7 %collective-permute-start.3 = (f32[5,8,8,128]{3,2,1,0:T(8,128)S(1)}, f32[5,8,8,128]{3,2,1,0:T(8,128)S(1)}, u32[]{:S(2)}, u32[]{:S(2)}) collective-permute-start(f32[5,8,8,128]{3,2,1,0:T(8,128)S(1)} %get-tuple-element.65), channel_id=1, source_target_pairs={{0,1},{1,0},{2,3},{3,2},{4,5},{5,4},{6,7},{7,6},{8,9},{9,8},{10,11... | collective-permute-start | bytes 491528 | tf_op jit(solution)/shard_map/ppermute | solution.py:664
  28.6 2.2 %collective-permute-start.4 = (f32[5,8,8,128]{3,2,1,0:T(8,128)S(1)}, f32[5,8,8,128]{3,2,1,0:T(8,128)S(1)}, u32[]{:S(2)}, u32[]{:S(2)}) collective-permute-start(f32[5,8,8,128]{3,2,1,0:T(8,128)S(1)} %get-tuple-element.66), channel_id=1, source_target_pairs={{0,3},{1,2},{2,1},{3,0},{4,7},{5,6},{6,5},{7,4},{8,11},{9,10},{10,... | collective-permute-start | bytes 491528 | tf_op jit(solution)/shard_map/ppermute | solution.py:665
  30.9 0.0 collective-permute-done.2.two
  30.9 0.0 copy-start.1
  30.9 2.5 %block.1 = (f32[5,16,32,128]{3,2,1,0:T(8,128)S(1)}, f32[16,32,128]{2,1,0:T(8,128)S(1)}) custom-call(f32[32,8,128]{2,1,0:T(8,128)S(1)} %get-tuple-element.61.inner, f32[5,16,32,128]{3,2,1,0:T(8,128)} %s_hbm.2, f32[5,16,32,128]{3,2,1,0:T(8,128)} %f_hbm.2, f32[5,4,32,128]{3,2,1,0:T(8,128)S(1)} %collective-permute-done.1.one, ...), custom_call_target="tpu_custom_call" | custom-call | flops 33554432 | bytes 8388608 | tf_op jit(solution)/shard_map/block/pallas_call | solution.py:539
  33.4 0.0 collective-permute-done.3.yone
  33.4 0.6 %collective-permute-done.4.ytwo = f32[5,8,8,128]{3,2,1,0:T(8,128)S(1)} collective-permute-done((f32[5,8,8,128]{3,2,1,0:T(8,128)S(1)}, f32[5,8,8,128]{3,2,1,0:T(8,128)S(1)}, u32[]{:S(2)}, u32[]{:S(2)}) %collective-permute-start.4) | collective-permute-done | bytes 163872 | tf_op jit(solution)/shard_map/ppermute | solution.py:665
  34.0 2.6 %ydiff.1.base = f32[5,16,32,128]{3,2,1,0:T(8,128)S(1)} custom-call(f32[5,16,32,128]{3,2,1,0:T(8,128)S(1)} %get-tuple-element.64.base, f32[5,16,32,128]{3,2,1,0:T(8,128)} %fy_hbm, f32[5,8,8,128]{3,2,1,0:T(8,128)S(1)} %collective-permute-done.3.yone, f32[5,8,8,128]{3,2,1,0:T(8,128)S(1)} %collective-permute-done.4.ytwo, ...), custom_call_target="tpu_custom_call", output_to_operand_aliasing={{}: (0, {})} | custom-call | flops 33554432 | bytes 4194304 | tf_op jit(solution)/shard_map/ydiff/pallas_call | solution.py:584
  36.7 0.0 all-to-all-done.1
  36.7 0.1 split.1
  36.7 4.4 %collective-permute-start.5 = (f32[400,128]{1,0:T(8,128)S(1)}, f32[400,128]{1,0:T(8,128)S(1)}, u32[]{:S(2)}, u32[]{:S(2)}) collective-permute-start(f32[400,128]{1,0:T(8,128)S(1)} %get-tuple-element.76), channel_id=1, source_target_pairs={{0,4},{4,0},{8,12},{12,8},{16,20},{20,16},{24,28},{28,24},{32,36},... | collective-permute-start | bytes 614408 | tf_op jit(solution)/shard_map/ppermute | solution.py:673
  41.1 1.1 %collective-permute-done.5.got = f32[400,128]{1,0:T(8,128)S(1)} collective-permute-done((f32[400,128]{1,0:T(8,128)S(1)}, f32[400,128]{1,0:T(8,128)S(1)}, u32[]{:S(2)}, u32[]{:S(2)}) %collective-permute-start.5) | collective-permute-done | bytes 204832 | tf_op jit(solution)/shard_map/ppermute | solution.py:673
  42.2 1.2 %finish.1 = f32[5,16,32,128]{3,2,1,0:T(8,128)} custom-call(f32[35,8,128]{2,1,0:T(8,128)S(1)} %get-tuple-element.41.outer, f32[5,16,32,128]{3,2,1,0:T(8,128)S(1)} %ydiff.1.base, f32[16,32,128]{2,1,0:T(8,128)S(1)} %get-tuple-element.70.mxb, f32[320,128]{1,0:T(8,128)S(1)} %get-tuple-element.75.own, f32[400,128]{1,0:T(8,128)S(1)} %collective-permute-done.5.got, ...), custom_call_target="tpu_custom_call" | custom-call | flops 4194304 | bytes 3145728 | tf_op jit(solution)/shard_map/finish/pallas_call | solution.py:630
  (5 shorter events, 0.0 us)
Async XLA Ops:
  1.8 2.9 %collective-permute-start = (f32[816,128]{1,0:T(8,128)S(1)}, f32[816,128]{1,0:T(8,128)S(1)}, u32[]{:S(2)}, u32[]{:S(2)}) collective-permute-start(f32[816,128]{1,0:T(8,128)S(1)} %get-tuple-element.44), channel_id=1, source_target_pairs={{0,4},{4,0},{8,12},{12,8},{16,20},{20,16},{24,28},{28,24},{32,36},... | collective-permute-start | bytes 1253384 | tf_op jit(solution)/shard_map/ppermute | solution.py:657
  5.6 25.3 %copy-start = (f32[16,32]{1,0:T(8,128)S(1)}, f32[16,32]{1,0:T(8,128)}, u32[]{:S(2)}) copy-start(f32[16,32]{1,0:T(8,128)} %mx.1) | copy-start | bytes 6148
  5.6 16.8 %all-to-all-start = ((f32[16,56,128]{2,1,0:T(8,128)}), f32[16,56,128]{2,1,0:T(8,128)S(1)}, u32[]{:S(2)}, u32[]{:S(2)}) async-start(f32[16,56,128]{2,1,0:T(8,128)} %bitcast), calls=%async_computation | async-start | bytes 917504 | tf_op jit(solution)/shard_map/all_to_all | solution.py:644
  12.5 10.9 %collective-permute-start.1 = (f32[5,4,32,128]{3,2,1,0:T(8,128)S(1)}, f32[5,4,32,128]{3,2,1,0:T(8,128)S(1)}, u32[]{:S(2)}, u32[]{:S(2)}) collective-permute-start(f32[5,4,32,128]{3,2,1,0:T(8,128)S(1)} %get-tuple-element.59), channel_id=1, source_target_pairs={{0,4},{4,0},{8,12},{12,8},{16,20},{20,16},{24,28},{28,24},{32,36},... | collective-permute-start | bytes 983048 | tf_op jit(solution)/shard_map/ppermute | solution.py:662
  13.2 17.7 %collective-permute-start.2 = (f32[5,4,32,128]{3,2,1,0:T(8,128)S(1)}, f32[5,4,32,128]{3,2,1,0:T(8,128)S(1)}, u32[]{:S(2)}, u32[]{:S(2)}) collective-permute-start(f32[5,4,32,128]{3,2,1,0:T(8,128)S(1)} %get-tuple-element.63), channel_id=1, source_target_pairs={{4,8},{8,4},{12,16},{16,12},{20,24},{24,20},{28,32},{32,28},{36,40... | collective-permute-start | bytes 983048 | tf_op jit(solution)/shard_map/ppermute | solution.py:663
  23.4 13.3 %all-to-all-start.1 = ((f32[16,24,128]{2,1,0:T(8,128)}), f32[16,24,128]{2,1,0:T(8,128)S(1)}, u32[]{:S(2)}, u32[]{:S(2)}) async-start(f32[16,24,128]{2,1,0:T(8,128)} %bitcast.2), calls=%async_computation.1 | async-start | bytes 393216 | tf_op jit(solution)/shard_map/all_to_all | solution.py:644
  26.9 6.5 %collective-permute-start.3 = (f32[5,8,8,128]{3,2,1,0:T(8,128)S(1)}, f32[5,8,8,128]{3,2,1,0:T(8,128)S(1)}, u32[]{:S(2)}, u32[]{:S(2)}) collective-permute-start(f32[5,8,8,128]{3,2,1,0:T(8,128)S(1)} %get-tuple-element.65), channel_id=1, source_target_pairs={{0,1},{1,0},{2,3},{3,2},{4,5},{5,4},{6,7},{7,6},{8,9},{9,8},{10,11... | collective-permute-start | bytes 491528 | tf_op jit(solution)/shard_map/ppermute | solution.py:664
  28.6 5.4 %collective-permute-start.4 = (f32[5,8,8,128]{3,2,1,0:T(8,128)S(1)}, f32[5,8,8,128]{3,2,1,0:T(8,128)S(1)}, u32[]{:S(2)}, u32[]{:S(2)}) collective-permute-start(f32[5,8,8,128]{3,2,1,0:T(8,128)S(1)} %get-tuple-element.66), channel_id=1, source_target_pairs={{0,3},{1,2},{2,1},{3,0},{4,7},{5,6},{6,5},{7,4},{8,11},{9,10},{10,... | collective-permute-start | bytes 491528 | tf_op jit(solution)/shard_map/ppermute | solution.py:665
  30.9 3.1 %copy-start.1 = (f32[16,32]{1,0:T(8,128)S(1)}, f32[16,32]{1,0:T(8,128)}, u32[]{:S(2)}) copy-start(f32[16,32]{1,0:T(8,128)} %my.1) | copy-start | bytes 6148
  36.7 5.5 %collective-permute-start.5 = (f32[400,128]{1,0:T(8,128)S(1)}, f32[400,128]{1,0:T(8,128)S(1)}, u32[]{:S(2)}, u32[]{:S(2)}) collective-permute-start(f32[400,128]{1,0:T(8,128)S(1)} %get-tuple-element.76), channel_id=1, source_target_pairs={{0,4},{4,0},{8,12},{12,8},{16,20},{20,16},{24,28},{28,24},{32,36},... | collective-permute-start | bytes 614408 | tf_op jit(solution)/shard_map/ppermute | solution.py:673

commit v10 on v8

--- a/solution.py
+++ b/solution.py
@@ -68,45 +68,66 @@
     return lax.rem(lax.axis_index(name), 2)
 
 
-def pack_body(s, f, fy, one, two, yone, ytwo, lo, hi, sem):
-    core, odd = parity("gx"), parity("gy")
-    copies = [
-        pltpu.make_async_copy(fy.at[:, :, 0:SUB, :], lo, sem.at[0]),
-        pltpu.make_async_copy(fy.at[:, :, NJ - SUB : NJ, :], hi, sem.at[1]),
-    ]
-    for c in copies:
-        c.start()
+def pack_x_body(s, f, one, two, sem):
+    core = parity("gx")
 
     def faces(right, left):
         moves = [
-            pltpu.make_async_copy(s.at[:, NI - 3 : NI], right.at[:, 0:3], sem.at[2]),
-            pltpu.make_async_copy(f.at[:, NI - 1 : NI], right.at[:, 3:4], sem.at[3]),
-            pltpu.make_async_copy(s.at[:, 0:3], left.at[:, 0:3], sem.at[4]),
-            pltpu.make_async_copy(f.at[:, 0:1], left.at[:, 3:4], sem.at[5]),
+            pltpu.make_async_copy(s.at[:, NI - 3 : NI], right.at[:, 0:3], sem.at[0]),
+            pltpu.make_async_copy(f.at[:, NI - 1 : NI], right.at[:, 3:4], sem.at[1]),
+            pltpu.make_async_copy(s.at[:, 0:3], left.at[:, 0:3], sem.at[2]),
+            pltpu.make_async_copy(f.at[:, 0:1], left.at[:, 3:4], sem.at[3]),
         ]
         for c in moves:
             c.start()
         for c in moves:
             c.wait()
 
+    @pl.when(core == 0)
+    def _():
+        faces(one, two)
+
+    @pl.when(core == 1)
+    def _():
+        faces(two, one)
+
+
+def pack_x(state, flux_x):
+    out = jax.ShapeDtypeStruct((NV, 4, NJ, NK), F32)
+    return pl.pallas_call(
+        pack_x_body,
+        out_shape=(out, out),
+        in_specs=[pl.BlockSpec(memory_space=pltpu.HBM)] * 2,
+        out_specs=(pl.BlockSpec(memory_space=pltpu.VMEM),) * 2,
+        scratch_shapes=[pltpu.SemaphoreType.DMA((4,))],
+        compiler_params=pltpu.CompilerParams(vmem_limit_bytes=8 << 20),
+        cost_estimate=pl.CostEstimate(flops=0, bytes_accessed=1 << 20, transcendentals=0),
+        name="pack_x",
+    )(*in_hbm(state, flux_x))
+
+
+def pack_y_body(fy, yone, ytwo, lo, hi, sem):
+    odd = parity("gy")
+    copies = [
+        (
+            pltpu.make_async_copy(fy.at[v, :, 0:SUB, :], lo.at[v], sem.at[0, v]),
+            pltpu.make_async_copy(fy.at[v, :, NJ - SUB : NJ, :], hi.at[v], sem.at[1, v]),
+        )
+        for v in range(NV)
+    ]
+    for both in copies:
+        for c in both:
+            c.start()
+
     def rows(top, bottom):
         for v in range(NV):
+            for c in copies[v]:
+                c.wait()
             for i in range(NI):
                 part = pl.ds(4 * (i % 2), 4)
                 top[v, i // 2, part, :] = hi[v, i, 4:8, :]
                 bottom[v, i // 2, part, :] = lo[v, i, 0:4, :]
 
-    @pl.when(core == 0)
-    def _():
-        faces(one, two)
-
-    @pl.when(core == 1)
-    def _():
-        faces(two, one)
-
-    for c in copies:
-        c.wait()
-
     @pl.when(odd == 0)
     def _():
         rows(yone, ytwo)
@@ -116,23 +137,22 @@
         rows(ytwo, yone)
 
 
-def pack(state, flux_x, flux_y):
-    x_out = jax.ShapeDtypeStruct((NV, 4, NJ, NK), F32)
-    y_out = jax.ShapeDtypeStruct((NV, NI // 2, SUB, NK), F32)
-    return pl.pallas_call(
-        pack_body,
-        out_shape=(x_out, x_out, y_out, y_out),
-        in_specs=[pl.BlockSpec(memory_space=pltpu.HBM)] * 3,
-        out_specs=(pl.BlockSpec(memory_space=pltpu.VMEM),) * 4,
+def pack_y(flux_y):
+    out = jax.ShapeDtypeStruct((NV, NI // 2, SUB, NK), F32)
+    return pl.pallas_call(
+        pack_y_body,
+        out_shape=(out, out),
+        in_specs=[pl.BlockSpec(memory_space=pltpu.HBM)],
+        out_specs=(pl.BlockSpec(memory_space=pltpu.VMEM),) * 2,
         scratch_shapes=[
             pltpu.VMEM((NV, NI, SUB, NK), F32),
             pltpu.VMEM((NV, NI, SUB, NK), F32),
-            pltpu.SemaphoreType.DMA((6,)),
+            pltpu.SemaphoreType.DMA((2, NV)),
         ],
         compiler_params=pltpu.CompilerParams(vmem_limit_bytes=8 << 20),
-        cost_estimate=pl.CostEstimate(flops=0, bytes_accessed=2 << 20, transcendentals=0),
-        name="pack",
-    )(*in_hbm(state, flux_x, flux_y))
+        cost_estimate=pl.CostEstimate(flops=0, bytes_accessed=1 << 20, transcendentals=0),
+        name="pack_y",
+    )(*in_hbm(flux_y))
 
 
 def own_body(gap_hbm, s_hbm, f_hbm, inner, outer, mine, send, gap, s, f, own, gap_sem, sem):
@@ -624,10 +644,11 @@
     inner, outer, mine, send = own_share(filter_gap, state, flux_x)
     send, state, flux_x, flux_y = lax.optimization_barrier((send, state, flux_x, flux_y))
     got = lax.ppermute(send, "gx", pair_in)
-    got, *faces = lax.optimization_barrier((got, *pack(state, flux_x, flux_y)))
+    got, *faces = lax.optimization_barrier((got, *pack_y(flux_y)))
     ends, mids = pair(mine, got)
-    ends, send_one, send_two, ysend_one, ysend_two = lax.optimization_barrier((ends, *faces))
+    ends, ysend_one, ysend_two, state, flux_x = lax.optimization_barrier((ends, *faces, state, flux_x))
     ends = exchange(ends, WIDE)
+    send_one, send_two = pack_x(state, flux_x)
     one = lax.ppermute(send_one, "gx", pair_in)
     two = lax.ppermute(send_two, "gx", pair_out)
     yone = lax.ppermute(ysend_one, "gy", y_in)

time: 40.9 us -> 40.9 us (level)
  waiting for transfers between devices: 6.83 us -> 5.62 us
  Pallas kernels: 9.52 us -> 10.6 us
    ppermute x2, starting transfers between devices: 4.82 us -> 3.44 us  [per_device(): got = lax.ppermute(send, 'gx', pair_in)]
    all_to_all x2, starting transfers between devices: 11.2 us -> 12.5 us  [exchange(): lax.all_to_all(x.reshape(PAIRS, rows, NK), 'gx', 0, 0, tiled=True, axis_i...]
    all_to_all x2, waiting for transfers between devices: 5.73 us -> 4.37 us  [exchange(): lax.all_to_all(x.reshape(PAIRS, rows, NK), 'gx', 0, 0, tiled=True, axis_i...]
    pallas_call x1 -> x2, Pallas kernels: 1.38 us -> 2.45 us  [the longest x1 1.23 us: pack_x(): pl.pallas_call(pack_x_body, out_shape=(out, out), in_specs=[pl.BlockSpec(...]
  transfers between devices with their start and end apart: 8 -> 8, of which waited for: 3 -> 4; matrix products, arithmetic and copies ran while one was open for 0% -> 0% of each run, Pallas kernels for 14% -> 16%
where the time goes in v10:
time: 40.9 us; the launch traced here: 40.5 us
  starting transfers between devices  24.1 us (59%)
  Pallas kernels  10.6 us (26%)
  waiting for transfers between devices  5.62 us (14%)
    all_to_all x2, starting transfers between devices, exchange(): lax.all_to_all(x.reshape(PAIRS, rows, NK), 'gx', 0, 0, tiled=True, axis_i...  12.5 us
    all_to_all x2, waiting for transfers between devices, exchange(): lax.all_to_all(x.reshape(PAIRS, rows, NK), 'gx', 0, 0, tiled=True, axis_i...  4.37 us
    ppermute x2, starting transfers between devices, per_device(): got = lax.ppermute(send, 'gx', pair_in)  3.44 us
    ppermute x1, starting transfers between devices, per_device(): two = lax.ppermute(send_two, 'gx', pair_out)  3.44 us
    pallas_call x1, Pallas kernels, block(): pl.pallas_call(block_body, out_shape=(jax.ShapeDtypeStruct((NV, NI, NJ, N...  3.25 us
    ppermute x1, starting transfers between devices, per_device(): ytwo = lax.ppermute(ysend_two, 'gy', y_out)  2.24 us
    pallas_call x1, Pallas kernels, own_share(): pl.pallas_call(own_body, out_shape=(coef, coef_far, values, values), in_s...  1.84 us
    ppermute x1, starting transfers between devices, per_device(): yone = lax.ppermute(ysend_one, 'gy', y_in)  1.72 us
  transfers between devices with their start and end apart: 8, of which 4 were waited for; matrix products, arithmetic and copies ran while one was open for 0% of the time, Pallas kernels for 16%

profile of v10, /device:TPU:1, one launch (start us, length us, event | category | flops | bytes accessed | tf_op | source)
XLA Modules:
  0.0 40.5 jit_solution(9592424258552765257)
XLA Ops:
  0.0 1.8 %own_share.1 = (f32[32,8,128]{2,1,0:T(8,128)S(1)}, f32[35,8,128]{2,1,0:T(8,128)S(1)}, f32[816,128]{1,0:T(8,128)S(1)}, f32[816,128]{1,0:T(8,128)S(1)}) custom-call(f32[16]{0:T(128)} %gap_hbm.1, f32[5,16,32,128]{3,2,1,0:T(8,128)} %s_hbm.2, f32[5,16,32,128]{3,2,1,0:T(8,128)} %f_hbm.2), custom_call_target="tpu_custom_call" | custom-call | flops 16777216 | bytes 4194304 | tf_op jit(solution)/shard_map/own_share/pallas_call | solution.py:261
  1.8 1.5 %collective-permute-start = (f32[816,128]{1,0:T(8,128)S(1)}, f32[816,128]{1,0:T(8,128)S(1)}, u32[]{:S(2)}, u32[]{:S(2)}) collective-permute-start(f32[816,128]{1,0:T(8,128)S(1)} %get-tuple-element.45), channel_id=1, source_target_pairs={{0,4},{4,0},{8,12},{12,8},{16,20},{20,16},{24,28},{28,24},{32,36},... | collective-permute-start | bytes 1253384 | tf_op jit(solution)/shard_map/ppermute | solution.py:646
  3.3 1.2 %pack_y.1 = (f32[5,8,8,128]{3,2,1,0:T(8,128)S(1)}, f32[5,8,8,128]{3,2,1,0:T(8,128)S(1)}) custom-call(f32[5,16,32,128]{3,2,1,0:T(8,128)} %fy_hbm), custom_call_target="tpu_custom_call" | custom-call | bytes 1048576 | tf_op jit(solution)/shard_map/pack_y/pallas_call | solution.py:142
  4.6 0.2 collective-permute-done.got
  4.7 0.9 %pair.1 = (f32[896,128]{1,0:T(8,128)}, f32[328,128]{1,0:T(8,128)S(1)}) custom-call(f32[816,128]{1,0:T(8,128)S(1)} %get-tuple-element.43.mine, f32[816,128]{1,0:T(8,128)S(1)} %collective-permute-done.got), custom_call_target="tpu_custom_call" | custom-call | flops 1048576 | bytes 1048576 | tf_op jit(solution)/shard_map/pair/pallas_call | solution.py:336
  5.6 6.8 %all-to-all-start = ((f32[16,56,128]{2,1,0:T(8,128)}), f32[16,56,128]{2,1,0:T(8,128)S(1)}, u32[]{:S(2)}, u32[]{:S(2)}) async-start(f32[16,56,128]{2,1,0:T(8,128)} %bitcast), calls=%async_computation | async-start | bytes 917504 | tf_op jit(solution)/shard_map/all_to_all | solution.py:633
  12.5 1.2 %pack_x.1 = (f32[5,4,32,128]{3,2,1,0:T(8,128)S(1)}, f32[5,4,32,128]{3,2,1,0:T(8,128)S(1)}) custom-call(f32[5,16,32,128]{3,2,1,0:T(8,128)} %s_hbm.2, f32[5,16,32,128]{3,2,1,0:T(8,128)} %f_hbm.2), custom_call_target="tpu_custom_call" | custom-call | bytes 1048576 | tf_op jit(solution)/shard_map/pack_x/pallas_call | solution.py:97
  13.7 0.0 copy-start
  13.7 0.0 copy-start.1
  13.7 0.7 %collective-permute-start.1 = (f32[5,4,32,128]{3,2,1,0:T(8,128)S(1)}, f32[5,4,32,128]{3,2,1,0:T(8,128)S(1)}, u32[]{:S(2)}, u32[]{:S(2)}) collective-permute-start(f32[5,4,32,128]{3,2,1,0:T(8,128)S(1)} %get-tuple-element.58), channel_id=1, source_target_pairs={{0,4},{4,0},{8,12},{12,8},{16,20},{20,16},{24,28},{28,24},{32,36},... | collective-permute-start | bytes 983048 | tf_op jit(solution)/shard_map/ppermute | solution.py:652
  14.4 3.4 %collective-permute-start.2 = (f32[5,4,32,128]{3,2,1,0:T(8,128)S(1)}, f32[5,4,32,128]{3,2,1,0:T(8,128)S(1)}, u32[]{:S(2)}, u32[]{:S(2)}) collective-permute-start(f32[5,4,32,128]{3,2,1,0:T(8,128)S(1)} %get-tuple-element.62), channel_id=1, source_target_pairs={{4,8},{8,4},{12,16},{16,12},{20,24},{24,20},{28,32},{32,28},{36,40... | collective-permute-start | bytes 983048 | tf_op jit(solution)/shard_map/ppermute | solution.py:653
  17.9 1.7 %collective-permute-start.3 = (f32[5,8,8,128]{3,2,1,0:T(8,128)S(1)}, f32[5,8,8,128]{3,2,1,0:T(8,128)S(1)}, u32[]{:S(2)}, u32[]{:S(2)}) collective-permute-start(f32[5,8,8,128]{3,2,1,0:T(8,128)S(1)} %get-tuple-element.63), channel_id=1, source_target_pairs={{0,1},{1,0},{2,3},{3,2},{4,5},{5,4},{6,7},{7,6},{8,9},{9,8},{10,11... | collective-permute-start | bytes 491528 | tf_op jit(solution)/shard_map/ppermute | solution.py:654
  19.6 2.2 %collective-permute-start.4 = (f32[5,8,8,128]{3,2,1,0:T(8,128)S(1)}, f32[5,8,8,128]{3,2,1,0:T(8,128)S(1)}, u32[]{:S(2)}, u32[]{:S(2)}) collective-permute-start(f32[5,8,8,128]{3,2,1,0:T(8,128)S(1)} %get-tuple-element.64), channel_id=1, source_target_pairs={{0,3},{1,2},{2,1},{3,0},{4,7},{5,6},{6,5},{7,4},{8,11},{9,10},{10,... | collective-permute-start | bytes 491528 | tf_op jit(solution)/shard_map/ppermute | solution.py:655
  21.8 0.5 %all-to-all-done = f32[16,56,128]{2,1,0:T(8,128)S(1)} async-done(((f32[16,56,128]{2,1,0:T(8,128)}), f32[16,56,128]{2,1,0:T(8,128)S(1)}, u32[]{:S(2)}, u32[]{:S(2)}) %all-to-all-start) | async-done | bytes 458784 | tf_op jit(solution)/shard_map/all_to_all | solution.py:633
  22.4 0.9 %join.1 = f32[384,128]{1,0:T(8,128)} custom-call(f32[896,128]{1,0:T(8,128)S(1)} %bitcast.4), custom_call_target="tpu_custom_call" | custom-call | flops 1048576 | bytes 1048576 | tf_op jit(solution)/shard_map/join/pallas_call | solution.py:425
  23.3 0.0 collective-permute-done.1.one
  23.3 5.7 %all-to-all-start.1 = ((f32[16,24,128]{2,1,0:T(8,128)}), f32[16,24,128]{2,1,0:T(8,128)S(1)}, u32[]{:S(2)}, u32[]{:S(2)}) async-start(f32[16,24,128]{2,1,0:T(8,128)} %bitcast.2), calls=%async_computation.1 | async-start | bytes 393216 | tf_op jit(solution)/shard_map/all_to_all | solution.py:633
  29.0 0.0 collective-permute-done.3.yone
  29.1 3.2 %block.1 = (f32[5,16,32,128]{3,2,1,0:T(8,128)S(1)}, f32[16,32,128]{2,1,0:T(8,128)S(1)}) custom-call(f32[32,8,128]{2,1,0:T(8,128)S(1)} %get-tuple-element.60.inner, f32[5,16,32,128]{3,2,1,0:T(8,128)} %s_hbm.2, f32[5,16,32,128]{3,2,1,0:T(8,128)} %f_hbm.2, f32[5,16,32,128]{3,2,1,0:T(8,128)} %fy_hbm, f32[5,4,32,128]{3,2,1,0:T(8,128)S(1)} %collective-permute-done.1.one, ...), custom_call_target="tpu_custom_call" | custom-call | flops 1073741824 | bytes 67108864 | tf_op jit(solution)/shard_map/block/pallas_call | solution.py:575
  32.3 3.8 %all-to-all-done.1 = f32[16,24,128]{2,1,0:T(8,128)S(1)} async-done(((f32[16,24,128]{2,1,0:T(8,128)}), f32[16,24,128]{2,1,0:T(8,128)S(1)}, u32[]{:S(2)}, u32[]{:S(2)}) %all-to-all-start.1) | async-done | bytes 196640 | tf_op jit(solution)/shard_map/all_to_all | solution.py:633
  36.2 0.1 split.1
  36.2 1.9 %collective-permute-start.5 = (f32[400,128]{1,0:T(8,128)S(1)}, f32[400,128]{1,0:T(8,128)S(1)}, u32[]{:S(2)}, u32[]{:S(2)}) collective-permute-start(f32[400,128]{1,0:T(8,128)S(1)} %get-tuple-element.78), channel_id=1, source_target_pairs={{0,4},{4,0},{8,12},{12,8},{16,20},{20,16},{24,28},{28,24},{32,36},... | collective-permute-start | bytes 614408 | tf_op jit(solution)/shard_map/ppermute | solution.py:663
  38.2 1.1 %collective-permute-done.5.got = f32[400,128]{1,0:T(8,128)S(1)} collective-permute-done((f32[400,128]{1,0:T(8,128)S(1)}, f32[400,128]{1,0:T(8,128)S(1)}, u32[]{:S(2)}, u32[]{:S(2)}) %collective-permute-start.5) | collective-permute-done | bytes 204832 | tf_op jit(solution)/shard_map/ppermute | solution.py:663
  39.3 1.2 %finish.1 = f32[5,16,32,128]{3,2,1,0:T(8,128)} custom-call(f32[35,8,128]{2,1,0:T(8,128)S(1)} %get-tuple-element.42.outer, f32[5,16,32,128]{3,2,1,0:T(8,128)S(1)} %get-tuple-element.71.base, f32[16,32,128]{2,1,0:T(8,128)S(1)} %get-tuple-element.72.mxb, f32[320,128]{1,0:T(8,128)S(1)} %get-tuple-element.77.own, f32[400,128]{1,0:T(8,128)S(1)} %collective-permute-done.5.got, ...), custom_call_target="tpu_custom_call" | custom-call | flops 4194304 | bytes 3145728 | tf_op jit(solution)/shard_map/finish/pallas_call | solution.py:619
  (5 shorter events, 0.0 us)
Async XLA Ops:
  1.8 2.9 %collective-permute-start = (f32[816,128]{1,0:T(8,128)S(1)}, f32[816,128]{1,0:T(8,128)S(1)}, u32[]{:S(2)}, u32[]{:S(2)}) collective-permute-start(f32[816,128]{1,0:T(8,128)S(1)} %get-tuple-element.45), channel_id=1, source_target_pairs={{0,4},{4,0},{8,12},{12,8},{16,20},{20,16},{24,28},{28,24},{32,36},... | collective-permute-start | bytes 1253384 | tf_op jit(solution)/shard_map/ppermute | solution.py:646
  5.6 16.8 %all-to-all-start = ((f32[16,56,128]{2,1,0:T(8,128)}), f32[16,56,128]{2,1,0:T(8,128)S(1)}, u32[]{:S(2)}, u32[]{:S(2)}) async-start(f32[16,56,128]{2,1,0:T(8,128)} %bitcast), calls=%async_computation | async-start | bytes 917504 | tf_op jit(solution)/shard_map/all_to_all | solution.py:633
  13.7 15.4 %copy-start = (f32[16,32]{1,0:T(8,128)S(1)}, f32[16,32]{1,0:T(8,128)}, u32[]{:S(2)}) copy-start(f32[16,32]{1,0:T(8,128)} %mx.1) | copy-start | bytes 6148
  13.7 15.4 %copy-start.1 = (f32[16,32]{1,0:T(8,128)S(1)}, f32[16,32]{1,0:T(8,128)}, u32[]{:S(2)}) copy-start(f32[16,32]{1,0:T(8,128)} %my.1) | copy-start | bytes 6148
  13.7 9.6 %collective-permute-start.1 = (f32[5,4,32,128]{3,2,1,0:T(8,128)S(1)}, f32[5,4,32,128]{3,2,1,0:T(8,128)S(1)}, u32[]{:S(2)}, u32[]{:S(2)}) collective-permute-start(f32[5,4,32,128]{3,2,1,0:T(8,128)S(1)} %get-tuple-element.58), channel_id=1, source_target_pairs={{0,4},{4,0},{8,12},{12,8},{16,20},{20,16},{24,28},{28,24},{32,36},... | collective-permute-start | bytes 983048 | tf_op jit(solution)/shard_map/ppermute | solution.py:652
  14.4 14.6 %collective-permute-start.2 = (f32[5,4,32,128]{3,2,1,0:T(8,128)S(1)}, f32[5,4,32,128]{3,2,1,0:T(8,128)S(1)}, u32[]{:S(2)}, u32[]{:S(2)}) collective-permute-start(f32[5,4,32,128]{3,2,1,0:T(8,128)S(1)} %get-tuple-element.62), channel_id=1, source_target_pairs={{4,8},{8,4},{12,16},{16,12},{20,24},{24,20},{28,32},{32,28},{36,40... | collective-permute-start | bytes 983048 | tf_op jit(solution)/shard_map/ppermute | solution.py:653
  17.9 11.1 %collective-permute-start.3 = (f32[5,8,8,128]{3,2,1,0:T(8,128)S(1)}, f32[5,8,8,128]{3,2,1,0:T(8,128)S(1)}, u32[]{:S(2)}, u32[]{:S(2)}) collective-permute-start(f32[5,8,8,128]{3,2,1,0:T(8,128)S(1)} %get-tuple-element.63), channel_id=1, source_target_pairs={{0,1},{1,0},{2,3},{3,2},{4,5},{5,4},{6,7},{7,6},{8,9},{9,8},{10,11... | collective-permute-start | bytes 491528 | tf_op jit(solution)/shard_map/ppermute | solution.py:654
  19.6 9.4 %collective-permute-start.4 = (f32[5,8,8,128]{3,2,1,0:T(8,128)S(1)}, f32[5,8,8,128]{3,2,1,0:T(8,128)S(1)}, u32[]{:S(2)}, u32[]{:S(2)}) collective-permute-start(f32[5,8,8,128]{3,2,1,0:T(8,128)S(1)} %get-tuple-element.64), channel_id=1, source_target_pairs={{0,3},{1,2},{2,1},{3,0},{4,7},{5,6},{6,5},{7,4},{8,11},{9,10},{10,... | collective-permute-start | bytes 491528 | tf_op jit(solution)/shard_map/ppermute | solution.py:655
  23.3 12.9 %all-to-all-start.1 = ((f32[16,24,128]{2,1,0:T(8,128)}), f32[16,24,128]{2,1,0:T(8,128)S(1)}, u32[]{:S(2)}, u32[]{:S(2)}) async-start(f32[16,24,128]{2,1,0:T(8,128)} %bitcast.2), calls=%async_computation.1 | async-start | bytes 393216 | tf_op jit(solution)/shard_map/all_to_all | solution.py:633
  36.2 3.0 %collective-permute-start.5 = (f32[400,128]{1,0:T(8,128)S(1)}, f32[400,128]{1,0:T(8,128)S(1)}, u32[]{:S(2)}, u32[]{:S(2)}) collective-permute-start(f32[400,128]{1,0:T(8,128)S(1)} %get-tuple-element.78), channel_id=1, source_target_pairs={{0,4},{4,0},{8,12},{12,8},{16,20},{20,16},{24,28},{28,24},{32,36},... | collective-permute-start | bytes 614408 | tf_op jit(solution)/shard_map/ppermute | solution.py:663

commit v11 on v8

--- a/solution.py
+++ b/solution.py
@@ -568,44 +568,71 @@
     )(inner, *in_hbm(state, flux_x, flux_y), one, two, yone, ytwo, mx, my)
 
 
-def finish_body(outer, base, mxb, own, got, mids, far_other, out_hbm, out, sem):
+def add_outside(v, half, r, outer, base, mxb, values, out):
+    rows = pl.ds(pl.multiple_of(HALF * half + SUB * r, SUB), SUB)
+    lf, rf, ld, rd = values
+    for i in range(NI):
+        d = float(CS["left"][i]) * ld + float(CS["right"][i]) * rd
+        e = outer[C_LEFT + i] * lf + outer[C_RIGHT + i] * rf
+        out[v, i, rows, :] = (base[v, i, rows, :] + e) + mxb[i, rows, :] * d
+
+
+def finish_own_body(outer, base, mxb, own, out):
+    core = parity("gx")
+    for v in range(NV):
+        for r in range(HALF // SUB):
+            values = [own[pl.ds((NV * k + v) * HALF + SUB * r, SUB), :] for k in range(4)]
+            add_outside(v, core, r, outer, base, mxb, values, out)
+
+
+def finish_own(outer, base, mxb, own):
+    vmem = pl.BlockSpec(memory_space=pltpu.VMEM)
+    return pl.pallas_call(
+        finish_own_body,
+        out_shape=jax.ShapeDtypeStruct((NV, NI, NJ, NK), F32),
+        in_specs=[vmem] * 4,
+        out_specs=vmem,
+        input_output_aliases={1: 0},
+        compiler_params=pltpu.CompilerParams(vmem_limit_bytes=12 << 20),
+        cost_estimate=pl.CostEstimate(flops=1 << 22, bytes_accessed=2 << 20, transcendentals=0),
+        name="finish_own",
+    )(outer, base, mxb, own)
+
+
+def finish_body(outer, base, mxb, got, mids, far_other, out_hbm, out, sem):
     core = parity("gx")
     is0 = core == 0
     hl_inv, inv, tr_inv = (jnp.broadcast_to(mids[pl.ds(4 * NV * HALF + k, 1), :], (SUB, NK)) for k in (4, 5, 6))
     zero = jnp.zeros((SUB, NK), F32)
-    own_far = (jnp.where(is0, zero, inv), jnp.where(is0, inv, zero))
     got_far = (jnp.where(is0, zero, tr_inv), jnp.where(is0, hl_inv, zero))
+    side = jnp.where(is0, C_RIGHT, C_LEFT)
     stores = [pltpu.make_async_copy(out.at[v], out_hbm.at[v], sem.at[v]) for v in range(NV)]
     for v in range(NV):
-        for z, half, far_w, far_z, far_at in (
-            (own, core, own_far, got, 4 * NV),
-            (got, 1 - core, got_far, far_other, 0),
-        ):
-            for r in range(HALF // SUB):
-                rows = pl.ds(pl.multiple_of(HALF * half + SUB * r, SUB), SUB)
-                lf, rf, ld, rd = (z[pl.ds((NV * k + v) * HALF + SUB * r, SUB), :] for k in range(4))
-                w = far_z[pl.ds((far_at + v) * HALF + SUB * r, SUB), :]
-                lf, rf = lf + far_w[0] * w, rf + far_w[1] * w
-                for i in range(NI):
-                    d = float(CS["left"][i]) * ld + float(CS["right"][i]) * rd
-                    e = outer[C_LEFT + i] * lf + outer[C_RIGHT + i] * rf
-                    out[v, i, rows, :] = (base[v, i, rows, :] + e) + mxb[i, rows, :] * d
+        for r in range(HALF // SUB):
+            rows = pl.ds(pl.multiple_of(HALF * core + SUB * r, SUB), SUB)
+            w = inv * got[pl.ds((4 * NV + v) * HALF + SUB * r, SUB), :]
+            for i in range(NI):
+                out[v, i, rows, :] = base[v, i, rows, :] + outer[side + i] * w
+            lf, rf, ld, rd = (got[pl.ds((NV * k + v) * HALF + SUB * r, SUB), :] for k in range(4))
+            w = far_other[pl.ds(v * HALF + SUB * r, SUB), :]
+            values = (lf + got_far[0] * w, rf + got_far[1] * w, ld, rd)
+            add_outside(v, 1 - core, r, outer, base, mxb, values, out)
         stores[v].start()
     for c in stores:
         c.wait()
 
 
-def finish(outer, base, mxb, own, got, mids, far_other):
+def finish(outer, base, mxb, got, mids, far_other):
     return pl.pallas_call(
         finish_body,
         out_shape=jax.ShapeDtypeStruct((NV, NI, NJ, NK), F32),
-        in_specs=[pl.BlockSpec(memory_space=pltpu.VMEM)] * 7,
+        in_specs=[pl.BlockSpec(memory_space=pltpu.VMEM)] * 6,
         out_specs=pl.BlockSpec(memory_space=pltpu.HBM),
         scratch_shapes=[pltpu.VMEM((NV, NI, NJ, NK), F32), pltpu.SemaphoreType.DMA((NV,))],
         compiler_params=pltpu.CompilerParams(vmem_limit_bytes=12 << 20),
         cost_estimate=pl.CostEstimate(flops=1 << 22, bytes_accessed=3 << 20, transcendentals=0),
         name="finish",
-    )(outer, base, mxb, own, got, mids, far_other)
+    )(outer, base, mxb, got, mids, far_other)
 
 
 def exchange(x, rows):
@@ -640,7 +667,8 @@
     outside, base, mxb, far_own = lax.optimization_barrier((exchange(outside, ROWS), base, mxb, far_own))
     own, send = split(outside, mids, far_own, far_other)
     got = lax.ppermute(send, "gx", pair_in)
-    return finish(outer, base, mxb, own, got, mids, far_other)
+    got, base = lax.optimization_barrier((got, finish_own(outer, base, mxb, own)))
+    return finish(outer, base, mxb, got, mids, far_other)
 
 
 def solution(mesh):

time: 40.9 us -> 40.9 us (level)
  waiting for transfers between devices: 6.83 us -> 6.38 us
  Pallas kernels: 9.52 us -> 9.94 us
  transfers between devices with their start and end apart: 8 -> 8, of which waited for: 3 -> 3; matrix products, arithmetic and copies ran while one was open for 0% -> 0% of each run, Pallas kernels for 14% -> 15%
where the time goes in v11:
time: 40.9 us; the launch traced here: 40.5 us
  starting transfers between devices  24 us (59%)
  Pallas kernels  9.94 us (24%)
  waiting for transfers between devices  6.38 us (16%)
    all_to_all x2, starting transfers between devices, exchange(): lax.all_to_all(x.reshape(PAIRS, rows, NK), 'gx', 0, 0, tiled=True, axis_i...  11.2 us
    all_to_all x2, waiting for transfers between devices, exchange(): lax.all_to_all(x.reshape(PAIRS, rows, NK), 'gx', 0, 0, tiled=True, axis_i...  5.66 us
    ppermute x2, starting transfers between devices, per_device(): got = lax.ppermute(send, 'gx', pair_in)  4.82 us
    ppermute x1, starting transfers between devices, per_device(): two = lax.ppermute(send_two, 'gx', pair_out)  3.37 us
    pallas_call x1, Pallas kernels, block(): pl.pallas_call(block_body, out_shape=(jax.ShapeDtypeStruct((NV, NI, NJ, N...  3.33 us
    ppermute x1, starting transfers between devices, per_device(): ytwo = lax.ppermute(ysend_two, 'gy', y_out)  2.24 us
    pallas_call x1, Pallas kernels, own_share(): pl.pallas_call(own_body, out_shape=(coef, coef_far, values, values), in_s...  1.84 us
    ppermute x1, starting transfers between devices, per_device(): yone = lax.ppermute(ysend_one, 'gy', y_in)  1.72 us
  transfers between devices with their start and end apart: 8, of which 3 were waited for; matrix products, arithmetic and copies ran while one was open for 0% of the time, Pallas kernels for 15%

profile of v11, /device:TPU:1, one launch (start us, length us, event | category | flops | bytes accessed | tf_op | source)
XLA Modules:
  0.0 40.5 jit_solution(3589609496368751369)
XLA Ops:
  0.0 1.8 %own_share.1 = (f32[32,8,128]{2,1,0:T(8,128)S(1)}, f32[35,8,128]{2,1,0:T(8,128)S(1)}, f32[816,128]{1,0:T(8,128)S(1)}, f32[816,128]{1,0:T(8,128)S(1)}) custom-call(f32[16]{0:T(128)} %gap_hbm.1, f32[5,16,32,128]{3,2,1,0:T(8,128)} %s_hbm.2, f32[5,16,32,128]{3,2,1,0:T(8,128)} %f_hbm.2), custom_call_target="tpu_custom_call" | custom-call | flops 16777216 | bytes 4194304 | tf_op jit(solution)/shard_map/own_share/pallas_call | solution.py:241
  1.8 1.5 %collective-permute-start = (f32[816,128]{1,0:T(8,128)S(1)}, f32[816,128]{1,0:T(8,128)S(1)}, u32[]{:S(2)}, u32[]{:S(2)}) collective-permute-start(f32[816,128]{1,0:T(8,128)S(1)} %get-tuple-element.49), channel_id=1, source_target_pairs={{0,4},{4,0},{8,12},{12,8},{16,20},{20,16},{24,28},{28,24},{32,36},... | collective-permute-start | bytes 1253384 | tf_op jit(solution)/shard_map/ppermute | solution.py:653
  3.3 1.4 %pack.1 = (f32[5,4,32,128]{3,2,1,0:T(8,128)S(1)}, f32[5,4,32,128]{3,2,1,0:T(8,128)S(1)}, f32[5,8,8,128]{3,2,1,0:T(8,128)S(1)}, f32[5,8,8,128]{3,2,1,0:T(8,128)S(1)}) custom-call(f32[5,16,32,128]{3,2,1,0:T(8,128)} %s_hbm.2, f32[5,16,32,128]{3,2,1,0:T(8,128)} %f_hbm.2, f32[5,16,32,128]{3,2,1,0:T(8,128)} %fy_hbm), custom_call_target="tpu_custom_call" | custom-call | bytes 2097152 | tf_op jit(solution)/shard_map/pack/pallas_call | solution.py:122
  4.7 0.9 %pair.1 = (f32[896,128]{1,0:T(8,128)}, f32[328,128]{1,0:T(8,128)S(1)}) custom-call(f32[816,128]{1,0:T(8,128)S(1)} %get-tuple-element.47.mine, f32[816,128]{1,0:T(8,128)S(1)} %collective-permute-done.got), custom_call_target="tpu_custom_call" | custom-call | flops 1048576 | bytes 1048576 | tf_op jit(solution)/shard_map/pair/pallas_call | solution.py:316
  5.6 0.0 copy-start
  5.6 0.0 copy-start.1
  5.6 6.8 %all-to-all-start = ((f32[16,56,128]{2,1,0:T(8,128)}), f32[16,56,128]{2,1,0:T(8,128)S(1)}, u32[]{:S(2)}, u32[]{:S(2)}) async-start(f32[16,56,128]{2,1,0:T(8,128)} %bitcast), calls=%async_computation | async-start | bytes 917504 | tf_op jit(solution)/shard_map/all_to_all | solution.py:640
  12.5 0.7 %collective-permute-start.1 = (f32[5,4,32,128]{3,2,1,0:T(8,128)S(1)}, f32[5,4,32,128]{3,2,1,0:T(8,128)S(1)}, u32[]{:S(2)}, u32[]{:S(2)}) collective-permute-start(f32[5,4,32,128]{3,2,1,0:T(8,128)S(1)} %get-tuple-element.64), channel_id=1, source_target_pairs={{0,4},{4,0},{8,12},{12,8},{16,20},{20,16},{24,28},{28,24},{32,36},... | collective-permute-start | bytes 983048 | tf_op jit(solution)/shard_map/ppermute | solution.py:658
  13.2 3.4 %collective-permute-start.2 = (f32[5,4,32,128]{3,2,1,0:T(8,128)S(1)}, f32[5,4,32,128]{3,2,1,0:T(8,128)S(1)}, u32[]{:S(2)}, u32[]{:S(2)}) collective-permute-start(f32[5,4,32,128]{3,2,1,0:T(8,128)S(1)} %get-tuple-element.68), channel_id=1, source_target_pairs={{4,8},{8,4},{12,16},{16,12},{20,24},{24,20},{28,32},{32,28},{36,40... | collective-permute-start | bytes 983048 | tf_op jit(solution)/shard_map/ppermute | solution.py:659
  16.6 1.7 %collective-permute-start.3 = (f32[5,8,8,128]{3,2,1,0:T(8,128)S(1)}, f32[5,8,8,128]{3,2,1,0:T(8,128)S(1)}, u32[]{:S(2)}, u32[]{:S(2)}) collective-permute-start(f32[5,8,8,128]{3,2,1,0:T(8,128)S(1)} %get-tuple-element.69), channel_id=1, source_target_pairs={{0,1},{1,0},{2,3},{3,2},{4,5},{5,4},{6,7},{7,6},{8,9},{9,8},{10,11... | collective-permute-start | bytes 491528 | tf_op jit(solution)/shard_map/ppermute | solution.py:660
  18.3 2.2 %collective-permute-start.4 = (f32[5,8,8,128]{3,2,1,0:T(8,128)S(1)}, f32[5,8,8,128]{3,2,1,0:T(8,128)S(1)}, u32[]{:S(2)}, u32[]{:S(2)}) collective-permute-start(f32[5,8,8,128]{3,2,1,0:T(8,128)S(1)} %get-tuple-element.70), channel_id=1, source_target_pairs={{0,3},{1,2},{2,1},{3,0},{4,7},{5,6},{6,5},{7,4},{8,11},{9,10},{10,... | collective-permute-start | bytes 491528 | tf_op jit(solution)/shard_map/ppermute | solution.py:661
  20.6 1.9 %all-to-all-done = f32[16,56,128]{2,1,0:T(8,128)S(1)} async-done(((f32[16,56,128]{2,1,0:T(8,128)}), f32[16,56,128]{2,1,0:T(8,128)S(1)}, u32[]{:S(2)}, u32[]{:S(2)}) %all-to-all-start) | async-done | bytes 458784 | tf_op jit(solution)/shard_map/all_to_all | solution.py:640
  22.4 0.9 %join.1 = f32[384,128]{1,0:T(8,128)} custom-call(f32[896,128]{1,0:T(8,128)S(1)} %bitcast.4), custom_call_target="tpu_custom_call" | custom-call | flops 1048576 | bytes 1048576 | tf_op jit(solution)/shard_map/join/pallas_call | solution.py:405
  23.4 0.0 collective-permute-done.1.one
  23.4 4.3 %all-to-all-start.1 = ((f32[16,24,128]{2,1,0:T(8,128)}), f32[16,24,128]{2,1,0:T(8,128)S(1)}, u32[]{:S(2)}, u32[]{:S(2)}) async-start(f32[16,24,128]{2,1,0:T(8,128)} %bitcast.2), calls=%async_computation.1 | async-start | bytes 393216 | tf_op jit(solution)/shard_map/all_to_all | solution.py:640
  27.7 0.0 collective-permute-done.3.yone
  27.7 0.0 collective-permute-done.2.two
  27.8 3.3 %block.1 = (f32[5,16,32,128]{3,2,1,0:T(8,128)S(1)}, f32[16,32,128]{2,1,0:T(8,128)S(1)}) custom-call(f32[32,8,128]{2,1,0:T(8,128)S(1)} %get-tuple-element.66.inner, f32[5,16,32,128]{3,2,1,0:T(8,128)} %s_hbm.2, f32[5,16,32,128]{3,2,1,0:T(8,128)} %f_hbm.2, f32[5,16,32,128]{3,2,1,0:T(8,128)} %fy_hbm, f32[5,4,32,128]{3,2,1,0:T(8,128)S(1)} %collective-permute-done.1.one, ...), custom_call_target="tpu_custom_call" | custom-call | flops 1073741824 | bytes 67108864 | tf_op jit(solution)/shard_map/block/pallas_call | solution.py:555
  31.1 3.8 %all-to-all-done.1 = f32[16,24,128]{2,1,0:T(8,128)S(1)} async-done(((f32[16,24,128]{2,1,0:T(8,128)}), f32[16,24,128]{2,1,0:T(8,128)S(1)}, u32[]{:S(2)}, u32[]{:S(2)}) %all-to-all-start.1) | async-done | bytes 196640 | tf_op jit(solution)/shard_map/all_to_all | solution.py:640
  34.9 0.1 split.1
  34.9 3.3 %collective-permute-start.5 = (f32[400,128]{1,0:T(8,128)S(1)}, f32[400,128]{1,0:T(8,128)S(1)}, u32[]{:S(2)}, u32[]{:S(2)}) collective-permute-start(f32[400,128]{1,0:T(8,128)S(1)} %get-tuple-element.81), channel_id=1, source_target_pairs={{0,4},{4,0},{8,12},{12,8},{16,20},{20,16},{24,28},{28,24},{32,36},... | collective-permute-start | bytes 614408 | tf_op jit(solution)/shard_map/ppermute | solution.py:669
  38.3 0.4 finish_own.1.base
  38.6 0.7 %collective-permute-done.5.got = f32[400,128]{1,0:T(8,128)S(1)} collective-permute-done((f32[400,128]{1,0:T(8,128)S(1)}, f32[400,128]{1,0:T(8,128)S(1)}, u32[]{:S(2)}, u32[]{:S(2)}) %collective-permute-start.5) | collective-permute-done | bytes 204832 | tf_op jit(solution)/shard_map/ppermute | solution.py:669
  39.3 1.2 %finish.1 = f32[5,16,32,128]{3,2,1,0:T(8,128)} custom-call(f32[35,8,128]{2,1,0:T(8,128)S(1)} %get-tuple-element.46.outer, f32[5,16,32,128]{3,2,1,0:T(8,128)S(1)} %finish_own.1.base, f32[16,32,128]{2,1,0:T(8,128)S(1)} %get-tuple-element.83.mxb, f32[400,128]{1,0:T(8,128)S(1)} %collective-permute-done.5.got, f32[328,128]{1,0:T(8,128)S(1)} %get-tuple-element.78.mids, ...), custom_call_target="tpu_custom_call" | custom-call | flops 4194304 | bytes 3145728 | tf_op jit(solution)/shard_map/finish/pallas_call | solution.py:626
  (5 shorter events, 0.0 us)
Async XLA Ops:
  1.8 2.9 %collective-permute-start = (f32[816,128]{1,0:T(8,128)S(1)}, f32[816,128]{1,0:T(8,128)S(1)}, u32[]{:S(2)}, u32[]{:S(2)}) collective-permute-start(f32[816,128]{1,0:T(8,128)S(1)} %get-tuple-element.49), channel_id=1, source_target_pairs={{0,4},{4,0},{8,12},{12,8},{16,20},{20,16},{24,28},{28,24},{32,36},... | collective-permute-start | bytes 1253384 | tf_op jit(solution)/shard_map/ppermute | solution.py:653
  5.6 22.1 %copy-start = (f32[16,32]{1,0:T(8,128)S(1)}, f32[16,32]{1,0:T(8,128)}, u32[]{:S(2)}) copy-start(f32[16,32]{1,0:T(8,128)} %mx.1) | copy-start | bytes 6148
  5.6 22.1 %copy-start.1 = (f32[16,32]{1,0:T(8,128)S(1)}, f32[16,32]{1,0:T(8,128)}, u32[]{:S(2)}) copy-start(f32[16,32]{1,0:T(8,128)} %my.1) | copy-start | bytes 6148
  5.6 16.8 %all-to-all-start = ((f32[16,56,128]{2,1,0:T(8,128)}), f32[16,56,128]{2,1,0:T(8,128)S(1)}, u32[]{:S(2)}, u32[]{:S(2)}) async-start(f32[16,56,128]{2,1,0:T(8,128)} %bitcast), calls=%async_computation | async-start | bytes 917504 | tf_op jit(solution)/shard_map/all_to_all | solution.py:640
  12.5 10.9 %collective-permute-start.1 = (f32[5,4,32,128]{3,2,1,0:T(8,128)S(1)}, f32[5,4,32,128]{3,2,1,0:T(8,128)S(1)}, u32[]{:S(2)}, u32[]{:S(2)}) collective-permute-start(f32[5,4,32,128]{3,2,1,0:T(8,128)S(1)} %get-tuple-element.64), channel_id=1, source_target_pairs={{0,4},{4,0},{8,12},{12,8},{16,20},{20,16},{24,28},{28,24},{32,36},... | collective-permute-start | bytes 983048 | tf_op jit(solution)/shard_map/ppermute | solution.py:658
  13.2 14.5 %collective-permute-start.2 = (f32[5,4,32,128]{3,2,1,0:T(8,128)S(1)}, f32[5,4,32,128]{3,2,1,0:T(8,128)S(1)}, u32[]{:S(2)}, u32[]{:S(2)}) collective-permute-start(f32[5,4,32,128]{3,2,1,0:T(8,128)S(1)} %get-tuple-element.68), channel_id=1, source_target_pairs={{4,8},{8,4},{12,16},{16,12},{20,24},{24,20},{28,32},{32,28},{36,40... | collective-permute-start | bytes 983048 | tf_op jit(solution)/shard_map/ppermute | solution.py:659
  16.6 11.1 %collective-permute-start.3 = (f32[5,8,8,128]{3,2,1,0:T(8,128)S(1)}, f32[5,8,8,128]{3,2,1,0:T(8,128)S(1)}, u32[]{:S(2)}, u32[]{:S(2)}) collective-permute-start(f32[5,8,8,128]{3,2,1,0:T(8,128)S(1)} %get-tuple-element.69), channel_id=1, source_target_pairs={{0,1},{1,0},{2,3},{3,2},{4,5},{5,4},{6,7},{7,6},{8,9},{9,8},{10,11... | collective-permute-start | bytes 491528 | tf_op jit(solution)/shard_map/ppermute | solution.py:660
  18.3 9.4 %collective-permute-start.4 = (f32[5,8,8,128]{3,2,1,0:T(8,128)S(1)}, f32[5,8,8,128]{3,2,1,0:T(8,128)S(1)}, u32[]{:S(2)}, u32[]{:S(2)}) collective-permute-start(f32[5,8,8,128]{3,2,1,0:T(8,128)S(1)} %get-tuple-element.70), channel_id=1, source_target_pairs={{0,3},{1,2},{2,1},{3,0},{4,7},{5,6},{6,5},{7,4},{8,11},{9,10},{10,... | collective-permute-start | bytes 491528 | tf_op jit(solution)/shard_map/ppermute | solution.py:661
  23.4 11.5 %all-to-all-start.1 = ((f32[16,24,128]{2,1,0:T(8,128)}), f32[16,24,128]{2,1,0:T(8,128)S(1)}, u32[]{:S(2)}, u32[]{:S(2)}) async-start(f32[16,24,128]{2,1,0:T(8,128)} %bitcast.2), calls=%async_computation.1 | async-start | bytes 393216 | tf_op jit(solution)/shard_map/all_to_all | solution.py:640
  34.9 4.4 %collective-permute-start.5 = (f32[400,128]{1,0:T(8,128)S(1)}, f32[400,128]{1,0:T(8,128)S(1)}, u32[]{:S(2)}, u32[]{:S(2)}) collective-permute-start(f32[400,128]{1,0:T(8,128)S(1)} %get-tuple-element.81), channel_id=1, source_target_pairs={{0,4},{4,0},{8,12},{12,8},{16,20},{20,16},{24,28},{28,24},{32,36},... | collective-permute-start | bytes 614408 | tf_op jit(solution)/shard_map/ppermute | solution.py:669

commit v12 on v8

--- a/solution.py
+++ b/solution.py
@@ -444,19 +444,19 @@
     )(outer, two)
 
 
-def split_body(z, mids, far_own, far_other, own, send):
+def split_body(z, mids, far_own, far_got, own, send):
     is0 = parity("gx") == 0
     c = CS["pair"]
     down = [jnp.broadcast_to(mids[pl.ds(4 * NV * HALF + k, 1), :], (SUB, NK)) for k in range(7)]
-    head_far, tail_far = jnp.where(is0, down[4], down[5]), jnp.where(is0, down[5], down[6])
     for r in range(HALF // SUB):
         for v in range(NV):
             lf, rf, ld, rd = (z[pl.ds(ROWS * SUB * r + NV * k + v, SUB, stride=ROWS), :] for k in range(4))
             head, tail, dhead, dtail = (mids[pl.ds((NV * k + v) * HALF + SUB * r, SUB), :] for k in range(4))
             part = pl.ds(v * HALF + SUB * r, SUB)
-            w = far_own[part, :]
-            head = (head + head_far * w) + down[0] * lf + down[1] * rf
-            tail = (tail + tail_far * w) + down[2] * lf + down[3] * rf
+            x, y = far_own[part, :], far_got[part, :]
+            fa, fb = jnp.where(is0, x, y), jnp.where(is0, y, x)
+            head = (head + down[4] * fa + down[5] * fb) + down[0] * lf + down[1] * rf
+            tail = (tail + down[5] * fa + down[6] * fb) + down[2] * lf + down[3] * rf
             dhead = dhead + c["down"][0] * ld + c["down"][1] * rd
             dtail = dtail + c["down"][2] * ld + c["down"][3] * rd
             a, b = (lf, head, ld, dhead), (tail, rf, dtail, rd)
@@ -464,13 +464,12 @@
                 rows = pl.ds((NV * k + v) * HALF + SUB * r, SUB)
                 own[rows, :] = jnp.where(is0, a[k], b[k])
                 send[rows, :] = jnp.where(is0, b[k], a[k])
-            send[pl.ds((4 * NV + v) * HALF + SUB * r, SUB), :] = far_other[part, :]
-
-
-def split(z, mids, far_own, far_other):
+
+
+def split(z, mids, far_own, far_got):
     vmem = pl.BlockSpec(memory_space=pltpu.VMEM)
     own = jax.ShapeDtypeStruct((4 * NV * HALF, NK), F32)
-    send = jax.ShapeDtypeStruct((5 * NV * HALF, NK), F32)
+    send = jax.ShapeDtypeStruct((4 * NV * HALF, NK), F32)
     return pl.pallas_call(
         split_body,
         out_shape=(own, send),
@@ -479,7 +478,7 @@
         compiler_params=pltpu.CompilerParams(vmem_limit_bytes=8 << 20),
         cost_estimate=pl.CostEstimate(flops=1 << 20, bytes_accessed=1 << 20, transcendentals=0),
         name="split",
-    )(z, mids, far_own, far_other)
+    )(z, mids, far_own, far_got)
 
 
 def block_body(inner, s_hbm, f_hbm, fy_hbm, one, two, yone, ytwo, mx, my, base, mxb, s, f, fy, pad, sem):
@@ -568,44 +567,43 @@
     )(inner, *in_hbm(state, flux_x, flux_y), one, two, yone, ytwo, mx, my)
 
 
-def finish_body(outer, base, mxb, own, got, mids, far_other, out_hbm, out, sem):
-    core = parity("gx")
-    is0 = core == 0
-    hl_inv, inv, tr_inv = (jnp.broadcast_to(mids[pl.ds(4 * NV * HALF + k, 1), :], (SUB, NK)) for k in (4, 5, 6))
-    zero = jnp.zeros((SUB, NK), F32)
-    own_far = (jnp.where(is0, zero, inv), jnp.where(is0, inv, zero))
-    got_far = (jnp.where(is0, zero, tr_inv), jnp.where(is0, hl_inv, zero))
-    stores = [pltpu.make_async_copy(out.at[v], out_hbm.at[v], sem.at[v]) for v in range(NV)]
+def add_outside(half, outer, base, mxb, z, out_hbm, out, sem):
+    target = pl.ds(pl.multiple_of(HALF * half, HALF), HALF)
+    stores = [pltpu.make_async_copy(out.at[v], out_hbm.at[v, :, target, :], sem.at[v]) for v in range(NV)]
     for v in range(NV):
-        for z, half, far_w, far_z, far_at in (
-            (own, core, own_far, got, 4 * NV),
-            (got, 1 - core, got_far, far_other, 0),
-        ):
-            for r in range(HALF // SUB):
-                rows = pl.ds(pl.multiple_of(HALF * half + SUB * r, SUB), SUB)
-                lf, rf, ld, rd = (z[pl.ds((NV * k + v) * HALF + SUB * r, SUB), :] for k in range(4))
-                w = far_z[pl.ds((far_at + v) * HALF + SUB * r, SUB), :]
-                lf, rf = lf + far_w[0] * w, rf + far_w[1] * w
-                for i in range(NI):
-                    d = float(CS["left"][i]) * ld + float(CS["right"][i]) * rd
-                    e = outer[C_LEFT + i] * lf + outer[C_RIGHT + i] * rf
-                    out[v, i, rows, :] = (base[v, i, rows, :] + e) + mxb[i, rows, :] * d
+        for r in range(HALF // SUB):
+            rows, part = pl.ds(pl.multiple_of(HALF * half + SUB * r, SUB), SUB), pl.ds(SUB * r, SUB)
+            lf, rf, ld, rd = (z[pl.ds((NV * k + v) * HALF + SUB * r, SUB), :] for k in range(4))
+            for i in range(NI):
+                d = float(CS["left"][i]) * ld + float(CS["right"][i]) * rd
+                e = outer[C_LEFT + i] * lf + outer[C_RIGHT + i] * rf
+                out[v, i, part, :] = (base[v, i, rows, :] + e) + mxb[i, rows, :] * d
         stores[v].start()
     for c in stores:
         c.wait()
 
 
-def finish(outer, base, mxb, own, got, mids, far_other):
-    return pl.pallas_call(
-        finish_body,
+def finish_own_body(outer, base, mxb, z, out_hbm, out, sem):
+    add_outside(parity("gx"), outer, base, mxb, z, out_hbm, out, sem)
+
+
+def finish_body(outer, base, mxb, z, written, out_hbm, out, sem):
+    add_outside(1 - parity("gx"), outer, base, mxb, z, out_hbm, out, sem)
+
+
+def finish(outer, base, mxb, z, *written):
+    vmem, hbm = pl.BlockSpec(memory_space=pltpu.VMEM), pl.BlockSpec(memory_space=pltpu.HBM)
+    return pl.pallas_call(
+        finish_body if written else finish_own_body,
         out_shape=jax.ShapeDtypeStruct((NV, NI, NJ, NK), F32),
-        in_specs=[pl.BlockSpec(memory_space=pltpu.VMEM)] * 7,
-        out_specs=pl.BlockSpec(memory_space=pltpu.HBM),
-        scratch_shapes=[pltpu.VMEM((NV, NI, NJ, NK), F32), pltpu.SemaphoreType.DMA((NV,))],
+        in_specs=[vmem] * 4 + [hbm] * len(written),
+        out_specs=hbm,
+        scratch_shapes=[pltpu.VMEM((NV, NI, HALF, NK), F32), pltpu.SemaphoreType.DMA((NV,))],
+        input_output_aliases={4: 0} if written else {},
         compiler_params=pltpu.CompilerParams(vmem_limit_bytes=12 << 20),
-        cost_estimate=pl.CostEstimate(flops=1 << 22, bytes_accessed=3 << 20, transcendentals=0),
-        name="finish",
-    )(outer, base, mxb, own, got, mids, far_other)
+        cost_estimate=pl.CostEstimate(flops=1 << 22, bytes_accessed=2 << 20, transcendentals=0),
+        name="finish" if written else "finish_own",
+    )(outer, base, mxb, z, *written)
 
 
 def exchange(x, rows):
@@ -635,12 +633,15 @@
     outside = join(ends)
     outside, one = lax.optimization_barrier((outside, one))
     two, yone, ytwo = lax.optimization_barrier((two, yone, ytwo))
-    far_own, far_other = far(outer, two)
     base, mxb = block(inner, state, flux_x, flux_y, one, two, yone, ytwo, metric_x, metric_y)
-    outside, base, mxb, far_own = lax.optimization_barrier((exchange(outside, ROWS), base, mxb, far_own))
-    own, send = split(outside, mids, far_own, far_other)
+    two, base = lax.optimization_barrier((two, base))
+    far_own, far_send = far(outer, two)
+    far_got = lax.ppermute(far_send, "gx", pair_in)
+    outside, base, mxb, far_got = lax.optimization_barrier((exchange(outside, ROWS), base, mxb, far_got))
+    own, send = split(outside, mids, far_own, far_got)
     got = lax.ppermute(send, "gx", pair_in)
-    return finish(outer, base, mxb, own, got, mids, far_other)
+    got, out = lax.optimization_barrier((got, finish(outer, base, mxb, own)))
+    return finish(outer, base, mxb, got, out)
 
 
 def solution(mesh):

time: 40.9 us -> 40.6 us (level)
  waiting for transfers between devices: 6.83 us -> 3.68 us
  starting transfers between devices: 24 us -> 26.2 us
  Pallas kernels: 9.52 us -> 10.2 us
    all_to_all x2, waiting for transfers between devices: 5.73 us -> 2.7 us  [exchange(): lax.all_to_all(x.reshape(PAIRS, rows, NK), 'gx', 0, 0, tiled=True, axis_i...]
    ppermute x0 -> x1, starting transfers between devices: none -> 2.21 us  [per_device(): far_got = lax.ppermute(far_send, 'gx', pair_in)]
    ppermute x2, waiting for transfers between devices: 1.08 us -> 0.1 us  [per_device(): got = lax.ppermute(send, 'gx', pair_in)]
    ppermute x0 -> x1, waiting for transfers between devices: none -> 0.87 us  [per_device(): far_got = lax.ppermute(far_send, 'gx', pair_in)]
    pallas_call x1 -> x2, Pallas kernels: 1.18 us -> 1.84 us  [finish(): pl.pallas_call(finish_body if written else finish_own_body, out_shape=jax...]
  transfers between devices with their start and end apart: 8 -> 9, of which waited for: 3 -> 4; matrix products, arithmetic and copies ran while one was open for 0% -> 0% of each run, Pallas kernels for 14% -> 16%
where the time goes in v12:
time: 40.6 us; the launch traced here: 40.2 us
  starting transfers between devices  26.2 us (65%)
  Pallas kernels  10.2 us (25%)
  waiting for transfers between devices  3.68 us (9%)
    all_to_all x2, starting transfers between devices, exchange(): lax.all_to_all(x.reshape(PAIRS, rows, NK), 'gx', 0, 0, tiled=True, axis_i...  11.1 us
    ppermute x2, starting transfers between devices, per_device(): got = lax.ppermute(send, 'gx', pair_in)  4.83 us
    ppermute x1, starting transfers between devices, per_device(): two = lax.ppermute(send_two, 'gx', pair_out)  3.37 us
    pallas_call x1, Pallas kernels, block(): pl.pallas_call(block_body, out_shape=(jax.ShapeDtypeStruct((NV, NI, NJ, N...  3.23 us
    all_to_all x2, waiting for transfers between devices, exchange(): lax.all_to_all(x.reshape(PAIRS, rows, NK), 'gx', 0, 0, tiled=True, axis_i...  2.7 us
    ppermute x1, starting transfers between devices, per_device(): ytwo = lax.ppermute(ysend_two, 'gy', y_out)  2.24 us
    ppermute x1, starting transfers between devices, per_device(): far_got = lax.ppermute(far_send, 'gx', pair_in)  2.21 us
    pallas_call x2, Pallas kernels, finish(): pl.pallas_call(finish_body if written else finish_own_body, out_shape=jax...  1.84 us
  transfers between devices with their start and end apart: 9, of which 4 were waited for; matrix products, arithmetic and copies ran while one was open for 0% of the time, Pallas kernels for 16%

profile of v12, /device:TPU:1, one launch (start us, length us, event | category | flops | bytes accessed | tf_op | source)
XLA Modules:
  0.0 40.2 jit_solution(1284169365100490638)
XLA Ops:
  0.0 1.8 %own_share.1 = (f32[32,8,128]{2,1,0:T(8,128)S(1)}, f32[35,8,128]{2,1,0:T(8,128)S(1)}, f32[816,128]{1,0:T(8,128)S(1)}, f32[816,128]{1,0:T(8,128)S(1)}) custom-call(f32[16]{0:T(128)} %gap_hbm.1, f32[5,16,32,128]{3,2,1,0:T(8,128)} %s_hbm.2, f32[5,16,32,128]{3,2,1,0:T(8,128)} %f_hbm.2), custom_call_target="tpu_custom_call" | custom-call | flops 16777216 | bytes 4194304 | tf_op jit(solution)/shard_map/own_share/pallas_call | solution.py:241
  1.8 1.5 %collective-permute-start = (f32[816,128]{1,0:T(8,128)S(1)}, f32[816,128]{1,0:T(8,128)S(1)}, u32[]{:S(2)}, u32[]{:S(2)}) collective-permute-start(f32[816,128]{1,0:T(8,128)S(1)} %get-tuple-element.51), channel_id=1, source_target_pairs={{0,4},{4,0},{8,12},{12,8},{16,20},{20,16},{24,28},{28,24},{32,36},... | collective-permute-start | bytes 1253384 | tf_op jit(solution)/shard_map/ppermute | solution.py:624
  3.3 1.4 %pack.1 = (f32[5,4,32,128]{3,2,1,0:T(8,128)S(1)}, f32[5,4,32,128]{3,2,1,0:T(8,128)S(1)}, f32[5,8,8,128]{3,2,1,0:T(8,128)S(1)}, f32[5,8,8,128]{3,2,1,0:T(8,128)S(1)}) custom-call(f32[5,16,32,128]{3,2,1,0:T(8,128)} %s_hbm.2, f32[5,16,32,128]{3,2,1,0:T(8,128)} %f_hbm.2, f32[5,16,32,128]{3,2,1,0:T(8,128)} %fy_hbm), custom_call_target="tpu_custom_call" | custom-call | bytes 2097152 | tf_op jit(solution)/shard_map/pack/pallas_call | solution.py:122
  4.7 0.0 copy-start
  4.8 0.0 copy-start.1
  4.8 0.9 %pair.1 = (f32[896,128]{1,0:T(8,128)}, f32[328,128]{1,0:T(8,128)S(1)}) custom-call(f32[816,128]{1,0:T(8,128)S(1)} %get-tuple-element.49.mine, f32[816,128]{1,0:T(8,128)S(1)} %collective-permute-done.got), custom_call_target="tpu_custom_call" | custom-call | flops 1048576 | bytes 1048576 | tf_op jit(solution)/shard_map/pair/pallas_call | solution.py:316
  5.6 6.8 %all-to-all-start = ((f32[16,56,128]{2,1,0:T(8,128)}), f32[16,56,128]{2,1,0:T(8,128)S(1)}, u32[]{:S(2)}, u32[]{:S(2)}) async-start(f32[16,56,128]{2,1,0:T(8,128)} %bitcast), calls=%async_computation | async-start | bytes 917504 | tf_op jit(solution)/shard_map/all_to_all | solution.py:611
  12.5 0.7 %collective-permute-start.1 = (f32[5,4,32,128]{3,2,1,0:T(8,128)S(1)}, f32[5,4,32,128]{3,2,1,0:T(8,128)S(1)}, u32[]{:S(2)}, u32[]{:S(2)}) collective-permute-start(f32[5,4,32,128]{3,2,1,0:T(8,128)S(1)} %get-tuple-element.66), channel_id=1, source_target_pairs={{0,4},{4,0},{8,12},{12,8},{16,20},{20,16},{24,28},{28,24},{32,36},... | collective-permute-start | bytes 983048 | tf_op jit(solution)/shard_map/ppermute | solution.py:629
  13.2 3.4 %collective-permute-start.2 = (f32[5,4,32,128]{3,2,1,0:T(8,128)S(1)}, f32[5,4,32,128]{3,2,1,0:T(8,128)S(1)}, u32[]{:S(2)}, u32[]{:S(2)}) collective-permute-start(f32[5,4,32,128]{3,2,1,0:T(8,128)S(1)} %get-tuple-element.68), channel_id=1, source_target_pairs={{4,8},{8,4},{12,16},{16,12},{20,24},{24,20},{28,32},{32,28},{36,40... | collective-permute-start | bytes 983048 | tf_op jit(solution)/shard_map/ppermute | solution.py:630
  16.6 1.7 %collective-permute-start.3 = (f32[5,8,8,128]{3,2,1,0:T(8,128)S(1)}, f32[5,8,8,128]{3,2,1,0:T(8,128)S(1)}, u32[]{:S(2)}, u32[]{:S(2)}) collective-permute-start(f32[5,8,8,128]{3,2,1,0:T(8,128)S(1)} %get-tuple-element.69), channel_id=1, source_target_pairs={{0,1},{1,0},{2,3},{3,2},{4,5},{5,4},{6,7},{7,6},{8,9},{9,8},{10,11... | collective-permute-start | bytes 491528 | tf_op jit(solution)/shard_map/ppermute | solution.py:631
  18.3 2.2 %collective-permute-start.4 = (f32[5,8,8,128]{3,2,1,0:T(8,128)S(1)}, f32[5,8,8,128]{3,2,1,0:T(8,128)S(1)}, u32[]{:S(2)}, u32[]{:S(2)}) collective-permute-start(f32[5,8,8,128]{3,2,1,0:T(8,128)S(1)} %get-tuple-element.70), channel_id=1, source_target_pairs={{0,3},{1,2},{2,1},{3,0},{4,7},{5,6},{6,5},{7,4},{8,11},{9,10},{10,... | collective-permute-start | bytes 491528 | tf_op jit(solution)/shard_map/ppermute | solution.py:632
  20.5 1.9 %all-to-all-done = f32[16,56,128]{2,1,0:T(8,128)S(1)} async-done(((f32[16,56,128]{2,1,0:T(8,128)}), f32[16,56,128]{2,1,0:T(8,128)S(1)}, u32[]{:S(2)}, u32[]{:S(2)}) %all-to-all-start) | async-done | bytes 458784 | tf_op jit(solution)/shard_map/all_to_all | solution.py:611
  22.5 0.9 %join.1 = f32[384,128]{1,0:T(8,128)} custom-call(f32[896,128]{1,0:T(8,128)S(1)} %bitcast.4), custom_call_target="tpu_custom_call" | custom-call | flops 1048576 | bytes 1048576 | tf_op jit(solution)/shard_map/join/pallas_call | solution.py:405
  23.4 4.3 %all-to-all-start.1 = ((f32[16,24,128]{2,1,0:T(8,128)}), f32[16,24,128]{2,1,0:T(8,128)S(1)}, u32[]{:S(2)}, u32[]{:S(2)}) async-start(f32[16,24,128]{2,1,0:T(8,128)} %bitcast.2), calls=%async_computation.1 | async-start | bytes 393216 | tf_op jit(solution)/shard_map/all_to_all | solution.py:611
  27.7 0.0 collective-permute-done.4.ytwo
  27.7 3.2 %block.1 = (f32[5,16,32,128]{3,2,1,0:T(8,128)S(1)}, f32[16,32,128]{2,1,0:T(8,128)S(1)}) custom-call(f32[32,8,128]{2,1,0:T(8,128)S(1)} %get-tuple-element.72.inner, f32[5,16,32,128]{3,2,1,0:T(8,128)} %s_hbm.2, f32[5,16,32,128]{3,2,1,0:T(8,128)} %f_hbm.2, f32[5,16,32,128]{3,2,1,0:T(8,128)} %fy_hbm, f32[5,4,32,128]{3,2,1,0:T(8,128)S(1)} %collective-permute-done.1.one, ...), custom_call_target="tpu_custom_call" | custom-call | flops 1073741824 | bytes 67108864 | tf_op jit(solution)/shard_map/block/pallas_call | solution.py:554
  31.0 2.2 %collective-permute-start.5 = (f32[80,128]{1,0:T(8,128)S(1)}, f32[80,128]{1,0:T(8,128)S(1)}, u32[]{:S(2)}, u32[]{:S(2)}) collective-permute-start(f32[80,128]{1,0:T(8,128)S(1)} %get-tuple-element.80), channel_id=1, source_target_pairs={{0,4},{4,0},{8,12},{12,8},{16,20},{20,16},{24,28},{28,24},{32,36},... | collective-permute-start | bytes 122888 | tf_op jit(solution)/shard_map/ppermute | solution.py:639
  33.2 0.9 %collective-permute-done.5.far_got = f32[80,128]{1,0:T(8,128)S(1)} collective-permute-done((f32[80,128]{1,0:T(8,128)S(1)}, f32[80,128]{1,0:T(8,128)S(1)}, u32[]{:S(2)}, u32[]{:S(2)}) %collective-permute-start.5) | collective-permute-done | bytes 40992 | tf_op jit(solution)/shard_map/ppermute | solution.py:639
  34.1 0.8 %all-to-all-done.1 = f32[16,24,128]{2,1,0:T(8,128)S(1)} async-done(((f32[16,24,128]{2,1,0:T(8,128)}), f32[16,24,128]{2,1,0:T(8,128)S(1)}, u32[]{:S(2)}, u32[]{:S(2)}) %all-to-all-start.1) | async-done | bytes 196640 | tf_op jit(solution)/shard_map/all_to_all | solution.py:611
  34.9 0.1 split.1
  34.9 3.3 %collective-permute-start.6 = (f32[320,128]{1,0:T(8,128)S(1)}, f32[320,128]{1,0:T(8,128)S(1)}, u32[]{:S(2)}, u32[]{:S(2)}) collective-permute-start(f32[320,128]{1,0:T(8,128)S(1)} %get-tuple-element.87), channel_id=1, source_target_pairs={{0,4},{4,0},{8,12},{12,8},{16,20},{20,16},{24,28},{28,24},{32,36},... | collective-permute-start | bytes 491528 | tf_op jit(solution)/shard_map/ppermute | solution.py:642
  38.3 0.9 %finish_own.1.written = f32[5,16,32,128]{3,2,1,0:T(8,128)} custom-call(f32[35,8,128]{2,1,0:T(8,128)S(1)} %get-tuple-element.48.outer, f32[5,16,32,128]{3,2,1,0:T(8,128)S(1)} %get-tuple-element.81.base, f32[16,32,128]{2,1,0:T(8,128)S(1)} %get-tuple-element.82.mxb, f32[320,128]{1,0:T(8,128)S(1)} %get-tuple-element.88.z), custom_call_target="tpu_custom_call" | custom-call | flops 4194304 | bytes 2097152 | tf_op jit(solution)/shard_map/finish_own/pallas_call | solution.py:596
  39.2 0.1 collective-permute-done.6.z
  39.3 0.9 %finish.1 = f32[5,16,32,128]{3,2,1,0:T(8,128)} custom-call(f32[35,8,128]{2,1,0:T(8,128)S(1)} %get-tuple-element.48.outer, f32[5,16,32,128]{3,2,1,0:T(8,128)S(1)} %get-tuple-element.81.base, f32[16,32,128]{2,1,0:T(8,128)S(1)} %get-tuple-element.82.mxb, f32[320,128]{1,0:T(8,128)S(1)} %collective-permute-done.6.z, ...), custom_call_target="tpu_custom_call", output_to_operand_aliasing={{}: (4, {})} | custom-call | flops 4194304 | bytes 2097152 | tf_op jit(solution)/shard_map/finish/pallas_call | solution.py:596
  (7 shorter events, 0.0 us)
Async XLA Ops:
  1.8 2.9 %collective-permute-start = (f32[816,128]{1,0:T(8,128)S(1)}, f32[816,128]{1,0:T(8,128)S(1)}, u32[]{:S(2)}, u32[]{:S(2)}) collective-permute-start(f32[816,128]{1,0:T(8,128)S(1)} %get-tuple-element.51), channel_id=1, source_target_pairs={{0,4},{4,0},{8,12},{12,8},{16,20},{20,16},{24,28},{28,24},{32,36},... | collective-permute-start | bytes 1253384 | tf_op jit(solution)/shard_map/ppermute | solution.py:624
  4.7 23.0 %copy-start = (f32[16,32]{1,0:T(8,128)S(1)}, f32[16,32]{1,0:T(8,128)}, u32[]{:S(2)}) copy-start(f32[16,32]{1,0:T(8,128)} %mx.1) | copy-start | bytes 6148
  4.8 23.0 %copy-start.1 = (f32[16,32]{1,0:T(8,128)S(1)}, f32[16,32]{1,0:T(8,128)}, u32[]{:S(2)}) copy-start(f32[16,32]{1,0:T(8,128)} %my.1) | copy-start | bytes 6148
  5.6 16.8 %all-to-all-start = ((f32[16,56,128]{2,1,0:T(8,128)}), f32[16,56,128]{2,1,0:T(8,128)S(1)}, u32[]{:S(2)}, u32[]{:S(2)}) async-start(f32[16,56,128]{2,1,0:T(8,128)} %bitcast), calls=%async_computation | async-start | bytes 917504 | tf_op jit(solution)/shard_map/all_to_all | solution.py:611
  12.5 10.9 %collective-permute-start.1 = (f32[5,4,32,128]{3,2,1,0:T(8,128)S(1)}, f32[5,4,32,128]{3,2,1,0:T(8,128)S(1)}, u32[]{:S(2)}, u32[]{:S(2)}) collective-permute-start(f32[5,4,32,128]{3,2,1,0:T(8,128)S(1)} %get-tuple-element.66), channel_id=1, source_target_pairs={{0,4},{4,0},{8,12},{12,8},{16,20},{20,16},{24,28},{28,24},{32,36},... | collective-permute-start | bytes 983048 | tf_op jit(solution)/shard_map/ppermute | solution.py:629
  13.2 14.5 %collective-permute-start.2 = (f32[5,4,32,128]{3,2,1,0:T(8,128)S(1)}, f32[5,4,32,128]{3,2,1,0:T(8,128)S(1)}, u32[]{:S(2)}, u32[]{:S(2)}) collective-permute-start(f32[5,4,32,128]{3,2,1,0:T(8,128)S(1)} %get-tuple-element.68), channel_id=1, source_target_pairs={{4,8},{8,4},{12,16},{16,12},{20,24},{24,20},{28,32},{32,28},{36,40... | collective-permute-start | bytes 983048 | tf_op jit(solution)/shard_map/ppermute | solution.py:630
  16.6 11.1 %collective-permute-start.3 = (f32[5,8,8,128]{3,2,1,0:T(8,128)S(1)}, f32[5,8,8,128]{3,2,1,0:T(8,128)S(1)}, u32[]{:S(2)}, u32[]{:S(2)}) collective-permute-start(f32[5,8,8,128]{3,2,1,0:T(8,128)S(1)} %get-tuple-element.69), channel_id=1, source_target_pairs={{0,1},{1,0},{2,3},{3,2},{4,5},{5,4},{6,7},{7,6},{8,9},{9,8},{10,11... | collective-permute-start | bytes 491528 | tf_op jit(solution)/shard_map/ppermute | solution.py:631
  18.3 9.4 %collective-permute-start.4 = (f32[5,8,8,128]{3,2,1,0:T(8,128)S(1)}, f32[5,8,8,128]{3,2,1,0:T(8,128)S(1)}, u32[]{:S(2)}, u32[]{:S(2)}) collective-permute-start(f32[5,8,8,128]{3,2,1,0:T(8,128)S(1)} %get-tuple-element.70), channel_id=1, source_target_pairs={{0,3},{1,2},{2,1},{3,0},{4,7},{5,6},{6,5},{7,4},{8,11},{9,10},{10,... | collective-permute-start | bytes 491528 | tf_op jit(solution)/shard_map/ppermute | solution.py:632
  23.4 11.5 %all-to-all-start.1 = ((f32[16,24,128]{2,1,0:T(8,128)}), f32[16,24,128]{2,1,0:T(8,128)S(1)}, u32[]{:S(2)}, u32[]{:S(2)}) async-start(f32[16,24,128]{2,1,0:T(8,128)} %bitcast.2), calls=%async_computation.1 | async-start | bytes 393216 | tf_op jit(solution)/shard_map/all_to_all | solution.py:611
  31.0 3.1 %collective-permute-start.5 = (f32[80,128]{1,0:T(8,128)S(1)}, f32[80,128]{1,0:T(8,128)S(1)}, u32[]{:S(2)}, u32[]{:S(2)}) collective-permute-start(f32[80,128]{1,0:T(8,128)S(1)} %get-tuple-element.80), channel_id=1, source_target_pairs={{0,4},{4,0},{8,12},{12,8},{16,20},{20,16},{24,28},{28,24},{32,36},... | collective-permute-start | bytes 122888 | tf_op jit(solution)/shard_map/ppermute | solution.py:639
  34.9 4.4 %collective-permute-start.6 = (f32[320,128]{1,0:T(8,128)S(1)}, f32[320,128]{1,0:T(8,128)S(1)}, u32[]{:S(2)}, u32[]{:S(2)}) collective-permute-start(f32[320,128]{1,0:T(8,128)S(1)} %get-tuple-element.87), channel_id=1, source_target_pairs={{0,4},{4,0},{8,12},{12,8},{16,20},{20,16},{24,28},{28,24},{32,36},... | collective-permute-start | bytes 491528 | tf_op jit(solution)/shard_map/ppermute | solution.py:642

commit v13 on v12

--- a/solution.py
+++ b/solution.py
@@ -68,14 +68,18 @@
     return lax.rem(lax.axis_index(name), 2)
 
 
-def pack_body(s, f, fy, one, two, yone, ytwo, lo, hi, sem):
+def pack_body(s, f, fy, one, two, yone, ytwo, lo, hi, sem, y_sem):
     core, odd = parity("gx"), parity("gy")
     copies = [
-        pltpu.make_async_copy(fy.at[:, :, 0:SUB, :], lo, sem.at[0]),
-        pltpu.make_async_copy(fy.at[:, :, NJ - SUB : NJ, :], hi, sem.at[1]),
+        (
+            pltpu.make_async_copy(fy.at[v, :, 0:SUB, :], lo.at[v], y_sem.at[0, v]),
+            pltpu.make_async_copy(fy.at[v, :, NJ - SUB : NJ, :], hi.at[v], y_sem.at[1, v]),
+        )
+        for v in range(NV)
     ]
-    for c in copies:
-        c.start()
+    for both in copies:
+        for c in both:
+            c.start()
 
     def faces(right, left):
         moves = [
@@ -91,6 +95,8 @@
 
     def rows(top, bottom):
         for v in range(NV):
+            for c in copies[v]:
+                c.wait()
             for i in range(NI):
                 part = pl.ds(4 * (i % 2), 4)
                 top[v, i // 2, part, :] = hi[v, i, 4:8, :]
@@ -103,9 +109,6 @@
     @pl.when(core == 1)
     def _():
         faces(two, one)
-
-    for c in copies:
-        c.wait()
 
     @pl.when(odd == 0)
     def _():
@@ -128,6 +131,7 @@
             pltpu.VMEM((NV, NI, SUB, NK), F32),
             pltpu.VMEM((NV, NI, SUB, NK), F32),
             pltpu.SemaphoreType.DMA((6,)),
+            pltpu.SemaphoreType.DMA((2, NV)),
         ],
         compiler_params=pltpu.CompilerParams(vmem_limit_bytes=8 << 20),
         cost_estimate=pl.CostEstimate(flops=0, bytes_accessed=2 << 20, transcendentals=0),

time: 40.6 us -> 40.6 us (level)
  starting transfers between devices: 26.2 us -> 25.6 us
  waiting for transfers between devices: 3.68 us -> 4.12 us
    all_to_all x2, starting transfers between devices: 11.1 us -> 10.7 us  [exchange(): lax.all_to_all(x.reshape(PAIRS, rows, NK), 'gx', 0, 0, tiled=True, axis_i...]
    all_to_all x2, waiting for transfers between devices: 2.7 us -> 3.14 us  [exchange(): lax.all_to_all(x.reshape(PAIRS, rows, NK), 'gx', 0, 0, tiled=True, axis_i...]
  transfers between devices with their start and end apart: 9 -> 9, of which waited for: 4 -> 4; matrix products, arithmetic and copies ran while one was open for 0% -> 0% of each run, Pallas kernels for 16% -> 17%
where the time goes in v13:
time: 40.6 us; the launch traced here: 40.2 us
  starting transfers between devices  25.6 us (63%)
  Pallas kernels  10.4 us (26%)
  waiting for transfers between devices  4.12 us (10%)
    all_to_all x2, starting transfers between devices, exchange(): lax.all_to_all(x.reshape(PAIRS, rows, NK), 'gx', 0, 0, tiled=True, axis_i...  10.7 us
    ppermute x2, starting transfers between devices, per_device(): got = lax.ppermute(send, 'gx', pair_in)  4.84 us
    ppermute x1, starting transfers between devices, per_device(): two = lax.ppermute(send_two, 'gx', pair_out)  3.37 us
    pallas_call x1, Pallas kernels, block(): pl.pallas_call(block_body, out_shape=(jax.ShapeDtypeStruct((NV, NI, NJ, N...  3.23 us
    all_to_all x2, waiting for transfers between devices, exchange(): lax.all_to_all(x.reshape(PAIRS, rows, NK), 'gx', 0, 0, tiled=True, axis_i...  3.14 us
    ppermute x1, starting transfers between devices, per_device(): ytwo = lax.ppermute(ysend_two, 'gy', y_out)  2.24 us
    ppermute x1, starting transfers between devices, per_device(): far_got = lax.ppermute(far_send, 'gx', pair_in)  2.22 us
    pallas_call x2, Pallas kernels, finish(): pl.pallas_call(finish_body if written else finish_own_body, out_shape=jax...  1.84 us
  transfers between devices with their start and end apart: 9, of which 4 were waited for; matrix products, arithmetic and copies ran while one was open for 0% of the time, Pallas kernels for 17%

profile of v13, /device:TPU:1, one launch (start us, length us, event | category | flops | bytes accessed | tf_op | source)
XLA Modules:
  0.0 40.2 jit_solution(8893561788183625959)
XLA Ops:
  0.0 1.8 %own_share.1 = (f32[32,8,128]{2,1,0:T(8,128)S(1)}, f32[35,8,128]{2,1,0:T(8,128)S(1)}, f32[816,128]{1,0:T(8,128)S(1)}, f32[816,128]{1,0:T(8,128)S(1)}) custom-call(f32[16]{0:T(128)} %gap_hbm.1, f32[5,16,32,128]{3,2,1,0:T(8,128)} %s_hbm.2, f32[5,16,32,128]{3,2,1,0:T(8,128)} %f_hbm.2), custom_call_target="tpu_custom_call" | custom-call | flops 16777216 | bytes 4194304 | tf_op jit(solution)/shard_map/own_share/pallas_call | solution.py:245
  1.8 1.5 %collective-permute-start = (f32[816,128]{1,0:T(8,128)S(1)}, f32[816,128]{1,0:T(8,128)S(1)}, u32[]{:S(2)}, u32[]{:S(2)}) collective-permute-start(f32[816,128]{1,0:T(8,128)S(1)} %get-tuple-element.51), channel_id=1, source_target_pairs={{0,4},{4,0},{8,12},{12,8},{16,20},{20,16},{24,28},{28,24},{32,36},... | collective-permute-start | bytes 1253384 | tf_op jit(solution)/shard_map/ppermute | solution.py:628
  3.3 1.6 %pack.1 = (f32[5,4,32,128]{3,2,1,0:T(8,128)S(1)}, f32[5,4,32,128]{3,2,1,0:T(8,128)S(1)}, f32[5,8,8,128]{3,2,1,0:T(8,128)S(1)}, f32[5,8,8,128]{3,2,1,0:T(8,128)S(1)}) custom-call(f32[5,16,32,128]{3,2,1,0:T(8,128)} %s_hbm.2, f32[5,16,32,128]{3,2,1,0:T(8,128)} %f_hbm.2, f32[5,16,32,128]{3,2,1,0:T(8,128)} %fy_hbm), custom_call_target="tpu_custom_call" | custom-call | bytes 2097152 | tf_op jit(solution)/shard_map/pack/pallas_call | solution.py:125
  5.0 0.0 copy-start
  5.0 0.0 copy-start.1
  5.0 0.9 %pair.1 = (f32[896,128]{1,0:T(8,128)}, f32[328,128]{1,0:T(8,128)S(1)}) custom-call(f32[816,128]{1,0:T(8,128)S(1)} %get-tuple-element.49.mine, f32[816,128]{1,0:T(8,128)S(1)} %collective-permute-done.got), custom_call_target="tpu_custom_call" | custom-call | flops 1048576 | bytes 1048576 | tf_op jit(solution)/shard_map/pair/pallas_call | solution.py:320
  5.8 6.8 %all-to-all-start = ((f32[16,56,128]{2,1,0:T(8,128)}), f32[16,56,128]{2,1,0:T(8,128)S(1)}, u32[]{:S(2)}, u32[]{:S(2)}) async-start(f32[16,56,128]{2,1,0:T(8,128)} %bitcast), calls=%async_computation | async-start | bytes 917504 | tf_op jit(solution)/shard_map/all_to_all | solution.py:615
  12.7 0.5 %collective-permute-start.1 = (f32[5,4,32,128]{3,2,1,0:T(8,128)S(1)}, f32[5,4,32,128]{3,2,1,0:T(8,128)S(1)}, u32[]{:S(2)}, u32[]{:S(2)}) collective-permute-start(f32[5,4,32,128]{3,2,1,0:T(8,128)S(1)} %get-tuple-element.66), channel_id=1, source_target_pairs={{0,4},{4,0},{8,12},{12,8},{16,20},{20,16},{24,28},{28,24},{32,36},... | collective-permute-start | bytes 983048 | tf_op jit(solution)/shard_map/ppermute | solution.py:633
  13.2 3.4 %collective-permute-start.2 = (f32[5,4,32,128]{3,2,1,0:T(8,128)S(1)}, f32[5,4,32,128]{3,2,1,0:T(8,128)S(1)}, u32[]{:S(2)}, u32[]{:S(2)}) collective-permute-start(f32[5,4,32,128]{3,2,1,0:T(8,128)S(1)} %get-tuple-element.68), channel_id=1, source_target_pairs={{4,8},{8,4},{12,16},{16,12},{20,24},{24,20},{28,32},{32,28},{36,40... | collective-permute-start | bytes 983048 | tf_op jit(solution)/shard_map/ppermute | solution.py:634
  16.6 1.7 %collective-permute-start.3 = (f32[5,8,8,128]{3,2,1,0:T(8,128)S(1)}, f32[5,8,8,128]{3,2,1,0:T(8,128)S(1)}, u32[]{:S(2)}, u32[]{:S(2)}) collective-permute-start(f32[5,8,8,128]{3,2,1,0:T(8,128)S(1)} %get-tuple-element.69), channel_id=1, source_target_pairs={{0,1},{1,0},{2,3},{3,2},{4,5},{5,4},{6,7},{7,6},{8,9},{9,8},{10,11... | collective-permute-start | bytes 491528 | tf_op jit(solution)/shard_map/ppermute | solution.py:635
  18.3 2.2 %collective-permute-start.4 = (f32[5,8,8,128]{3,2,1,0:T(8,128)S(1)}, f32[5,8,8,128]{3,2,1,0:T(8,128)S(1)}, u32[]{:S(2)}, u32[]{:S(2)}) collective-permute-start(f32[5,8,8,128]{3,2,1,0:T(8,128)S(1)} %get-tuple-element.70), channel_id=1, source_target_pairs={{0,3},{1,2},{2,1},{3,0},{4,7},{5,6},{6,5},{7,4},{8,11},{9,10},{10,... | collective-permute-start | bytes 491528 | tf_op jit(solution)/shard_map/ppermute | solution.py:636
  20.6 2.4 %all-to-all-done = f32[16,56,128]{2,1,0:T(8,128)S(1)} async-done(((f32[16,56,128]{2,1,0:T(8,128)}), f32[16,56,128]{2,1,0:T(8,128)S(1)}, u32[]{:S(2)}, u32[]{:S(2)}) %all-to-all-start) | async-done | bytes 458784 | tf_op jit(solution)/shard_map/all_to_all | solution.py:615
  22.9 0.9 %join.1 = f32[384,128]{1,0:T(8,128)} custom-call(f32[896,128]{1,0:T(8,128)S(1)} %bitcast.4), custom_call_target="tpu_custom_call" | custom-call | flops 1048576 | bytes 1048576 | tf_op jit(solution)/shard_map/join/pallas_call | solution.py:409
  23.9 3.8 %all-to-all-start.1 = ((f32[16,24,128]{2,1,0:T(8,128)}), f32[16,24,128]{2,1,0:T(8,128)S(1)}, u32[]{:S(2)}, u32[]{:S(2)}) async-start(f32[16,24,128]{2,1,0:T(8,128)} %bitcast.2), calls=%async_computation.1 | async-start | bytes 393216 | tf_op jit(solution)/shard_map/all_to_all | solution.py:615
  27.7 0.0 collective-permute-done.4.ytwo
  27.7 3.2 %block.1 = (f32[5,16,32,128]{3,2,1,0:T(8,128)S(1)}, f32[16,32,128]{2,1,0:T(8,128)S(1)}) custom-call(f32[32,8,128]{2,1,0:T(8,128)S(1)} %get-tuple-element.72.inner, f32[5,16,32,128]{3,2,1,0:T(8,128)} %s_hbm.2, f32[5,16,32,128]{3,2,1,0:T(8,128)} %f_hbm.2, f32[5,16,32,128]{3,2,1,0:T(8,128)} %fy_hbm, f32[5,4,32,128]{3,2,1,0:T(8,128)S(1)} %collective-permute-done.1.one, ...), custom_call_target="tpu_custom_call" | custom-call | flops 1073741824 | bytes 67108864 | tf_op jit(solution)/shard_map/block/pallas_call | solution.py:558
  31.0 2.2 %collective-permute-start.5 = (f32[80,128]{1,0:T(8,128)S(1)}, f32[80,128]{1,0:T(8,128)S(1)}, u32[]{:S(2)}, u32[]{:S(2)}) collective-permute-start(f32[80,128]{1,0:T(8,128)S(1)} %get-tuple-element.80), channel_id=1, source_target_pairs={{0,4},{4,0},{8,12},{12,8},{16,20},{20,16},{24,28},{28,24},{32,36},... | collective-permute-start | bytes 122888 | tf_op jit(solution)/shard_map/ppermute | solution.py:643
  33.2 0.9 %collective-permute-done.5.far_got = f32[80,128]{1,0:T(8,128)S(1)} collective-permute-done((f32[80,128]{1,0:T(8,128)S(1)}, f32[80,128]{1,0:T(8,128)S(1)}, u32[]{:S(2)}, u32[]{:S(2)}) %collective-permute-start.5) | collective-permute-done | bytes 40992 | tf_op jit(solution)/shard_map/ppermute | solution.py:643
  34.1 0.8 %all-to-all-done.1 = f32[16,24,128]{2,1,0:T(8,128)S(1)} async-done(((f32[16,24,128]{2,1,0:T(8,128)}), f32[16,24,128]{2,1,0:T(8,128)S(1)}, u32[]{:S(2)}, u32[]{:S(2)}) %all-to-all-start.1) | async-done | bytes 196640 | tf_op jit(solution)/shard_map/all_to_all | solution.py:615
  34.9 0.1 split.1
  35.0 3.3 %collective-permute-start.6 = (f32[320,128]{1,0:T(8,128)S(1)}, f32[320,128]{1,0:T(8,128)S(1)}, u32[]{:S(2)}, u32[]{:S(2)}) collective-permute-start(f32[320,128]{1,0:T(8,128)S(1)} %get-tuple-element.87), channel_id=1, source_target_pairs={{0,4},{4,0},{8,12},{12,8},{16,20},{20,16},{24,28},{28,24},{32,36},... | collective-permute-start | bytes 491528 | tf_op jit(solution)/shard_map/ppermute | solution.py:646
  38.3 0.9 %finish_own.1.written = f32[5,16,32,128]{3,2,1,0:T(8,128)} custom-call(f32[35,8,128]{2,1,0:T(8,128)S(1)} %get-tuple-element.48.outer, f32[5,16,32,128]{3,2,1,0:T(8,128)S(1)} %get-tuple-element.81.base, f32[16,32,128]{2,1,0:T(8,128)S(1)} %get-tuple-element.82.mxb, f32[320,128]{1,0:T(8,128)S(1)} %get-tuple-element.88.z), custom_call_target="tpu_custom_call" | custom-call | flops 4194304 | bytes 2097152 | tf_op jit(solution)/shard_map/finish_own/pallas_call | solution.py:600
  39.2 0.1 collective-permute-done.6.z
  39.3 0.9 %finish.1 = f32[5,16,32,128]{3,2,1,0:T(8,128)} custom-call(f32[35,8,128]{2,1,0:T(8,128)S(1)} %get-tuple-element.48.outer, f32[5,16,32,128]{3,2,1,0:T(8,128)S(1)} %get-tuple-element.81.base, f32[16,32,128]{2,1,0:T(8,128)S(1)} %get-tuple-element.82.mxb, f32[320,128]{1,0:T(8,128)S(1)} %collective-permute-done.6.z, ...), custom_call_target="tpu_custom_call", output_to_operand_aliasing={{}: (4, {})} | custom-call | flops 4194304 | bytes 2097152 | tf_op jit(solution)/shard_map/finish/pallas_call | solution.py:600
  (7 shorter events, 0.0 us)
Async XLA Ops:
  1.8 3.1 %collective-permute-start = (f32[816,128]{1,0:T(8,128)S(1)}, f32[816,128]{1,0:T(8,128)S(1)}, u32[]{:S(2)}, u32[]{:S(2)}) collective-permute-start(f32[816,128]{1,0:T(8,128)S(1)} %get-tuple-element.51), channel_id=1, source_target_pairs={{0,4},{4,0},{8,12},{12,8},{16,20},{20,16},{24,28},{28,24},{32,36},... | collective-permute-start | bytes 1253384 | tf_op jit(solution)/shard_map/ppermute | solution.py:628
  5.0 22.8 %copy-start = (f32[16,32]{1,0:T(8,128)S(1)}, f32[16,32]{1,0:T(8,128)}, u32[]{:S(2)}) copy-start(f32[16,32]{1,0:T(8,128)} %mx.1) | copy-start | bytes 6148
  5.0 22.8 %copy-start.1 = (f32[16,32]{1,0:T(8,128)S(1)}, f32[16,32]{1,0:T(8,128)}, u32[]{:S(2)}) copy-start(f32[16,32]{1,0:T(8,128)} %my.1) | copy-start | bytes 6148
  5.8 17.1 %all-to-all-start = ((f32[16,56,128]{2,1,0:T(8,128)}), f32[16,56,128]{2,1,0:T(8,128)S(1)}, u32[]{:S(2)}, u32[]{:S(2)}) async-start(f32[16,56,128]{2,1,0:T(8,128)} %bitcast), calls=%async_computation | async-start | bytes 917504 | tf_op jit(solution)/shard_map/all_to_all | solution.py:615
  12.7 11.2 %collective-permute-start.1 = (f32[5,4,32,128]{3,2,1,0:T(8,128)S(1)}, f32[5,4,32,128]{3,2,1,0:T(8,128)S(1)}, u32[]{:S(2)}, u32[]{:S(2)}) collective-permute-start(f32[5,4,32,128]{3,2,1,0:T(8,128)S(1)} %get-tuple-element.66), channel_id=1, source_target_pairs={{0,4},{4,0},{8,12},{12,8},{16,20},{20,16},{24,28},{28,24},{32,36},... | collective-permute-start | bytes 983048 | tf_op jit(solution)/shard_map/ppermute | solution.py:633
  13.2 14.5 %collective-permute-start.2 = (f32[5,4,32,128]{3,2,1,0:T(8,128)S(1)}, f32[5,4,32,128]{3,2,1,0:T(8,128)S(1)}, u32[]{:S(2)}, u32[]{:S(2)}) collective-permute-start(f32[5,4,32,128]{3,2,1,0:T(8,128)S(1)} %get-tuple-element.68), channel_id=1, source_target_pairs={{4,8},{8,4},{12,16},{16,12},{20,24},{24,20},{28,32},{32,28},{36,40... | collective-permute-start | bytes 983048 | tf_op jit(solution)/shard_map/ppermute | solution.py:634
  16.6 11.1 %collective-permute-start.3 = (f32[5,8,8,128]{3,2,1,0:T(8,128)S(1)}, f32[5,8,8,128]{3,2,1,0:T(8,128)S(1)}, u32[]{:S(2)}, u32[]{:S(2)}) collective-permute-start(f32[5,8,8,128]{3,2,1,0:T(8,128)S(1)} %get-tuple-element.69), channel_id=1, source_target_pairs={{0,1},{1,0},{2,3},{3,2},{4,5},{5,4},{6,7},{7,6},{8,9},{9,8},{10,11... | collective-permute-start | bytes 491528 | tf_op jit(solution)/shard_map/ppermute | solution.py:635
  18.3 9.4 %collective-permute-start.4 = (f32[5,8,8,128]{3,2,1,0:T(8,128)S(1)}, f32[5,8,8,128]{3,2,1,0:T(8,128)S(1)}, u32[]{:S(2)}, u32[]{:S(2)}) collective-permute-start(f32[5,8,8,128]{3,2,1,0:T(8,128)S(1)} %get-tuple-element.70), channel_id=1, source_target_pairs={{0,3},{1,2},{2,1},{3,0},{4,7},{5,6},{6,5},{7,4},{8,11},{9,10},{10,... | collective-permute-start | bytes 491528 | tf_op jit(solution)/shard_map/ppermute | solution.py:636
  23.9 11.0 %all-to-all-start.1 = ((f32[16,24,128]{2,1,0:T(8,128)}), f32[16,24,128]{2,1,0:T(8,128)S(1)}, u32[]{:S(2)}, u32[]{:S(2)}) async-start(f32[16,24,128]{2,1,0:T(8,128)} %bitcast.2), calls=%async_computation.1 | async-start | bytes 393216 | tf_op jit(solution)/shard_map/all_to_all | solution.py:615
  31.0 3.1 %collective-permute-start.5 = (f32[80,128]{1,0:T(8,128)S(1)}, f32[80,128]{1,0:T(8,128)S(1)}, u32[]{:S(2)}, u32[]{:S(2)}) collective-permute-start(f32[80,128]{1,0:T(8,128)S(1)} %get-tuple-element.80), channel_id=1, source_target_pairs={{0,4},{4,0},{8,12},{12,8},{16,20},{20,16},{24,28},{28,24},{32,36},... | collective-permute-start | bytes 122888 | tf_op jit(solution)/shard_map/ppermute | solution.py:643
  35.0 4.4 %collective-permute-start.6 = (f32[320,128]{1,0:T(8,128)S(1)}, f32[320,128]{1,0:T(8,128)S(1)}, u32[]{:S(2)}, u32[]{:S(2)}) collective-permute-start(f32[320,128]{1,0:T(8,128)S(1)} %get-tuple-element.87), channel_id=1, source_target_pairs={{0,4},{4,0},{8,12},{12,8},{16,20},{20,16},{24,28},{28,24},{32,36},... | collective-permute-start | bytes 491528 | tf_op jit(solution)/shard_map/ppermute | solution.py:646
